TPU v7x, 768 devices: a whole 4x8x12 slice. The times are simulated.
768 devices in a mesh: dp: 48 (over y, z_lo), ctx: 16 (over x, z_hi, core).
Axes of the slice: x: 4, y: 8, z: 12 (z_hi: 2, z_lo: 6; z = z_hi * 6 + z_lo), core: 2. Of those that a mesh axis runs over, the one named last changes fastest.
Arguments:
- grad_tokens: bfloat16 [12288, 8192], P(('dp', 'ctx')), may hold values from -9 to 9
- pre_act: bfloat16 [5120, 12288], P('ctx', 'dp'), may hold values from -6 to 6
- w_fc1: bfloat16 [5120, 5120], P(None, 'ctx'), may hold values from -0.078125 to 0.078125
- w_fc2: bfloat16 [5120, 8192], P(None, 'ctx'), may hold values from -0.078125 to 0.078125
- patch_in: bfloat16 [12288, 5120], P(('dp', 'ctx')), may hold values from -54 to 54
- norm_gain: float32 [1280], replicated, may hold values from 0.25 to 1.75
- owner_pos: int32 [12288], P('dp'), may hold values from 0 to 255, as said below
Outputs:
- patch_grad: bfloat16 [12288, 5120], P(('dp', 'ctx'))
- gain_grad: float32 [1280], replicated
Inputs may be any that keep to these rules, and one draw needn't show every extreme that they name: `owner_pos`: each group's 256 entries (g * 256 to g * 256 + 255) are a permutation of 0 to 255; entry g * 256 + o * 16 + i is the sequence position of owner o's token i. Of the 16 positions held by one ctx shard (s * 16 to s * 16 + 15), at most 2 belong to one owner, and in every group some shard gives exactly 2 to some owner.
All inputs are finite; a program needn't handle non-finite values.
Results may differ from a plain program's by a relative error of at most 0.0057.
Values may be sent and summed in bfloat16 or wider, within the bound.
No kernel may reach another device: no remote copies, remote signals or barrier semaphores. Data moves between devices by JAX's collectives and lax.ppermute only.
A program may use at most 64 MiB of HBM per device.

v0:
```python
import jax
import jax.numpy as jnp
from jax import lax
from jax.sharding import PartitionSpec as P


def gelu_slope(values):
    normal_cdf = 0.5 * (1.0 + lax.erf(values * 0.7071067811865476))
    density = jnp.exp(-0.5 * values * values) * 0.3989422804014327
    return normal_cdf + values * density


def deliver_rows(merged_rows, owner_pos, ctx_index, ctx_count):
    own_rows = merged_rows.shape[0]
    feature_count = merged_rows.shape[1]
    group_rows = owner_pos.shape[0]
    capacity = 2 * own_rows // ctx_count
    inverse = (
        jnp.zeros((group_rows,), jnp.int32)
        .at[owner_pos]
        .set(jnp.arange(group_rows, dtype=jnp.int32))
    )
    my_targets = lax.dynamic_slice_in_dim(inverse, ctx_index * own_rows, own_rows)
    target_owner = my_targets // own_rows
    target_slot = my_targets % own_rows
    owner_table = (target_owner[:, None] == jnp.arange(ctx_count, dtype=jnp.int32)[None, :]).astype(
        jnp.int32
    )
    rank_within = jnp.sum(jnp.cumsum(owner_table, axis=0) * owner_table, axis=1) - 1
    placement = target_owner * capacity + rank_within
    send_rows = (
        jnp.zeros((ctx_count * capacity, feature_count), jnp.bfloat16)
        .at[placement]
        .set(merged_rows)
    )
    send_slots = (
        jnp.full((ctx_count * capacity,), own_rows, jnp.int32).at[placement].set(target_slot)
    )
    got_rows, got_slots = (
        lax.all_to_all(
            send_rows.reshape(ctx_count, capacity, feature_count),
            "ctx",
            split_axis=0,
            concat_axis=0,
            tiled=True,
        ),
        lax.all_to_all(
            send_slots.reshape(ctx_count, capacity), "ctx", split_axis=0, concat_axis=0, tiled=True
        ),
    )
    landing = jnp.zeros((own_rows, feature_count), jnp.bfloat16)
    return landing.at[got_slots.reshape(-1)].set(got_rows.reshape(-1, feature_count), mode="drop")


def local(grad_tokens, pre_act, w_fc1, w_fc2, patch_in, norm_gain, owner_pos):
    ctx_count = lax.axis_size("ctx")
    ctx_index = lax.axis_index("ctx")
    column_grads = lax.all_to_all(grad_tokens, "ctx", split_axis=1, concat_axis=0, tiled=True)
    hidden_grad = lax.psum_scatter(
        lax.dot_general(
            w_fc2, column_grads, (((1,), (1,)), ((), ())), preferred_element_type=jnp.float32
        ),
        "ctx",
        scatter_dimension=0,
        tiled=True,
    )
    act_grad = (hidden_grad * gelu_slope(pre_act.astype(jnp.float32))).astype(jnp.bfloat16)
    merged_rows = lax.psum_scatter(
        lax.dot_general(
            act_grad, w_fc1, (((0,), (1,)), ((), ())), preferred_element_type=jnp.float32
        ),
        "ctx",
        scatter_dimension=0,
        tiled=True,
    ).astype(jnp.bfloat16)
    owner_grad = deliver_rows(merged_rows, owner_pos, ctx_index, ctx_count)
    width = norm_gain.shape[0]
    upstream = owner_grad.astype(jnp.float32).reshape(-1, width)
    patches = patch_in.astype(jnp.float32).reshape(-1, width)
    inv_rms = lax.rsqrt(jnp.mean(patches * patches, axis=-1, keepdims=True) + 1e-06)
    normed = patches * inv_rms
    scaled_grad = upstream * norm_gain
    inner_mean = jnp.mean(scaled_grad * normed, axis=-1, keepdims=True)
    patch_grad = (
        (inv_rms * (scaled_grad - normed * inner_mean)).astype(jnp.bfloat16).reshape(patch_in.shape)
    )
    local_terms = jnp.sum(upstream * normed, axis=0)
    gain_total = lax.psum(local_terms, ("dp", "ctx"))
    gain_grad = gain_total / (lax.axis_size("dp") * ctx_count)
    return (patch_grad, gain_grad)


def solution(mesh):
    return jax.shard_map(
        local,
        mesh=mesh,
        in_specs=(
            P(("dp", "ctx"), None),
            P("ctx", "dp"),
            P(None, "ctx"),
            P(None, "ctx"),
            P(("dp", "ctx"), None),
            P(),
            P("dp"),
        ),
        out_specs=(P(("dp", "ctx"), None), P()),
        check_vma=False,
    )
```

profile of v0, /device:TPU:1, one launch (start us, length us, event | category | flops | bytes accessed | tf_op | source)
XLA Modules:
  0.0 496.9 jit_solution(5049158549859848225)
XLA Ops:
  7.2 0.0 copy-start
  7.2 0.0 reduce-scatter.3.cloned.1.call-start
  7.2 1.1 copy.16
  8.3 32.0 %all_to_all.33 = bf16[16,16,512]{2,0,1:T(8,128)(2,1)S(1)} all-to-all(bf16[16,16,512]{2,0,1:T(8,128)(2,1)S(1)} %bitcast.22), channel_id=1, replica_groups=mesh['dp'=48,'ctx'=16] {'ctx'}, dimensions={1} | all-to-all | bytes 524288 | tf_op jit(solution)/shard_map/all_to_all | solution.py:58
  40.4 6.4 %fusion.31 = f32[5120,256]{1,0:T(8,128)} fusion(bf16[5120,512]{1,0:T(8,128)(2,1)} %param.10, bf16[256,512]{1,0:T(8,128)(2,1)S(1)} %bitcast.21), kind=kOutput, calls=%fused_computation.56 | convolution fusion | flops 1342177280 | bytes 10747904 | tf_op jit(solution)/shard_map/dot_general | solution.py:60
  46.7 0.0 reduce-scatter.3.cloned.1.call-update
  46.7 0.0 copy-start.4
  46.7 0.0 reduce-scatter.5.cloned.1.call-start
  46.8 150.3 %reduce-scatter.3.cloned.1.call-done = f32[320,256]{1,0:T(8,128)} async-done(((f32[5120,256]{1,0:T(8,128)}), f32[320,256]{1,0:T(8,128)}) %reduce-scatter.3.cloned.1.call-update) | async-done | bytes 327696 | tf_op jit(solution)/shard_map/reduce_scatter | solution.py:59
  197.1 0.0 copy-done
  197.1 0.0 copy-done.2
  197.1 4.9 fusion.8
  202.1 0.0 reduce-scatter.5.cloned.1.call-update
  202.1 0.0 copy-done.4
  202.1 1.4 scatter_custom_fusion
  203.5 0.1 and_select_fusion
  203.6 0.1 and_select_fusion.1
  203.7 0.1 fusion.20
  203.8 0.2 select_reduce_fusion
  204.0 0.6 scatter_custom_fusion.1
  204.6 0.7 all_to_all.23
  205.3 5.5 %all-to-all-start = ((s32[16,1,2]{2,1,0:T(1,128)}), s32[16,1,2]{2,1,0:T(1,128)S(1)}, u32[]{:S(2)}, u32[]{:S(2)}) async-start(s32[16,1,2]{2,1,0:T(1,128)} %bitcast), calls=%async_computation | async-start | bytes 16384 | tf_op jit(solution)/shard_map/all_to_all | solution.py:47
  210.9 135.2 %reduce-scatter.5.cloned.1.call-done = f32[16,5120]{1,0:T(8,128)} async-done(((f32[256,5120]{1,0:T(8,128)}), f32[16,5120]{1,0:T(8,128)}) %reduce-scatter.5.cloned.1.call-update) | async-done | bytes 327696 | tf_op jit(solution)/shard_map/reduce_scatter | solution.py:68
  346.0 2.0 scatter_custom_fusion.2
  348.0 1.8 reshape.91
  349.8 0.0 all-to-all-done
  349.8 5.8 %all-to-all-start.2 = ((bf16[16,2,5120]{2,1,0:T(2,128)(2,1)}), bf16[16,2,5120]{2,1,0:T(2,128)(2,1)}, u32[]{:S(2)}, u32[]{:S(2)}) async-start(bf16[16,2,5120]{2,1,0:T(2,128)(2,1)} %reshape.91), calls=%async_computation.4 | async-start | bytes 655360 | tf_op jit(solution)/shard_map/all_to_all | solution.py:40
  355.6 0.0 copy-done.1
  355.6 0.8 reshape.89
  356.5 1.1 multiply_reduce_fusion.2
  357.6 0.1 rsqrt.13
  357.7 0.1 mul.102
  357.8 0.8 copy.13
  358.6 0.0 copy-done.3
  358.6 0.5 broadcast.120
  359.1 0.7 reduce.3
  359.8 0.1 reshape.90
  359.9 10.4 %all-to-all-done.2 = bf16[16,2,5120]{2,1,0:T(2,128)(2,1)} async-done(((bf16[16,2,5120]{2,1,0:T(2,128)(2,1)}), bf16[16,2,5120]{2,1,0:T(2,128)(2,1)}, u32[]{:S(2)}, u32[]{:S(2)}) %all-to-all-start.2) | async-done | bytes 327712 | tf_op jit(solution)/shard_map/all_to_all | solution.py:40
  370.3 1.8 reshape.122
  372.1 1.5 scatter_custom_fusion.3
  373.6 0.8 reshape.93
  374.5 1.3 multiply_reduce_fusion
  375.8 0.1 div.32
  375.9 0.1 mul.128
  376.0 0.8 copy.14
  376.8 110.8 %psum.7 = f32[1280]{0:T(1024)S(1)} all-reduce(f32[1280]{0:T(1024)S(1)} %get-tuple-element.2), channel_id=1, replica_groups=mesh['dp'=48,'ctx'=16] {'dp','ctx'}, use_global_device_ids=true, to_apply=%region_11.12 | all-reduce | flops 1280 | bytes 10240 | tf_op jit(solution)/shard_map/psum | solution.py:88
  487.6 0.6 broadcast_multiply_fusion
  488.2 1.9 multiply_convert_fusion
  (12 shorter events, 0.1 us)
Async XLA Ops:
  7.2 190.0 %copy-start = (bf16[5120,320]{0,1:T(8,128)(2,1)S(1)}, bf16[5120,320]{0,1:T(8,128)(2,1)}, u32[]{:S(2)}) copy-start(bf16[5120,320]{0,1:T(8,128)(2,1)} %param.9) | copy-start | bytes 9830404
  7.2 190.0 %reduce-scatter.3.cloned.1.call-start = ((), (), s32[]{:S(2)}) async-start(), calls=%async_computation.5 | async-start | bytes 5570560 | tf_op jit(solution)/shard_map/reduce_scatter | solution.py:59
  46.7 150.4 %copy-start.2 = (bf16[320,256]{1,0:T(8,128)(2,1)S(1)}, bf16[320,256]{1,0:T(8,128)(2,1)}, u32[]{:S(2)}) copy-start(bf16[320,256]{1,0:T(8,128)(2,1)} %param.8) | copy-start | bytes 491524
  46.7 155.4 %copy-start.4 = (s32[256]{0:T(256)S(1)}, s32[256]{0:T(256)}, u32[]{:S(2)}) copy-start(s32[256]{0:T(256)} %param.13) | copy-start | bytes 3076
  46.7 299.3 %reduce-scatter.5.cloned.1.call-start = ((), (), s32[]{:S(2)}) async-start(), calls=%async_computation.6 | async-start | bytes 5570560 | tf_op jit(solution)/shard_map/reduce_scatter | solution.py:68
  202.1 153.6 %copy-start.1 = (bf16[16,5120]{1,0:T(8,128)(2,1)S(1)}, bf16[16,5120]{1,0:T(8,128)(2,1)}, u32[]{:S(2)}) copy-start(bf16[16,5120]{1,0:T(8,128)(2,1)} %param.11) | copy-start | bytes 491524
  202.1 156.5 %copy-start.3 = (f32[1280]{0:T(1024)S(1)}, f32[1280]{0:T(1024)}, u32[]{:S(2)}) copy-start(f32[1280]{0:T(1024)} %param.12) | copy-start | bytes 15364
  205.3 144.5 %all-to-all-start = ((s32[16,1,2]{2,1,0:T(1,128)}), s32[16,1,2]{2,1,0:T(1,128)S(1)}, u32[]{:S(2)}, u32[]{:S(2)}) async-start(s32[16,1,2]{2,1,0:T(1,128)} %bitcast), calls=%async_computation | async-start | bytes 16384 | tf_op jit(solution)/shard_map/all_to_all | solution.py:47
  349.8 20.5 %all-to-all-start.2 = ((bf16[16,2,5120]{2,1,0:T(2,128)(2,1)}), bf16[16,2,5120]{2,1,0:T(2,128)(2,1)}, u32[]{:S(2)}, u32[]{:S(2)}) async-start(bf16[16,2,5120]{2,1,0:T(2,128)(2,1)} %reshape.91), calls=%async_computation.4 | async-start | bytes 655360 | tf_op jit(solution)/shard_map/all_to_all | solution.py:40
Sparse Core Ops, SparseCore 0:
  46.9 150.2 reduce-scatter.2
  202.7 143.2 reduce-scatter.4
where the time goes:
time: 498 us; the launch traced here: 497 us
  waiting for transfers between devices  296 us (59%)
  blocking collectives  143 us (29%)
  between operations  14.2 us (3%)
  local copies, waits for them, and re-layouts  13.3 us (3%)
  starting transfers between devices  11.4 us (2%)
  matrix products  11.3 us (2%)
  other arithmetic  7.99 us (2%)
    reduce_scatter x1, waiting for transfers between devices, local(): lax.psum_scatter(lax.dot_general(w_fc2, column_grads, (((1,), (1,)), ((),...  150 us
    reduce_scatter x1, waiting for transfers between devices, local(): lax.psum_scatter(lax.dot_general(act_grad, w_fc1, (((0,), (1,)), ((), ())...  135 us
    psum x1, blocking collectives, local(): gain_total = lax.psum(local_terms, ('dp', 'ctx'))  111 us
    all_to_all x1, blocking collectives, local(): lax.all_to_all(grad_tokens, 'ctx', split_axis=1, concat_axis=0, tiled=True)  32 us
    all_to_all x1, waiting for transfers between devices, deliver_rows(): lax.all_to_all(send_rows.reshape(ctx_count, capacity, feature_count), 'ct...  10.4 us
  transfers between devices with their start and end apart: 4, of which 3 were waited for; matrix products, arithmetic and copies ran while one was open for 2% of the time, Pallas kernels for 0%

commit v1 on v0

v1 whole, which is shorter than its diff:
```python
import functools

import jax
import jax.numpy as jnp
from jax import lax
from jax.experimental import pallas as pl
from jax.experimental.pallas import tpu as pltpu
from jax.sharding import Mesh
from jax.sharding import PartitionSpec as P

NY, NZL, NX, NZH, NCO = 8, 6, 4, 2, 2
AXES = ("y", "zl", "x", "zh", "co")
DP = ("y", "zl")
CTX = ("x", "zh", "co")
EPS = 1e-06
F32 = jnp.float32
BF16 = jnp.bfloat16
VMEM_LIMIT = 40 * 1024 * 1024


def gelu_slope(values):
    normal_cdf = 0.5 * (1.0 + lax.erf(values * 0.7071067811865476))
    density = jnp.exp(-0.5 * values * values) * 0.3989422804014327
    return normal_cdf + values * density


def params():
    return pltpu.CompilerParams(vmem_limit_bytes=VMEM_LIMIT)


def cost(flops, nbytes):
    return pl.CostEstimate(flops=flops, bytes_accessed=nbytes, transcendentals=0)


def swap(value, axis):
    return lax.ppermute(value, axis, [(0, 1), (1, 0)])


def hidden_kernel(which, w_ref, t_ref, out_ref):
    n, m = out_ref.shape[1], out_ref.shape[2]
    w = w_ref[...].reshape(n * m, w_ref.shape[-1])
    acc = lax.dot_general(w, t_ref[...], (((1,), (1,)), ((), ())), preferred_element_type=F32)
    out_ref[...] = acc.reshape(out_ref.shape).astype(out_ref.dtype)


def hidden_part(w_fc2, tokens, which, out_dtype):
    rows, depth = w_fc2.shape
    block = rows // (NX * NZH * NCO)
    count = tokens.shape[0]
    w = w_fc2.reshape(NX, NZH, NCO, block, depth)
    return pl.pallas_call(
        hidden_kernel,
        grid_spec=pltpu.PrefetchScalarGridSpec(
            num_scalar_prefetch=1,
            grid=(NX,),
            in_specs=[
                pl.BlockSpec((1, NZH, 1, block, depth), lambda i, s: (i, 0, s[0], 0, 0)),
                pl.BlockSpec((count, depth), lambda i, s: (0, 0)),
            ],
            out_specs=pl.BlockSpec((1, NZH, block, count), lambda i, s: (i, 0, 0, 0)),
        ),
        out_shape=jax.ShapeDtypeStruct((NX, NZH, block, count), out_dtype),
        compiler_params=params(),
        cost_estimate=cost(rows * depth * count, rows * depth + rows * count),
        name="hidden_part",
    )(which.reshape(1), w, tokens)


def add_kernel(a_ref, b_ref, out_ref):
    out_ref[...] = (a_ref[...] + b_ref[...].astype(F32)).astype(BF16)


def add_round(kept, got):
    shape = kept.shape
    blocks = shape[0]
    spec = pl.BlockSpec((1,) + shape[1:], lambda i: (i,) + (0,) * (len(shape) - 1))
    return pl.pallas_call(
        add_kernel,
        grid=(blocks,),
        in_specs=[spec, spec],
        out_specs=spec,
        out_shape=jax.ShapeDtypeStruct(shape, BF16),
        compiler_params=params(),
        cost_estimate=cost(kept.size, kept.size * 8),
        name="add_round",
    )(kept, got)


def sum_kernel(which, v_ref, out_ref):
    total = v_ref[0, 0].astype(F32)
    for i in range(1, v_ref.shape[0]):
        total += v_ref[i, 0].astype(F32)
    out_ref[...] = total.astype(BF16)


def sum_part(parts, which):
    n, two, rows, cols = parts.shape
    return pl.pallas_call(
        sum_kernel,
        grid_spec=pltpu.PrefetchScalarGridSpec(
            num_scalar_prefetch=1,
            grid=(1,),
            in_specs=[pl.BlockSpec((n, 1, rows, cols), lambda i, s: (0, s[0], 0, 0))],
            out_specs=pl.BlockSpec((rows, cols), lambda i, s: (0, 0)),
        ),
        out_shape=jax.ShapeDtypeStruct((rows, cols), BF16),
        compiler_params=params(),
        cost_estimate=cost(n * rows * cols, n * rows * cols * 2),
        name="sum_part",
    )(which.reshape(1), parts)


def act_kernel(which, v_ref, got_ref, slope_ref, pos_ref, out_ref):
    hidden = got_ref[...].astype(F32)
    for i in range(v_ref.shape[0]):
        hidden += v_ref[i, 0].astype(F32)
    act = (hidden * slope_ref[...]).astype(BF16)
    count = act.shape[1]
    pick = (pos_ref[...] == lax.broadcasted_iota(jnp.int32, (count, count), 1)).astype(F32).astype(BF16)
    out_ref[...] = lax.dot_general(pick, act, (((1,), (1,)), ((), ())), preferred_element_type=F32).astype(BF16)


def act_rows(parts, which, got, slope, positions):
    n, two, rows, cols = parts.shape
    return pl.pallas_call(
        act_kernel,
        grid_spec=pltpu.PrefetchScalarGridSpec(
            num_scalar_prefetch=1,
            grid=(1,),
            in_specs=[
                pl.BlockSpec((n, 1, rows, cols), lambda i, s: (0, s[0], 0, 0)),
                pl.BlockSpec((rows, cols), lambda i, s: (0, 0)),
                pl.BlockSpec((rows, cols), lambda i, s: (0, 0)),
                pl.BlockSpec((cols, 1), lambda i, s: (0, 0)),
            ],
            out_specs=pl.BlockSpec((cols, rows), lambda i, s: (0, 0)),
        ),
        out_shape=jax.ShapeDtypeStruct((cols, rows), BF16),
        compiler_params=params(),
        cost_estimate=cost(2 * rows * cols * cols, rows * cols * 16),
        name="act_rows",
    )(which.reshape(1), parts, got, slope, positions)


def merged_kernel(a_ref, w_ref, out_ref):
    acc = lax.dot_general(a_ref[...], w_ref[...], (((1,), (0,)), ((), ())), preferred_element_type=F32)
    out_ref[...] = acc.astype(out_ref.dtype)


def merged_part(act, w_fc1_t, out_dtype):
    rows, depth = act.shape
    cols = w_fc1_t.shape[1]
    steps = 4
    return pl.pallas_call(
        merged_kernel,
        grid=(steps,),
        in_specs=[
            pl.BlockSpec((rows, depth), lambda i: (0, 0)),
            pl.BlockSpec((depth, cols // steps), lambda i: (0, i)),
        ],
        out_specs=pl.BlockSpec((rows, cols // steps), lambda i: (0, i)),
        out_shape=jax.ShapeDtypeStruct((rows, cols), out_dtype),
        compiler_params=params(),
        cost_estimate=cost(2 * rows * depth * cols, depth * cols * 2),
        name="merged_part",
    )(act, w_fc1_t)


def norm_kernel(which, v_ref, got_ref, patch_ref, gain_ref, out_ref, terms_ref):
    width = gain_ref.shape[1]
    gain = gain_ref[...]
    terms = jnp.zeros((1, width), F32)
    for p in range(patch_ref.shape[1] // width):
        cols = pl.ds(p * width, width)
        owner = got_ref[:, cols].astype(F32)
        for i in range(v_ref.shape[0]):
            owner += v_ref[i, 0, :, cols].astype(F32)
        owner = owner.astype(BF16).astype(F32)
        patch = patch_ref[:, cols].astype(F32)
        inv_rms = lax.rsqrt(jnp.mean(patch * patch, axis=-1, keepdims=True) + EPS)
        normed = patch * inv_rms
        scaled = owner * gain
        inner = jnp.mean(scaled * normed, axis=-1, keepdims=True)
        out_ref[:, cols] = (inv_rms * (scaled - normed * inner)).astype(BF16)
        terms += jnp.sum(owner * normed, axis=0, keepdims=True)
    terms_ref[...] = terms


def norm_part(parts, which, got, patch_in, norm_gain):
    n, two, rows, cols = parts.shape
    width = norm_gain.shape[0]
    return pl.pallas_call(
        norm_kernel,
        grid_spec=pltpu.PrefetchScalarGridSpec(
            num_scalar_prefetch=1,
            grid=(1,),
            in_specs=[
                pl.BlockSpec((n, 1, rows, cols), lambda i, s: (0, s[0], 0, 0)),
                pl.BlockSpec((rows, cols), lambda i, s: (0, 0)),
                pl.BlockSpec((rows, cols), lambda i, s: (0, 0)),
                pl.BlockSpec((1, width), lambda i, s: (0, 0)),
            ],
            out_specs=[
                pl.BlockSpec((rows, cols), lambda i, s: (0, 0)),
                pl.BlockSpec((1, width), lambda i, s: (0, 0)),
            ],
        ),
        out_shape=[
            jax.ShapeDtypeStruct((rows, cols), BF16),
            jax.ShapeDtypeStruct((1, width), F32),
        ],
        compiler_params=params(),
        cost_estimate=cost(rows * cols * 20, rows * cols * 16),
        name="norm_part",
    )(which.reshape(1), parts, got, patch_in, norm_gain.reshape(1, width))


def local(grad_tokens, pre_act, w_fc1, w_fc2, patch_in, norm_gain, owner_pos):
    zh = lax.axis_index("zh").astype(jnp.int32)
    co = lax.axis_index("co").astype(jnp.int32)
    ctx = NX * NZH * NCO
    own, width = grad_tokens.shape
    group = own * ctx
    features = patch_in.shape[1]
    slope = gelu_slope(pre_act.astype(F32))
    by_core = owner_pos.reshape(NX * NZH, NCO, own)
    theirs = lax.dynamic_index_in_dim(by_core, 1 - co, axis=1, keepdims=False)
    mine = lax.dynamic_index_in_dim(by_core, co, axis=1, keepdims=False)
    positions = jnp.concatenate([theirs.reshape(-1, 1), mine.reshape(-1, 1)], axis=0)
    with jax.named_scope("tokens"):
        outgoing = grad_tokens.reshape(own, ctx, width // ctx).transpose(1, 0, 2)
        tokens = lax.all_to_all(outgoing, CTX, 0, 0, tiled=True).reshape(group, width // ctx)
    with jax.named_scope("hidden"):
        sent = hidden_part(w_fc2, tokens, 1 - co, BF16)
        got = swap(sent, "co")
        kept = hidden_part(w_fc2, tokens, co, F32)
        parts = add_round(kept, got)
        parts = lax.all_to_all(parts, "x", 0, 0, tiled=True)
        got = swap(sum_part(parts, 1 - zh), "zh")
    with jax.named_scope("merged"):
        act = act_rows(parts, zh, got, slope, positions)
        half = group // NCO
        w_fc1_t = w_fc1.T
        sent = merged_part(act[:half], w_fc1_t, BF16)
        got = swap(sent, "co")
        kept = merged_part(act[half:], w_fc1_t, F32)
        parts = add_round(
            kept.reshape(NX, NZH * own, features), got.reshape(NX, NZH * own, features)
        )
        parts = lax.all_to_all(parts, "x", 0, 0, tiled=True).reshape(NX, NZH, own, features)
        got = swap(sum_part(parts, 1 - zh), "zh")
    with jax.named_scope("norm"):
        patch_grad, terms = norm_part(parts, zh, got, patch_in, norm_gain)
    with jax.named_scope("gain"):
        terms = terms.reshape(-1)
        for axis in ("co", "x", "y"):
            terms = lax.psum(terms, axis)
        rows = terms.reshape(1, -1, 128)
        rows = jnp.broadcast_to(rows, (NZL * NZH,) + rows.shape[1:])
        rows = lax.all_to_all(rows, ("zl", "zh"), 0, 0, tiled=True)
        total = jnp.sum(rows, axis=0).reshape(-1)
        gain_grad = total / (NY * NZL * ctx)
    return (patch_grad, gain_grad)


def solution(mesh):
    fine = Mesh(mesh.devices.reshape(NY, NZL, NX, NZH, NCO), AXES)
    return jax.shard_map(
        local,
        mesh=fine,
        in_specs=(
            P(DP + CTX, None),
            P(CTX, DP),
            P(None, CTX),
            P(None, CTX),
            P(DP + CTX, None),
            P(),
            P(DP),
        ),
        out_specs=(P(DP + CTX, None), P()),
        check_vma=False,
    )
```

time: 498 us -> 181 us (0.36)
  the two profiles are of different devices: /device:TPU:1 before, /device:TPU:2 now
where the time goes in v1:
time: 181 us
  blocking collectives  67.4 us (37%)
  waiting for transfers between devices  64.6 us (36%)
  starting transfers between devices  32.3 us (18%)
  Pallas kernels  10.2 us (6%)
  local copies, waits for them, and re-layouts  4.63 us (3%)
    ppermute x4, waiting for transfers between devices, swap(): return lax.ppermute(value, axis, [(0, 1), (1, 0)])  35.8 us
    psum x3, blocking collectives, local(): terms = lax.psum(terms, axis)  29.7 us
    all_to_all x1, blocking collectives, local(): lax.all_to_all(parts, 'x', 0, 0, tiled=True).reshape(NX, NZH, own, features)  20.9 us
    all_to_all x1, starting transfers between devices, local(): lax.all_to_all(outgoing, CTX, 0, 0, tiled=True).reshape(group, width // ctx)  17.5 us
    all_to_all x1, blocking collectives, local(): rows = lax.all_to_all(rows, ('zl', 'zh'), 0, 0, tiled=True)  16.9 us
    all_to_all x1, waiting for transfers between devices, local(): parts = lax.all_to_all(parts, 'x', 0, 0, tiled=True)  16.6 us
    all_to_all x1, waiting for transfers between devices, local(): lax.all_to_all(outgoing, CTX, 0, 0, tiled=True).reshape(group, width // ctx)  12.2 us
    ppermute x4, starting transfers between devices, swap(): return lax.ppermute(value, axis, [(0, 1), (1, 0)])  8.7 us
  transfers between devices with their start and end apart: 6, of which 6 were waited for; matrix products, arithmetic and copies ran while one was open for 0% of the time, Pallas kernels for 2%

profile of v1, /device:TPU:2, one launch (start us, length us, event | category | flops | bytes accessed | tf_op | source)
XLA Modules:
  0.0 180.7 jit_solution(9914527035460935281)
XLA Ops:
  0.6 1.7 copy.25
  2.3 17.5 %all-to-all-start = ((bf16[16,16,512]{2,1,0:T(8,128)(2,1)}), bf16[16,16,512]{2,1,0:T(8,128)(2,1)S(1)}, u32[]{:S(2)}, u32[]{:S(2)}) async-start(bf16[16,16,512]{2,1,0:T(8,128)(2,1)} %bitcast.19), calls=%async_computation | async-start | bytes 524288 | tf_op jit(solution)/shard_map/tokens/all_to_all | solution.py:232
  19.8 12.2 %all-to-all-done = bf16[16,16,512]{2,1,0:T(8,128)(2,1)S(1)} async-done(((bf16[16,16,512]{2,1,0:T(8,128)(2,1)}), bf16[16,16,512]{2,1,0:T(8,128)(2,1)S(1)}, u32[]{:S(2)}, u32[]{:S(2)}) %all-to-all-start) | async-done | bytes 262176 | tf_op jit(solution)/shard_map/tokens/all_to_all | solution.py:232
  32.0 0.0 copy-start
  32.0 2.5 %copy-done = bf16[5120,512]{1,0:T(8,128)(2,1)S(1)} copy-done((bf16[5120,512]{1,0:T(8,128)(2,1)S(1)}, bf16[5120,512]{1,0:T(8,128)(2,1)}, u32[]{:S(2)}) %copy-start) | copy-done | bytes 5242904
  34.5 0.0 copy-start.1
  34.5 1.7 hidden_part.3
  36.2 2.4 %collective-permute-start = (bf16[4,2,320,256]{3,2,1,0:T(8,128)(2,1)S(1)}, bf16[4,2,320,256]{3,2,1,0:T(8,128)(2,1)S(1)}, u32[]{:S(2)}, u32[]{:S(2)}) collective-permute-start(bf16[4,2,320,256]{3,2,1,0:T(8,128)(2,1)S(1)} %hidden_part.3), channel_id=1, source_target_pairs={{0,1},{1,0},{2,3},{3,2},{4,5},{5,4},{6,7},{7,6},{8,9},{9,8},{10,11... | collective-permute-start | bytes 3932168 | tf_op jit(solution)/shard_map/hidden/ppermute | solution.py:36
  38.6 0.0 copy-done.1
  38.6 1.7 hidden_part.2.a_ref
  40.4 0.9 collective-permute-done.b_ref
  41.3 1.7 add_round.2
  42.9 0.0 copy-start.6
  42.9 6.1 %all-to-all-start.1 = ((bf16[4,2,320,256]{3,2,1,0:T(8,128)(2,1)}), bf16[4,2,320,256]{3,2,1,0:T(8,128)(2,1)S(1)}, u32[]{:S(2)}, u32[]{:S(2)}) async-start(bf16[4,2,320,256]{3,2,1,0:T(8,128)(2,1)} %add_round.2), calls=%async_computation.1 | async-start | bytes 2621440 | tf_op jit(solution)/shard_map/hidden/all_to_all | solution.py:238
  49.0 0.0 copy-start.4
  49.0 0.0 copy-done.6
  49.0 0.1 reshape.66
  49.1 0.1 reshape.68
  49.2 0.1 reshape.67
  49.3 0.1 copy.20.pos_ref
  49.4 16.6 %all-to-all-done.1.v_ref = bf16[4,2,320,256]{3,2,1,0:T(8,128)(2,1)S(1)} async-done(((bf16[4,2,320,256]{3,2,1,0:T(8,128)(2,1)}), bf16[4,2,320,256]{3,2,1,0:T(8,128)(2,1)S(1)}, u32[]{:S(2)}, u32[]{:S(2)}) %all-to-all-start.1) | async-done | bytes 1310752 | tf_op jit(solution)/shard_map/hidden/all_to_all | solution.py:238
  66.0 0.0 copy-start.2
  66.0 0.1 sum_part.2
  66.1 2.4 %collective-permute-start.1 = (bf16[320,256]{1,0:T(8,128)(2,1)S(1)}, bf16[320,256]{1,0:T(8,128)(2,1)S(1)}, u32[]{:S(2)}, u32[]{:S(2)}) collective-permute-start(bf16[320,256]{1,0:T(8,128)(2,1)S(1)} %sum_part.2), channel_id=1, source_target_pairs={{0,2},{2,0},{1,3},{3,1},{4,6},{6,4},{5,7},{7,5},{8,10},{10,8},{9,1... | collective-permute-start | bytes 491528 | tf_op jit(solution)/shard_map/hidden/ppermute | solution.py:36
  68.6 0.0 copy-done.4
  68.6 0.1 fusion.3.slope_ref
  68.7 18.3 %collective-permute-done.1.got_ref = bf16[320,256]{1,0:T(8,128)(2,1)S(1)} collective-permute-done((bf16[320,256]{1,0:T(8,128)(2,1)S(1)}, bf16[320,256]{1,0:T(8,128)(2,1)S(1)}, u32[]{:S(2)}, u32[]{:S(2)}) %collective-permute-start.1) | collective-permute-done | bytes 163872 | tf_op jit(solution)/shard_map/hidden/ppermute | solution.py:36
  87.0 0.3 act_rows.1
  87.4 0.0 copy-done.2
  87.4 1.7 merged_part.3
  89.1 1.9 %collective-permute-start.2 = (bf16[128,5120]{1,0:T(8,128)(2,1)S(1)}, bf16[128,5120]{1,0:T(8,128)(2,1)S(1)}, u32[]{:S(2)}, u32[]{:S(2)}) collective-permute-start(bf16[128,5120]{1,0:T(8,128)(2,1)S(1)} %merged_part.3), channel_id=1, source_target_pairs={{0,1},{1,0},{2,3},{3,2},{4,5},{5,4},{6,7},{7,6},{8,9},{9,8},{10,11... | collective-permute-start | bytes 3932168 | tf_op jit(solution)/shard_map/merged/ppermute | solution.py:36
  91.0 1.7 merged_part.2
  92.7 1.3 collective-permute-done.2
  94.0 0.3 add_round.3
  94.3 20.9 %all_to_all.20 = bf16[4,32,5120]{2,1,0:T(8,128)(2,1)S(1)} all-to-all(bf16[4,32,5120]{2,1,0:T(8,128)(2,1)S(1)} %add_round.3), channel_id=1, replica_groups=mesh['y'=8,'zl'=6,'x'=4,'zh'=2,'co'=2] {'x'}, dimensions={0} | all-to-all | bytes 2621440 | tf_op jit(solution)/shard_map/merged/all_to_all | solution.py:250
  115.2 0.0 copy-start.5
  115.2 0.0 copy-start.3
  115.2 0.1 sum_part.3
  115.3 1.9 %collective-permute-start.3 = (bf16[16,5120]{1,0:T(8,128)(2,1)S(1)}, bf16[16,5120]{1,0:T(8,128)(2,1)S(1)}, u32[]{:S(2)}, u32[]{:S(2)}) collective-permute-start(bf16[16,5120]{1,0:T(8,128)(2,1)S(1)} %sum_part.3), channel_id=1, source_target_pairs={{0,2},{2,0},{1,3},{3,1},{4,6},{6,4},{5,7},{7,5},{8,10},{10,8},{9,1... | collective-permute-start | bytes 491528 | tf_op jit(solution)/shard_map/merged/ppermute | solution.py:36
  117.2 0.0 copy-done.5
  117.3 15.3 %collective-permute-done.3.got_ref = bf16[16,5120]{1,0:T(8,128)(2,1)S(1)} collective-permute-done((bf16[16,5120]{1,0:T(8,128)(2,1)S(1)}, bf16[16,5120]{1,0:T(8,128)(2,1)S(1)}, u32[]{:S(2)}, u32[]{:S(2)}) %collective-permute-start.3) | collective-permute-done | bytes 163872 | tf_op jit(solution)/shard_map/merged/ppermute | solution.py:36
  132.5 0.0 copy-done.3
  132.5 1.0 norm_part.1
  133.5 2.5 %psum.21 = f32[1280]{0:T(1024)S(1)} all-reduce(f32[1280]{0:T(1024)S(1)} %reduce.2), channel_id=1, replica_groups=mesh['y'=8,'zl'=6,'x'=4,'zh'=2,'co'=2] {'co'}, use_global_device_ids=true, to_apply=%region_0.1 | all-reduce | flops 1280 | bytes 10240 | tf_op jit(solution)/shard_map/gain/psum | solution.py:257
  136.0 9.3 %psum.22 = f32[1280]{0:T(1024)S(1)} all-reduce(f32[1280]{0:T(1024)S(1)} %psum.21), channel_id=1, replica_groups=mesh['y'=8,'zl'=6,'x'=4,'zh'=2,'co'=2] {'x'}, use_global_device_ids=true, to_apply=%region_1.2 | all-reduce | flops 1280 | bytes 10240 | tf_op jit(solution)/shard_map/gain/psum | solution.py:257
  145.3 17.9 %psum.23 = f32[10,128]{1,0:T(8,128)S(1)} all-reduce(f32[10,128]{1,0:T(8,128)S(1)} %bitcast.31), channel_id=1, replica_groups=mesh['y'=8,'zl'=6,'x'=4,'zh'=2,'co'=2] {'y'}, use_global_device_ids=true, to_apply=%region_2.3 | all-reduce | flops 1280 | bytes 10240 | tf_op jit(solution)/shard_map/gain/psum | solution.py:257
  163.2 16.9 %all_to_all.21 = f32[12,10,128]{2,1,0:T(8,128)S(1)} all-to-all(f32[12,10,128]{2,1,0:T(8,128)S(1)} %broadcast_in_dim.8), channel_id=1, replica_groups=mesh['y'=8,'zl'=6,'x'=4,'zh'=2,'co'=2] {'zl','zh'}, dimensions={0} | all-to-all | bytes 122880 | tf_op jit(solution)/shard_map/gain/all_to_all | solution.py:260
  180.1 0.6 multiply_bitcast_fusion
  (7 shorter events, 0.1 us)
Async XLA Ops:
  2.3 29.7 %all-to-all-start = ((bf16[16,16,512]{2,1,0:T(8,128)(2,1)}), bf16[16,16,512]{2,1,0:T(8,128)(2,1)S(1)}, u32[]{:S(2)}, u32[]{:S(2)}) async-start(bf16[16,16,512]{2,1,0:T(8,128)(2,1)} %bitcast.19), calls=%async_computation | async-start | bytes 524288 | tf_op jit(solution)/shard_map/tokens/all_to_all | solution.py:232
  32.0 2.5 %copy-start = (bf16[5120,512]{1,0:T(8,128)(2,1)S(1)}, bf16[5120,512]{1,0:T(8,128)(2,1)}, u32[]{:S(2)}) copy-start(bf16[5120,512]{1,0:T(8,128)(2,1)} %param.10) | copy-start | bytes 15728644
  34.5 4.1 %copy-start.1 = (bf16[5120,512]{1,0:T(8,128)(2,1)S(1)}, bf16[5120,512]{1,0:T(8,128)(2,1)}, u32[]{:S(2)}) copy-start(bf16[5120,512]{1,0:T(8,128)(2,1)} %param.10) | copy-start | bytes 15728644
  36.2 5.1 %collective-permute-start = (bf16[4,2,320,256]{3,2,1,0:T(8,128)(2,1)S(1)}, bf16[4,2,320,256]{3,2,1,0:T(8,128)(2,1)S(1)}, u32[]{:S(2)}, u32[]{:S(2)}) collective-permute-start(bf16[4,2,320,256]{3,2,1,0:T(8,128)(2,1)S(1)} %hidden_part.3), channel_id=1, source_target_pairs={{0,1},{1,0},{2,3},{3,2},{4,5},{5,4},{6,7},{7,6},{8,9},{9,8},{10,11... | collective-permute-start | bytes 3932168 | tf_op jit(solution)/shard_map/hidden/ppermute | solution.py:36
  42.9 6.1 %copy-start.6 = (s32[256]{0:T(256)S(1)}, s32[256]{0:T(256)}, u32[]{:S(2)}) copy-start(s32[256]{0:T(256)} %param.13) | copy-start | bytes 3076
  42.9 23.1 %all-to-all-start.1 = ((bf16[4,2,320,256]{3,2,1,0:T(8,128)(2,1)}), bf16[4,2,320,256]{3,2,1,0:T(8,128)(2,1)S(1)}, u32[]{:S(2)}, u32[]{:S(2)}) async-start(bf16[4,2,320,256]{3,2,1,0:T(8,128)(2,1)} %add_round.2), calls=%async_computation.1 | async-start | bytes 2621440 | tf_op jit(solution)/shard_map/hidden/all_to_all | solution.py:238
  49.0 19.6 %copy-start.4 = (bf16[320,256]{1,0:T(8,128)(2,1)S(1)}, bf16[320,256]{1,0:T(8,128)(2,1)}, u32[]{:S(2)}) copy-start(bf16[320,256]{1,0:T(8,128)(2,1)} %param.8) | copy-start | bytes 491524
  66.0 21.4 %copy-start.2 = (bf16[5120,320]{0,1:T(8,128)(2,1)S(1)}, bf16[5120,320]{0,1:T(8,128)(2,1)}, u32[]{:S(2)}) copy-start(bf16[5120,320]{0,1:T(8,128)(2,1)} %param.9) | copy-start | bytes 9830404
  66.1 20.9 %collective-permute-start.1 = (bf16[320,256]{1,0:T(8,128)(2,1)S(1)}, bf16[320,256]{1,0:T(8,128)(2,1)S(1)}, u32[]{:S(2)}, u32[]{:S(2)}) collective-permute-start(bf16[320,256]{1,0:T(8,128)(2,1)S(1)} %sum_part.2), channel_id=1, source_target_pairs={{0,2},{2,0},{1,3},{3,1},{4,6},{6,4},{5,7},{7,5},{8,10},{10,8},{9,1... | collective-permute-start | bytes 491528 | tf_op jit(solution)/shard_map/hidden/ppermute | solution.py:36
  89.1 4.9 %collective-permute-start.2 = (bf16[128,5120]{1,0:T(8,128)(2,1)S(1)}, bf16[128,5120]{1,0:T(8,128)(2,1)S(1)}, u32[]{:S(2)}, u32[]{:S(2)}) collective-permute-start(bf16[128,5120]{1,0:T(8,128)(2,1)S(1)} %merged_part.3), channel_id=1, source_target_pairs={{0,1},{1,0},{2,3},{3,2},{4,5},{5,4},{6,7},{7,6},{8,9},{9,8},{10,11... | collective-permute-start | bytes 3932168 | tf_op jit(solution)/shard_map/merged/ppermute | solution.py:36
  115.2 2.0 %copy-start.5 = (f32[1280]{0:T(1024)S(1)}, f32[1280]{0:T(1024)}, u32[]{:S(2)}) copy-start(f32[1280]{0:T(1024)} %param.12) | copy-start | bytes 15364
  115.2 17.3 %copy-start.3 = (bf16[16,5120]{1,0:T(8,128)(2,1)S(1)}, bf16[16,5120]{1,0:T(8,128)(2,1)}, u32[]{:S(2)}) copy-start(bf16[16,5120]{1,0:T(8,128)(2,1)} %patch_ref.1) | copy-start | bytes 491524
  115.3 17.2 %collective-permute-start.3 = (bf16[16,5120]{1,0:T(8,128)(2,1)S(1)}, bf16[16,5120]{1,0:T(8,128)(2,1)S(1)}, u32[]{:S(2)}, u32[]{:S(2)}) collective-permute-start(bf16[16,5120]{1,0:T(8,128)(2,1)S(1)} %sum_part.3), channel_id=1, source_target_pairs={{0,2},{2,0},{1,3},{3,1},{4,6},{6,4},{5,7},{7,5},{8,10},{10,8},{9,1... | collective-permute-start | bytes 491528 | tf_op jit(solution)/shard_map/merged/ppermute | solution.py:36

commit v2 on v0

v2 whole, which is shorter than its diff:
```python
import functools

import jax
import jax.numpy as jnp
from jax import lax
from jax.experimental import pallas as pl
from jax.experimental.pallas import tpu as pltpu
from jax.sharding import Mesh
from jax.sharding import PartitionSpec as P

NY, NZL, NX, NZH, NCO = 8, 6, 4, 2, 2
AXES = ("y", "zl", "x", "zh", "co")
DP = ("y", "zl")
CTX = ("x", "zh", "co")
EPS = 1e-06
F32 = jnp.float32
BF16 = jnp.bfloat16


def gelu_slope(values):
    normal_cdf = 0.5 * (1.0 + lax.erf(values * 0.7071067811865476))
    density = jnp.exp(-0.5 * values * values) * 0.3989422804014327
    return normal_cdf + values * density


def params(mib=12):
    return pltpu.CompilerParams(vmem_limit_bytes=mib * 1024 * 1024)


def cost():
    return pl.CostEstimate(flops=1, bytes_accessed=1, transcendentals=0)


def swap(value, axis):
    return lax.ppermute(value, axis, [(0, 1), (1, 0)])


def hidden_kernel(place, own_w, got_w, own_t, got_t, out_ref):
    total = None
    for w_ref, t_ref in ((own_w, own_t), (got_w, got_t)):
        term = lax.dot_general(
            w_ref[0, 0], t_ref[...], (((1,), (1,)), ((), ())), preferred_element_type=F32
        )
        total = term if total is None else total + term
    out_ref[0] = total.astype(BF16)


def hidden_part(weights, tokens, place):
    _, _, units, depth = weights[0].shape
    count = tokens[0].shape[0]
    w_spec = pl.BlockSpec((1, 1, units, depth), lambda i, s: (i, s[0], 0, 0))
    t_spec = pl.BlockSpec((count, depth), lambda i, s: (0, 0))
    return pl.pallas_call(
        hidden_kernel,
        grid_spec=pltpu.PrefetchScalarGridSpec(
            num_scalar_prefetch=1,
            grid=(NX,),
            in_specs=[w_spec, w_spec, t_spec, t_spec],
            out_specs=pl.BlockSpec((1, units, count), lambda i, s: (i, 0, 0)),
        ),
        out_shape=jax.ShapeDtypeStruct((NX, units, count), BF16),
        compiler_params=params(),
        cost_estimate=cost(),
        name="hidden_part",
    )(place, *weights, *tokens)


def total_of(ref):
    total = ref[0].astype(F32)
    for i in range(1, ref.shape[0]):
        total += ref[i].astype(F32)
    return total


def sum_kernel(v_ref, out_ref):
    out_ref[...] = total_of(v_ref).astype(BF16)


def sum_parts(parts):
    return pl.pallas_call(
        sum_kernel,
        out_shape=jax.ShapeDtypeStruct(parts.shape[1:], BF16),
        compiler_params=params(),
        cost_estimate=cost(),
        name="sum_parts",
    )(parts)


def act_kernel(v_ref, got_ref, slope_ref, pos_ref, out_ref):
    act = (total_of(v_ref) + got_ref[...].astype(F32)) * slope_ref[...]
    high = act.astype(BF16)
    low = (act - high.astype(F32)).astype(BF16)
    count = act.shape[1]
    pick = (lax.broadcasted_iota(jnp.int32, (count, count), 0) == pos_ref[...]).astype(F32)
    pick = pick.T.astype(BF16)
    for k, value in enumerate((high, low)):
        moved = lax.dot_general(pick, value, (((1,), (1,)), ((), ())), preferred_element_type=F32)
        out_ref[k] = moved.astype(BF16).reshape(out_ref.shape[1:])


def act_rows(parts, got, slope, owner_pos):
    units, count = got.shape
    return pl.pallas_call(
        act_kernel,
        out_shape=jax.ShapeDtypeStruct((2, NX, NZH, count // (NX * NZH), units), BF16),
        compiler_params=params(),
        cost_estimate=cost(),
        name="act_rows",
    )(parts, got, slope, owner_pos.reshape(1, count))


def merged_kernel(place, own_a, got_a, own_w, got_w, out_ref):
    depth = own_w.shape[0]
    total = None
    for a_ref, w_ref in ((own_a, own_w), (got_a, got_w)):
        term = lax.dot_general(
            a_ref[...].reshape(-1, depth),
            w_ref[...],
            (((1,), (0,)), ((), ())),
            preferred_element_type=F32,
        )
        total = term if total is None else total + term
    rows = total.shape[0] // 2
    out_ref[...] = (total[:rows] + total[rows:]).astype(BF16).reshape(out_ref.shape)


def merged_part(acts, weights, place):
    two, _, _, rows, depth = acts[0].shape
    cols = weights[0].shape[1]
    steps = 2
    a_spec = pl.BlockSpec((two, NX, 1, rows, depth), lambda i, s: (0, 0, s[0], 0, 0))
    w_spec = pl.BlockSpec((depth, cols // steps), lambda i, s: (0, i))
    return pl.pallas_call(
        merged_kernel,
        grid_spec=pltpu.PrefetchScalarGridSpec(
            num_scalar_prefetch=1,
            grid=(steps,),
            in_specs=[a_spec, a_spec, w_spec, w_spec],
            out_specs=pl.BlockSpec((NX, rows, cols // steps), lambda i, s: (0, 0, i)),
        ),
        out_shape=jax.ShapeDtypeStruct((NX, rows, cols), BF16),
        compiler_params=params(),
        cost_estimate=cost(),
        name="merged_part",
    )(place, *acts, *weights)


def halves_kernel(v_ref, out_ref):
    for c in range(NCO):
        total = v_ref[c].astype(F32)
        for x in range(1, NX):
            total += v_ref[NCO * x + c].astype(F32)
        out_ref[c] = total.astype(BF16)


def sum_halves(parts):
    return pl.pallas_call(
        halves_kernel,
        out_shape=jax.ShapeDtypeStruct((NCO,) + parts.shape[1:], BF16),
        compiler_params=params(),
        cost_estimate=cost(),
        name="sum_halves",
    )(parts)


def norm_of(patch):
    inv_rms = lax.rsqrt(jnp.mean(patch * patch, axis=-1, keepdims=True) + EPS)
    return patch * inv_rms, inv_rms


def gain_kernel(place, far_ref, near_ref, patch_ref, out_ref):
    width = out_ref.shape[1]
    terms = jnp.zeros((1, width), F32)
    for grad_ref, z in ((far_ref, 1 - place[0]), (near_ref, place[0])):
        for i in range(grad_ref.shape[0]):
            for p in range(grad_ref.shape[2] // width):
                cols = pl.ds(p * width, width)
                normed, _ = norm_of(patch_ref[i, z, :, cols].astype(F32))
                terms += jnp.sum(grad_ref[i, :, cols].astype(F32) * normed, axis=0, keepdims=True)
    out_ref[...] = terms


def gain_terms(far, near, patches, place, width):
    vmem = pl.BlockSpec(memory_space=pltpu.VMEM)
    return pl.pallas_call(
        gain_kernel,
        in_specs=[pl.BlockSpec(memory_space=pltpu.SMEM), vmem, vmem, vmem],
        out_specs=vmem,
        out_shape=jax.ShapeDtypeStruct((1, width), F32),
        compiler_params=params(),
        cost_estimate=cost(),
        name="gain_terms",
    )(place, far, near, patches)


def norm_kernel(v_ref, got_ref, patch_ref, gain_ref, out_ref):
    width = gain_ref.shape[1]
    gain = gain_ref[...]
    in_half = patch_ref.shape[1] // width // NCO
    for p in range(patch_ref.shape[1] // width):
        c, q = p // in_half, pl.ds(p % in_half * width, width)
        cols = pl.ds(p * width, width)
        owner = got_ref[c, :, q].astype(F32)
        for x in range(NX):
            owner += v_ref[NCO * x + c, :, q].astype(F32)
        normed, inv_rms = norm_of(patch_ref[:, cols].astype(F32))
        scaled = owner * gain
        inner = jnp.mean(scaled * normed, axis=-1, keepdims=True)
        out_ref[:, cols] = (inv_rms * (scaled - normed * inner)).astype(BF16)


def norm_part(parts, got, patch_in, norm_gain):
    return pl.pallas_call(
        norm_kernel,
        out_shape=jax.ShapeDtypeStruct(patch_in.shape, BF16),
        compiler_params=params(),
        cost_estimate=cost(),
        name="norm_part",
    )(parts, got, patch_in, norm_gain.reshape(1, -1))


def sum_over(terms, axes, count):
    rows = jnp.broadcast_to(terms[None], (count,) + terms.shape)
    return jnp.sum(lax.all_to_all(rows, axes, 0, 0, tiled=True), axis=0)


def local(grad_tokens, pre_act, w_fc1, w_fc2, patch_in, norm_gain, owner_pos):
    zh = lax.axis_index("zh").astype(jnp.int32)
    co = lax.axis_index("co").astype(jnp.int32)
    ctx = NX * NZH * NCO
    own, depth = grad_tokens.shape
    group = own * ctx
    width = norm_gain.shape[0]
    slope = gelu_slope(pre_act.astype(F32))
    far_z, near_z = (1 - zh).reshape(1), zh.reshape(1)
    features = patch_in.shape[1]
    half = features // NCO
    with jax.named_scope("tokens"):
        outgoing = grad_tokens.reshape(own, ctx, depth // ctx).transpose(1, 0, 2)
        outgoing, w_fc1, w_fc2, rows = lax.optimization_barrier((outgoing, w_fc1, w_fc2, patch_in))
        tokens = lax.all_to_all(outgoing, CTX, 0, 0, tiled=True).reshape(group, depth // ctx)
        tokens = (tokens, swap(tokens, "co"))
    with jax.named_scope("weights"):
        units = w_fc2.shape[0] // ctx
        w = w_fc2.reshape(NX, NZH, NCO, units, depth // ctx)
        take = lambda c: lax.dynamic_index_in_dim(w, c, axis=2, keepdims=False)
        weights_2 = (take(co), swap(take(1 - co), "co"))
        w_t = w_fc1.T
        take_1 = lambda c: lax.dynamic_slice_in_dim(w_t, c * half, half, axis=1)
        weights_1 = (take_1(co), swap(take_1(1 - co), "co"))
    with jax.named_scope("patches"):
        take_p = lambda c: lax.dynamic_slice_in_dim(rows, c * half, half, axis=1)
        kept, got = take_p(co), swap(take_p(1 - co), "co")
        both = jnp.where(co == 0, jnp.stack([kept, got]), jnp.stack([got, kept]))
        patches = lax.all_gather(both.reshape(NCO * own, half), ("x", "zh"))
        patches = patches.reshape(NX, NZH, NCO * own, half)
    with jax.named_scope("hidden"):
        far_sum = hidden_part(weights_2, tokens, far_z)
        far = lax.all_to_all(far_sum, "x", 0, 0, tiled=True)
        far = sum_parts(far)
        tokens, _ = lax.optimization_barrier((tokens, far))
        near_sum = hidden_part(weights_2, tokens, near_z)
        near = lax.all_to_all(near_sum, "x", 0, 0, tiled=True)
        got = swap(far, "zh")
    with jax.named_scope("merged"):
        act = act_rows(near, got, slope, owner_pos)
        acts = (act, swap(act, "co"))
        far_sum = merged_part(acts, weights_1, far_z)
        deliver = lambda v: lax.all_to_all(
            v.reshape(NX * NCO, own, half), ("x", "co"), 0, 0, tiled=True
        )
        far = deliver(far_sum)
        acts, _ = lax.optimization_barrier((acts, far_sum))
        near_sum = merged_part(acts, weights_1, near_z)
        far = sum_halves(far)
        late_sum, _ = lax.optimization_barrier((near_sum, far))
        near = deliver(late_sum)
        got = swap(far, "zh")
    with jax.named_scope("gain"):
        terms = gain_terms(far_sum, near_sum, patches, near_z, width).reshape(-1, 128)
        terms = lax.psum(lax.psum(terms, "co"), "x")
        terms, _ = lax.optimization_barrier((terms, near))
        terms = lax.psum(terms, "y")
        terms = sum_over(terms, ("zl", "zh"), NZL * NZH)
        gain_grad = terms.reshape(-1) / (NY * NZL * ctx)
    with jax.named_scope("norm"):
        patch_grad = norm_part(near, got, patch_in, norm_gain)
    return (patch_grad, gain_grad)


def solution(mesh):
    fine = Mesh(mesh.devices.reshape(NY, NZL, NX, NZH, NCO), AXES)
    return jax.shard_map(
        local,
        mesh=fine,
        in_specs=(
            P(DP + CTX, None),
            P(CTX, DP),
            P(None, CTX),
            P(None, CTX),
            P(DP + CTX, None),
            P(),
            P(DP),
        ),
        out_specs=(P(DP + CTX, None), P()),
        check_vma=False,
    )
```

time: 498 us -> 228 us (0.46)
  the two profiles are of different devices: /device:TPU:1 before, /device:TPU:24 now
where the time goes in v2:
time: 228 us; the launch traced here: 227 us
  waiting for transfers between devices  89.5 us (39%)
  starting transfers between devices  58.2 us (26%)
  blocking collectives  28.7 us (13%)
  Pallas kernels  19.1 us (8%)
  local copies, waits for them, and re-layouts  14.5 us (6%)
  between operations  14.3 us (6%)
  other arithmetic  2.49 us (1%)
    all_gather x1, waiting for transfers between devices, local(): patches = lax.all_gather(both.reshape(NCO * own, half), ('x', 'zh'))  40.2 us
    ppermute x7, starting transfers between devices, swap(): return lax.ppermute(value, axis, [(0, 1), (1, 0)])  22.8 us
    ppermute x7, waiting for transfers between devices, swap(): return lax.ppermute(value, axis, [(0, 1), (1, 0)])  22 us
    all_to_all x1, starting transfers between devices, local(): lax.all_to_all(outgoing, CTX, 0, 0, tiled=True).reshape(group, depth // ctx)  17.2 us
    psum x1, blocking collectives, local(): terms = lax.psum(terms, 'y')  15.9 us
    psum x2, blocking collectives, local(): terms = lax.psum(lax.psum(terms, 'co'), 'x')  12.8 us
    all_to_all x1, waiting for transfers between devices, local(): far = lax.all_to_all(far_sum, 'x', 0, 0, tiled=True)  9.51 us
    all_to_all x2, waiting for transfers between devices, local(): lax.all_to_all(v.reshape(NX * NCO, own, half), ('x', 'co'), 0, 0, tiled=T...  9.29 us
  transfers between devices with their start and end apart: 14, of which 7 were waited for; matrix products, arithmetic and copies ran while one was open for 3% of the time, Pallas kernels for 8%

profile of v2, /device:TPU:24, one launch (start us, length us, event | category | flops | bytes accessed | tf_op | source)
XLA Modules:
  0.0 226.7 jit_solution(1698508146220125057)
XLA Ops:
  7.2 1.7 copy.27
  8.9 4.6 %dynamic-slice_bitcast_fusion = (bf16[4,2,320,512]{3,2,1,0:T(8,128)(2,1)}, bf16[4,2,320,512]{3,2,1,0:T(8,128)(2,1)S(1)}) fusion(bf16[4,2,2,320,512]{4,3,2,1,0:T(8,128)(2,1)} %bitcast.39, s32[]{:T(128)S(6)} %select_n.34, s32[]{:T(128)S(6)} %select_n.33), kind=kLoop, calls=%fused_computation | loop fusion | bytes 10485768 | tf_op jit(solution)/shard_map/weights/jit(dynamic_index_in_dim)/squeeze | solution.py:246
  13.5 1.9 collective-permute-start
  15.4 17.2 %all-to-all-start = ((bf16[16,16,512]{2,1,0:T(8,128)(2,1)}), bf16[16,16,512]{2,1,0:T(8,128)(2,1)S(1)}, u32[]{:S(2)}, u32[]{:S(2)}) async-start(bf16[16,16,512]{2,1,0:T(8,128)(2,1)} %bitcast.33), calls=%async_computation | async-start | bytes 524288 | tf_op jit(solution)/shard_map/tokens/all_to_all | solution.py:241
  32.6 0.0 copy-start.4
  32.6 3.9 %dynamic-slice_bitcast_fusion.2 = (bf16[320,2560]{1,0:T(8,128)(2,1)}, bf16[320,2560]{1,0:T(8,128)(2,1)}) fusion(bf16[5120,320]{0,1:T(8,128)(2,1)} %param.9, s32[]{:T(128)S(6)} %select_n.36, s32[]{:T(128)S(6)} %select_n.35), kind=kLoop, calls=%fused_computation.2 | loop fusion | bytes 6553608 | tf_op jit(solution)/shard_map/weights/dynamic_slice | solution.py:249
  36.5 2.3 %collective-permute-start.4 = (bf16[320,2560]{1,0:T(8,128)(2,1)}, bf16[320,2560]{1,0:T(8,128)(2,1)}, u32[]{:S(2)}, u32[]{:S(2)}) collective-permute-start(bf16[320,2560]{1,0:T(8,128)(2,1)} %get-tuple-element.24), channel_id=1, source_target_pairs={{0,1},{1,0},{2,3},{3,2},{4,5},{5,4},{6,7},{7,6},{8,9},{9,8},{10,11... | collective-permute-start | bytes 4915208 | tf_op jit(solution)/shard_map/weights/ppermute | solution.py:35
  38.8 8.4 %all-to-all-done = bf16[16,16,512]{2,1,0:T(8,128)(2,1)S(1)} async-done(((bf16[16,16,512]{2,1,0:T(8,128)(2,1)}), bf16[16,16,512]{2,1,0:T(8,128)(2,1)S(1)}, u32[]{:S(2)}, u32[]{:S(2)}) %all-to-all-start) | async-done | bytes 262176 | tf_op jit(solution)/shard_map/tokens/all_to_all | solution.py:241
  47.2 1.9 collective-permute-start.1
  49.2 0.7 dynamic-slice_bitcast_fusion.4
  49.8 2.4 %collective-permute-start.6 = (bf16[16,2560]{1,0:T(8,128)(2,1)}, bf16[16,2560]{1,0:T(8,128)(2,1)}, u32[]{:S(2)}, u32[]{:S(2)}) collective-permute-start(bf16[16,2560]{1,0:T(8,128)(2,1)} %get-tuple-element.27), channel_id=1, source_target_pairs={{0,1},{1,0},{2,3},{3,2},{4,5},{5,4},{6,7},{7,6},{8,9},{9,8},{10,11... | collective-permute-start | bytes 245768 | tf_op jit(solution)/shard_map/patches/ppermute | solution.py:35
  52.3 0.0 collective-permute-done.1.got_t
  52.3 4.1 %hidden_part.2 = bf16[4,320,256]{2,1,0:T(8,128)(2,1)} custom-call(s32[1]{0:T(128)} %bitcast.6.place, bf16[4,2,320,512]{3,2,1,0:T(8,128)(2,1)S(1)} %get-tuple-element.23.own_w, bf16[4,2,320,512]{3,2,1,0:T(8,128)(2,1)} %collective-permute-done.got_w, bf16[256,512]{1,0:T(8,128)(2,1)S(1)} %bitcast.35, bf16[256,512]{1,0:T(8,128)(2,1)S(1)} %collective-permute-done.1.got_t), custom_call_target="tpu_custom_call" | custom-call | flops 1 | bytes 1 | tf_op jit(solution)/shard_map/hidden/hidden_part/pallas_call | solution.py:53
  56.4 3.5 %all-to-all-start.1 = ((bf16[4,320,256]{2,1,0:T(8,128)(2,1)}), bf16[4,320,256]{2,1,0:T(8,128)(2,1)S(1)}, u32[]{:S(2)}, u32[]{:S(2)}) async-start(bf16[4,320,256]{2,1,0:T(8,128)(2,1)} %hidden_part.2), calls=%async_computation.1 | async-start | bytes 1310720 | tf_op jit(solution)/shard_map/hidden/all_to_all | solution.py:259
  59.9 0.0 all-gather.2.cloned.1.call-start
  60.0 1.7 maximum_select_fusion
  61.7 0.0 all-gather.2.cloned.1.call-update
  61.7 9.5 %all-to-all-done.1.v_ref = bf16[4,320,256]{2,1,0:T(8,128)(2,1)S(1)} async-done(((bf16[4,320,256]{2,1,0:T(8,128)(2,1)}), bf16[4,320,256]{2,1,0:T(8,128)(2,1)S(1)}, u32[]{:S(2)}, u32[]{:S(2)}) %all-to-all-start.1) | async-done | bytes 655392 | tf_op jit(solution)/shard_map/hidden/all_to_all | solution.py:259
  71.2 0.1 sum_parts.1
  71.3 0.0 copy-start.6
  71.3 0.7 copy-done.6
  72.0 0.9 copy-done.3
  72.9 4.1 %hidden_part.3 = bf16[4,320,256]{2,1,0:T(8,128)(2,1)} custom-call(s32[1]{0:T(128)} %bitcast.place, bf16[4,2,320,512]{3,2,1,0:T(8,128)(2,1)S(1)} %get-tuple-element.23.own_w, bf16[4,2,320,512]{3,2,1,0:T(8,128)(2,1)} %collective-permute-done.got_w, bf16[256,512]{1,0:T(8,128)(2,1)S(1)} %bitcast.36, bf16[256,512]{1,0:T(8,128)(2,1)S(1)} %copy-done.3), custom_call_target="tpu_custom_call" | custom-call | flops 1 | bytes 1 | tf_op jit(solution)/shard_map/hidden/hidden_part/pallas_call | solution.py:53
  77.0 3.6 %all-to-all-start.2 = ((bf16[4,320,256]{2,1,0:T(8,128)(2,1)}), bf16[4,320,256]{2,1,0:T(8,128)(2,1)S(1)}, u32[]{:S(2)}, u32[]{:S(2)}) async-start(bf16[4,320,256]{2,1,0:T(8,128)(2,1)} %hidden_part.3), calls=%async_computation.2 | async-start | bytes 1310720 | tf_op jit(solution)/shard_map/hidden/all_to_all | solution.py:263
  80.7 2.3 %collective-permute-start.2 = (bf16[320,256]{1,0:T(8,128)(2,1)S(1)}, bf16[320,256]{1,0:T(8,128)(2,1)S(1)}, u32[]{:S(2)}, u32[]{:S(2)}) collective-permute-start(bf16[320,256]{1,0:T(8,128)(2,1)S(1)} %copy-done.7), channel_id=1, source_target_pairs={{0,2},{2,0},{1,3},{3,1},{4,6},{6,4},{5,7},{7,5},{8,10},{10,8},{9,1... | collective-permute-start | bytes 491528 | tf_op jit(solution)/shard_map/hidden/ppermute | solution.py:35
  83.0 0.1 fusion.3.slope_ref
  83.1 12.0 %collective-permute-done.2.got_ref = bf16[320,256]{1,0:T(8,128)(2,1)S(1)} collective-permute-done((bf16[320,256]{1,0:T(8,128)(2,1)S(1)}, bf16[320,256]{1,0:T(8,128)(2,1)S(1)}, u32[]{:S(2)}, u32[]{:S(2)}) %collective-permute-start.2) | collective-permute-done | bytes 163872 | tf_op jit(solution)/shard_map/hidden/ppermute | solution.py:35
  95.2 0.5 act_rows.1.own_a
  95.6 1.9 collective-permute-start.3
  97.6 1.7 collective-permute-done.3.got_a
  99.3 3.6 %merged_part.2.far_ref = bf16[4,32,2560]{2,1,0:T(8,128)(2,1)} custom-call(s32[1]{0:T(128)} %bitcast.6.place, bf16[2,4,2,32,320]{4,3,2,1,0:T(8,128)(2,1)S(1)} %act_rows.1.own_a, bf16[2,4,2,32,320]{4,3,2,1,0:T(8,128)(2,1)S(1)} %collective-permute-done.3.got_a, bf16[320,2560]{1,0:T(8,128)(2,1)S(1)} %copy-done, bf16[320,2560]{1,0:T(8,128)(2,1)} %collective-permute-done.4.got_w), custom_call_target="tpu_custom_call" | custom-call | flops 1 | bytes 1 | tf_op jit(solution)/shard_map/merged/merged_part/pallas_call | solution.py:133
  102.9 4.0 %all-to-all-start.3 = ((bf16[8,16,2560]{2,1,0:T(8,128)(2,1)}), bf16[8,16,2560]{2,1,0:T(8,128)(2,1)S(1)}, u32[]{:S(2)}, u32[]{:S(2)}) async-start(bf16[8,16,2560]{2,1,0:T(8,128)(2,1)} %bitcast.10), calls=%async_computation.3 | async-start | bytes 1310720 | tf_op jit(solution)/shard_map/merged/all_to_all | solution.py:269
  106.9 3.7 %merged_part.3.near_ref = bf16[4,32,2560]{2,1,0:T(8,128)(2,1)} custom-call(s32[1]{0:T(128)} %bitcast.place, bf16[2,4,2,32,320]{4,3,2,1,0:T(8,128)(2,1)S(1)} %act_rows.1.own_a, bf16[2,4,2,32,320]{4,3,2,1,0:T(8,128)(2,1)S(1)} %collective-permute-done.3.got_a, bf16[320,2560]{1,0:T(8,128)(2,1)S(1)} %copy-done, bf16[320,2560]{1,0:T(8,128)(2,1)} %collective-permute-done.4.got_w), custom_call_target="tpu_custom_call" | custom-call | flops 1 | bytes 1 | tf_op jit(solution)/shard_map/merged/merged_part/pallas_call | solution.py:133
  110.5 9.3 %all-to-all-done.3.v_ref = bf16[8,16,2560]{2,1,0:T(8,128)(2,1)S(1)} async-done(((bf16[8,16,2560]{2,1,0:T(8,128)(2,1)}), bf16[8,16,2560]{2,1,0:T(8,128)(2,1)S(1)}, u32[]{:S(2)}, u32[]{:S(2)}) %all-to-all-start.3) | async-done | bytes 655392 | tf_op jit(solution)/shard_map/merged/all_to_all | solution.py:269
  119.8 0.1 sum_halves.1
  119.9 3.6 %all-to-all-start.4 = ((bf16[8,16,2560]{2,1,0:T(8,128)(2,1)}), bf16[8,16,2560]{2,1,0:T(8,128)(2,1)S(1)}, u32[]{:S(2)}, u32[]{:S(2)}) async-start(bf16[8,16,2560]{2,1,0:T(8,128)(2,1)} %bitcast.11), calls=%async_computation.4 | async-start | bytes 1310720 | tf_op jit(solution)/shard_map/merged/all_to_all | solution.py:269
  123.4 40.2 %all-gather.2.cloned.1.call-done = bf16[8,32,2560]{2,1,0:T(8,128)(2,1)} async-done(((bf16[1,32,2560]{2,1,0:T(8,128)(2,1)}), bf16[8,32,2560]{2,1,0:T(8,128)(2,1)}) %all-gather.2.cloned.1.call-update) | async-done | bytes 1310736 | tf_op jit(solution)/shard_map/patches/all_gather | solution.py:255
  163.7 1.3 copy-done.1
  165.0 2.0 gain_terms.1
  167.1 2.5 %psum.21 = f32[10,128]{1,0:T(8,128)S(1)} all-reduce(f32[10,128]{1,0:T(8,128)S(1)} %bitcast.42), channel_id=1, replica_groups=mesh['y'=8,'zl'=6,'x'=4,'zh'=2,'co'=2] {'co'}, use_global_device_ids=true, to_apply=%region_0.1 | all-reduce | flops 1280 | bytes 10240 | tf_op jit(solution)/shard_map/gain/psum | solution.py:281
  169.6 10.3 %psum.22 = f32[10,128]{1,0:T(8,128)S(1)} all-reduce(f32[10,128]{1,0:T(8,128)S(1)} %psum.21), channel_id=1, replica_groups=mesh['y'=8,'zl'=6,'x'=4,'zh'=2,'co'=2] {'x'}, use_global_device_ids=true, to_apply=%region_1.2 | all-reduce | flops 1280 | bytes 10240 | tf_op jit(solution)/shard_map/gain/psum | solution.py:281
  179.9 15.9 %psum.23 = f32[10,128]{1,0:T(8,128)S(1)} all-reduce(f32[10,128]{1,0:T(8,128)S(1)} %psum.22), channel_id=1, replica_groups=mesh['y'=8,'zl'=6,'x'=4,'zh'=2,'co'=2] {'y'}, use_global_device_ids=true, to_apply=%region_2.3 | all-reduce | flops 1280 | bytes 10240 | tf_op jit(solution)/shard_map/gain/psum | solution.py:283
  195.8 0.6 broadcast_in_dim.2
  196.4 3.5 %all-to-all-start.5 = ((f32[12,10,128]{2,1,0:T(8,128)}), f32[12,10,128]{2,1,0:T(8,128)S(1)}, u32[]{:S(2)}, u32[]{:S(2)}) async-start(f32[12,10,128]{2,1,0:T(8,128)} %broadcast_in_dim.2), calls=%async_computation.5 | async-start | bytes 196608 | tf_op jit(solution)/shard_map/gain/all_to_all | solution.py:224
  199.9 10.1 %collective-permute-start.5 = (bf16[2,16,2560]{2,1,0:T(8,128)(2,1)S(1)}, bf16[2,16,2560]{2,1,0:T(8,128)(2,1)S(1)}, u32[]{:S(2)}, u32[]{:S(2)}) collective-permute-start(bf16[2,16,2560]{2,1,0:T(8,128)(2,1)S(1)} %sum_halves.1), channel_id=1, source_target_pairs={{0,2},{2,0},{1,3},{3,1},{4,6},{6,4},{5,7},{7,5},{8,10},{10,8},{9,1... | collective-permute-start | bytes 491528 | tf_op jit(solution)/shard_map/merged/ppermute | solution.py:35
  210.0 8.3 %collective-permute-done.5.got_ref = bf16[2,16,2560]{2,1,0:T(8,128)(2,1)S(1)} collective-permute-done((bf16[2,16,2560]{2,1,0:T(8,128)(2,1)S(1)}, bf16[2,16,2560]{2,1,0:T(8,128)(2,1)S(1)}, u32[]{:S(2)}, u32[]{:S(2)}) %collective-permute-start.5) | collective-permute-done | bytes 163872 | tf_op jit(solution)/shard_map/merged/ppermute | solution.py:35
  218.3 0.9 norm_part.1
  219.3 0.6 multiply_bitcast_fusion
  (26 shorter events, 0.1 us)
Async XLA Ops:
  13.5 38.8 %collective-permute-start = (bf16[4,2,320,512]{3,2,1,0:T(8,128)(2,1)}, bf16[4,2,320,512]{3,2,1,0:T(8,128)(2,1)}, u32[]{:S(2)}, u32[]{:S(2)}) collective-permute-start(bf16[4,2,320,512]{3,2,1,0:T(8,128)(2,1)} %get-tuple-element.22), channel_id=1, source_target_pairs={{0,1},{1,0},{2,3},{3,2},{4,5},{5,4},{6,7},{7,6},{8,9},{9,8},{10,11... | collective-permute-start | bytes 7864328 | tf_op jit(solution)/shard_map/weights/ppermute | solution.py:35
  15.4 31.9 %all-to-all-start = ((bf16[16,16,512]{2,1,0:T(8,128)(2,1)}), bf16[16,16,512]{2,1,0:T(8,128)(2,1)S(1)}, u32[]{:S(2)}, u32[]{:S(2)}) async-start(bf16[16,16,512]{2,1,0:T(8,128)(2,1)} %bitcast.33), calls=%async_computation | async-start | bytes 524288 | tf_op jit(solution)/shard_map/tokens/all_to_all | solution.py:241
  32.6 16.6 %copy-start.4 = (bf16[16,5120]{1,0:T(8,128)(2,1)S(1)}, bf16[16,5120]{1,0:T(8,128)(2,1)}, u32[]{:S(2)}) copy-start(bf16[16,5120]{1,0:T(8,128)(2,1)} %patch_ref.1) | copy-start | bytes 491524
  36.5 61.1 %collective-permute-start.4 = (bf16[320,2560]{1,0:T(8,128)(2,1)}, bf16[320,2560]{1,0:T(8,128)(2,1)}, u32[]{:S(2)}, u32[]{:S(2)}) collective-permute-start(bf16[320,2560]{1,0:T(8,128)(2,1)} %get-tuple-element.24), channel_id=1, source_target_pairs={{0,1},{1,0},{2,3},{3,2},{4,5},{5,4},{6,7},{7,6},{8,9},{9,8},{10,11... | collective-permute-start | bytes 4915208 | tf_op jit(solution)/shard_map/weights/ppermute | solution.py:35
  47.2 5.0 %collective-permute-start.1 = (bf16[256,512]{1,0:T(8,128)(2,1)S(1)}, bf16[256,512]{1,0:T(8,128)(2,1)S(1)}, u32[]{:S(2)}, u32[]{:S(2)}) collective-permute-start(bf16[256,512]{1,0:T(8,128)(2,1)S(1)} %bitcast.34), channel_id=1, source_target_pairs={{0,1},{1,0},{2,3},{3,2},{4,5},{5,4},{6,7},{7,6},{8,9},{9,8},{10,11... | collective-permute-start | bytes 786440 | tf_op jit(solution)/shard_map/tokens/ppermute | solution.py:35
  49.8 10.1 %collective-permute-start.6 = (bf16[16,2560]{1,0:T(8,128)(2,1)}, bf16[16,2560]{1,0:T(8,128)(2,1)}, u32[]{:S(2)}, u32[]{:S(2)}) collective-permute-start(bf16[16,2560]{1,0:T(8,128)(2,1)} %get-tuple-element.27), channel_id=1, source_target_pairs={{0,1},{1,0},{2,3},{3,2},{4,5},{5,4},{6,7},{7,6},{8,9},{9,8},{10,11... | collective-permute-start | bytes 245768 | tf_op jit(solution)/shard_map/patches/ppermute | solution.py:35
  52.3 4.2 %copy-start.2 = (bf16[256,512]{1,0:T(8,128)(2,1)}, bf16[256,512]{1,0:T(8,128)(2,1)S(1)}, u32[]{:S(2)}) copy-start(bf16[256,512]{1,0:T(8,128)(2,1)S(1)} %collective-permute-done.1.got_t) | copy-start | bytes 786436
  56.4 14.8 %all-to-all-start.1 = ((bf16[4,320,256]{2,1,0:T(8,128)(2,1)}), bf16[4,320,256]{2,1,0:T(8,128)(2,1)S(1)}, u32[]{:S(2)}, u32[]{:S(2)}) async-start(bf16[4,320,256]{2,1,0:T(8,128)(2,1)} %hidden_part.2), calls=%async_computation.1 | async-start | bytes 1310720 | tf_op jit(solution)/shard_map/hidden/all_to_all | solution.py:259
  59.9 103.8 %all-gather.2.cloned.1.call-start = ((), (), s32[]{:S(2)}) async-start(), calls=%async_computation.6 | async-start | bytes 1474560 | tf_op jit(solution)/shard_map/patches/all_gather | solution.py:255
  71.3 0.7 copy-start.6
  72.0 0.9 copy-start.3
  72.9 7.7 %copy-start.7 = (bf16[320,256]{1,0:T(8,128)(2,1)S(1)}, bf16[320,256]{1,0:T(8,128)(2,1)}, u32[]{:S(2)}) copy-start(bf16[320,256]{1,0:T(8,128)(2,1)} %copy-done.6) | copy-start | bytes 491524
  72.9 10.1 %copy-start.9 = (bf16[320,256]{1,0:T(8,128)(2,1)S(1)}, bf16[320,256]{1,0:T(8,128)(2,1)}, u32[]{:S(2)}) copy-start(bf16[320,256]{1,0:T(8,128)(2,1)} %param.8) | copy-start | bytes 491524
  72.9 22.3 %copy-start.8 = (s32[256]{0:T(256)S(1)}, s32[256]{0:T(256)}, u32[]{:S(2)}) copy-start(s32[256]{0:T(256)} %param.13) | copy-start | bytes 3076
  77.0 22.2 %copy-start = (bf16[320,2560]{1,0:T(8,128)(2,1)S(1)}, bf16[320,2560]{1,0:T(8,128)(2,1)}, u32[]{:S(2)}) copy-start(bf16[320,2560]{1,0:T(8,128)(2,1)} %get-tuple-element.25.own_w) | copy-start | bytes 4915204
  77.0 18.2 %all-to-all-start.2 = ((bf16[4,320,256]{2,1,0:T(8,128)(2,1)}), bf16[4,320,256]{2,1,0:T(8,128)(2,1)S(1)}, u32[]{:S(2)}, u32[]{:S(2)}) async-start(bf16[4,320,256]{2,1,0:T(8,128)(2,1)} %hidden_part.3), calls=%async_computation.2 | async-start | bytes 1310720 | tf_op jit(solution)/shard_map/hidden/all_to_all | solution.py:263
  80.7 14.5 %collective-permute-start.2 = (bf16[320,256]{1,0:T(8,128)(2,1)S(1)}, bf16[320,256]{1,0:T(8,128)(2,1)S(1)}, u32[]{:S(2)}, u32[]{:S(2)}) collective-permute-start(bf16[320,256]{1,0:T(8,128)(2,1)S(1)} %copy-done.7), channel_id=1, source_target_pairs={{0,2},{2,0},{1,3},{3,1},{4,6},{6,4},{5,7},{7,5},{8,10},{10,8},{9,1... | collective-permute-start | bytes 491528 | tf_op jit(solution)/shard_map/hidden/ppermute | solution.py:35
  95.6 3.6 %collective-permute-start.3 = (bf16[2,4,2,32,320]{4,3,2,1,0:T(8,128)(2,1)S(1)}, bf16[2,4,2,32,320]{4,3,2,1,0:T(8,128)(2,1)S(1)}, u32[]{:S(2)}, u32[]{:S(2)}) collective-permute-start(bf16[2,4,2,32,320]{4,3,2,1,0:T(8,128)(2,1)S(1)} %act_rows.1.own_a), channel_id=1, source_target_pairs={{0,1},{1,0},{2,3},{3,2},{4,5},{5,4},{6,7},{7,6},{8,9},{9,8},{10,11... | collective-permute-start | bytes 983048 | tf_op jit(solution)/shard_map/merged/ppermute | solution.py:35
  102.9 16.9 %all-to-all-start.3 = ((bf16[8,16,2560]{2,1,0:T(8,128)(2,1)}), bf16[8,16,2560]{2,1,0:T(8,128)(2,1)S(1)}, u32[]{:S(2)}, u32[]{:S(2)}) async-start(bf16[8,16,2560]{2,1,0:T(8,128)(2,1)} %bitcast.10), calls=%async_computation.3 | async-start | bytes 1310720 | tf_op jit(solution)/shard_map/merged/all_to_all | solution.py:269
  110.5 99.5 %copy-start.10 = (f32[1280]{0:T(1024)S(1)}, f32[1280]{0:T(1024)}, u32[]{:S(2)}) copy-start(f32[1280]{0:T(1024)} %param.12) | copy-start | bytes 15364
  110.5 107.8 %copy-start.5 = (bf16[16,5120]{1,0:T(8,128)(2,1)S(1)}, bf16[16,5120]{1,0:T(8,128)(2,1)}, u32[]{:S(2)}) copy-start(bf16[16,5120]{1,0:T(8,128)(2,1)} %patch_ref.1) | copy-start | bytes 491524
  119.9 60.0 %all-to-all-start.4 = ((bf16[8,16,2560]{2,1,0:T(8,128)(2,1)}), bf16[8,16,2560]{2,1,0:T(8,128)(2,1)S(1)}, u32[]{:S(2)}, u32[]{:S(2)}) async-start(bf16[8,16,2560]{2,1,0:T(8,128)(2,1)} %bitcast.11), calls=%async_computation.4 | async-start | bytes 1310720 | tf_op jit(solution)/shard_map/merged/all_to_all | solution.py:269
  163.7 1.3 copy-start.1
  196.4 22.9 %all-to-all-start.5 = ((f32[12,10,128]{2,1,0:T(8,128)}), f32[12,10,128]{2,1,0:T(8,128)S(1)}, u32[]{:S(2)}, u32[]{:S(2)}) async-start(f32[12,10,128]{2,1,0:T(8,128)} %broadcast_in_dim.2), calls=%async_computation.5 | async-start | bytes 196608 | tf_op jit(solution)/shard_map/gain/all_to_all | solution.py:224
  199.9 18.4 %collective-permute-start.5 = (bf16[2,16,2560]{2,1,0:T(8,128)(2,1)S(1)}, bf16[2,16,2560]{2,1,0:T(8,128)(2,1)S(1)}, u32[]{:S(2)}, u32[]{:S(2)}) collective-permute-start(bf16[2,16,2560]{2,1,0:T(8,128)(2,1)S(1)} %sum_halves.1), channel_id=1, source_target_pairs={{0,2},{2,0},{1,3},{3,1},{4,6},{6,4},{5,7},{7,5},{8,10},{10,8},{9,1... | collective-permute-start | bytes 491528 | tf_op jit(solution)/shard_map/merged/ppermute | solution.py:35
Sparse Core Ops, SparseCore 0:
  64.5 99.1 all-gather.1

commit v3 on v2

v3 whole, which is shorter than its diff:
```python
import functools

import jax
import jax.numpy as jnp
from jax import lax
from jax.experimental import pallas as pl
from jax.experimental.pallas import tpu as pltpu
from jax.sharding import Mesh
from jax.sharding import PartitionSpec as P

NY, NZL, NX, NZH, NCO = 8, 6, 4, 2, 2
AXES = ("y", "zl", "x", "zh", "co")
DP = ("y", "zl")
CTX = ("x", "zh", "co")
EPS = 1e-06
F32 = jnp.float32
BF16 = jnp.bfloat16


def gelu_slope(values):
    normal_cdf = 0.5 * (1.0 + lax.erf(values * 0.7071067811865476))
    density = jnp.exp(-0.5 * values * values) * 0.3989422804014327
    return normal_cdf + values * density


def params(mib=12):
    return pltpu.CompilerParams(vmem_limit_bytes=mib * 1024 * 1024)


def cost(flops=1):
    return pl.CostEstimate(flops=flops, bytes_accessed=1, transcendentals=0)


LONG = 20_000_000_000
ANYWHERE = pl.BlockSpec(memory_space=pl.ANY)
IN_VMEM = pl.BlockSpec(memory_space=pltpu.VMEM)
IN_SMEM = pl.BlockSpec(memory_space=pltpu.SMEM)


def swap(value, axis):
    return lax.ppermute(value, axis, [(0, 1), (1, 0)])


def hidden_kernel(place, own_w, got_w, own_t, got_t, out_ref, block, arrived):
    copies = [
        [
            pltpu.make_async_copy(w_ref.at[i, place[0], place[1]], block.at[i, k], arrived.at[i, k])
            for k, w_ref in enumerate((own_w, got_w))
        ]
        for i in range(NX)
    ]
    for pair in copies:
        for copy in pair:
            copy.start()
    for i, pair in enumerate(copies):
        total = None
        for k, t_ref in enumerate((own_t, got_t)):
            pair[k].wait()
            term = lax.dot_general(
                block[i, k], t_ref[...], (((1,), (1,)), ((), ())), preferred_element_type=F32
            )
            total = term if total is None else total + term
        out_ref[i] = total.astype(BF16)


def hidden_part(weights, tokens, place):
    rows, depth = weights[0].shape
    units = rows // (NX * NZH * NCO)
    count = tokens[0].shape[0]
    weights = [w.reshape(NX, NZH, NCO, units, depth) for w in weights]
    return pl.pallas_call(
        hidden_kernel,
        in_specs=[IN_SMEM, ANYWHERE, ANYWHERE, IN_VMEM, IN_VMEM],
        out_specs=IN_VMEM,
        out_shape=jax.ShapeDtypeStruct((NX, units, count), BF16),
        scratch_shapes=[
            pltpu.VMEM((NX, 2, units, depth), BF16),
            pltpu.SemaphoreType.DMA((NX, 2)),
        ],
        compiler_params=params(60),
        cost_estimate=cost(),
        name="hidden_part",
    )(place, *weights, *tokens)


def total_of(ref):
    total = ref[0].astype(F32)
    for i in range(1, ref.shape[0]):
        total += ref[i].astype(F32)
    return total


def sum_kernel(v_ref, out_ref):
    out_ref[...] = total_of(v_ref).astype(BF16)


def sum_parts(parts):
    return pl.pallas_call(
        sum_kernel,
        out_shape=jax.ShapeDtypeStruct(parts.shape[1:], BF16),
        compiler_params=params(),
        cost_estimate=cost(),
        name="sum_parts",
    )(parts)


def wide_kernel(v_ref, out_ref):
    out_ref[...] = v_ref[...].astype(F32)


def widen(value):
    return pl.pallas_call(
        wide_kernel,
        out_shape=jax.ShapeDtypeStruct(value.shape, F32),
        compiler_params=params(),
        cost_estimate=cost(LONG),
        name="widen",
    )(value)


def act_kernel(v_ref, got_ref, slope_ref, pos_ref, out_ref):
    act = ((total_of(v_ref) + got_ref[...]) * slope_ref[...]).astype(BF16)
    count = act.shape[1]
    pick = (lax.broadcasted_iota(jnp.int32, (count, count), 0) == pos_ref[...]).astype(F32)
    pick = pick.T.astype(BF16)
    moved = lax.dot_general(pick, act, (((1,), (1,)), ((), ())), preferred_element_type=F32)
    out_ref[...] = moved.astype(BF16).reshape(out_ref.shape)


def act_rows(parts, got, slope, owner_pos):
    units, count = got.shape
    return pl.pallas_call(
        act_kernel,
        out_shape=jax.ShapeDtypeStruct((NX, NZH, count // (NX * NZH), units), BF16),
        compiler_params=params(),
        cost_estimate=cost(),
        name="act_rows",
    )(parts, got, slope, owner_pos.reshape(1, count))


def merged_kernel(place, own_a, got_a, own_w, got_w, out_ref):
    depth = own_w.shape[0]
    total = None
    for a_ref, w_ref in ((own_a, own_w), (got_a, got_w)):
        term = lax.dot_general(
            a_ref[...].reshape(-1, depth),
            w_ref[...],
            (((1,), (0,)), ((), ())),
            preferred_element_type=F32,
        )
        total = term if total is None else total + term
    out_ref[...] = total.astype(BF16).reshape(out_ref.shape)


def merged_part(acts, weights, place):
    _, _, rows, depth = acts[0].shape
    cols = weights[0].shape[1] // NCO
    steps = 2
    a_spec = pl.BlockSpec((NX, 1, rows, depth), lambda i, s: (0, s[0], 0, 0))
    w_spec = pl.BlockSpec((depth, cols // steps), lambda i, s: (0, s[1] * steps + i))
    return pl.pallas_call(
        merged_kernel,
        grid_spec=pltpu.PrefetchScalarGridSpec(
            num_scalar_prefetch=1,
            grid=(steps,),
            in_specs=[a_spec, a_spec, w_spec, w_spec],
            out_specs=pl.BlockSpec((NX, rows, cols // steps), lambda i, s: (0, 0, i)),
        ),
        out_shape=jax.ShapeDtypeStruct((NX, rows, cols), BF16),
        compiler_params=params(),
        cost_estimate=cost(),
        name="merged_part",
    )(place, *acts, *weights)


def halves_kernel(v_ref, out_ref):
    for c in range(NCO):
        total = v_ref[c].astype(F32)
        for x in range(1, NX):
            total += v_ref[NCO * x + c].astype(F32)
        out_ref[c] = total.astype(BF16)


def sum_halves(parts):
    return pl.pallas_call(
        halves_kernel,
        out_shape=jax.ShapeDtypeStruct((NCO,) + parts.shape[1:], BF16),
        compiler_params=params(),
        cost_estimate=cost(),
        name="sum_halves",
    )(parts)


def norm_of(patch):
    inv_rms = lax.rsqrt(jnp.mean(patch * patch, axis=-1, keepdims=True) + EPS)
    return patch * inv_rms, inv_rms


def norm_kernel(v_ref, got_ref, patch_ref, gain_ref, out_ref, terms_ref):
    width = gain_ref.shape[1]
    gain = gain_ref[...]
    in_half = patch_ref.shape[1] // width // NCO
    terms = jnp.zeros((1, width), F32)
    for p in range(patch_ref.shape[1] // width):
        c, q = p // in_half, pl.ds(p % in_half * width, width)
        cols = pl.ds(p * width, width)
        owner = got_ref[c, :, q]
        for x in range(NX):
            owner += v_ref[NCO * x + c, :, q].astype(F32)
        normed, inv_rms = norm_of(patch_ref[:, cols].astype(F32))
        scaled = owner * gain
        inner = jnp.mean(scaled * normed, axis=-1, keepdims=True)
        out_ref[:, cols] = (inv_rms * (scaled - normed * inner)).astype(BF16)
        terms += jnp.sum(owner * normed, axis=0, keepdims=True)
    terms_ref[...] = terms


def norm_part(parts, got, patch_in, norm_gain):
    width = norm_gain.shape[0]
    return pl.pallas_call(
        norm_kernel,
        out_shape=[
            jax.ShapeDtypeStruct(patch_in.shape, BF16),
            jax.ShapeDtypeStruct((1, width), F32),
        ],
        compiler_params=params(),
        cost_estimate=cost(),
        name="norm_part",
    )(parts, got, patch_in, norm_gain.reshape(1, width))


def sum_over(terms, axes, count):
    rows = jnp.broadcast_to(terms[None], (count,) + terms.shape)
    return jnp.sum(lax.all_to_all(rows, axes, 0, 0, tiled=True), axis=0)


def local(grad_tokens, pre_act, w_fc1, w_fc2, patch_in, norm_gain, owner_pos):
    zh = lax.axis_index("zh").astype(jnp.int32)
    co = lax.axis_index("co").astype(jnp.int32)
    ctx = NX * NZH * NCO
    own, depth = grad_tokens.shape
    group = own * ctx
    slope = gelu_slope(pre_act.astype(F32))
    far_z, near_z = jnp.stack([1 - zh, co]), jnp.stack([zh, co])
    half = patch_in.shape[1] // NCO
    with jax.named_scope("tokens"):
        outgoing = grad_tokens.reshape(own, ctx, depth // ctx).transpose(1, 0, 2)
        tokens = lax.all_to_all(outgoing, CTX, 0, 0, tiled=True).reshape(group, depth // ctx)
        tokens = (tokens, swap(tokens, "co"))
    with jax.named_scope("weights"):
        weights_2 = (w_fc2, swap(w_fc2, "co"))
        w_fc1_t = w_fc1.T
        weights_1 = (w_fc1_t, swap(w_fc1_t, "co"))

    def exchange(part, deliver, add_up):
        far_sum = part(far_z, None)
        far = deliver(far_sum)
        near_sum = part(near_z, far_sum)
        far, near_sum = lax.optimization_barrier((far, near_sum))
        far = add_up(far)
        near_sum, _ = lax.optimization_barrier((near_sum, far))
        return deliver(near_sum), widen(swap(far, "zh"))

    def after(values, first):
        return values if first is None else lax.optimization_barrier((values, first))[0]

    with jax.named_scope("hidden"):
        near, got = exchange(
            lambda z, first: hidden_part(weights_2, after(tokens, first), z),
            lambda v: lax.all_to_all(v, "x", 0, 0, tiled=True),
            sum_parts,
        )
    with jax.named_scope("merged"):
        act = act_rows(near, got, slope, owner_pos)
        acts = (act, swap(act, "co"))
        near, got = exchange(
            lambda z, first: merged_part(after(acts, first), weights_1, z),
            lambda v: lax.all_to_all(
                v.reshape(NX * NCO, own, half), ("x", "co"), 0, 0, tiled=True
            ),
            sum_halves,
        )
    with jax.named_scope("norm"):
        patch_grad, terms = norm_part(near, got, patch_in, norm_gain)
    with jax.named_scope("gain"):
        terms = terms.reshape(-1, 128)
        terms = sum_over(terms, ("x", "co"), NX * NCO)
        terms = sum_over(terms, "y", NY)
        terms = sum_over(terms, ("zl", "zh"), NZL * NZH)
        gain_grad = terms.reshape(-1) / (NY * NZL * ctx)
    return (patch_grad, gain_grad)


def solution(mesh):
    fine = Mesh(mesh.devices.reshape(NY, NZL, NX, NZH, NCO), AXES)
    return jax.shard_map(
        local,
        mesh=fine,
        in_specs=(
            P(DP + CTX, None),
            P(CTX, DP),
            P(None, CTX),
            P(None, CTX),
            P(DP + CTX, None),
            P(),
            P(DP),
        ),
        out_specs=(P(DP + CTX, None), P()),
        check_vma=False,
    )
```

time: 228 us -> 178 us (0.78)
  the two profiles are of different devices: /device:TPU:24 before, /device:TPU:1 now
where the time goes in v3:
time: 178 us; the launch traced here: 176 us
  starting transfers between devices  58.1 us (33%)
  waiting for transfers between devices  43.1 us (24%)
  blocking collectives  42.3 us (24%)
  Pallas kernels  20.8 us (12%)
  local copies, waits for them, and re-layouts  7.76 us (4%)
  other arithmetic  2.73 us (2%)
    all_to_all x3, blocking collectives, sum_over(): return jnp.sum(lax.all_to_all(rows, axes, 0, 0, tiled=True), axis=0)  42.3 us
    ppermute x6, starting transfers between devices, swap(): return lax.ppermute(value, axis, [(0, 1), (1, 0)])  33.2 us
    all_to_all x2, waiting for transfers between devices, local(): lax.all_to_all(v.reshape(NX * NCO, own, half), ('x', 'co'), 0, 0, tiled=T...  13.8 us
    all_to_all x1, waiting for transfers between devices, local(): lax.all_to_all(outgoing, CTX, 0, 0, tiled=True).reshape(group, depth // ctx)  11.7 us
    ppermute x6, waiting for transfers between devices, swap(): return lax.ppermute(value, axis, [(0, 1), (1, 0)])  10.8 us
    pallas_call x2, Pallas kernels, hidden_part(): pl.pallas_call(hidden_kernel, in_specs=[IN_SMEM, ANYWHERE, ANYWHERE, IN_V...  10.5 us
    all_to_all x2, starting transfers between devices, local(): lax.all_to_all(v.reshape(NX * NCO, own, half), ('x', 'co'), 0, 0, tiled=T...  9.2 us
    all_to_all x1, starting transfers between devices, local(): lax.all_to_all(outgoing, CTX, 0, 0, tiled=True).reshape(group, depth // ctx)  8.08 us
  transfers between devices with their start and end apart: 11, of which 9 were waited for; matrix products, arithmetic and copies ran while one was open for 2% of the time, Pallas kernels for 9%

profile of v3, /device:TPU:1, one launch (start us, length us, event | category | flops | bytes accessed | tf_op | source)
XLA Modules:
  0.0 175.7 jit_solution(6517863111591325379)
XLA Ops:
  0.6 12.4 %collective-permute-start = (bf16[5120,512]{1,0:T(8,128)(2,1)}, bf16[5120,512]{1,0:T(8,128)(2,1)}, u32[]{:S(2)}, u32[]{:S(2)}) collective-permute-start(bf16[5120,512]{1,0:T(8,128)(2,1)} %param.10), channel_id=1, source_target_pairs={{0,1},{1,0},{2,3},{3,2},{4,5},{5,4},{6,7},{7,6},{8,9},{9,8},{10,11... | collective-permute-start | bytes 15728648 | tf_op jit(solution)/shard_map/weights/ppermute | solution.py:41
  13.1 1.7 copy.20
  14.8 8.1 %all-to-all-start = ((bf16[16,16,512]{2,1,0:T(8,128)(2,1)}), bf16[16,16,512]{2,1,0:T(8,128)(2,1)S(1)}, u32[]{:S(2)}, u32[]{:S(2)}) async-start(bf16[16,16,512]{2,1,0:T(8,128)(2,1)} %bitcast.19), calls=%async_computation | async-start | bytes 524288 | tf_op jit(solution)/shard_map/tokens/all_to_all | solution.py:248
  22.8 2.0 %collective-permute-start.4 = (bf16[320,5120]{1,0:T(8,128)(2,1)}, bf16[320,5120]{1,0:T(8,128)(2,1)}, u32[]{:S(2)}, u32[]{:S(2)}) collective-permute-start(bf16[320,5120]{1,0:T(8,128)(2,1)} %bitcast.20), channel_id=1, source_target_pairs={{0,1},{1,0},{2,3},{3,2},{4,5},{5,4},{6,7},{7,6},{8,9},{9,8},{10,11... | collective-permute-start | bytes 9830408 | tf_op jit(solution)/shard_map/weights/ppermute | solution.py:41
  24.9 11.7 %all-to-all-done = bf16[16,16,512]{2,1,0:T(8,128)(2,1)S(1)} async-done(((bf16[16,16,512]{2,1,0:T(8,128)(2,1)}), bf16[16,16,512]{2,1,0:T(8,128)(2,1)S(1)}, u32[]{:S(2)}, u32[]{:S(2)}) %all-to-all-start) | async-done | bytes 262176 | tf_op jit(solution)/shard_map/tokens/all_to_all | solution.py:248
  36.6 2.9 %collective-permute-start.1 = (bf16[256,512]{1,0:T(8,128)(2,1)S(1)}, bf16[256,512]{1,0:T(8,128)(2,1)S(1)}, u32[]{:S(2)}, u32[]{:S(2)}) collective-permute-start(bf16[256,512]{1,0:T(8,128)(2,1)S(1)} %bitcast.28), channel_id=1, source_target_pairs={{0,1},{1,0},{2,3},{3,2},{4,5},{5,4},{6,7},{7,6},{8,9},{9,8},{10,11... | collective-permute-start | bytes 786440 | tf_op jit(solution)/shard_map/tokens/ppermute | solution.py:41
  39.5 0.6 pad_add_fusion.place
  40.1 0.5 collective-permute-done.1.got_t
  40.7 0.0 collective-permute-done
  40.7 0.7 copy-done.13
  41.4 5.2 %hidden_part.2 = bf16[4,320,256]{2,1,0:T(8,128)(2,1)} custom-call(s32[2]{0:T(128)} %pad_add_fusion.place, bf16[4,2,2,320,512]{4,3,2,1,0:T(8,128)(2,1)} %bitcast.26, bf16[4,2,2,320,512]{4,3,2,1,0:T(8,128)(2,1)} %bitcast.3.got_w, bf16[256,512]{1,0:T(8,128)(2,1)} %bitcast.29, bf16[256,512]{1,0:T(8,128)(2,1)} %copy-done.13), custom_call_target="tpu_custom_call" | custom-call | flops 1 | bytes 1 | tf_op jit(solution)/shard_map/hidden/hidden_part/pallas_call | solution.py:71
  46.6 3.5 %all-to-all-start.1 = ((bf16[4,320,256]{2,1,0:T(8,128)(2,1)}), bf16[4,320,256]{2,1,0:T(8,128)(2,1)S(1)}, u32[]{:S(2)}, u32[]{:S(2)}) async-start(bf16[4,320,256]{2,1,0:T(8,128)(2,1)} %hidden_part.2), calls=%async_computation.1 | async-start | bytes 1310720 | tf_op jit(solution)/shard_map/hidden/all_to_all | solution.py:270
  50.1 0.6 pad_add_fusion.1.place
  50.7 5.3 %hidden_part.3 = bf16[4,320,256]{2,1,0:T(8,128)(2,1)} custom-call(s32[2]{0:T(128)} %pad_add_fusion.1.place, bf16[4,2,2,320,512]{4,3,2,1,0:T(8,128)(2,1)} %bitcast.27, bf16[4,2,2,320,512]{4,3,2,1,0:T(8,128)(2,1)} %bitcast.3.got_w, bf16[256,512]{1,0:T(8,128)(2,1)} %bitcast.30, bf16[256,512]{1,0:T(8,128)(2,1)} %copy-done.13), custom_call_target="tpu_custom_call" | custom-call | flops 1 | bytes 1 | tf_op jit(solution)/shard_map/hidden/hidden_part/pallas_call | solution.py:71
  56.0 4.7 %all-to-all-done.1.v_ref = bf16[4,320,256]{2,1,0:T(8,128)(2,1)S(1)} async-done(((bf16[4,320,256]{2,1,0:T(8,128)(2,1)}), bf16[4,320,256]{2,1,0:T(8,128)(2,1)S(1)}, u32[]{:S(2)}, u32[]{:S(2)}) %all-to-all-start.1) | async-done | bytes 655392 | tf_op jit(solution)/shard_map/hidden/all_to_all | solution.py:270
  60.7 0.1 sum_parts.1
  60.8 1.9 %collective-permute-start.2 = (bf16[320,256]{1,0:T(8,128)(2,1)S(1)}, bf16[320,256]{1,0:T(8,128)(2,1)}, u32[]{:S(2)}, u32[]{:S(2)}) collective-permute-start(bf16[320,256]{1,0:T(8,128)(2,1)S(1)} %sum_parts.1), channel_id=1, source_target_pairs={{0,2},{2,0},{1,3},{3,1},{4,6},{6,4},{5,7},{7,5},{8,10},{10,8},{9,1... | collective-permute-start | bytes 491528 | tf_op jit(solution)/shard_map/hidden/ppermute | solution.py:41
  62.7 0.9 fusion.3.slope_ref
  63.6 4.2 %all-to-all-start.2 = ((bf16[4,320,256]{2,1,0:T(8,128)(2,1)}), bf16[4,320,256]{2,1,0:T(8,128)(2,1)}, u32[]{:S(2)}, u32[]{:S(2)}) async-start(bf16[4,320,256]{2,1,0:T(8,128)(2,1)} %hidden_part.3), calls=%async_computation.2 | async-start | bytes 1310720 | tf_op jit(solution)/shard_map/hidden/all_to_all | solution.py:270
  67.8 0.0 copy-start.11
  67.8 0.0 copy-start
  67.8 5.8 %collective-permute-done.2.v_ref = bf16[320,256]{1,0:T(8,128)(2,1)} collective-permute-done((bf16[320,256]{1,0:T(8,128)(2,1)S(1)}, bf16[320,256]{1,0:T(8,128)(2,1)}, u32[]{:S(2)}, u32[]{:S(2)}) %collective-permute-start.2) | collective-permute-done | bytes 163872 | tf_op jit(solution)/shard_map/hidden/ppermute | solution.py:41
  73.6 0.9 widen.2.got_ref
  74.5 0.7 copy-done.6
  75.3 2.1 %all-to-all-done.2.v_ref = bf16[4,320,256]{2,1,0:T(8,128)(2,1)} async-done(((bf16[4,320,256]{2,1,0:T(8,128)(2,1)}), bf16[4,320,256]{2,1,0:T(8,128)(2,1)}, u32[]{:S(2)}, u32[]{:S(2)}) %all-to-all-start.2) | async-done | bytes 655392 | tf_op jit(solution)/shard_map/hidden/all_to_all | solution.py:270
  77.4 1.0 copy-done.3
  78.3 1.0 copy-done.7
  79.3 1.4 act_rows.1.own_a
  80.7 9.0 %collective-permute-start.3 = (bf16[4,2,32,320]{3,2,1,0:T(8,128)(2,1)S(1)}, bf16[4,2,32,320]{3,2,1,0:T(8,128)(2,1)S(1)}, u32[]{:S(2)}, u32[]{:S(2)}) collective-permute-start(bf16[4,2,32,320]{3,2,1,0:T(8,128)(2,1)S(1)} %act_rows.1.own_a), channel_id=1, source_target_pairs={{0,1},{1,0},{2,3},{3,2},{4,5},{5,4},{6,7},{7,6},{8,9},{9,8},{10,11... | collective-permute-start | bytes 491528 | tf_op jit(solution)/shard_map/merged/ppermute | solution.py:41
  89.7 0.0 collective-permute-done.4.got_w
  89.7 1.0 collective-permute-done.3.got_a
  90.8 2.8 %merged_part.2 = bf16[4,32,2560]{2,1,0:T(8,128)(2,1)S(1)} custom-call(s32[2]{0:T(128)S(1)} %copy-done.9, bf16[4,2,32,320]{3,2,1,0:T(8,128)(2,1)S(1)} %act_rows.1.own_a, bf16[4,2,32,320]{3,2,1,0:T(8,128)(2,1)S(1)} %collective-permute-done.3.got_a, bf16[320,5120]{1,0:T(8,128)(2,1)S(1)} %bitcast.21, bf16[320,5120]{1,0:T(8,128)(2,1)} %collective-permute-done.4.got_w), custom_call_target="tpu_custom_call" | custom-call | flops 1 | bytes 1 | tf_op jit(solution)/shard_map/merged/merged_part/pallas_call | solution.py:161
  93.6 0.8 copy-done.2
  94.5 4.6 %all-to-all-start.3 = ((bf16[8,16,2560]{2,1,0:T(8,128)(2,1)}), bf16[8,16,2560]{2,1,0:T(8,128)(2,1)}, u32[]{:S(2)}, u32[]{:S(2)}) async-start(bf16[8,16,2560]{2,1,0:T(8,128)(2,1)} %bitcast.24), calls=%async_computation.3 | async-start | bytes 1310720 | tf_op jit(solution)/shard_map/merged/all_to_all | solution.py:278
  99.1 0.9 copy-done.5
  100.0 2.8 %merged_part.3 = bf16[4,32,2560]{2,1,0:T(8,128)(2,1)S(1)} custom-call(s32[2]{0:T(128)S(1)} %copy-done.10, bf16[4,2,32,320]{3,2,1,0:T(8,128)(2,1)S(1)} %act_rows.1.own_a, bf16[4,2,32,320]{3,2,1,0:T(8,128)(2,1)S(1)} %copy-done.5, bf16[320,5120]{1,0:T(8,128)(2,1)S(1)} %bitcast.22, bf16[320,5120]{1,0:T(8,128)(2,1)} %collective-permute-done.4.got_w), custom_call_target="tpu_custom_call" | custom-call | flops 1 | bytes 1 | tf_op jit(solution)/shard_map/merged/merged_part/pallas_call | solution.py:161
  102.8 0.8 copy-done.1
  103.7 6.4 %all-to-all-done.3.v_ref = bf16[8,16,2560]{2,1,0:T(8,128)(2,1)} async-done(((bf16[8,16,2560]{2,1,0:T(8,128)(2,1)}), bf16[8,16,2560]{2,1,0:T(8,128)(2,1)}, u32[]{:S(2)}, u32[]{:S(2)}) %all-to-all-start.3) | async-done | bytes 655392 | tf_op jit(solution)/shard_map/merged/all_to_all | solution.py:278
  110.1 1.2 sum_halves.1
  111.3 4.9 %collective-permute-start.5 = (bf16[2,16,2560]{2,1,0:T(8,128)(2,1)S(1)}, bf16[2,16,2560]{2,1,0:T(8,128)(2,1)S(1)}, u32[]{:S(2)}, u32[]{:S(2)}) collective-permute-start(bf16[2,16,2560]{2,1,0:T(8,128)(2,1)S(1)} %sum_halves.1), channel_id=1, source_target_pairs={{0,2},{2,0},{1,3},{3,1},{4,6},{6,4},{5,7},{7,5},{8,10},{10,8},{9,1... | collective-permute-start | bytes 491528 | tf_op jit(solution)/shard_map/merged/ppermute | solution.py:41
  116.2 4.6 %all-to-all-start.4 = ((bf16[8,16,2560]{2,1,0:T(8,128)(2,1)}), bf16[8,16,2560]{2,1,0:T(8,128)(2,1)S(1)}, u32[]{:S(2)}, u32[]{:S(2)}) async-start(bf16[8,16,2560]{2,1,0:T(8,128)(2,1)} %bitcast.23), calls=%async_computation.4 | async-start | bytes 1310720 | tf_op jit(solution)/shard_map/merged/all_to_all | solution.py:278
  120.8 3.5 %collective-permute-done.5.v_ref = bf16[2,16,2560]{2,1,0:T(8,128)(2,1)S(1)} collective-permute-done((bf16[2,16,2560]{2,1,0:T(8,128)(2,1)S(1)}, bf16[2,16,2560]{2,1,0:T(8,128)(2,1)S(1)}, u32[]{:S(2)}, u32[]{:S(2)}) %collective-permute-start.5) | collective-permute-done | bytes 163872 | tf_op jit(solution)/shard_map/merged/ppermute | solution.py:41
  124.3 7.4 %all-to-all-done.4.v_ref = bf16[8,16,2560]{2,1,0:T(8,128)(2,1)S(1)} async-done(((bf16[8,16,2560]{2,1,0:T(8,128)(2,1)}), bf16[8,16,2560]{2,1,0:T(8,128)(2,1)S(1)}, u32[]{:S(2)}, u32[]{:S(2)}) %all-to-all-start.4) | async-done | bytes 655392 | tf_op jit(solution)/shard_map/merged/all_to_all | solution.py:278
  131.7 0.9 norm_part.1
  132.7 8.1 %all_to_all.40 = f32[8,10,128]{2,1,0:T(8,128)S(1)} all-to-all(f32[8,10,128]{2,1,0:T(8,128)S(1)} %broadcast_in_dim.9), channel_id=1, replica_groups=mesh['y'=8,'zl'=6,'x'=4,'zh'=2,'co'=2] {'x','co'}, dimensions={0} | all-to-all | bytes 81920 | tf_op jit(solution)/shard_map/gain/all_to_all | solution.py:234
  140.8 13.8 %all_to_all.41 = f32[8,10,128]{2,1,0:T(8,128)S(1)} all-to-all(f32[8,10,128]{2,1,0:T(8,128)S(1)} %broadcast_in_dim.10), channel_id=1, replica_groups=mesh['y'=8,'zl'=6,'x'=4,'zh'=2,'co'=2] {'y'}, dimensions={0} | all-to-all | bytes 81920 | tf_op jit(solution)/shard_map/gain/all_to_all | solution.py:234
  154.7 20.4 %all_to_all.42 = f32[12,10,128]{2,1,0:T(8,128)S(1)} all-to-all(f32[12,10,128]{2,1,0:T(8,128)S(1)} %broadcast_in_dim.22), channel_id=1, replica_groups=mesh['y'=8,'zl'=6,'x'=4,'zh'=2,'co'=2] {'zl','zh'}, dimensions={0} | all-to-all | bytes 122880 | tf_op jit(solution)/shard_map/gain/all_to_all | solution.py:234
  175.1 0.6 multiply_bitcast_fusion
  (32 shorter events, 0.2 us)
Async XLA Ops:
  0.6 40.0 %collective-permute-start = (bf16[5120,512]{1,0:T(8,128)(2,1)}, bf16[5120,512]{1,0:T(8,128)(2,1)}, u32[]{:S(2)}, u32[]{:S(2)}) collective-permute-start(bf16[5120,512]{1,0:T(8,128)(2,1)} %param.10), channel_id=1, source_target_pairs={{0,1},{1,0},{2,3},{3,2},{4,5},{5,4},{6,7},{7,6},{8,9},{9,8},{10,11... | collective-permute-start | bytes 15728648 | tf_op jit(solution)/shard_map/weights/ppermute | solution.py:41
  14.8 21.8 %all-to-all-start = ((bf16[16,16,512]{2,1,0:T(8,128)(2,1)}), bf16[16,16,512]{2,1,0:T(8,128)(2,1)S(1)}, u32[]{:S(2)}, u32[]{:S(2)}) async-start(bf16[16,16,512]{2,1,0:T(8,128)(2,1)} %bitcast.19), calls=%async_computation | async-start | bytes 524288 | tf_op jit(solution)/shard_map/tokens/all_to_all | solution.py:248
  22.8 66.9 %collective-permute-start.4 = (bf16[320,5120]{1,0:T(8,128)(2,1)}, bf16[320,5120]{1,0:T(8,128)(2,1)}, u32[]{:S(2)}, u32[]{:S(2)}) collective-permute-start(bf16[320,5120]{1,0:T(8,128)(2,1)} %bitcast.20), channel_id=1, source_target_pairs={{0,1},{1,0},{2,3},{3,2},{4,5},{5,4},{6,7},{7,6},{8,9},{9,8},{10,11... | collective-permute-start | bytes 9830408 | tf_op jit(solution)/shard_map/weights/ppermute | solution.py:41
  36.6 4.1 %copy-start.12 = (bf16[16,16,512]{2,1,0:T(8,128)(2,1)}, bf16[16,16,512]{2,1,0:T(8,128)(2,1)S(1)}, u32[]{:S(2)}) copy-start(bf16[16,16,512]{2,1,0:T(8,128)(2,1)S(1)} %all-to-all-done) | copy-start | bytes 786436
  36.6 4.1 %collective-permute-start.1 = (bf16[256,512]{1,0:T(8,128)(2,1)S(1)}, bf16[256,512]{1,0:T(8,128)(2,1)S(1)}, u32[]{:S(2)}, u32[]{:S(2)}) collective-permute-start(bf16[256,512]{1,0:T(8,128)(2,1)S(1)} %bitcast.28), channel_id=1, source_target_pairs={{0,1},{1,0},{2,3},{3,2},{4,5},{5,4},{6,7},{7,6},{8,9},{9,8},{10,11... | collective-permute-start | bytes 786440 | tf_op jit(solution)/shard_map/tokens/ppermute | solution.py:41
  40.7 0.7 copy-start.13
  46.6 14.1 %all-to-all-start.1 = ((bf16[4,320,256]{2,1,0:T(8,128)(2,1)}), bf16[4,320,256]{2,1,0:T(8,128)(2,1)S(1)}, u32[]{:S(2)}, u32[]{:S(2)}) async-start(bf16[4,320,256]{2,1,0:T(8,128)(2,1)} %hidden_part.2), calls=%async_computation.1 | async-start | bytes 1310720 | tf_op jit(solution)/shard_map/hidden/all_to_all | solution.py:270
  50.7 12.1 %copy-start.14 = (bf16[320,256]{1,0:T(8,128)(2,1)S(1)}, bf16[320,256]{1,0:T(8,128)(2,1)}, u32[]{:S(2)}) copy-start(bf16[320,256]{1,0:T(8,128)(2,1)} %param.8) | copy-start | bytes 491524
  60.8 12.8 %collective-permute-start.2 = (bf16[320,256]{1,0:T(8,128)(2,1)S(1)}, bf16[320,256]{1,0:T(8,128)(2,1)}, u32[]{:S(2)}, u32[]{:S(2)}) collective-permute-start(bf16[320,256]{1,0:T(8,128)(2,1)S(1)} %sum_parts.1), channel_id=1, source_target_pairs={{0,2},{2,0},{1,3},{3,1},{4,6},{6,4},{5,7},{7,5},{8,10},{10,8},{9,1... | collective-permute-start | bytes 491528 | tf_op jit(solution)/shard_map/hidden/ppermute | solution.py:41
  63.6 13.7 %all-to-all-start.2 = ((bf16[4,320,256]{2,1,0:T(8,128)(2,1)}), bf16[4,320,256]{2,1,0:T(8,128)(2,1)}, u32[]{:S(2)}, u32[]{:S(2)}) async-start(bf16[4,320,256]{2,1,0:T(8,128)(2,1)} %hidden_part.3), calls=%async_computation.2 | async-start | bytes 1310720 | tf_op jit(solution)/shard_map/hidden/all_to_all | solution.py:270
  67.8 9.6 %copy-start.11 = (s32[256]{0:T(256)S(1)}, s32[256]{0:T(256)}, u32[]{:S(2)}) copy-start(s32[256]{0:T(256)} %param.13) | copy-start | bytes 3076
  67.8 23.0 %copy-start = (bf16[5120,320]{0,1:T(8,128)(2,1)S(1)}, bf16[5120,320]{0,1:T(8,128)(2,1)}, u32[]{:S(2)}) copy-start(bf16[5120,320]{0,1:T(8,128)(2,1)} %param.9) | copy-start | bytes 9830404
  67.8 23.0 %copy-start.9 = (s32[2]{0:T(128)S(1)}, s32[2]{0:T(128)}, u32[]{:S(2)}) copy-start(s32[2]{0:T(128)} %pad_add_fusion.place) | copy-start | bytes 28
  74.5 0.7 copy-start.6
  75.3 23.8 %copy-start.10 = (s32[2]{0:T(128)S(1)}, s32[2]{0:T(128)}, u32[]{:S(2)}) copy-start(s32[2]{0:T(128)} %pad_add_fusion.1.place) | copy-start | bytes 28
  77.4 1.0 copy-start.3
  78.3 1.0 copy-start.7
  80.7 10.0 %collective-permute-start.3 = (bf16[4,2,32,320]{3,2,1,0:T(8,128)(2,1)S(1)}, bf16[4,2,32,320]{3,2,1,0:T(8,128)(2,1)S(1)}, u32[]{:S(2)}, u32[]{:S(2)}) collective-permute-start(bf16[4,2,32,320]{3,2,1,0:T(8,128)(2,1)S(1)} %act_rows.1.own_a), channel_id=1, source_target_pairs={{0,1},{1,0},{2,3},{3,2},{4,5},{5,4},{6,7},{7,6},{8,9},{9,8},{10,11... | collective-permute-start | bytes 491528 | tf_op jit(solution)/shard_map/merged/ppermute | solution.py:41
  90.8 2.8 %copy-start.4 = (bf16[4,2,32,320]{3,2,1,0:T(8,128)(2,1)}, bf16[4,2,32,320]{3,2,1,0:T(8,128)(2,1)S(1)}, u32[]{:S(2)}) copy-start(bf16[4,2,32,320]{3,2,1,0:T(8,128)(2,1)S(1)} %collective-permute-done.3.got_a) | copy-start | bytes 491524
  93.6 0.9 copy-start.2
  94.5 21.7 %copy-start.15 = (f32[1280]{0:T(1024)S(1)}, f32[1280]{0:T(1024)}, u32[]{:S(2)}) copy-start(f32[1280]{0:T(1024)} %param.12) | copy-start | bytes 15364
  94.5 15.6 %all-to-all-start.3 = ((bf16[8,16,2560]{2,1,0:T(8,128)(2,1)}), bf16[8,16,2560]{2,1,0:T(8,128)(2,1)}, u32[]{:S(2)}, u32[]{:S(2)}) async-start(bf16[8,16,2560]{2,1,0:T(8,128)(2,1)} %bitcast.24), calls=%async_computation.3 | async-start | bytes 1310720 | tf_op jit(solution)/shard_map/merged/all_to_all | solution.py:278
  99.1 0.9 copy-start.5
  102.8 0.8 copy-start.1
  111.3 13.0 %collective-permute-start.5 = (bf16[2,16,2560]{2,1,0:T(8,128)(2,1)S(1)}, bf16[2,16,2560]{2,1,0:T(8,128)(2,1)S(1)}, u32[]{:S(2)}, u32[]{:S(2)}) collective-permute-start(bf16[2,16,2560]{2,1,0:T(8,128)(2,1)S(1)} %sum_halves.1), channel_id=1, source_target_pairs={{0,2},{2,0},{1,3},{3,1},{4,6},{6,4},{5,7},{7,5},{8,10},{10,8},{9,1... | collective-permute-start | bytes 491528 | tf_op jit(solution)/shard_map/merged/ppermute | solution.py:41
  116.2 15.5 %all-to-all-start.4 = ((bf16[8,16,2560]{2,1,0:T(8,128)(2,1)}), bf16[8,16,2560]{2,1,0:T(8,128)(2,1)S(1)}, u32[]{:S(2)}, u32[]{:S(2)}) async-start(bf16[8,16,2560]{2,1,0:T(8,128)(2,1)} %bitcast.23), calls=%async_computation.4 | async-start | bytes 1310720 | tf_op jit(solution)/shard_map/merged/all_to_all | solution.py:278
  120.8 10.9 %copy-start.8 = (bf16[16,5120]{1,0:T(8,128)(2,1)S(1)}, bf16[16,5120]{1,0:T(8,128)(2,1)}, u32[]{:S(2)}) copy-start(bf16[16,5120]{1,0:T(8,128)(2,1)} %patch_ref.1) | copy-start | bytes 491524

commit v4 on v3

--- a/solution.py
+++ b/solution.py
@@ -41,10 +41,15 @@
     return lax.ppermute(value, axis, [(0, 1), (1, 0)])
 
 
-def hidden_kernel(place, own_w, got_w, own_t, got_t, out_ref, block, arrived):
+def hidden_kernel(place, own_w, got_w, own_t, got_t, out_ref, block, tokens, arrived):
+    depth = own_t.shape[1]
     copies = [
         [
-            pltpu.make_async_copy(w_ref.at[i, place[0], place[1]], block.at[i, k], arrived.at[i, k])
+            pltpu.make_async_copy(
+                w_ref.at[i, place[0], place[1]],
+                block.at[i, :, pl.ds(k * depth, depth)],
+                arrived.at[i, k],
+            )
             for k, w_ref in enumerate((own_w, got_w))
         ]
         for i in range(NX)
@@ -52,14 +57,14 @@
     for pair in copies:
         for copy in pair:
             copy.start()
+    for k, t_ref in enumerate((own_t, got_t)):
+        tokens[k * depth : (k + 1) * depth, :] = t_ref[...].T
     for i, pair in enumerate(copies):
-        total = None
-        for k, t_ref in enumerate((own_t, got_t)):
-            pair[k].wait()
-            term = lax.dot_general(
-                block[i, k], t_ref[...], (((1,), (1,)), ((), ())), preferred_element_type=F32
-            )
-            total = term if total is None else total + term
+        for copy in pair:
+            copy.wait()
+        total = lax.dot_general(
+            block[i], tokens[...], (((1,), (0,)), ((), ())), preferred_element_type=F32
+        )
         out_ref[i] = total.astype(BF16)
 
 
@@ -74,7 +79,8 @@
         out_specs=IN_VMEM,
         out_shape=jax.ShapeDtypeStruct((NX, units, count), BF16),
         scratch_shapes=[
-            pltpu.VMEM((NX, 2, units, depth), BF16),
+            pltpu.VMEM((NX, units, 2 * depth), BF16),
+            pltpu.VMEM((2 * depth, count), BF16),
             pltpu.SemaphoreType.DMA((NX, 2)),
         ],
         compiler_params=params(60),
@@ -124,14 +130,20 @@
     pick = (lax.broadcasted_iota(jnp.int32, (count, count), 0) == pos_ref[...]).astype(F32)
     pick = pick.T.astype(BF16)
     moved = lax.dot_general(pick, act, (((1,), (1,)), ((), ())), preferred_element_type=F32)
-    out_ref[...] = moved.astype(BF16).reshape(out_ref.shape)
+    moved = moved.astype(BF16)
+    own = out_ref.shape[3]
+    for x in range(NX):
+        for z in range(NZH):
+            for c in range(NCO):
+                first = ((x * NZH + z) * NCO + c) * own
+                out_ref[x, c, z] = moved[first : first + own]
 
 
 def act_rows(parts, got, slope, owner_pos):
     units, count = got.shape
     return pl.pallas_call(
         act_kernel,
-        out_shape=jax.ShapeDtypeStruct((NX, NZH, count // (NX * NZH), units), BF16),
+        out_shape=jax.ShapeDtypeStruct((NX, NCO, NZH, count // (NX * NCO * NZH), units), BF16),
         compiler_params=params(),
         cost_estimate=cost(),
         name="act_rows",
@@ -152,43 +164,67 @@
     out_ref[...] = total.astype(BF16).reshape(out_ref.shape)
 
 
-def merged_part(acts, weights, place):
-    _, _, rows, depth = acts[0].shape
+def merged_part(acts, weights, core):
+    depth = acts[0].shape[-1]
     cols = weights[0].shape[1] // NCO
     steps = 2
-    a_spec = pl.BlockSpec((NX, 1, rows, depth), lambda i, s: (0, s[0], 0, 0))
-    w_spec = pl.BlockSpec((depth, cols // steps), lambda i, s: (0, s[1] * steps + i))
+    a_spec = pl.BlockSpec(acts[0].shape, lambda i, s: (0, 0, 0, 0, 0))
+    w_spec = pl.BlockSpec((depth, cols // steps), lambda i, s: (0, s[0] * steps + i))
+    shape = acts[0].shape[:-1]
     return pl.pallas_call(
         merged_kernel,
         grid_spec=pltpu.PrefetchScalarGridSpec(
             num_scalar_prefetch=1,
             grid=(steps,),
             in_specs=[a_spec, a_spec, w_spec, w_spec],
-            out_specs=pl.BlockSpec((NX, rows, cols // steps), lambda i, s: (0, 0, i)),
+            out_specs=pl.BlockSpec(shape + (cols // steps,), lambda i, s: (0, 0, 0, 0, i)),
         ),
-        out_shape=jax.ShapeDtypeStruct((NX, rows, cols), BF16),
+        out_shape=jax.ShapeDtypeStruct(shape + (cols,), BF16),
         compiler_params=params(),
         cost_estimate=cost(),
         name="merged_part",
-    )(place, *acts, *weights)
-
-
-def halves_kernel(v_ref, out_ref):
+    )(core, *acts, *weights)
+
+
+def halves_kernel(place, v_ref, out_ref):
+    z = place[0]
     for c in range(NCO):
-        total = v_ref[c].astype(F32)
+        total = v_ref[c, z].astype(F32)
         for x in range(1, NX):
-            total += v_ref[NCO * x + c].astype(F32)
+            total += v_ref[NCO * x + c, z].astype(F32)
         out_ref[c] = total.astype(BF16)
 
 
-def sum_halves(parts):
+def sum_halves(parts, place):
     return pl.pallas_call(
         halves_kernel,
-        out_shape=jax.ShapeDtypeStruct((NCO,) + parts.shape[1:], BF16),
+        in_specs=[IN_SMEM, IN_VMEM],
+        out_specs=IN_VMEM,
+        out_shape=jax.ShapeDtypeStruct((NCO,) + parts.shape[2:], BF16),
         compiler_params=params(),
         cost_estimate=cost(),
         name="sum_halves",
-    )(parts)
+    )(place, parts)
+
+
+def pack_kernel(core, own_ref, got_ref, out_ref):
+    half = out_ref.shape[2]
+    cols = pl.ds(pl.multiple_of(core[0] * half, 128), half)
+    out_ref[core[0]] = own_ref[:, cols]
+    out_ref[1 - core[0]] = got_ref[:, cols]
+
+
+def pack_patches(own, got, core):
+    rows, cols = own.shape
+    return pl.pallas_call(
+        pack_kernel,
+        in_specs=[IN_SMEM, IN_VMEM, IN_VMEM],
+        out_specs=IN_VMEM,
+        out_shape=jax.ShapeDtypeStruct((NCO, rows, cols // NCO), BF16),
+        compiler_params=params(),
+        cost_estimate=cost(),
+        name="pack_patches",
+    )(core, own, got)
 
 
 def norm_of(patch):
@@ -196,37 +232,62 @@
     return patch * inv_rms, inv_rms
 
 
-def norm_kernel(v_ref, got_ref, patch_ref, gain_ref, out_ref, terms_ref):
+def gain_kernel(place, grad_ref, *refs):
+    out_ref = refs[-1]
+    width = out_ref.shape[1]
+    terms = jnp.zeros((1, width), F32)
+    for shift, patch_ref in enumerate(refs[:-1]):
+        x = lax.rem(place[0] + shift, NX)
+        for k in range(NZH):
+            z = place[1] if k == 0 else 1 - place[1]
+            for c in range(NCO):
+                for p in range(grad_ref.shape[4] // width):
+                    cols = pl.ds(p * width, width)
+                    normed, _ = norm_of(patch_ref[k, c, :, cols].astype(F32))
+                    grad = grad_ref[x, c, z, :, cols].astype(F32)
+                    terms += jnp.sum(grad * normed, axis=0, keepdims=True)
+    out_ref[...] = terms
+
+
+def gain_terms(grads, patches, place, width):
+    return pl.pallas_call(
+        gain_kernel,
+        in_specs=[IN_SMEM] + [IN_VMEM] * (1 + NX),
+        out_specs=IN_VMEM,
+        out_shape=jax.ShapeDtypeStruct((1, width), F32),
+        compiler_params=params(),
+        cost_estimate=cost(LONG),
+        name="gain_terms",
+    )(place, grads, *patches)
+
+
+def norm_kernel(place, v_ref, got_ref, patch_ref, gain_ref, out_ref):
     width = gain_ref.shape[1]
     gain = gain_ref[...]
+    z = place[0]
     in_half = patch_ref.shape[1] // width // NCO
-    terms = jnp.zeros((1, width), F32)
     for p in range(patch_ref.shape[1] // width):
         c, q = p // in_half, pl.ds(p % in_half * width, width)
         cols = pl.ds(p * width, width)
-        owner = got_ref[c, :, q]
+        owner = got_ref[c, :, q].astype(F32)
         for x in range(NX):
-            owner += v_ref[NCO * x + c, :, q].astype(F32)
+            owner += v_ref[NCO * x + c, z, :, q].astype(F32)
         normed, inv_rms = norm_of(patch_ref[:, cols].astype(F32))
         scaled = owner * gain
         inner = jnp.mean(scaled * normed, axis=-1, keepdims=True)
         out_ref[:, cols] = (inv_rms * (scaled - normed * inner)).astype(BF16)
-        terms += jnp.sum(owner * normed, axis=0, keepdims=True)
-    terms_ref[...] = terms
-
-
-def norm_part(parts, got, patch_in, norm_gain):
-    width = norm_gain.shape[0]
+
+
+def norm_part(parts, got, patch_in, norm_gain, place):
     return pl.pallas_call(
         norm_kernel,
-        out_shape=[
-            jax.ShapeDtypeStruct(patch_in.shape, BF16),
-            jax.ShapeDtypeStruct((1, width), F32),
-        ],
-        compiler_params=params(),
-        cost_estimate=cost(),
+        in_specs=[IN_SMEM] + [IN_VMEM] * 4,
+        out_specs=IN_VMEM,
+        out_shape=jax.ShapeDtypeStruct(patch_in.shape, BF16),
+        compiler_params=params(),
+        cost_estimate=cost(LONG),
         name="norm_part",
-    )(parts, got, patch_in, norm_gain.reshape(1, width))
+    )(place, parts, got, patch_in, norm_gain.reshape(1, -1))
 
 
 def sum_over(terms, axes, count):
@@ -252,40 +313,42 @@
         w_fc1_t = w_fc1.T
         weights_1 = (w_fc1_t, swap(w_fc1_t, "co"))
 
-    def exchange(part, deliver, add_up):
-        far_sum = part(far_z, None)
-        far = deliver(far_sum)
-        near_sum = part(near_z, far_sum)
+    with jax.named_scope("patches"):
+        patches = pack_patches(patch_in, swap(patch_in, "co"), co.reshape(1))
+
+    def tie(value, first):
+        return lax.optimization_barrier((value, first))[0]
+
+    with jax.named_scope("hidden"):
+        far_sum = hidden_part(weights_2, tokens, far_z)
+        far = lax.all_to_all(far_sum, "x", 0, 0, tiled=True)
+        patches = jnp.stack([patches, swap(tie(patches, far_sum), "zh")])
+        near_sum = hidden_part(weights_2, tie(tokens, far_sum), near_z)
         far, near_sum = lax.optimization_barrier((far, near_sum))
-        far = add_up(far)
-        near_sum, _ = lax.optimization_barrier((near_sum, far))
-        return deliver(near_sum), widen(swap(far, "zh"))
-
-    def after(values, first):
-        return values if first is None else lax.optimization_barrier((values, first))[0]
-
-    with jax.named_scope("hidden"):
-        near, got = exchange(
-            lambda z, first: hidden_part(weights_2, after(tokens, first), z),
-            lambda v: lax.all_to_all(v, "x", 0, 0, tiled=True),
-            sum_parts,
-        )
+        far = sum_parts(far)
+        near = lax.all_to_all(tie(near_sum, far), "x", 0, 0, tiled=True)
+        got = widen(swap(far, "zh"))
+        patches = tie(patches, far)
+        around = [patches] + [
+            lax.ppermute(patches, "x", [(i, (i - d) % NX) for i in range(NX)]) for d in (1, 2, 3)
+        ]
     with jax.named_scope("merged"):
         act = act_rows(near, got, slope, owner_pos)
-        acts = (act, swap(act, "co"))
-        near, got = exchange(
-            lambda z, first: merged_part(after(acts, first), weights_1, z),
-            lambda v: lax.all_to_all(
-                v.reshape(NX * NCO, own, half), ("x", "co"), 0, 0, tiled=True
-            ),
-            sum_halves,
-        )
+        grads = merged_part((act, swap(act, "co")), weights_1, co.reshape(1))
+        parts = lax.all_to_all(
+            grads.reshape(NX * NCO, NZH * own, half), ("x", "co"), 0, 0, tiled=True
+        ).reshape(NX * NCO, NZH, own, half)
+        here = jnp.stack([lax.axis_index("x").astype(jnp.int32), zh])
+        terms = gain_terms(grads, around, here, norm_gain.shape[0]).reshape(-1, 128)
+        terms = lax.psum(lax.psum(terms, "co"), "x")
+        parts, terms = lax.optimization_barrier((parts, terms))
+        far = sum_halves(parts, (1 - zh).reshape(1))
+        got = swap(far, "zh")
+    with jax.named_scope("gain"):
+        terms = lax.psum(tie(terms, far), "y")
     with jax.named_scope("norm"):
-        patch_grad, terms = norm_part(near, got, patch_in, norm_gain)
+        patch_grad = norm_part(parts, got, patch_in, norm_gain, zh.reshape(1))
     with jax.named_scope("gain"):
-        terms = terms.reshape(-1, 128)
-        terms = sum_over(terms, ("x", "co"), NX * NCO)
-        terms = sum_over(terms, "y", NY)
         terms = sum_over(terms, ("zl", "zh"), NZL * NZH)
         gain_grad = terms.reshape(-1) / (NY * NZL * ctx)
     return (patch_grad, gain_grad)

time: 178 us -> 185 us (1.039)
  the two profiles are of different devices: /device:TPU:1 before, /device:TPU:8 now
where the time goes in v4:
time: 185 us; the launch traced here: 184 us
  starting transfers between devices  77.6 us (42%)
  waiting for transfers between devices  42.1 us (23%)
  blocking collectives  34.9 us (19%)
  Pallas kernels  19.1 us (10%)
  local copies, waits for them, and re-layouts  5.75 us (3%)
  other arithmetic  3.51 us (2%)
    ppermute x8, starting transfers between devices, swap(): return lax.ppermute(value, axis, [(0, 1), (1, 0)])  22.4 us
    psum x2, blocking collectives, local(): terms = lax.psum(lax.psum(terms, 'co'), 'x')  18.4 us
    all_to_all x1, starting transfers between devices, local(): lax.all_to_all(outgoing, CTX, 0, 0, tiled=True).reshape(group, depth // ctx)  17.2 us
    psum x1, blocking collectives, local(): terms = lax.psum(tie(terms, far), 'y')  16.4 us
    all_to_all x1, starting transfers between devices, sum_over(): return jnp.sum(lax.all_to_all(rows, axes, 0, 0, tiled=True), axis=0)  16.4 us
    all_to_all x1, waiting for transfers between devices, local(): near = lax.all_to_all(tie(near_sum, far), 'x', 0, 0, tiled=True)  13.4 us
    all_to_all x1, waiting for transfers between devices, local(): lax.all_to_all(outgoing, CTX, 0, 0, tiled=True).reshape(group, depth // ctx)  12.3 us
    ppermute x3, starting transfers between devices, local(): lax.ppermute(patches, 'x', [(i, (i - d) % NX) for i in range(NX)])  10.4 us
  transfers between devices with their start and end apart: 16, of which 6 were waited for; matrix products, arithmetic and copies ran while one was open for 3% of the time, Pallas kernels for 10%

profile of v4, /device:TPU:8, one launch (start us, length us, event | category | flops | bytes accessed | tf_op | source)
XLA Modules:
  0.0 183.9 jit_solution(16934978251721010063)
XLA Ops:
  0.6 1.9 %collective-permute-start = (bf16[5120,512]{1,0:T(8,128)(2,1)}, bf16[5120,512]{1,0:T(8,128)(2,1)}, u32[]{:S(2)}, u32[]{:S(2)}) collective-permute-start(bf16[5120,512]{1,0:T(8,128)(2,1)} %param.10), channel_id=1, source_target_pairs={{0,1},{1,0},{2,3},{3,2},{4,5},{5,4},{6,7},{7,6},{8,9},{9,8},{10,11... | collective-permute-start | bytes 15728648 | tf_op jit(solution)/shard_map/weights/ppermute | solution.py:41
  2.6 1.7 copy.16
  4.3 17.2 %all-to-all-start = ((bf16[16,16,512]{2,1,0:T(8,128)(2,1)}), bf16[16,16,512]{2,1,0:T(8,128)(2,1)S(1)}, u32[]{:S(2)}, u32[]{:S(2)}) async-start(bf16[16,16,512]{2,1,0:T(8,128)(2,1)} %bitcast.22), calls=%async_computation | async-start | bytes 524288 | tf_op jit(solution)/shard_map/tokens/all_to_all | solution.py:309
  21.4 2.3 %collective-permute-start.4 = (bf16[320,5120]{1,0:T(8,128)(2,1)}, bf16[320,5120]{1,0:T(8,128)(2,1)}, u32[]{:S(2)}, u32[]{:S(2)}) collective-permute-start(bf16[320,5120]{1,0:T(8,128)(2,1)} %bitcast.25), channel_id=1, source_target_pairs={{0,1},{1,0},{2,3},{3,2},{4,5},{5,4},{6,7},{7,6},{8,9},{9,8},{10,11... | collective-permute-start | bytes 9830408 | tf_op jit(solution)/shard_map/weights/ppermute | solution.py:41
  23.8 12.3 %all-to-all-done = bf16[16,16,512]{2,1,0:T(8,128)(2,1)S(1)} async-done(((bf16[16,16,512]{2,1,0:T(8,128)(2,1)}), bf16[16,16,512]{2,1,0:T(8,128)(2,1)S(1)}, u32[]{:S(2)}, u32[]{:S(2)}) %all-to-all-start) | async-done | bytes 262176 | tf_op jit(solution)/shard_map/tokens/all_to_all | solution.py:309
  36.1 1.9 %collective-permute-start.1 = (bf16[256,512]{1,0:T(8,128)(2,1)S(1)}, bf16[256,512]{1,0:T(8,128)(2,1)S(1)}, u32[]{:S(2)}, u32[]{:S(2)}) collective-permute-start(bf16[256,512]{1,0:T(8,128)(2,1)S(1)} %bitcast.31), channel_id=1, source_target_pairs={{0,1},{1,0},{2,3},{3,2},{4,5},{5,4},{6,7},{7,6},{8,9},{9,8},{10,11... | collective-permute-start | bytes 786440 | tf_op jit(solution)/shard_map/tokens/ppermute | solution.py:41
  38.0 2.4 %collective-permute-start.5 = (bf16[16,5120]{1,0:T(8,128)(2,1)}, bf16[16,5120]{1,0:T(8,128)(2,1)S(1)}, u32[]{:S(2)}, u32[]{:S(2)}) collective-permute-start(bf16[16,5120]{1,0:T(8,128)(2,1)} %patch_ref.1), channel_id=1, source_target_pairs={{0,1},{1,0},{2,3},{3,2},{4,5},{5,4},{6,7},{7,6},{8,9},{9,8},{10,11... | collective-permute-start | bytes 491528 | tf_op jit(solution)/shard_map/patches/ppermute | solution.py:41
  40.4 0.6 pad_add_fusion.place
  41.1 0.7 copy-done.8
  41.8 5.0 %hidden_part.2 = bf16[4,320,256]{2,1,0:T(8,128)(2,1)} custom-call(s32[2]{0:T(128)} %pad_add_fusion.place, bf16[4,2,2,320,512]{4,3,2,1,0:T(8,128)(2,1)} %bitcast.29, bf16[4,2,2,320,512]{4,3,2,1,0:T(8,128)(2,1)} %bitcast.4.got_w, bf16[256,512]{1,0:T(8,128)(2,1)} %bitcast.32, bf16[256,512]{1,0:T(8,128)(2,1)} %copy-done.8), custom_call_target="tpu_custom_call" | custom-call | flops 1 | bytes 1 | tf_op jit(solution)/shard_map/hidden/hidden_part/pallas_call | solution.py:76
  46.8 3.5 %all-to-all-start.1 = ((bf16[4,320,256]{2,1,0:T(8,128)(2,1)}), bf16[4,320,256]{2,1,0:T(8,128)(2,1)S(1)}, u32[]{:S(2)}, u32[]{:S(2)}) async-start(bf16[4,320,256]{2,1,0:T(8,128)(2,1)} %hidden_part.2), calls=%async_computation.1 | async-start | bytes 1310720 | tf_op jit(solution)/shard_map/hidden/all_to_all | solution.py:324
  50.4 2.1 %collective-permute-start.6 = (bf16[2,16,2560]{2,1,0:T(8,128)(2,1)S(1)}, bf16[2,16,2560]{2,1,0:T(8,128)(2,1)S(1)}, u32[]{:S(2)}, u32[]{:S(2)}) collective-permute-start(bf16[2,16,2560]{2,1,0:T(8,128)(2,1)S(1)} %pack_patches.1), channel_id=1, source_target_pairs={{0,2},{2,0},{1,3},{3,1},{4,6},{6,4},{5,7},{7,5},{8,10},{10,8},{9,1... | collective-permute-start | bytes 491528 | tf_op jit(solution)/shard_map/hidden/ppermute | solution.py:41
  52.5 0.9 fusion.3.slope_ref
  53.3 0.6 pad_add_fusion.1.place
  53.9 5.1 %hidden_part.3 = bf16[4,320,256]{2,1,0:T(8,128)(2,1)} custom-call(s32[2]{0:T(128)} %pad_add_fusion.1.place, bf16[4,2,2,320,512]{4,3,2,1,0:T(8,128)(2,1)} %bitcast.30, bf16[4,2,2,320,512]{4,3,2,1,0:T(8,128)(2,1)} %bitcast.4.got_w, bf16[256,512]{1,0:T(8,128)(2,1)} %bitcast.33, bf16[256,512]{1,0:T(8,128)(2,1)} %copy-done.8), custom_call_target="tpu_custom_call" | custom-call | flops 1 | bytes 1 | tf_op jit(solution)/shard_map/hidden/hidden_part/pallas_call | solution.py:76
  59.0 2.7 %all-to-all-done.1.v_ref = bf16[4,320,256]{2,1,0:T(8,128)(2,1)S(1)} async-done(((bf16[4,320,256]{2,1,0:T(8,128)(2,1)}), bf16[4,320,256]{2,1,0:T(8,128)(2,1)S(1)}, u32[]{:S(2)}, u32[]{:S(2)}) %all-to-all-start.1) | async-done | bytes 655392 | tf_op jit(solution)/shard_map/hidden/all_to_all | solution.py:324
  61.6 0.1 sum_parts.1
  61.7 7.4 %collective-permute-start.2 = (bf16[320,256]{1,0:T(8,128)(2,1)S(1)}, bf16[320,256]{1,0:T(8,128)(2,1)S(1)}, u32[]{:S(2)}, u32[]{:S(2)}) collective-permute-start(bf16[320,256]{1,0:T(8,128)(2,1)S(1)} %sum_parts.1), channel_id=1, source_target_pairs={{0,2},{2,0},{1,3},{3,1},{4,6},{6,4},{5,7},{7,5},{8,10},{10,8},{9,1... | collective-permute-start | bytes 491528 | tf_op jit(solution)/shard_map/hidden/ppermute | solution.py:41
  69.1 2.6 %collective-permute-done.6 = bf16[2,16,2560]{2,1,0:T(8,128)(2,1)S(1)} collective-permute-done((bf16[2,16,2560]{2,1,0:T(8,128)(2,1)S(1)}, bf16[2,16,2560]{2,1,0:T(8,128)(2,1)S(1)}, u32[]{:S(2)}, u32[]{:S(2)}) %collective-permute-start.6) | collective-permute-done | bytes 163872 | tf_op jit(solution)/shard_map/hidden/ppermute | solution.py:41
  71.7 0.7 pad_maximum_fusion.refs_0_
  72.5 4.8 %collective-permute-start.7 = (bf16[2,2,16,2560]{3,2,1,0:T(8,128)(2,1)}, bf16[2,2,16,2560]{3,2,1,0:T(8,128)(2,1)}, u32[]{:S(2)}, u32[]{:S(2)}) collective-permute-start(bf16[2,2,16,2560]{3,2,1,0:T(8,128)(2,1)} %pad_maximum_fusion.refs_0_), channel_id=1, source_target_pairs={{0,12},{4,0},{8,4},{12,8},{1,13},{5,1},{9,5},{13,9},{2,14},{6,2},{... | collective-permute-start | bytes 983048 | tf_op jit(solution)/shard_map/hidden/ppermute | solution.py:333
  77.3 2.8 %collective-permute-start.8 = (bf16[2,2,16,2560]{3,2,1,0:T(8,128)(2,1)}, bf16[2,2,16,2560]{3,2,1,0:T(8,128)(2,1)}, u32[]{:S(2)}, u32[]{:S(2)}) collective-permute-start(bf16[2,2,16,2560]{3,2,1,0:T(8,128)(2,1)} %pad_maximum_fusion.refs_0_), channel_id=1, source_target_pairs={{0,8},{4,12},{8,0},{12,4},{1,9},{5,13},{9,1},{13,5},{2,10},{6,14},... | collective-permute-start | bytes 983048 | tf_op jit(solution)/shard_map/hidden/ppermute | solution.py:333
  80.1 2.8 %collective-permute-start.9 = (bf16[2,2,16,2560]{3,2,1,0:T(8,128)(2,1)}, bf16[2,2,16,2560]{3,2,1,0:T(8,128)(2,1)}, u32[]{:S(2)}, u32[]{:S(2)}) collective-permute-start(bf16[2,2,16,2560]{3,2,1,0:T(8,128)(2,1)} %pad_maximum_fusion.refs_0_), channel_id=1, source_target_pairs={{0,4},{4,8},{8,12},{12,0},{1,5},{5,9},{9,13},{13,1},{2,6},{6,10},{... | collective-permute-start | bytes 983048 | tf_op jit(solution)/shard_map/hidden/ppermute | solution.py:333
  82.8 4.2 %all-to-all-start.2 = ((bf16[4,320,256]{2,1,0:T(8,128)(2,1)}), bf16[4,320,256]{2,1,0:T(8,128)(2,1)}, u32[]{:S(2)}, u32[]{:S(2)}) async-start(bf16[4,320,256]{2,1,0:T(8,128)(2,1)} %hidden_part.3), calls=%async_computation.2 | async-start | bytes 1310720 | tf_op jit(solution)/shard_map/hidden/all_to_all | solution.py:329
  87.0 0.0 copy-start.6
  87.1 0.0 copy-start
  87.1 0.7 copy-done.2
  87.8 13.4 %all-to-all-done.2.v_ref = bf16[4,320,256]{2,1,0:T(8,128)(2,1)} async-done(((bf16[4,320,256]{2,1,0:T(8,128)(2,1)}), bf16[4,320,256]{2,1,0:T(8,128)(2,1)}, u32[]{:S(2)}, u32[]{:S(2)}) %all-to-all-start.2) | async-done | bytes 655392 | tf_op jit(solution)/shard_map/hidden/all_to_all | solution.py:329
  101.2 1.0 copy-done.1
  102.2 1.0 copy-done.3
  103.2 1.4 act_rows.1.own_a
  104.6 1.9 %collective-permute-start.3 = (bf16[4,2,2,16,320]{4,3,2,1,0:T(8,128)(2,1)S(1)}, bf16[4,2,2,16,320]{4,3,2,1,0:T(8,128)(2,1)}, u32[]{:S(2)}, u32[]{:S(2)}) collective-permute-start(bf16[4,2,2,16,320]{4,3,2,1,0:T(8,128)(2,1)S(1)} %act_rows.1.own_a), channel_id=1, source_target_pairs={{0,1},{1,0},{2,3},{3,2},{4,5},{5,4},{6,7},{7,6},{8,9},{9,8},{10,11... | collective-permute-start | bytes 491528 | tf_op jit(solution)/shard_map/merged/ppermute | solution.py:41
  106.5 0.1 pad_add_fusion.2.place
  106.6 1.5 collective-permute-done.3.got_a
  108.1 3.8 %merged_part.1.grad_ref = bf16[4,2,2,16,2560]{4,3,2,1,0:T(8,128)(2,1)} custom-call(s32[1]{0:T(128)} %bitcast.1.place.core, bf16[4,2,2,16,320]{4,3,2,1,0:T(8,128)(2,1)S(1)} %act_rows.1.own_a, bf16[4,2,2,16,320]{4,3,2,1,0:T(8,128)(2,1)} %collective-permute-done.3.got_a, bf16[320,5120]{1,0:T(8,128)(2,1)S(1)} %bitcast.26, ...), custom_call_target="tpu_custom_call" | custom-call | flops 1 | bytes 1 | tf_op jit(solution)/shard_map/merged/merged_part/pallas_call | solution.py:174
  111.9 3.6 %all-to-all-start.3 = ((bf16[8,32,2560]{2,1,0:T(8,128)(2,1)}), bf16[8,32,2560]{2,1,0:T(8,128)(2,1)S(1)}, u32[]{:S(2)}, u32[]{:S(2)}) async-start(bf16[8,32,2560]{2,1,0:T(8,128)(2,1)} %bitcast.9), calls=%async_computation.3 | async-start | bytes 2621440 | tf_op jit(solution)/shard_map/merged/all_to_all | solution.py:338
  115.5 0.0 copy-start.10
  115.6 2.6 %gain_terms.1 = f32[1,1280]{1,0:T(1,128)S(1)} custom-call(s32[2]{0:T(128)S(1)} %pad_add_fusion.2.place, bf16[4,2,2,16,2560]{4,3,2,1,0:T(8,128)(2,1)} %merged_part.1.grad_ref, bf16[2,2,16,2560]{3,2,1,0:T(8,128)(2,1)} %pad_maximum_fusion.refs_0_, bf16[2,2,16,2560]{3,2,1,0:T(8,128)(2,1)} %collective-permute-done.7.refs_1_, ...), custom_call_target="tpu_custom_call" | custom-call | flops 20000000000 | bytes 1 | tf_op jit(solution)/shard_map/merged/gain_terms/pallas_call | solution.py:253
  118.2 2.6 %psum.21 = f32[10,128]{1,0:T(8,128)S(1)} all-reduce(f32[10,128]{1,0:T(8,128)S(1)} %bitcast.36), channel_id=1, replica_groups=mesh['y'=8,'zl'=6,'x'=4,'zh'=2,'co'=2] {'co'}, use_global_device_ids=true, to_apply=%region_0.0 | all-reduce | flops 1280 | bytes 10240 | tf_op jit(solution)/shard_map/merged/psum | solution.py:343
  120.7 15.8 %psum.22 = f32[10,128]{1,0:T(8,128)S(1)} all-reduce(f32[10,128]{1,0:T(8,128)S(1)} %psum.21), channel_id=1, replica_groups=mesh['y'=8,'zl'=6,'x'=4,'zh'=2,'co'=2] {'x'}, use_global_device_ids=true, to_apply=%region_1.0 | all-reduce | flops 1280 | bytes 10240 | tf_op jit(solution)/shard_map/merged/psum | solution.py:343
  136.6 0.1 sum_halves.1
  136.7 2.4 %collective-permute-start.10 = (bf16[2,16,2560]{2,1,0:T(8,128)(2,1)S(1)}, bf16[2,16,2560]{2,1,0:T(8,128)(2,1)S(1)}, u32[]{:S(2)}, u32[]{:S(2)}) collective-permute-start(bf16[2,16,2560]{2,1,0:T(8,128)(2,1)S(1)} %sum_halves.1), channel_id=1, source_target_pairs={{0,2},{2,0},{1,3},{3,1},{4,6},{6,4},{5,7},{7,5},{8,10},{10,8},{9,1... | collective-permute-start | bytes 491528 | tf_op jit(solution)/shard_map/merged/ppermute | solution.py:41
  139.2 16.4 %psum.23 = f32[10,128]{1,0:T(8,128)S(1)} all-reduce(f32[10,128]{1,0:T(8,128)S(1)} %psum.22), channel_id=1, replica_groups=mesh['y'=8,'zl'=6,'x'=4,'zh'=2,'co'=2] {'y'}, use_global_device_ids=true, to_apply=%region_2.0 | all-reduce | flops 1280 | bytes 10240 | tf_op jit(solution)/shard_map/gain/psum | solution.py:348
  155.6 0.7 broadcast_in_dim.2
  156.3 16.4 %all-to-all-start.4 = ((f32[12,10,128]{2,1,0:T(8,128)}), f32[12,10,128]{2,1,0:T(8,128)S(1)}, u32[]{:S(2)}, u32[]{:S(2)}) async-start(f32[12,10,128]{2,1,0:T(8,128)} %broadcast_in_dim.2), calls=%async_computation.4 | async-start | bytes 196608 | tf_op jit(solution)/shard_map/gain/all_to_all | solution.py:295
  172.8 0.9 norm_part.1
  173.7 9.6 %all-to-all-done.4 = f32[12,10,128]{2,1,0:T(8,128)S(1)} async-done(((f32[12,10,128]{2,1,0:T(8,128)}), f32[12,10,128]{2,1,0:T(8,128)S(1)}, u32[]{:S(2)}, u32[]{:S(2)}) %all-to-all-start.4) | async-done | bytes 61472 | tf_op jit(solution)/shard_map/gain/all_to_all | solution.py:295
  183.3 0.6 multiply_bitcast_fusion
  (30 shorter events, 0.1 us)
Async XLA Ops:
  0.6 40.4 %collective-permute-start = (bf16[5120,512]{1,0:T(8,128)(2,1)}, bf16[5120,512]{1,0:T(8,128)(2,1)}, u32[]{:S(2)}, u32[]{:S(2)}) collective-permute-start(bf16[5120,512]{1,0:T(8,128)(2,1)} %param.10), channel_id=1, source_target_pairs={{0,1},{1,0},{2,3},{3,2},{4,5},{5,4},{6,7},{7,6},{8,9},{9,8},{10,11... | collective-permute-start | bytes 15728648 | tf_op jit(solution)/shard_map/weights/ppermute | solution.py:41
  4.3 31.8 %all-to-all-start = ((bf16[16,16,512]{2,1,0:T(8,128)(2,1)}), bf16[16,16,512]{2,1,0:T(8,128)(2,1)S(1)}, u32[]{:S(2)}, u32[]{:S(2)}) async-start(bf16[16,16,512]{2,1,0:T(8,128)(2,1)} %bitcast.22), calls=%async_computation | async-start | bytes 524288 | tf_op jit(solution)/shard_map/tokens/all_to_all | solution.py:309
  21.4 85.2 %collective-permute-start.4 = (bf16[320,5120]{1,0:T(8,128)(2,1)}, bf16[320,5120]{1,0:T(8,128)(2,1)}, u32[]{:S(2)}, u32[]{:S(2)}) collective-permute-start(bf16[320,5120]{1,0:T(8,128)(2,1)} %bitcast.25), channel_id=1, source_target_pairs={{0,1},{1,0},{2,3},{3,2},{4,5},{5,4},{6,7},{7,6},{8,9},{9,8},{10,11... | collective-permute-start | bytes 9830408 | tf_op jit(solution)/shard_map/weights/ppermute | solution.py:41
  36.1 5.0 %copy-start.7 = (bf16[16,16,512]{2,1,0:T(8,128)(2,1)}, bf16[16,16,512]{2,1,0:T(8,128)(2,1)S(1)}, u32[]{:S(2)}) copy-start(bf16[16,16,512]{2,1,0:T(8,128)(2,1)S(1)} %all-to-all-done) | copy-start | bytes 786436
  36.1 5.0 %collective-permute-start.1 = (bf16[256,512]{1,0:T(8,128)(2,1)S(1)}, bf16[256,512]{1,0:T(8,128)(2,1)S(1)}, u32[]{:S(2)}, u32[]{:S(2)}) collective-permute-start(bf16[256,512]{1,0:T(8,128)(2,1)S(1)} %bitcast.31), channel_id=1, source_target_pairs={{0,1},{1,0},{2,3},{3,2},{4,5},{5,4},{6,7},{7,6},{8,9},{9,8},{10,11... | collective-permute-start | bytes 786440 | tf_op jit(solution)/shard_map/tokens/ppermute | solution.py:41
  38.0 12.3 %collective-permute-start.5 = (bf16[16,5120]{1,0:T(8,128)(2,1)}, bf16[16,5120]{1,0:T(8,128)(2,1)S(1)}, u32[]{:S(2)}, u32[]{:S(2)}) collective-permute-start(bf16[16,5120]{1,0:T(8,128)(2,1)} %patch_ref.1), channel_id=1, source_target_pairs={{0,1},{1,0},{2,3},{3,2},{4,5},{5,4},{6,7},{7,6},{8,9},{9,8},{10,11... | collective-permute-start | bytes 491528 | tf_op jit(solution)/shard_map/patches/ppermute | solution.py:41
  41.1 0.7 copy-start.8
  41.8 8.6 %copy-start.4 = (bf16[16,5120]{1,0:T(8,128)(2,1)S(1)}, bf16[16,5120]{1,0:T(8,128)(2,1)}, u32[]{:S(2)}) copy-start(bf16[16,5120]{1,0:T(8,128)(2,1)} %patch_ref.1) | copy-start | bytes 491524
  41.8 10.7 %copy-start.9 = (bf16[320,256]{1,0:T(8,128)(2,1)S(1)}, bf16[320,256]{1,0:T(8,128)(2,1)}, u32[]{:S(2)}) copy-start(bf16[320,256]{1,0:T(8,128)(2,1)} %param.8) | copy-start | bytes 491524
  46.8 14.8 %all-to-all-start.1 = ((bf16[4,320,256]{2,1,0:T(8,128)(2,1)}), bf16[4,320,256]{2,1,0:T(8,128)(2,1)S(1)}, u32[]{:S(2)}, u32[]{:S(2)}) async-start(bf16[4,320,256]{2,1,0:T(8,128)(2,1)} %hidden_part.2), calls=%async_computation.1 | async-start | bytes 1310720 | tf_op jit(solution)/shard_map/hidden/all_to_all | solution.py:324
  50.4 21.4 %collective-permute-start.6 = (bf16[2,16,2560]{2,1,0:T(8,128)(2,1)S(1)}, bf16[2,16,2560]{2,1,0:T(8,128)(2,1)S(1)}, u32[]{:S(2)}, u32[]{:S(2)}) collective-permute-start(bf16[2,16,2560]{2,1,0:T(8,128)(2,1)S(1)} %pack_patches.1), channel_id=1, source_target_pairs={{0,2},{2,0},{1,3},{3,1},{4,6},{6,4},{5,7},{7,5},{8,10},{10,8},{9,1... | collective-permute-start | bytes 491528 | tf_op jit(solution)/shard_map/hidden/ppermute | solution.py:41
  61.7 25.4 %collective-permute-start.2 = (bf16[320,256]{1,0:T(8,128)(2,1)S(1)}, bf16[320,256]{1,0:T(8,128)(2,1)S(1)}, u32[]{:S(2)}, u32[]{:S(2)}) collective-permute-start(bf16[320,256]{1,0:T(8,128)(2,1)S(1)} %sum_parts.1), channel_id=1, source_target_pairs={{0,2},{2,0},{1,3},{3,1},{4,6},{6,4},{5,7},{7,5},{8,10},{10,8},{9,1... | collective-permute-start | bytes 491528 | tf_op jit(solution)/shard_map/hidden/ppermute | solution.py:41
  72.5 43.1 %collective-permute-start.7 = (bf16[2,2,16,2560]{3,2,1,0:T(8,128)(2,1)}, bf16[2,2,16,2560]{3,2,1,0:T(8,128)(2,1)}, u32[]{:S(2)}, u32[]{:S(2)}) collective-permute-start(bf16[2,2,16,2560]{3,2,1,0:T(8,128)(2,1)} %pad_maximum_fusion.refs_0_), channel_id=1, source_target_pairs={{0,12},{4,0},{8,4},{12,8},{1,13},{5,1},{9,5},{13,9},{2,14},{6,2},{... | collective-permute-start | bytes 983048 | tf_op jit(solution)/shard_map/hidden/ppermute | solution.py:333
  77.3 38.2 %collective-permute-start.8 = (bf16[2,2,16,2560]{3,2,1,0:T(8,128)(2,1)}, bf16[2,2,16,2560]{3,2,1,0:T(8,128)(2,1)}, u32[]{:S(2)}, u32[]{:S(2)}) collective-permute-start(bf16[2,2,16,2560]{3,2,1,0:T(8,128)(2,1)} %pad_maximum_fusion.refs_0_), channel_id=1, source_target_pairs={{0,8},{4,12},{8,0},{12,4},{1,9},{5,13},{9,1},{13,5},{2,10},{6,14},... | collective-permute-start | bytes 983048 | tf_op jit(solution)/shard_map/hidden/ppermute | solution.py:333
  80.1 35.5 %collective-permute-start.9 = (bf16[2,2,16,2560]{3,2,1,0:T(8,128)(2,1)}, bf16[2,2,16,2560]{3,2,1,0:T(8,128)(2,1)}, u32[]{:S(2)}, u32[]{:S(2)}) collective-permute-start(bf16[2,2,16,2560]{3,2,1,0:T(8,128)(2,1)} %pad_maximum_fusion.refs_0_), channel_id=1, source_target_pairs={{0,4},{4,8},{8,12},{12,0},{1,5},{5,9},{9,13},{13,1},{2,6},{6,10},{... | collective-permute-start | bytes 983048 | tf_op jit(solution)/shard_map/hidden/ppermute | solution.py:333
  82.8 18.4 %all-to-all-start.2 = ((bf16[4,320,256]{2,1,0:T(8,128)(2,1)}), bf16[4,320,256]{2,1,0:T(8,128)(2,1)}, u32[]{:S(2)}, u32[]{:S(2)}) async-start(bf16[4,320,256]{2,1,0:T(8,128)(2,1)} %hidden_part.3), calls=%async_computation.2 | async-start | bytes 1310720 | tf_op jit(solution)/shard_map/hidden/all_to_all | solution.py:329
  87.0 14.2 %copy-start.6 = (s32[256]{0:T(256)S(1)}, s32[256]{0:T(256)}, u32[]{:S(2)}) copy-start(s32[256]{0:T(256)} %param.13) | copy-start | bytes 3076
  87.1 21.0 %copy-start = (bf16[5120,320]{0,1:T(8,128)(2,1)S(1)}, bf16[5120,320]{0,1:T(8,128)(2,1)}, u32[]{:S(2)}) copy-start(bf16[5120,320]{0,1:T(8,128)(2,1)} %param.9) | copy-start | bytes 9830404
  87.1 0.7 copy-start.2
  101.2 1.0 copy-start.1
  102.2 1.0 copy-start.3
  104.6 3.5 %collective-permute-start.3 = (bf16[4,2,2,16,320]{4,3,2,1,0:T(8,128)(2,1)S(1)}, bf16[4,2,2,16,320]{4,3,2,1,0:T(8,128)(2,1)}, u32[]{:S(2)}, u32[]{:S(2)}) collective-permute-start(bf16[4,2,2,16,320]{4,3,2,1,0:T(8,128)(2,1)S(1)} %act_rows.1.own_a), channel_id=1, source_target_pairs={{0,1},{1,0},{2,3},{3,2},{4,5},{5,4},{6,7},{7,6},{8,9},{9,8},{10,11... | collective-permute-start | bytes 491528 | tf_op jit(solution)/shard_map/merged/ppermute | solution.py:41
  111.9 24.7 %all-to-all-start.3 = ((bf16[8,32,2560]{2,1,0:T(8,128)(2,1)}), bf16[8,32,2560]{2,1,0:T(8,128)(2,1)S(1)}, u32[]{:S(2)}, u32[]{:S(2)}) async-start(bf16[8,32,2560]{2,1,0:T(8,128)(2,1)} %bitcast.9), calls=%async_computation.3 | async-start | bytes 2621440 | tf_op jit(solution)/shard_map/merged/all_to_all | solution.py:338
  115.5 23.7 %copy-start.10 = (f32[1280]{0:T(1024)S(1)}, f32[1280]{0:T(1024)}, u32[]{:S(2)}) copy-start(f32[1280]{0:T(1024)} %param.12) | copy-start | bytes 15364
  115.5 57.2 %copy-start.5 = (bf16[16,5120]{1,0:T(8,128)(2,1)S(1)}, bf16[16,5120]{1,0:T(8,128)(2,1)}, u32[]{:S(2)}) copy-start(bf16[16,5120]{1,0:T(8,128)(2,1)} %patch_ref.1) | copy-start | bytes 491524
  136.7 36.0 %collective-permute-start.10 = (bf16[2,16,2560]{2,1,0:T(8,128)(2,1)S(1)}, bf16[2,16,2560]{2,1,0:T(8,128)(2,1)S(1)}, u32[]{:S(2)}, u32[]{:S(2)}) collective-permute-start(bf16[2,16,2560]{2,1,0:T(8,128)(2,1)S(1)} %sum_halves.1), channel_id=1, source_target_pairs={{0,2},{2,0},{1,3},{3,1},{4,6},{6,4},{5,7},{7,5},{8,10},{10,8},{9,1... | collective-permute-start | bytes 491528 | tf_op jit(solution)/shard_map/merged/ppermute | solution.py:41
  156.3 27.0 %all-to-all-start.4 = ((f32[12,10,128]{2,1,0:T(8,128)}), f32[12,10,128]{2,1,0:T(8,128)S(1)}, u32[]{:S(2)}, u32[]{:S(2)}) async-start(f32[12,10,128]{2,1,0:T(8,128)} %broadcast_in_dim.2), calls=%async_computation.4 | async-start | bytes 196608 | tf_op jit(solution)/shard_map/gain/all_to_all | solution.py:295

commit v5 on v4

--- a/solution.py
+++ b/solution.py
@@ -41,91 +41,67 @@
     return lax.ppermute(value, axis, [(0, 1), (1, 0)])
 
 
-def hidden_kernel(place, own_w, got_w, own_t, got_t, out_ref, block, tokens, arrived):
+def hidden_kernel(core, own_w, got_w, own_t, got_t, out_ref):
     depth = own_t.shape[1]
-    copies = [
-        [
-            pltpu.make_async_copy(
-                w_ref.at[i, place[0], place[1]],
-                block.at[i, :, pl.ds(k * depth, depth)],
-                arrived.at[i, k],
-            )
-            for k, w_ref in enumerate((own_w, got_w))
-        ]
-        for i in range(NX)
-    ]
-    for pair in copies:
-        for copy in pair:
-            copy.start()
-    for k, t_ref in enumerate((own_t, got_t)):
-        tokens[k * depth : (k + 1) * depth, :] = t_ref[...].T
-    for i, pair in enumerate(copies):
-        for copy in pair:
-            copy.wait()
-        total = lax.dot_general(
-            block[i], tokens[...], (((1,), (0,)), ((), ())), preferred_element_type=F32
+    total = None
+    for w_ref, t_ref in ((own_w, own_t), (got_w, got_t)):
+        term = lax.dot_general(
+            w_ref[...].reshape(-1, depth),
+            t_ref[...],
+            (((1,), (1,)), ((), ())),
+            preferred_element_type=F32,
         )
-        out_ref[i] = total.astype(BF16)
-
-
-def hidden_part(weights, tokens, place):
+        total = term if total is None else total + term
+    out_ref[...] = total.astype(BF16).reshape(out_ref.shape)
+
+
+def hidden_part(weights, tokens, core):
     rows, depth = weights[0].shape
     units = rows // (NX * NZH * NCO)
     count = tokens[0].shape[0]
     weights = [w.reshape(NX, NZH, NCO, units, depth) for w in weights]
+    w_spec = pl.BlockSpec((1, NZH, 1, units, depth), lambda i, s: (i, 0, s[0], 0, 0))
+    t_spec = pl.BlockSpec((count, depth), lambda i, s: (0, 0))
     return pl.pallas_call(
         hidden_kernel,
-        in_specs=[IN_SMEM, ANYWHERE, ANYWHERE, IN_VMEM, IN_VMEM],
-        out_specs=IN_VMEM,
-        out_shape=jax.ShapeDtypeStruct((NX, units, count), BF16),
-        scratch_shapes=[
-            pltpu.VMEM((NX, units, 2 * depth), BF16),
-            pltpu.VMEM((2 * depth, count), BF16),
-            pltpu.SemaphoreType.DMA((NX, 2)),
-        ],
+        grid_spec=pltpu.PrefetchScalarGridSpec(
+            num_scalar_prefetch=1,
+            grid=(NX,),
+            in_specs=[w_spec, w_spec, t_spec, t_spec],
+            out_specs=pl.BlockSpec((1, NZH, units, count), lambda i, s: (i, 0, 0, 0)),
+        ),
+        out_shape=jax.ShapeDtypeStruct((NX, NZH, units, count), BF16),
         compiler_params=params(60),
         cost_estimate=cost(),
         name="hidden_part",
-    )(place, *weights, *tokens)
-
-
-def total_of(ref):
-    total = ref[0].astype(F32)
+    )(core, *weights, *tokens)
+
+
+def total_of(ref, z):
+    total = ref[0, z].astype(F32)
     for i in range(1, ref.shape[0]):
-        total += ref[i].astype(F32)
+        total += ref[i, z].astype(F32)
     return total
 
 
-def sum_kernel(v_ref, out_ref):
-    out_ref[...] = total_of(v_ref).astype(BF16)
-
-
-def sum_parts(parts):
+def sum_kernel(place, v_ref, out_ref):
+    out_ref[...] = total_of(v_ref, place[0]).astype(BF16)
+
+
+def sum_parts(parts, place):
     return pl.pallas_call(
         sum_kernel,
-        out_shape=jax.ShapeDtypeStruct(parts.shape[1:], BF16),
+        in_specs=[IN_SMEM, IN_VMEM],
+        out_specs=IN_VMEM,
+        out_shape=jax.ShapeDtypeStruct(parts.shape[2:], BF16),
         compiler_params=params(),
         cost_estimate=cost(),
         name="sum_parts",
-    )(parts)
-
-
-def wide_kernel(v_ref, out_ref):
-    out_ref[...] = v_ref[...].astype(F32)
-
-
-def widen(value):
-    return pl.pallas_call(
-        wide_kernel,
-        out_shape=jax.ShapeDtypeStruct(value.shape, F32),
-        compiler_params=params(),
-        cost_estimate=cost(LONG),
-        name="widen",
-    )(value)
-
-
-def act_kernel(v_ref, got_ref, slope_ref, pos_ref, out_ref):
-    act = ((total_of(v_ref) + got_ref[...]) * slope_ref[...]).astype(BF16)
+    )(place, parts)
+
+
+def act_kernel(place, v_ref, got_ref, slope_ref, pos_ref, out_ref):
+    act = ((total_of(v_ref, place[0]) + got_ref[...].astype(F32)) * slope_ref[...]).astype(BF16)
     count = act.shape[1]
     pick = (lax.broadcasted_iota(jnp.int32, (count, count), 0) == pos_ref[...]).astype(F32)
     pick = pick.T.astype(BF16)
@@ -139,15 +115,17 @@
                 out_ref[x, c, z] = moved[first : first + own]
 
 
-def act_rows(parts, got, slope, owner_pos):
+def act_rows(parts, got, slope, owner_pos, place):
     units, count = got.shape
     return pl.pallas_call(
         act_kernel,
+        in_specs=[IN_SMEM] + [IN_VMEM] * 4,
+        out_specs=IN_VMEM,
         out_shape=jax.ShapeDtypeStruct((NX, NCO, NZH, count // (NX * NCO * NZH), units), BF16),
         compiler_params=params(),
         cost_estimate=cost(),
         name="act_rows",
-    )(parts, got, slope, owner_pos.reshape(1, count))
+    )(place, parts, got, slope, owner_pos.reshape(1, count))
 
 
 def merged_kernel(place, own_a, got_a, own_w, got_w, out_ref):
@@ -302,7 +280,7 @@
     own, depth = grad_tokens.shape
     group = own * ctx
     slope = gelu_slope(pre_act.astype(F32))
-    far_z, near_z = jnp.stack([1 - zh, co]), jnp.stack([zh, co])
+    far_z, near_z, core = (1 - zh).reshape(1), zh.reshape(1), co.reshape(1)
     half = patch_in.shape[1] // NCO
     with jax.named_scope("tokens"):
         outgoing = grad_tokens.reshape(own, ctx, depth // ctx).transpose(1, 0, 2)
@@ -311,43 +289,41 @@
     with jax.named_scope("weights"):
         weights_2 = (w_fc2, swap(w_fc2, "co"))
         w_fc1_t = w_fc1.T
-        weights_1 = (w_fc1_t, swap(w_fc1_t, "co"))
 
     with jax.named_scope("patches"):
-        patches = pack_patches(patch_in, swap(patch_in, "co"), co.reshape(1))
+        patches = pack_patches(patch_in, swap(patch_in, "co"), core)
 
     def tie(value, first):
         return lax.optimization_barrier((value, first))[0]
 
     with jax.named_scope("hidden"):
-        far_sum = hidden_part(weights_2, tokens, far_z)
-        far = lax.all_to_all(far_sum, "x", 0, 0, tiled=True)
-        patches = jnp.stack([patches, swap(tie(patches, far_sum), "zh")])
-        near_sum = hidden_part(weights_2, tie(tokens, far_sum), near_z)
-        far, near_sum = lax.optimization_barrier((far, near_sum))
-        far = sum_parts(far)
-        near = lax.all_to_all(tie(near_sum, far), "x", 0, 0, tiled=True)
-        got = widen(swap(far, "zh"))
-        patches = tie(patches, far)
+        sums = hidden_part(weights_2, tokens, core)
+        parts = lax.all_to_all(sums, "x", 0, 0, tiled=True)
+        ready = tie(patches, sums)
+        weights_1 = (w_fc1_t, swap(tie(w_fc1_t, ready), "co"))
+        beyond = swap(ready, "zh")
+        far = sum_parts(parts, far_z)
+        got = swap(far, "zh")
+        patches = jnp.stack([tie(patches, far), beyond])
         around = [patches] + [
             lax.ppermute(patches, "x", [(i, (i - d) % NX) for i in range(NX)]) for d in (1, 2, 3)
         ]
     with jax.named_scope("merged"):
-        act = act_rows(near, got, slope, owner_pos)
-        grads = merged_part((act, swap(act, "co")), weights_1, co.reshape(1))
+        act = act_rows(parts, got, slope, owner_pos, near_z)
+        sums = merged_part((act, swap(act, "co")), weights_1, core)
         parts = lax.all_to_all(
-            grads.reshape(NX * NCO, NZH * own, half), ("x", "co"), 0, 0, tiled=True
+            sums.reshape(NX * NCO, NZH * own, half), ("x", "co"), 0, 0, tiled=True
         ).reshape(NX * NCO, NZH, own, half)
         here = jnp.stack([lax.axis_index("x").astype(jnp.int32), zh])
-        terms = gain_terms(grads, around, here, norm_gain.shape[0]).reshape(-1, 128)
-        terms = lax.psum(lax.psum(terms, "co"), "x")
+        terms = gain_terms(sums, around, here, norm_gain.shape[0]).reshape(-1, 128)
+        terms = lax.psum(lax.psum(terms, "co"), "y")
         parts, terms = lax.optimization_barrier((parts, terms))
-        far = sum_halves(parts, (1 - zh).reshape(1))
+        far = sum_halves(parts, far_z)
         got = swap(far, "zh")
     with jax.named_scope("gain"):
-        terms = lax.psum(tie(terms, far), "y")
+        terms = lax.psum(tie(terms, far), "x")
     with jax.named_scope("norm"):
-        patch_grad = norm_part(parts, got, patch_in, norm_gain, zh.reshape(1))
+        patch_grad = norm_part(parts, got, patch_in, norm_gain, near_z)
     with jax.named_scope("gain"):
         terms = sum_over(terms, ("zl", "zh"), NZL * NZH)
         gain_grad = terms.reshape(-1) / (NY * NZL * ctx)

time: 185 us -> 165 us (0.89)
  starting transfers between devices: 77.6 us -> 49.2 us
  blocking collectives: 34.9 us -> 60.4 us
  Pallas kernels: 19.1 us -> 13 us
  waiting for transfers between devices: 42.1 us -> 36.5 us
  other arithmetic: 3.51 us -> 0.89 us
  local copies, waits for them, and re-layouts: 5.75 us -> 3.23 us
    all_to_all x0 -> x1, blocking collectives: none -> 31.6 us  [local(): lax.all_to_all(outgoing, CTX, 0, 0, tiled=True).reshape(group, depth // ctx)]
    all_to_all x4 -> x2, starting transfers between devices: 28.4 us -> 7.12 us  [the longest x1 3.57 us: local(): lax.all_to_all(sums.reshape(NX * NCO, NZH * own, half), ('x', 'co'), 0, 0...]
    all_to_all x4 -> x2, waiting for transfers between devices: 28.4 us -> 16.4 us  [the longest x1 16.4 us: local(): parts = lax.all_to_all(sums, 'x', 0, 0, tiled=True)]
    ppermute x8, waiting for transfers between devices: 4.06 us -> 10.5 us  [swap(): return lax.ppermute(value, axis, [(0, 1), (1, 0)])]
    psum x3, blocking collectives: 34.9 us -> 28.8 us  [the longest x2 18.5 us: local(): terms = lax.psum(lax.psum(terms, 'co'), 'y')]
    pallas_call x5 -> x3, Pallas kernels: 11.6 us -> 5.77 us  [the longest x1 5.34 us: hidden_part(): pl.pallas_call(hidden_kernel, grid_spec=pltpu.PrefetchScalarGridSpec(num_...]
    ppermute x8, starting transfers between devices: 22.4 us -> 17.4 us  [swap(): return lax.ppermute(value, axis, [(0, 1), (1, 0)])]
    all_to_all x1, starting transfers between devices: 16.4 us -> 14.4 us  [sum_over(): return jnp.sum(lax.all_to_all(rows, axes, 0, 0, tiled=True), axis=0)]
  transfers between devices with their start and end apart: 16 -> 14, of which waited for: 6 -> 6; matrix products, arithmetic and copies ran while one was open for 3% -> 1% of each run, Pallas kernels for 10% -> 5%
where the time goes in v5:
time: 165 us; the launch traced here: 164 us
  blocking collectives  60.4 us (37%)
  starting transfers between devices  49.2 us (30%)
  waiting for transfers between devices  36.5 us (22%)
  Pallas kernels  13 us (8%)
  local copies, waits for them, and re-layouts  3.23 us (2%)
    all_to_all x1, blocking collectives, local(): lax.all_to_all(outgoing, CTX, 0, 0, tiled=True).reshape(group, depth // ctx)  31.6 us
    psum x2, blocking collectives, local(): terms = lax.psum(lax.psum(terms, 'co'), 'y')  18.5 us
    ppermute x8, starting transfers between devices, swap(): return lax.ppermute(value, axis, [(0, 1), (1, 0)])  17.4 us
    all_to_all x1, waiting for transfers between devices, local(): parts = lax.all_to_all(sums, 'x', 0, 0, tiled=True)  16.4 us
    all_to_all x1, starting transfers between devices, sum_over(): return jnp.sum(lax.all_to_all(rows, axes, 0, 0, tiled=True), axis=0)  14.4 us
    ppermute x8, waiting for transfers between devices, swap(): return lax.ppermute(value, axis, [(0, 1), (1, 0)])  10.5 us
    ppermute x3, starting transfers between devices, local(): lax.ppermute(patches, 'x', [(i, (i - d) % NX) for i in range(NX)])  10.3 us
    psum x1, blocking collectives, local(): terms = lax.psum(tie(terms, far), 'x')  10.3 us
  transfers between devices with their start and end apart: 14, of which 6 were waited for; matrix products, arithmetic and copies ran while one was open for 1% of the time, Pallas kernels for 5%

profile of v5, /device:TPU:8, one launch (start us, length us, event | category | flops | bytes accessed | tf_op | source)
XLA Modules:
  0.0 164.2 jit_solution(17184600769664263759)
XLA Ops:
  0.6 1.9 %collective-permute-start = (bf16[5120,512]{1,0:T(8,128)(2,1)}, bf16[5120,512]{1,0:T(8,128)(2,1)}, u32[]{:S(2)}, u32[]{:S(2)}) collective-permute-start(bf16[5120,512]{1,0:T(8,128)(2,1)} %param.10), channel_id=1, source_target_pairs={{0,1},{1,0},{2,3},{3,2},{4,5},{5,4},{6,7},{7,6},{8,9},{9,8},{10,11... | collective-permute-start | bytes 15728648 | tf_op jit(solution)/shard_map/weights/ppermute | solution.py:41
  2.6 1.0 copy.16
  3.5 31.6 %all_to_all.20 = bf16[16,16,512]{2,1,0:T(8,128)(2,1)S(1)} all-to-all(bf16[16,16,512]{2,1,0:T(8,128)(2,1)S(1)} %bitcast.30), channel_id=1, replica_groups=mesh['y'=8,'zl'=6,'x'=4,'zh'=2,'co'=2] {'x','zh','co'}, dimensions={0} | all-to-all | bytes 524288 | tf_op jit(solution)/shard_map/tokens/all_to_all | solution.py:287
  35.2 1.9 %collective-permute-start.1 = (bf16[256,512]{1,0:T(8,128)(2,1)S(1)}, bf16[256,512]{1,0:T(8,128)(2,1)S(1)}, u32[]{:S(2)}, u32[]{:S(2)}) collective-permute-start(bf16[256,512]{1,0:T(8,128)(2,1)S(1)} %bitcast.28), channel_id=1, source_target_pairs={{0,1},{1,0},{2,3},{3,2},{4,5},{5,4},{6,7},{7,6},{8,9},{9,8},{10,11... | collective-permute-start | bytes 786440 | tf_op jit(solution)/shard_map/tokens/ppermute | solution.py:41
  37.1 2.4 %collective-permute-start.4 = (bf16[16,5120]{1,0:T(8,128)(2,1)}, bf16[16,5120]{1,0:T(8,128)(2,1)S(1)}, u32[]{:S(2)}, u32[]{:S(2)}) collective-permute-start(bf16[16,5120]{1,0:T(8,128)(2,1)} %patch_ref.1), channel_id=1, source_target_pairs={{0,1},{1,0},{2,3},{3,2},{4,5},{5,4},{6,7},{7,6},{8,9},{9,8},{10,11... | collective-permute-start | bytes 491528 | tf_op jit(solution)/shard_map/patches/ppermute | solution.py:41
  39.5 1.2 collective-permute-done.4.got_ref
  40.7 0.9 copy-done
  41.7 0.0 collective-permute-done.1.got_t
  41.7 0.0 collective-permute-done
  41.7 0.7 copy-done.4
  42.4 5.3 %hidden_part.1 = bf16[4,2,320,256]{3,2,1,0:T(8,128)(2,1)} custom-call(s32[1]{0:T(128)} %bitcast.1.core.place, bf16[4,2,2,320,512]{4,3,2,1,0:T(8,128)(2,1)} %bitcast.27, bf16[4,2,2,320,512]{4,3,2,1,0:T(8,128)(2,1)} %bitcast.3.got_w, bf16[256,512]{1,0:T(8,128)(2,1)} %bitcast.29, bf16[256,512]{1,0:T(8,128)(2,1)} %copy-done.4), custom_call_target="tpu_custom_call" | custom-call | flops 1 | bytes 1 | tf_op jit(solution)/shard_map/hidden/hidden_part/pallas_call | solution.py:65
  47.7 2.4 %collective-permute-start.5 = (bf16[320,5120]{1,0:T(8,128)(2,1)}, bf16[320,5120]{1,0:T(8,128)(2,1)}, u32[]{:S(2)}, u32[]{:S(2)}) collective-permute-start(bf16[320,5120]{1,0:T(8,128)(2,1)} %bitcast.8.own_w), channel_id=1, source_target_pairs={{0,1},{1,0},{2,3},{3,2},{4,5},{5,4},{6,7},{7,6},{8,9},{9,8},{10,11... | collective-permute-start | bytes 9830408 | tf_op jit(solution)/shard_map/hidden/ppermute | solution.py:41
  50.1 3.6 %all-to-all-start.1 = ((bf16[4,2,320,256]{3,2,1,0:T(8,128)(2,1)}), bf16[4,2,320,256]{3,2,1,0:T(8,128)(2,1)S(1)}, u32[]{:S(2)}, u32[]{:S(2)}) async-start(bf16[4,2,320,256]{3,2,1,0:T(8,128)(2,1)} %hidden_part.1), calls=%async_computation.1 | async-start | bytes 2621440 | tf_op jit(solution)/shard_map/hidden/all_to_all | solution.py:301
  53.7 2.1 %collective-permute-start.6 = (bf16[2,16,2560]{2,1,0:T(8,128)(2,1)S(1)}, bf16[2,16,2560]{2,1,0:T(8,128)(2,1)S(1)}, u32[]{:S(2)}, u32[]{:S(2)}) collective-permute-start(bf16[2,16,2560]{2,1,0:T(8,128)(2,1)S(1)} %pack_patches.1), channel_id=1, source_target_pairs={{0,2},{2,0},{1,3},{3,1},{4,6},{6,4},{5,7},{7,5},{8,10},{10,8},{9,1... | collective-permute-start | bytes 491528 | tf_op jit(solution)/shard_map/hidden/ppermute | solution.py:41
  55.8 16.4 %all-to-all-done.1.v_ref = bf16[4,2,320,256]{3,2,1,0:T(8,128)(2,1)S(1)} async-done(((bf16[4,2,320,256]{3,2,1,0:T(8,128)(2,1)}), bf16[4,2,320,256]{3,2,1,0:T(8,128)(2,1)S(1)}, u32[]{:S(2)}, u32[]{:S(2)}) %all-to-all-start.1) | async-done | bytes 1310752 | tf_op jit(solution)/shard_map/hidden/all_to_all | solution.py:301
  72.1 0.1 sum_parts.1
  72.2 2.1 %collective-permute-start.2 = (bf16[320,256]{1,0:T(8,128)(2,1)S(1)}, bf16[320,256]{1,0:T(8,128)(2,1)S(1)}, u32[]{:S(2)}, u32[]{:S(2)}) collective-permute-start(bf16[320,256]{1,0:T(8,128)(2,1)S(1)} %sum_parts.1), channel_id=1, source_target_pairs={{0,2},{2,0},{1,3},{3,1},{4,6},{6,4},{5,7},{7,5},{8,10},{10,8},{9,1... | collective-permute-start | bytes 491528 | tf_op jit(solution)/shard_map/hidden/ppermute | solution.py:41
  74.4 0.8 collective-permute-done.6
  75.2 4.8 %collective-permute-start.7 = (bf16[2,2,16,2560]{3,2,1,0:T(8,128)(2,1)S(1)}, bf16[2,2,16,2560]{3,2,1,0:T(8,128)(2,1)S(1)}, u32[]{:S(2)}, u32[]{:S(2)}) collective-permute-start(bf16[2,2,16,2560]{3,2,1,0:T(8,128)(2,1)S(1)} %pad_maximum_fusion.refs_0_), channel_id=1, source_target_pairs={{0,12},{4,0},{8,4},{12,8},{1,13},{5,1},{9,5},{13,9},{2,14},{6,2},{... | collective-permute-start | bytes 983048 | tf_op jit(solution)/shard_map/hidden/ppermute | solution.py:309
  80.1 2.8 %collective-permute-start.8 = (bf16[2,2,16,2560]{3,2,1,0:T(8,128)(2,1)S(1)}, bf16[2,2,16,2560]{3,2,1,0:T(8,128)(2,1)S(1)}, u32[]{:S(2)}, u32[]{:S(2)}) collective-permute-start(bf16[2,2,16,2560]{3,2,1,0:T(8,128)(2,1)S(1)} %pad_maximum_fusion.refs_0_), channel_id=1, source_target_pairs={{0,8},{4,12},{8,0},{12,4},{1,9},{5,13},{9,1},{13,5},{2,10},{6,14},... | collective-permute-start | bytes 983048 | tf_op jit(solution)/shard_map/hidden/ppermute | solution.py:309
  82.8 2.8 %collective-permute-start.9 = (bf16[2,2,16,2560]{3,2,1,0:T(8,128)(2,1)S(1)}, bf16[2,2,16,2560]{3,2,1,0:T(8,128)(2,1)S(1)}, u32[]{:S(2)}, u32[]{:S(2)}) collective-permute-start(bf16[2,2,16,2560]{3,2,1,0:T(8,128)(2,1)S(1)} %pad_maximum_fusion.refs_0_), channel_id=1, source_target_pairs={{0,4},{4,8},{8,12},{12,0},{1,5},{5,9},{9,13},{13,1},{2,6},{6,10},{... | collective-permute-start | bytes 983048 | tf_op jit(solution)/shard_map/hidden/ppermute | solution.py:309
  85.6 0.1 fusion.3.slope_ref
  85.8 7.1 %collective-permute-done.2.got_ref = bf16[320,256]{1,0:T(8,128)(2,1)S(1)} collective-permute-done((bf16[320,256]{1,0:T(8,128)(2,1)S(1)}, bf16[320,256]{1,0:T(8,128)(2,1)S(1)}, u32[]{:S(2)}, u32[]{:S(2)}) %collective-permute-start.2) | collective-permute-done | bytes 163872 | tf_op jit(solution)/shard_map/hidden/ppermute | solution.py:41
  92.9 0.3 act_rows.1.own_a
  93.2 1.9 %collective-permute-start.3 = (bf16[4,2,2,16,320]{4,3,2,1,0:T(8,128)(2,1)S(1)}, bf16[4,2,2,16,320]{4,3,2,1,0:T(8,128)(2,1)S(1)}, u32[]{:S(2)}, u32[]{:S(2)}) collective-permute-start(bf16[4,2,2,16,320]{4,3,2,1,0:T(8,128)(2,1)S(1)} %act_rows.1.own_a), channel_id=1, source_target_pairs={{0,1},{1,0},{2,3},{3,2},{4,5},{5,4},{6,7},{7,6},{8,9},{9,8},{10,11... | collective-permute-start | bytes 491528 | tf_op jit(solution)/shard_map/merged/ppermute | solution.py:41
  95.2 0.1 pad_add_fusion.place
  95.2 1.3 collective-permute-done.3.got_a
  96.6 0.0 collective-permute-done.5.got_w
  96.6 4.0 %merged_part.1.grad_ref = bf16[4,2,2,16,2560]{4,3,2,1,0:T(8,128)(2,1)} custom-call(s32[1]{0:T(128)} %bitcast.1.core.place, bf16[4,2,2,16,320]{4,3,2,1,0:T(8,128)(2,1)S(1)} %act_rows.1.own_a, bf16[4,2,2,16,320]{4,3,2,1,0:T(8,128)(2,1)S(1)} %collective-permute-done.3.got_a, bf16[320,5120]{1,0:T(8,128)(2,1)} %bitcast.8.own_w, ...), custom_call_target="tpu_custom_call" | custom-call | flops 1 | bytes 1 | tf_op jit(solution)/shard_map/merged/merged_part/pallas_call | solution.py:152
  100.5 3.6 %all-to-all-start.2 = ((bf16[8,32,2560]{2,1,0:T(8,128)(2,1)}), bf16[8,32,2560]{2,1,0:T(8,128)(2,1)S(1)}, u32[]{:S(2)}, u32[]{:S(2)}) async-start(bf16[8,32,2560]{2,1,0:T(8,128)(2,1)} %bitcast.9), calls=%async_computation.2 | async-start | bytes 2621440 | tf_op jit(solution)/shard_map/merged/all_to_all | solution.py:314
  104.1 0.0 copy-start.6
  104.1 0.0 copy-start.1
  104.1 0.0 collective-permute-done.7.refs_1_
  104.1 0.0 collective-permute-done.8.refs_2_
  104.2 0.0 collective-permute-done.9.refs_3_
  104.2 2.2 %gain_terms.1 = f32[1,1280]{1,0:T(1,128)S(1)} custom-call(s32[2]{0:T(128)S(1)} %pad_add_fusion.place, bf16[4,2,2,16,2560]{4,3,2,1,0:T(8,128)(2,1)} %merged_part.1.grad_ref, bf16[2,2,16,2560]{3,2,1,0:T(8,128)(2,1)S(1)} %pad_maximum_fusion.refs_0_, bf16[2,2,16,2560]{3,2,1,0:T(8,128)(2,1)S(1)} %collective-permute-done.7.refs_1_, ...), custom_call_target="tpu_custom_call" | custom-call | flops 20000000000 | bytes 1 | tf_op jit(solution)/shard_map/merged/gain_terms/pallas_call | solution.py:231
  106.4 2.6 %psum.21 = f32[10,128]{1,0:T(8,128)S(1)} all-reduce(f32[10,128]{1,0:T(8,128)S(1)} %bitcast.33), channel_id=1, replica_groups=mesh['y'=8,'zl'=6,'x'=4,'zh'=2,'co'=2] {'co'}, use_global_device_ids=true, to_apply=%region_0.0 | all-reduce | flops 1280 | bytes 10240 | tf_op jit(solution)/shard_map/merged/psum | solution.py:319
  109.0 15.9 %psum.22 = f32[10,128]{1,0:T(8,128)S(1)} all-reduce(f32[10,128]{1,0:T(8,128)S(1)} %psum.21), channel_id=1, replica_groups=mesh['y'=8,'zl'=6,'x'=4,'zh'=2,'co'=2] {'y'}, use_global_device_ids=true, to_apply=%region_1.0 | all-reduce | flops 1280 | bytes 10240 | tf_op jit(solution)/shard_map/merged/psum | solution.py:319
  124.9 0.0 all-to-all-done.2
  124.9 0.1 sum_halves.1
  125.0 2.6 %collective-permute-start.10 = (bf16[2,16,2560]{2,1,0:T(8,128)(2,1)S(1)}, bf16[2,16,2560]{2,1,0:T(8,128)(2,1)S(1)}, u32[]{:S(2)}, u32[]{:S(2)}) collective-permute-start(bf16[2,16,2560]{2,1,0:T(8,128)(2,1)S(1)} %sum_halves.1), channel_id=1, source_target_pairs={{0,2},{2,0},{1,3},{3,1},{4,6},{6,4},{5,7},{7,5},{8,10},{10,8},{9,1... | collective-permute-start | bytes 491528 | tf_op jit(solution)/shard_map/merged/ppermute | solution.py:41
  127.6 10.3 %psum.23 = f32[10,128]{1,0:T(8,128)S(1)} all-reduce(f32[10,128]{1,0:T(8,128)S(1)} %psum.22), channel_id=1, replica_groups=mesh['y'=8,'zl'=6,'x'=4,'zh'=2,'co'=2] {'x'}, use_global_device_ids=true, to_apply=%region_2.0 | all-reduce | flops 1280 | bytes 10240 | tf_op jit(solution)/shard_map/gain/psum | solution.py:324
  137.9 0.6 broadcast_in_dim.2
  138.6 14.4 %all-to-all-start.3 = ((f32[12,10,128]{2,1,0:T(8,128)}), f32[12,10,128]{2,1,0:T(8,128)S(1)}, u32[]{:S(2)}, u32[]{:S(2)}) async-start(f32[12,10,128]{2,1,0:T(8,128)} %broadcast_in_dim.2), calls=%async_computation.3 | async-start | bytes 196608 | tf_op jit(solution)/shard_map/gain/all_to_all | solution.py:273
  153.0 0.0 collective-permute-done.10.got_ref
  153.0 0.9 norm_part.1
  154.0 9.6 %all-to-all-done.3 = f32[12,10,128]{2,1,0:T(8,128)S(1)} async-done(((f32[12,10,128]{2,1,0:T(8,128)}), f32[12,10,128]{2,1,0:T(8,128)S(1)}, u32[]{:S(2)}, u32[]{:S(2)}) %all-to-all-start.3) | async-done | bytes 61472 | tf_op jit(solution)/shard_map/gain/all_to_all | solution.py:273
  163.6 0.6 multiply_bitcast_fusion
  (15 shorter events, 0.1 us)
Async XLA Ops:
  0.6 41.0 %collective-permute-start = (bf16[5120,512]{1,0:T(8,128)(2,1)}, bf16[5120,512]{1,0:T(8,128)(2,1)}, u32[]{:S(2)}, u32[]{:S(2)}) collective-permute-start(bf16[5120,512]{1,0:T(8,128)(2,1)} %param.10), channel_id=1, source_target_pairs={{0,1},{1,0},{2,3},{3,2},{4,5},{5,4},{6,7},{7,6},{8,9},{9,8},{10,11... | collective-permute-start | bytes 15728648 | tf_op jit(solution)/shard_map/weights/ppermute | solution.py:41
  35.2 6.5 %copy-start.3 = (bf16[16,16,512]{2,1,0:T(8,128)(2,1)}, bf16[16,16,512]{2,1,0:T(8,128)(2,1)S(1)}, u32[]{:S(2)}) copy-start(bf16[16,16,512]{2,1,0:T(8,128)(2,1)S(1)} %all_to_all.20) | copy-start | bytes 786436
  35.2 6.5 %collective-permute-start.1 = (bf16[256,512]{1,0:T(8,128)(2,1)S(1)}, bf16[256,512]{1,0:T(8,128)(2,1)S(1)}, u32[]{:S(2)}, u32[]{:S(2)}) collective-permute-start(bf16[256,512]{1,0:T(8,128)(2,1)S(1)} %bitcast.28), channel_id=1, source_target_pairs={{0,1},{1,0},{2,3},{3,2},{4,5},{5,4},{6,7},{7,6},{8,9},{9,8},{10,11... | collective-permute-start | bytes 786440 | tf_op jit(solution)/shard_map/tokens/ppermute | solution.py:41
  37.1 3.6 %collective-permute-start.4 = (bf16[16,5120]{1,0:T(8,128)(2,1)}, bf16[16,5120]{1,0:T(8,128)(2,1)S(1)}, u32[]{:S(2)}, u32[]{:S(2)}) collective-permute-start(bf16[16,5120]{1,0:T(8,128)(2,1)} %patch_ref.1), channel_id=1, source_target_pairs={{0,1},{1,0},{2,3},{3,2},{4,5},{5,4},{6,7},{7,6},{8,9},{9,8},{10,11... | collective-permute-start | bytes 491528 | tf_op jit(solution)/shard_map/patches/ppermute | solution.py:41
  40.7 0.9 copy-start
  41.7 0.7 copy-start.4
  47.7 37.9 %copy-start.5 = (bf16[320,256]{1,0:T(8,128)(2,1)S(1)}, bf16[320,256]{1,0:T(8,128)(2,1)}, u32[]{:S(2)}) copy-start(bf16[320,256]{1,0:T(8,128)(2,1)} %param.8) | copy-start | bytes 491524
  47.7 45.2 %copy-start.2 = (s32[256]{0:T(256)S(1)}, s32[256]{0:T(256)}, u32[]{:S(2)}) copy-start(s32[256]{0:T(256)} %param.13) | copy-start | bytes 3076
  47.7 48.9 %collective-permute-start.5 = (bf16[320,5120]{1,0:T(8,128)(2,1)}, bf16[320,5120]{1,0:T(8,128)(2,1)}, u32[]{:S(2)}, u32[]{:S(2)}) collective-permute-start(bf16[320,5120]{1,0:T(8,128)(2,1)} %bitcast.8.own_w), channel_id=1, source_target_pairs={{0,1},{1,0},{2,3},{3,2},{4,5},{5,4},{6,7},{7,6},{8,9},{9,8},{10,11... | collective-permute-start | bytes 9830408 | tf_op jit(solution)/shard_map/hidden/ppermute | solution.py:41
  50.1 22.0 %all-to-all-start.1 = ((bf16[4,2,320,256]{3,2,1,0:T(8,128)(2,1)}), bf16[4,2,320,256]{3,2,1,0:T(8,128)(2,1)S(1)}, u32[]{:S(2)}, u32[]{:S(2)}) async-start(bf16[4,2,320,256]{3,2,1,0:T(8,128)(2,1)} %hidden_part.1), calls=%async_computation.1 | async-start | bytes 2621440 | tf_op jit(solution)/shard_map/hidden/all_to_all | solution.py:301
  53.7 21.5 %collective-permute-start.6 = (bf16[2,16,2560]{2,1,0:T(8,128)(2,1)S(1)}, bf16[2,16,2560]{2,1,0:T(8,128)(2,1)S(1)}, u32[]{:S(2)}, u32[]{:S(2)}) collective-permute-start(bf16[2,16,2560]{2,1,0:T(8,128)(2,1)S(1)} %pack_patches.1), channel_id=1, source_target_pairs={{0,2},{2,0},{1,3},{3,1},{4,6},{6,4},{5,7},{7,5},{8,10},{10,8},{9,1... | collective-permute-start | bytes 491528 | tf_op jit(solution)/shard_map/hidden/ppermute | solution.py:41
  72.2 20.7 %collective-permute-start.2 = (bf16[320,256]{1,0:T(8,128)(2,1)S(1)}, bf16[320,256]{1,0:T(8,128)(2,1)S(1)}, u32[]{:S(2)}, u32[]{:S(2)}) collective-permute-start(bf16[320,256]{1,0:T(8,128)(2,1)S(1)} %sum_parts.1), channel_id=1, source_target_pairs={{0,2},{2,0},{1,3},{3,1},{4,6},{6,4},{5,7},{7,5},{8,10},{10,8},{9,1... | collective-permute-start | bytes 491528 | tf_op jit(solution)/shard_map/hidden/ppermute | solution.py:41
  75.2 28.9 %collective-permute-start.7 = (bf16[2,2,16,2560]{3,2,1,0:T(8,128)(2,1)S(1)}, bf16[2,2,16,2560]{3,2,1,0:T(8,128)(2,1)S(1)}, u32[]{:S(2)}, u32[]{:S(2)}) collective-permute-start(bf16[2,2,16,2560]{3,2,1,0:T(8,128)(2,1)S(1)} %pad_maximum_fusion.refs_0_), channel_id=1, source_target_pairs={{0,12},{4,0},{8,4},{12,8},{1,13},{5,1},{9,5},{13,9},{2,14},{6,2},{... | collective-permute-start | bytes 983048 | tf_op jit(solution)/shard_map/hidden/ppermute | solution.py:309
  80.1 24.1 %collective-permute-start.8 = (bf16[2,2,16,2560]{3,2,1,0:T(8,128)(2,1)S(1)}, bf16[2,2,16,2560]{3,2,1,0:T(8,128)(2,1)S(1)}, u32[]{:S(2)}, u32[]{:S(2)}) collective-permute-start(bf16[2,2,16,2560]{3,2,1,0:T(8,128)(2,1)S(1)} %pad_maximum_fusion.refs_0_), channel_id=1, source_target_pairs={{0,8},{4,12},{8,0},{12,4},{1,9},{5,13},{9,1},{13,5},{2,10},{6,14},... | collective-permute-start | bytes 983048 | tf_op jit(solution)/shard_map/hidden/ppermute | solution.py:309
  82.8 21.3 %collective-permute-start.9 = (bf16[2,2,16,2560]{3,2,1,0:T(8,128)(2,1)S(1)}, bf16[2,2,16,2560]{3,2,1,0:T(8,128)(2,1)S(1)}, u32[]{:S(2)}, u32[]{:S(2)}) collective-permute-start(bf16[2,2,16,2560]{3,2,1,0:T(8,128)(2,1)S(1)} %pad_maximum_fusion.refs_0_), channel_id=1, source_target_pairs={{0,4},{4,8},{8,12},{12,0},{1,5},{5,9},{9,13},{13,1},{2,6},{6,10},{... | collective-permute-start | bytes 983048 | tf_op jit(solution)/shard_map/hidden/ppermute | solution.py:309
  93.2 3.3 %collective-permute-start.3 = (bf16[4,2,2,16,320]{4,3,2,1,0:T(8,128)(2,1)S(1)}, bf16[4,2,2,16,320]{4,3,2,1,0:T(8,128)(2,1)S(1)}, u32[]{:S(2)}, u32[]{:S(2)}) collective-permute-start(bf16[4,2,2,16,320]{4,3,2,1,0:T(8,128)(2,1)S(1)} %act_rows.1.own_a), channel_id=1, source_target_pairs={{0,1},{1,0},{2,3},{3,2},{4,5},{5,4},{6,7},{7,6},{8,9},{9,8},{10,11... | collective-permute-start | bytes 491528 | tf_op jit(solution)/shard_map/merged/ppermute | solution.py:41
  100.5 24.4 %all-to-all-start.2 = ((bf16[8,32,2560]{2,1,0:T(8,128)(2,1)}), bf16[8,32,2560]{2,1,0:T(8,128)(2,1)S(1)}, u32[]{:S(2)}, u32[]{:S(2)}) async-start(bf16[8,32,2560]{2,1,0:T(8,128)(2,1)} %bitcast.9), calls=%async_computation.2 | async-start | bytes 2621440 | tf_op jit(solution)/shard_map/merged/all_to_all | solution.py:314
  104.1 23.5 %copy-start.6 = (f32[1280]{0:T(1024)S(1)}, f32[1280]{0:T(1024)}, u32[]{:S(2)}) copy-start(f32[1280]{0:T(1024)} %param.12) | copy-start | bytes 15364
  104.1 48.9 %copy-start.1 = (bf16[16,5120]{1,0:T(8,128)(2,1)S(1)}, bf16[16,5120]{1,0:T(8,128)(2,1)}, u32[]{:S(2)}) copy-start(bf16[16,5120]{1,0:T(8,128)(2,1)} %patch_ref.1) | copy-start | bytes 491524
  125.0 28.0 %collective-permute-start.10 = (bf16[2,16,2560]{2,1,0:T(8,128)(2,1)S(1)}, bf16[2,16,2560]{2,1,0:T(8,128)(2,1)S(1)}, u32[]{:S(2)}, u32[]{:S(2)}) collective-permute-start(bf16[2,16,2560]{2,1,0:T(8,128)(2,1)S(1)} %sum_halves.1), channel_id=1, source_target_pairs={{0,2},{2,0},{1,3},{3,1},{4,6},{6,4},{5,7},{7,5},{8,10},{10,8},{9,1... | collective-permute-start | bytes 491528 | tf_op jit(solution)/shard_map/merged/ppermute | solution.py:41
  138.6 25.0 %all-to-all-start.3 = ((f32[12,10,128]{2,1,0:T(8,128)}), f32[12,10,128]{2,1,0:T(8,128)S(1)}, u32[]{:S(2)}, u32[]{:S(2)}) async-start(f32[12,10,128]{2,1,0:T(8,128)} %broadcast_in_dim.2), calls=%async_computation.3 | async-start | bytes 196608 | tf_op jit(solution)/shard_map/gain/all_to_all | solution.py:273

commit v6 on v5

--- a/solution.py
+++ b/solution.py
@@ -285,13 +285,15 @@
     with jax.named_scope("tokens"):
         outgoing = grad_tokens.reshape(own, ctx, depth // ctx).transpose(1, 0, 2)
         tokens = lax.all_to_all(outgoing, CTX, 0, 0, tiled=True).reshape(group, depth // ctx)
+        beside = swap(patch_in, "co")
+        tokens, beside = lax.optimization_barrier((tokens, beside))
         tokens = (tokens, swap(tokens, "co"))
     with jax.named_scope("weights"):
         weights_2 = (w_fc2, swap(w_fc2, "co"))
         w_fc1_t = w_fc1.T
 
     with jax.named_scope("patches"):
-        patches = pack_patches(patch_in, swap(patch_in, "co"), core)
+        patches = pack_patches(patch_in, beside, core)
 
     def tie(value, first):
         return lax.optimization_barrier((value, first))[0]
@@ -316,12 +318,12 @@
         ).reshape(NX * NCO, NZH, own, half)
         here = jnp.stack([lax.axis_index("x").astype(jnp.int32), zh])
         terms = gain_terms(sums, around, here, norm_gain.shape[0]).reshape(-1, 128)
-        terms = lax.psum(lax.psum(terms, "co"), "y")
+        terms = lax.psum(terms, "co")
         parts, terms = lax.optimization_barrier((parts, terms))
         far = sum_halves(parts, far_z)
         got = swap(far, "zh")
     with jax.named_scope("gain"):
-        terms = lax.psum(tie(terms, far), "x")
+        terms = sum_over(tie(terms, far), ("x", "y"), NX * NY)
     with jax.named_scope("norm"):
         patch_grad = norm_part(parts, got, patch_in, norm_gain, near_z)
     with jax.named_scope("gain"):

time: 165 us -> 162 us (0.982)
  blocking collectives: 60.4 us -> 2.58 us
  waiting for transfers between devices: 36.5 us -> 72.6 us
  starting transfers between devices: 49.2 us -> 65.8 us
    all_to_all x1 -> x0, blocking collectives: 31.6 us -> none  [local(): lax.all_to_all(outgoing, CTX, 0, 0, tiled=True).reshape(group, depth // ctx)]
    psum x3 -> x1, blocking collectives: 28.8 us -> 2.58 us  [local(): terms = lax.psum(terms, 'co')]
    all_to_all x0 -> x1, starting transfers between devices: none -> 17.2 us  [local(): lax.all_to_all(outgoing, CTX, 0, 0, tiled=True).reshape(group, depth // ctx)]
    all_to_all x1, waiting for transfers between devices: 0.01 us -> 13.8 us  [local(): lax.all_to_all(sums.reshape(NX * NCO, NZH * own, half), ('x', 'co'), 0, 0...]
    all_to_all x0 -> x1, waiting for transfers between devices: none -> 11.1 us  [local(): lax.all_to_all(outgoing, CTX, 0, 0, tiled=True).reshape(group, depth // ctx)]
    all_to_all x1 -> x2, waiting for transfers between devices: 9.6 us -> 18.7 us  [sum_over(): return jnp.sum(lax.all_to_all(rows, axes, 0, 0, tiled=True), axis=0)]
    ppermute x8, waiting for transfers between devices: 10.5 us -> 12.5 us  [swap(): return lax.ppermute(value, axis, [(0, 1), (1, 0)])]
    all_to_all x1 -> x2, starting transfers between devices: 14.4 us -> 14.8 us  [sum_over(): return jnp.sum(lax.all_to_all(rows, axes, 0, 0, tiled=True), axis=0)]
  transfers between devices with their start and end apart: 14 -> 16, of which waited for: 6 -> 11; matrix products, arithmetic and copies ran while one was open for 1% -> 2% of each run, Pallas kernels for 5% -> 5%
where the time goes in v6:
time: 162 us; the launch traced here: 161 us
  waiting for transfers between devices  72.6 us (45%)
  starting transfers between devices  65.8 us (41%)
  Pallas kernels  13 us (8%)
  local copies, waits for them, and re-layouts  4.7 us (3%)
  blocking collectives  2.58 us (2%)
    all_to_all x2, waiting for transfers between devices, sum_over(): return jnp.sum(lax.all_to_all(rows, axes, 0, 0, tiled=True), axis=0)  18.7 us
    all_to_all x1, starting transfers between devices, local(): lax.all_to_all(outgoing, CTX, 0, 0, tiled=True).reshape(group, depth // ctx)  17.2 us
    all_to_all x1, waiting for transfers between devices, local(): parts = lax.all_to_all(sums, 'x', 0, 0, tiled=True)  16.5 us
    ppermute x8, starting transfers between devices, swap(): return lax.ppermute(value, axis, [(0, 1), (1, 0)])  16.4 us
    all_to_all x2, starting transfers between devices, sum_over(): return jnp.sum(lax.all_to_all(rows, axes, 0, 0, tiled=True), axis=0)  14.8 us
    all_to_all x1, waiting for transfers between devices, local(): lax.all_to_all(sums.reshape(NX * NCO, NZH * own, half), ('x', 'co'), 0, 0...  13.8 us
    ppermute x8, waiting for transfers between devices, swap(): return lax.ppermute(value, axis, [(0, 1), (1, 0)])  12.5 us
    all_to_all x1, waiting for transfers between devices, local(): lax.all_to_all(outgoing, CTX, 0, 0, tiled=True).reshape(group, depth // ctx)  11.1 us
  transfers between devices with their start and end apart: 16, of which 11 were waited for; matrix products, arithmetic and copies ran while one was open for 2% of the time, Pallas kernels for 5%

profile of v6, /device:TPU:8, one launch (start us, length us, event | category | flops | bytes accessed | tf_op | source)
XLA Modules:
  0.0 160.6 jit_solution(5938926708159991106)
XLA Ops:
  0.6 1.9 %collective-permute-start = (bf16[5120,512]{1,0:T(8,128)(2,1)}, bf16[5120,512]{1,0:T(8,128)(2,1)}, u32[]{:S(2)}, u32[]{:S(2)}) collective-permute-start(bf16[5120,512]{1,0:T(8,128)(2,1)} %param.10), channel_id=1, source_target_pairs={{0,1},{1,0},{2,3},{3,2},{4,5},{5,4},{6,7},{7,6},{8,9},{9,8},{10,11... | collective-permute-start | bytes 15728648 | tf_op jit(solution)/shard_map/weights/ppermute | solution.py:41
  2.6 1.7 %copy.18 = bf16[2,16,8,512]{3,2,0,1:T(8,128)(2,1)} copy(bf16[2,16,8,512]{3,2,1,0:T(8,128)(2,1)} %bitcast.30) | data formatting | bytes 524288 | tf_op jit(solution)/shard_map/tokens/reshape | solution.py:286
  4.3 17.2 %all-to-all-start = ((bf16[16,16,512]{2,1,0:T(8,128)(2,1)}), bf16[16,16,512]{2,1,0:T(8,128)(2,1)S(1)}, u32[]{:S(2)}, u32[]{:S(2)}) async-start(bf16[16,16,512]{2,1,0:T(8,128)(2,1)} %bitcast.22), calls=%async_computation | async-start | bytes 524288 | tf_op jit(solution)/shard_map/tokens/all_to_all | solution.py:287
  21.4 2.3 %collective-permute-start.1 = (bf16[16,5120]{1,0:T(8,128)(2,1)}, bf16[16,5120]{1,0:T(8,128)(2,1)S(1)}, u32[]{:S(2)}, u32[]{:S(2)}) collective-permute-start(bf16[16,5120]{1,0:T(8,128)(2,1)} %patch_ref.1), channel_id=1, source_target_pairs={{0,1},{1,0},{2,3},{3,2},{4,5},{5,4},{6,7},{7,6},{8,9},{9,8},{10,11... | collective-permute-start | bytes 491528 | tf_op jit(solution)/shard_map/tokens/ppermute | solution.py:41
  23.8 1.2 collective-permute-done.1.got_ref
  25.0 11.1 %all-to-all-done = bf16[16,16,512]{2,1,0:T(8,128)(2,1)S(1)} async-done(((bf16[16,16,512]{2,1,0:T(8,128)(2,1)}), bf16[16,16,512]{2,1,0:T(8,128)(2,1)S(1)}, u32[]{:S(2)}, u32[]{:S(2)}) %all-to-all-start) | async-done | bytes 262176 | tf_op jit(solution)/shard_map/tokens/all_to_all | solution.py:287
  36.1 1.9 %collective-permute-start.2 = (bf16[256,512]{1,0:T(8,128)(2,1)S(1)}, bf16[256,512]{1,0:T(8,128)(2,1)S(1)}, u32[]{:S(2)}, u32[]{:S(2)}) collective-permute-start(bf16[256,512]{1,0:T(8,128)(2,1)S(1)} %bitcast.28), channel_id=1, source_target_pairs={{0,1},{1,0},{2,3},{3,2},{4,5},{5,4},{6,7},{7,6},{8,9},{9,8},{10,11... | collective-permute-start | bytes 786440 | tf_op jit(solution)/shard_map/tokens/ppermute | solution.py:41
  38.0 0.0 copy-start
  38.0 0.9 copy-done
  39.0 0.6 collective-permute-done.2.got_t
  39.5 0.0 collective-permute-done
  39.5 0.7 copy-done.4
  40.2 5.4 %hidden_part.1 = bf16[4,2,320,256]{3,2,1,0:T(8,128)(2,1)} custom-call(s32[1]{0:T(128)} %bitcast.1.core.place, bf16[4,2,2,320,512]{4,3,2,1,0:T(8,128)(2,1)} %bitcast.27, bf16[4,2,2,320,512]{4,3,2,1,0:T(8,128)(2,1)} %bitcast.3.got_w, bf16[256,512]{1,0:T(8,128)(2,1)} %bitcast.29, bf16[256,512]{1,0:T(8,128)(2,1)} %copy-done.4), custom_call_target="tpu_custom_call" | custom-call | flops 1 | bytes 1 | tf_op jit(solution)/shard_map/hidden/hidden_part/pallas_call | solution.py:65
  45.6 2.2 %collective-permute-start.5 = (bf16[320,5120]{1,0:T(8,128)(2,1)}, bf16[320,5120]{1,0:T(8,128)(2,1)}, u32[]{:S(2)}, u32[]{:S(2)}) collective-permute-start(bf16[320,5120]{1,0:T(8,128)(2,1)} %bitcast.8.own_w), channel_id=1, source_target_pairs={{0,1},{1,0},{2,3},{3,2},{4,5},{5,4},{6,7},{7,6},{8,9},{9,8},{10,11... | collective-permute-start | bytes 9830408 | tf_op jit(solution)/shard_map/hidden/ppermute | solution.py:41
  47.8 3.6 %all-to-all-start.1 = ((bf16[4,2,320,256]{3,2,1,0:T(8,128)(2,1)}), bf16[4,2,320,256]{3,2,1,0:T(8,128)(2,1)S(1)}, u32[]{:S(2)}, u32[]{:S(2)}) async-start(bf16[4,2,320,256]{3,2,1,0:T(8,128)(2,1)} %hidden_part.1), calls=%async_computation.1 | async-start | bytes 2621440 | tf_op jit(solution)/shard_map/hidden/all_to_all | solution.py:303
  51.3 2.2 %collective-permute-start.6 = (bf16[2,16,2560]{2,1,0:T(8,128)(2,1)S(1)}, bf16[2,16,2560]{2,1,0:T(8,128)(2,1)S(1)}, u32[]{:S(2)}, u32[]{:S(2)}) collective-permute-start(bf16[2,16,2560]{2,1,0:T(8,128)(2,1)S(1)} %pack_patches.1), channel_id=1, source_target_pairs={{0,2},{2,0},{1,3},{3,1},{4,6},{6,4},{5,7},{7,5},{8,10},{10,8},{9,1... | collective-permute-start | bytes 491528 | tf_op jit(solution)/shard_map/hidden/ppermute | solution.py:41
  53.5 16.5 %all-to-all-done.1.v_ref = bf16[4,2,320,256]{3,2,1,0:T(8,128)(2,1)S(1)} async-done(((bf16[4,2,320,256]{3,2,1,0:T(8,128)(2,1)}), bf16[4,2,320,256]{3,2,1,0:T(8,128)(2,1)S(1)}, u32[]{:S(2)}, u32[]{:S(2)}) %all-to-all-start.1) | async-done | bytes 1310752 | tf_op jit(solution)/shard_map/hidden/all_to_all | solution.py:303
  70.0 0.1 sum_parts.1
  70.1 2.1 %collective-permute-start.3 = (bf16[320,256]{1,0:T(8,128)(2,1)S(1)}, bf16[320,256]{1,0:T(8,128)(2,1)S(1)}, u32[]{:S(2)}, u32[]{:S(2)}) collective-permute-start(bf16[320,256]{1,0:T(8,128)(2,1)S(1)} %sum_parts.1), channel_id=1, source_target_pairs={{0,2},{2,0},{1,3},{3,1},{4,6},{6,4},{5,7},{7,5},{8,10},{10,8},{9,1... | collective-permute-start | bytes 491528 | tf_op jit(solution)/shard_map/hidden/ppermute | solution.py:41
  72.2 0.9 collective-permute-done.6
  73.1 4.8 %collective-permute-start.7 = (bf16[2,2,16,2560]{3,2,1,0:T(8,128)(2,1)S(1)}, bf16[2,2,16,2560]{3,2,1,0:T(8,128)(2,1)S(1)}, u32[]{:S(2)}, u32[]{:S(2)}) collective-permute-start(bf16[2,2,16,2560]{3,2,1,0:T(8,128)(2,1)S(1)} %pad_maximum_fusion.refs_0_), channel_id=1, source_target_pairs={{0,12},{4,0},{8,4},{12,8},{1,13},{5,1},{9,5},{13,9},{2,14},{6,2},{... | collective-permute-start | bytes 983048 | tf_op jit(solution)/shard_map/hidden/ppermute | solution.py:311
  77.9 2.8 %collective-permute-start.8 = (bf16[2,2,16,2560]{3,2,1,0:T(8,128)(2,1)S(1)}, bf16[2,2,16,2560]{3,2,1,0:T(8,128)(2,1)S(1)}, u32[]{:S(2)}, u32[]{:S(2)}) collective-permute-start(bf16[2,2,16,2560]{3,2,1,0:T(8,128)(2,1)S(1)} %pad_maximum_fusion.refs_0_), channel_id=1, source_target_pairs={{0,8},{4,12},{8,0},{12,4},{1,9},{5,13},{9,1},{13,5},{2,10},{6,14},... | collective-permute-start | bytes 983048 | tf_op jit(solution)/shard_map/hidden/ppermute | solution.py:311
  80.7 2.8 %collective-permute-start.9 = (bf16[2,2,16,2560]{3,2,1,0:T(8,128)(2,1)S(1)}, bf16[2,2,16,2560]{3,2,1,0:T(8,128)(2,1)S(1)}, u32[]{:S(2)}, u32[]{:S(2)}) collective-permute-start(bf16[2,2,16,2560]{3,2,1,0:T(8,128)(2,1)S(1)} %pad_maximum_fusion.refs_0_), channel_id=1, source_target_pairs={{0,4},{4,8},{8,12},{12,0},{1,5},{5,9},{9,13},{13,1},{2,6},{6,10},{... | collective-permute-start | bytes 983048 | tf_op jit(solution)/shard_map/hidden/ppermute | solution.py:311
  83.5 0.1 fusion.3.slope_ref
  83.6 7.4 %collective-permute-done.3.got_ref = bf16[320,256]{1,0:T(8,128)(2,1)S(1)} collective-permute-done((bf16[320,256]{1,0:T(8,128)(2,1)S(1)}, bf16[320,256]{1,0:T(8,128)(2,1)S(1)}, u32[]{:S(2)}, u32[]{:S(2)}) %collective-permute-start.3) | collective-permute-done | bytes 163872 | tf_op jit(solution)/shard_map/hidden/ppermute | solution.py:41
  91.0 0.4 act_rows.1.own_a
  91.4 1.9 %collective-permute-start.4 = (bf16[4,2,2,16,320]{4,3,2,1,0:T(8,128)(2,1)S(1)}, bf16[4,2,2,16,320]{4,3,2,1,0:T(8,128)(2,1)S(1)}, u32[]{:S(2)}, u32[]{:S(2)}) collective-permute-start(bf16[4,2,2,16,320]{4,3,2,1,0:T(8,128)(2,1)S(1)} %act_rows.1.own_a), channel_id=1, source_target_pairs={{0,1},{1,0},{2,3},{3,2},{4,5},{5,4},{6,7},{7,6},{8,9},{9,8},{10,11... | collective-permute-start | bytes 491528 | tf_op jit(solution)/shard_map/merged/ppermute | solution.py:41
  93.3 0.1 pad_add_fusion.place
  93.4 1.3 collective-permute-done.4.got_a
  94.7 0.0 collective-permute-done.5.got_w
  94.7 3.9 %merged_part.1.grad_ref = bf16[4,2,2,16,2560]{4,3,2,1,0:T(8,128)(2,1)} custom-call(s32[1]{0:T(128)} %bitcast.1.core.place, bf16[4,2,2,16,320]{4,3,2,1,0:T(8,128)(2,1)S(1)} %act_rows.1.own_a, bf16[4,2,2,16,320]{4,3,2,1,0:T(8,128)(2,1)S(1)} %collective-permute-done.4.got_a, bf16[320,5120]{1,0:T(8,128)(2,1)} %bitcast.8.own_w, ...), custom_call_target="tpu_custom_call" | custom-call | flops 1 | bytes 1 | tf_op jit(solution)/shard_map/merged/merged_part/pallas_call | solution.py:152
  98.7 3.6 %all-to-all-start.2 = ((bf16[8,32,2560]{2,1,0:T(8,128)(2,1)}), bf16[8,32,2560]{2,1,0:T(8,128)(2,1)S(1)}, u32[]{:S(2)}, u32[]{:S(2)}) async-start(bf16[8,32,2560]{2,1,0:T(8,128)(2,1)} %bitcast.9), calls=%async_computation.2 | async-start | bytes 2621440 | tf_op jit(solution)/shard_map/merged/all_to_all | solution.py:316
  102.2 0.0 copy-start.6
  102.3 0.0 copy-start.1
  102.3 2.2 %gain_terms.1 = f32[1,1280]{1,0:T(1,128)S(1)} custom-call(s32[2]{0:T(128)S(1)} %pad_add_fusion.place, bf16[4,2,2,16,2560]{4,3,2,1,0:T(8,128)(2,1)} %merged_part.1.grad_ref, bf16[2,2,16,2560]{3,2,1,0:T(8,128)(2,1)S(1)} %pad_maximum_fusion.refs_0_, bf16[2,2,16,2560]{3,2,1,0:T(8,128)(2,1)S(1)} %collective-permute-done.7.refs_1_, ...), custom_call_target="tpu_custom_call" | custom-call | flops 20000000000 | bytes 1 | tf_op jit(solution)/shard_map/merged/gain_terms/pallas_call | solution.py:231
  104.6 2.6 %psum.7 = f32[10,128]{1,0:T(8,128)S(1)} all-reduce(f32[10,128]{1,0:T(8,128)S(1)} %bitcast.32), channel_id=1, replica_groups=mesh['y'=8,'zl'=6,'x'=4,'zh'=2,'co'=2] {'co'}, use_global_device_ids=true, to_apply=%region_0.0 | all-reduce | flops 1280 | bytes 10240 | tf_op jit(solution)/shard_map/merged/psum | solution.py:321
  107.2 13.8 %all-to-all-done.2 = bf16[8,32,2560]{2,1,0:T(8,128)(2,1)S(1)} async-done(((bf16[8,32,2560]{2,1,0:T(8,128)(2,1)}), bf16[8,32,2560]{2,1,0:T(8,128)(2,1)S(1)}, u32[]{:S(2)}, u32[]{:S(2)}) %all-to-all-start.2) | async-done | bytes 1310752 | tf_op jit(solution)/shard_map/merged/all_to_all | solution.py:316
  120.9 0.1 sum_halves.1
  121.0 0.7 broadcast_in_dim.4
  121.7 8.3 %all-to-all-start.3 = ((f32[32,10,128]{2,1,0:T(8,128)}), f32[32,10,128]{2,1,0:T(8,128)S(1)}, u32[]{:S(2)}, u32[]{:S(2)}) async-start(f32[32,10,128]{2,1,0:T(8,128)} %broadcast_in_dim.4), calls=%async_computation.3 | async-start | bytes 524288 | tf_op jit(solution)/shard_map/gain/all_to_all | solution.py:273
  130.0 1.9 %collective-permute-start.10 = (bf16[2,16,2560]{2,1,0:T(8,128)(2,1)S(1)}, bf16[2,16,2560]{2,1,0:T(8,128)(2,1)S(1)}, u32[]{:S(2)}, u32[]{:S(2)}) collective-permute-start(bf16[2,16,2560]{2,1,0:T(8,128)(2,1)S(1)} %sum_halves.1), channel_id=1, source_target_pairs={{0,2},{2,0},{1,3},{3,1},{4,6},{6,4},{5,7},{7,5},{8,10},{10,8},{9,1... | collective-permute-start | bytes 491528 | tf_op jit(solution)/shard_map/merged/ppermute | solution.py:41
  132.0 10.1 %all-to-all-done.3 = f32[32,10,128]{2,1,0:T(8,128)S(1)} async-done(((f32[32,10,128]{2,1,0:T(8,128)}), f32[32,10,128]{2,1,0:T(8,128)S(1)}, u32[]{:S(2)}, u32[]{:S(2)}) %all-to-all-start.3) | async-done | bytes 163872 | tf_op jit(solution)/shard_map/gain/all_to_all | solution.py:273
  142.2 0.7 broadcast_in_dim.5
  142.8 6.5 %all-to-all-start.4 = ((f32[12,10,128]{2,1,0:T(8,128)}), f32[12,10,128]{2,1,0:T(8,128)S(1)}, u32[]{:S(2)}, u32[]{:S(2)}) async-start(f32[12,10,128]{2,1,0:T(8,128)} %broadcast_in_dim.5), calls=%async_computation.4 | async-start | bytes 196608 | tf_op jit(solution)/shard_map/gain/all_to_all | solution.py:273
  149.4 1.1 collective-permute-done.10.got_ref
  150.5 0.9 norm_part.1
  151.4 8.5 %all-to-all-done.4 = f32[12,10,128]{2,1,0:T(8,128)S(1)} async-done(((f32[12,10,128]{2,1,0:T(8,128)}), f32[12,10,128]{2,1,0:T(8,128)S(1)}, u32[]{:S(2)}, u32[]{:S(2)}) %all-to-all-start.4) | async-done | bytes 61472 | tf_op jit(solution)/shard_map/gain/all_to_all | solution.py:273
  160.0 0.6 multiply_bitcast_fusion
  (18 shorter events, 0.2 us)
Async XLA Ops:
  0.6 38.9 %collective-permute-start = (bf16[5120,512]{1,0:T(8,128)(2,1)}, bf16[5120,512]{1,0:T(8,128)(2,1)}, u32[]{:S(2)}, u32[]{:S(2)}) collective-permute-start(bf16[5120,512]{1,0:T(8,128)(2,1)} %param.10), channel_id=1, source_target_pairs={{0,1},{1,0},{2,3},{3,2},{4,5},{5,4},{6,7},{7,6},{8,9},{9,8},{10,11... | collective-permute-start | bytes 15728648 | tf_op jit(solution)/shard_map/weights/ppermute | solution.py:41
  4.3 31.8 %all-to-all-start = ((bf16[16,16,512]{2,1,0:T(8,128)(2,1)}), bf16[16,16,512]{2,1,0:T(8,128)(2,1)S(1)}, u32[]{:S(2)}, u32[]{:S(2)}) async-start(bf16[16,16,512]{2,1,0:T(8,128)(2,1)} %bitcast.22), calls=%async_computation | async-start | bytes 524288 | tf_op jit(solution)/shard_map/tokens/all_to_all | solution.py:287
  21.4 3.5 %collective-permute-start.1 = (bf16[16,5120]{1,0:T(8,128)(2,1)}, bf16[16,5120]{1,0:T(8,128)(2,1)S(1)}, u32[]{:S(2)}, u32[]{:S(2)}) collective-permute-start(bf16[16,5120]{1,0:T(8,128)(2,1)} %patch_ref.1), channel_id=1, source_target_pairs={{0,1},{1,0},{2,3},{3,2},{4,5},{5,4},{6,7},{7,6},{8,9},{9,8},{10,11... | collective-permute-start | bytes 491528 | tf_op jit(solution)/shard_map/tokens/ppermute | solution.py:41
  36.1 3.4 %copy-start.3 = (bf16[16,16,512]{2,1,0:T(8,128)(2,1)}, bf16[16,16,512]{2,1,0:T(8,128)(2,1)S(1)}, u32[]{:S(2)}) copy-start(bf16[16,16,512]{2,1,0:T(8,128)(2,1)S(1)} %all-to-all-done) | copy-start | bytes 786436
  36.1 3.4 %collective-permute-start.2 = (bf16[256,512]{1,0:T(8,128)(2,1)S(1)}, bf16[256,512]{1,0:T(8,128)(2,1)S(1)}, u32[]{:S(2)}, u32[]{:S(2)}) collective-permute-start(bf16[256,512]{1,0:T(8,128)(2,1)S(1)} %bitcast.28), channel_id=1, source_target_pairs={{0,1},{1,0},{2,3},{3,2},{4,5},{5,4},{6,7},{7,6},{8,9},{9,8},{10,11... | collective-permute-start | bytes 786440 | tf_op jit(solution)/shard_map/tokens/ppermute | solution.py:41
  38.0 0.9 copy-start
  39.5 0.7 copy-start.4
  45.6 37.9 %copy-start.5 = (bf16[320,256]{1,0:T(8,128)(2,1)S(1)}, bf16[320,256]{1,0:T(8,128)(2,1)}, u32[]{:S(2)}) copy-start(bf16[320,256]{1,0:T(8,128)(2,1)} %param.8) | copy-start | bytes 491524
  45.6 45.4 %copy-start.2 = (s32[256]{0:T(256)S(1)}, s32[256]{0:T(256)}, u32[]{:S(2)}) copy-start(s32[256]{0:T(256)} %param.13) | copy-start | bytes 3076
  45.6 49.1 %collective-permute-start.5 = (bf16[320,5120]{1,0:T(8,128)(2,1)}, bf16[320,5120]{1,0:T(8,128)(2,1)}, u32[]{:S(2)}, u32[]{:S(2)}) collective-permute-start(bf16[320,5120]{1,0:T(8,128)(2,1)} %bitcast.8.own_w), channel_id=1, source_target_pairs={{0,1},{1,0},{2,3},{3,2},{4,5},{5,4},{6,7},{7,6},{8,9},{9,8},{10,11... | collective-permute-start | bytes 9830408 | tf_op jit(solution)/shard_map/hidden/ppermute | solution.py:41
  47.8 22.2 %all-to-all-start.1 = ((bf16[4,2,320,256]{3,2,1,0:T(8,128)(2,1)}), bf16[4,2,320,256]{3,2,1,0:T(8,128)(2,1)S(1)}, u32[]{:S(2)}, u32[]{:S(2)}) async-start(bf16[4,2,320,256]{3,2,1,0:T(8,128)(2,1)} %hidden_part.1), calls=%async_computation.1 | async-start | bytes 2621440 | tf_op jit(solution)/shard_map/hidden/all_to_all | solution.py:303
  51.3 21.7 %collective-permute-start.6 = (bf16[2,16,2560]{2,1,0:T(8,128)(2,1)S(1)}, bf16[2,16,2560]{2,1,0:T(8,128)(2,1)S(1)}, u32[]{:S(2)}, u32[]{:S(2)}) collective-permute-start(bf16[2,16,2560]{2,1,0:T(8,128)(2,1)S(1)} %pack_patches.1), channel_id=1, source_target_pairs={{0,2},{2,0},{1,3},{3,1},{4,6},{6,4},{5,7},{7,5},{8,10},{10,8},{9,1... | collective-permute-start | bytes 491528 | tf_op jit(solution)/shard_map/hidden/ppermute | solution.py:41
  70.1 20.9 %collective-permute-start.3 = (bf16[320,256]{1,0:T(8,128)(2,1)S(1)}, bf16[320,256]{1,0:T(8,128)(2,1)S(1)}, u32[]{:S(2)}, u32[]{:S(2)}) collective-permute-start(bf16[320,256]{1,0:T(8,128)(2,1)S(1)} %sum_parts.1), channel_id=1, source_target_pairs={{0,2},{2,0},{1,3},{3,1},{4,6},{6,4},{5,7},{7,5},{8,10},{10,8},{9,1... | collective-permute-start | bytes 491528 | tf_op jit(solution)/shard_map/hidden/ppermute | solution.py:41
  73.1 29.2 %collective-permute-start.7 = (bf16[2,2,16,2560]{3,2,1,0:T(8,128)(2,1)S(1)}, bf16[2,2,16,2560]{3,2,1,0:T(8,128)(2,1)S(1)}, u32[]{:S(2)}, u32[]{:S(2)}) collective-permute-start(bf16[2,2,16,2560]{3,2,1,0:T(8,128)(2,1)S(1)} %pad_maximum_fusion.refs_0_), channel_id=1, source_target_pairs={{0,12},{4,0},{8,4},{12,8},{1,13},{5,1},{9,5},{13,9},{2,14},{6,2},{... | collective-permute-start | bytes 983048 | tf_op jit(solution)/shard_map/hidden/ppermute | solution.py:311
  77.9 24.4 %collective-permute-start.8 = (bf16[2,2,16,2560]{3,2,1,0:T(8,128)(2,1)S(1)}, bf16[2,2,16,2560]{3,2,1,0:T(8,128)(2,1)S(1)}, u32[]{:S(2)}, u32[]{:S(2)}) collective-permute-start(bf16[2,2,16,2560]{3,2,1,0:T(8,128)(2,1)S(1)} %pad_maximum_fusion.refs_0_), channel_id=1, source_target_pairs={{0,8},{4,12},{8,0},{12,4},{1,9},{5,13},{9,1},{13,5},{2,10},{6,14},... | collective-permute-start | bytes 983048 | tf_op jit(solution)/shard_map/hidden/ppermute | solution.py:311
  80.7 21.6 %collective-permute-start.9 = (bf16[2,2,16,2560]{3,2,1,0:T(8,128)(2,1)S(1)}, bf16[2,2,16,2560]{3,2,1,0:T(8,128)(2,1)S(1)}, u32[]{:S(2)}, u32[]{:S(2)}) collective-permute-start(bf16[2,2,16,2560]{3,2,1,0:T(8,128)(2,1)S(1)} %pad_maximum_fusion.refs_0_), channel_id=1, source_target_pairs={{0,4},{4,8},{8,12},{12,0},{1,5},{5,9},{9,13},{13,1},{2,6},{6,10},{... | collective-permute-start | bytes 983048 | tf_op jit(solution)/shard_map/hidden/ppermute | solution.py:311
  91.4 3.3 %collective-permute-start.4 = (bf16[4,2,2,16,320]{4,3,2,1,0:T(8,128)(2,1)S(1)}, bf16[4,2,2,16,320]{4,3,2,1,0:T(8,128)(2,1)S(1)}, u32[]{:S(2)}, u32[]{:S(2)}) collective-permute-start(bf16[4,2,2,16,320]{4,3,2,1,0:T(8,128)(2,1)S(1)} %act_rows.1.own_a), channel_id=1, source_target_pairs={{0,1},{1,0},{2,3},{3,2},{4,5},{5,4},{6,7},{7,6},{8,9},{9,8},{10,11... | collective-permute-start | bytes 491528 | tf_op jit(solution)/shard_map/merged/ppermute | solution.py:41
  98.7 22.3 %all-to-all-start.2 = ((bf16[8,32,2560]{2,1,0:T(8,128)(2,1)}), bf16[8,32,2560]{2,1,0:T(8,128)(2,1)S(1)}, u32[]{:S(2)}, u32[]{:S(2)}) async-start(bf16[8,32,2560]{2,1,0:T(8,128)(2,1)} %bitcast.9), calls=%async_computation.2 | async-start | bytes 2621440 | tf_op jit(solution)/shard_map/merged/all_to_all | solution.py:316
  102.2 29.7 %copy-start.6 = (f32[1280]{0:T(1024)S(1)}, f32[1280]{0:T(1024)}, u32[]{:S(2)}) copy-start(f32[1280]{0:T(1024)} %param.12) | copy-start | bytes 15364
  102.3 48.2 %copy-start.1 = (bf16[16,5120]{1,0:T(8,128)(2,1)S(1)}, bf16[16,5120]{1,0:T(8,128)(2,1)}, u32[]{:S(2)}) copy-start(bf16[16,5120]{1,0:T(8,128)(2,1)} %patch_ref.1) | copy-start | bytes 491524
  121.7 20.4 %all-to-all-start.3 = ((f32[32,10,128]{2,1,0:T(8,128)}), f32[32,10,128]{2,1,0:T(8,128)S(1)}, u32[]{:S(2)}, u32[]{:S(2)}) async-start(f32[32,10,128]{2,1,0:T(8,128)} %broadcast_in_dim.4), calls=%async_computation.3 | async-start | bytes 524288 | tf_op jit(solution)/shard_map/gain/all_to_all | solution.py:273
  130.0 20.4 %collective-permute-start.10 = (bf16[2,16,2560]{2,1,0:T(8,128)(2,1)S(1)}, bf16[2,16,2560]{2,1,0:T(8,128)(2,1)S(1)}, u32[]{:S(2)}, u32[]{:S(2)}) collective-permute-start(bf16[2,16,2560]{2,1,0:T(8,128)(2,1)S(1)} %sum_halves.1), channel_id=1, source_target_pairs={{0,2},{2,0},{1,3},{3,1},{4,6},{6,4},{5,7},{7,5},{8,10},{10,8},{9,1... | collective-permute-start | bytes 491528 | tf_op jit(solution)/shard_map/merged/ppermute | solution.py:41
  142.8 17.1 %all-to-all-start.4 = ((f32[12,10,128]{2,1,0:T(8,128)}), f32[12,10,128]{2,1,0:T(8,128)S(1)}, u32[]{:S(2)}, u32[]{:S(2)}) async-start(f32[12,10,128]{2,1,0:T(8,128)} %broadcast_in_dim.5), calls=%async_computation.4 | async-start | bytes 196608 | tf_op jit(solution)/shard_map/gain/all_to_all | solution.py:273

commit v7 on v6

--- a/solution.py
+++ b/solution.py
@@ -100,8 +100,22 @@
     )(place, parts)
 
 
+def wide_kernel(v_ref, out_ref):
+    out_ref[...] = v_ref[...].astype(F32)
+
+
+def widen(value):
+    return pl.pallas_call(
+        wide_kernel,
+        out_shape=jax.ShapeDtypeStruct(value.shape, F32),
+        compiler_params=params(),
+        cost_estimate=cost(LONG),
+        name="widen",
+    )(value)
+
+
 def act_kernel(place, v_ref, got_ref, slope_ref, pos_ref, out_ref):
-    act = ((total_of(v_ref, place[0]) + got_ref[...].astype(F32)) * slope_ref[...]).astype(BF16)
+    act = ((total_of(v_ref, place[0]) + got_ref[...]) * slope_ref[...]).astype(BF16)
     count = act.shape[1]
     pick = (lax.broadcasted_iota(jnp.int32, (count, count), 0) == pos_ref[...]).astype(F32)
     pick = pick.T.astype(BF16)
@@ -205,23 +219,37 @@
     )(core, own, got)
 
 
+def spread_kernel(own_ref, beyond_ref, out_ref):
+    for x in range(NX):
+        out_ref[x, 0] = own_ref[...]
+        out_ref[x, 1] = beyond_ref[...]
+
+
+def spread_patches(own, beyond):
+    return pl.pallas_call(
+        spread_kernel,
+        out_shape=jax.ShapeDtypeStruct((NX, NZH) + own.shape, BF16),
+        compiler_params=params(),
+        cost_estimate=cost(),
+        name="spread_patches",
+    )(own, beyond)
+
+
 def norm_of(patch):
     inv_rms = lax.rsqrt(jnp.mean(patch * patch, axis=-1, keepdims=True) + EPS)
     return patch * inv_rms, inv_rms
 
 
-def gain_kernel(place, grad_ref, *refs):
-    out_ref = refs[-1]
+def gain_kernel(place, grad_ref, patch_ref, out_ref):
     width = out_ref.shape[1]
     terms = jnp.zeros((1, width), F32)
-    for shift, patch_ref in enumerate(refs[:-1]):
-        x = lax.rem(place[0] + shift, NX)
+    for x in range(NX):
         for k in range(NZH):
-            z = place[1] if k == 0 else 1 - place[1]
+            z = place[0] if k == 0 else 1 - place[0]
             for c in range(NCO):
                 for p in range(grad_ref.shape[4] // width):
                     cols = pl.ds(p * width, width)
-                    normed, _ = norm_of(patch_ref[k, c, :, cols].astype(F32))
+                    normed, _ = norm_of(patch_ref[x, k, c, :, cols].astype(F32))
                     grad = grad_ref[x, c, z, :, cols].astype(F32)
                     terms += jnp.sum(grad * normed, axis=0, keepdims=True)
     out_ref[...] = terms
@@ -230,13 +258,13 @@
 def gain_terms(grads, patches, place, width):
     return pl.pallas_call(
         gain_kernel,
-        in_specs=[IN_SMEM] + [IN_VMEM] * (1 + NX),
+        in_specs=[IN_SMEM] + [IN_VMEM] * 2,
         out_specs=IN_VMEM,
         out_shape=jax.ShapeDtypeStruct((1, width), F32),
         compiler_params=params(),
         cost_estimate=cost(LONG),
         name="gain_terms",
-    )(place, grads, *patches)
+    )(place, grads, patches)
 
 
 def norm_kernel(place, v_ref, got_ref, patch_ref, gain_ref, out_ref):
@@ -305,25 +333,22 @@
         weights_1 = (w_fc1_t, swap(tie(w_fc1_t, ready), "co"))
         beyond = swap(ready, "zh")
         far = sum_parts(parts, far_z)
-        got = swap(far, "zh")
-        patches = jnp.stack([tie(patches, far), beyond])
-        around = [patches] + [
-            lax.ppermute(patches, "x", [(i, (i - d) % NX) for i in range(NX)]) for d in (1, 2, 3)
-        ]
+        got = widen(swap(far, "zh"))
+        around = spread_patches(tie(patches, far), beyond)
+        around = lax.all_to_all(around, "x", 0, 0, tiled=True)
     with jax.named_scope("merged"):
         act = act_rows(parts, got, slope, owner_pos, near_z)
         sums = merged_part((act, swap(act, "co")), weights_1, core)
         parts = lax.all_to_all(
             sums.reshape(NX * NCO, NZH * own, half), ("x", "co"), 0, 0, tiled=True
         ).reshape(NX * NCO, NZH, own, half)
-        here = jnp.stack([lax.axis_index("x").astype(jnp.int32), zh])
-        terms = gain_terms(sums, around, here, norm_gain.shape[0]).reshape(-1, 128)
-        terms = lax.psum(terms, "co")
+        terms = gain_terms(sums, around, near_z, norm_gain.shape[0]).reshape(-1, 128)
+        terms = lax.psum(terms, "y")
         parts, terms = lax.optimization_barrier((parts, terms))
         far = sum_halves(parts, far_z)
         got = swap(far, "zh")
     with jax.named_scope("gain"):
-        terms = sum_over(tie(terms, far), ("x", "y"), NX * NY)
+        terms = sum_over(tie(terms, far), ("x", "co"), NX * NCO)
     with jax.named_scope("norm"):
         patch_grad = norm_part(parts, got, patch_in, norm_gain, near_z)
     with jax.named_scope("gain"):

time: 162 us -> 163 us (level)
  the two profiles are of different devices: /device:TPU:8 before, /device:TPU:1 now
where the time goes in v7:
time: 163 us; the launch traced here: 162 us
  starting transfers between devices  77.8 us (48%)
  waiting for transfers between devices  48.7 us (30%)
  blocking collectives  15.2 us (9%)
  Pallas kernels  14.2 us (9%)
  local copies, waits for them, and re-layouts  4.64 us (3%)
    ppermute x8, starting transfers between devices, swap(): return lax.ppermute(value, axis, [(0, 1), (1, 0)])  40.2 us
    all_to_all x2, starting transfers between devices, sum_over(): return jnp.sum(lax.all_to_all(rows, axes, 0, 0, tiled=True), axis=0)  18.6 us
    all_to_all x1, waiting for transfers between devices, local(): parts = lax.all_to_all(sums, 'x', 0, 0, tiled=True)  15.8 us
    psum x1, blocking collectives, local(): terms = lax.psum(terms, 'y')  15.2 us
    all_to_all x2, waiting for transfers between devices, sum_over(): return jnp.sum(lax.all_to_all(rows, axes, 0, 0, tiled=True), axis=0)  13.3 us
    all_to_all x1, waiting for transfers between devices, local(): lax.all_to_all(outgoing, CTX, 0, 0, tiled=True).reshape(group, depth // ctx)  10.2 us
    ppermute x8, waiting for transfers between devices, swap(): return lax.ppermute(value, axis, [(0, 1), (1, 0)])  8.86 us
    all_to_all x1, starting transfers between devices, local(): lax.all_to_all(outgoing, CTX, 0, 0, tiled=True).reshape(group, depth // ctx)  8.08 us
  transfers between devices with their start and end apart: 14, of which 9 were waited for; matrix products, arithmetic and copies ran while one was open for 2% of the time, Pallas kernels for 5%

profile of v7, /device:TPU:1, one launch (start us, length us, event | category | flops | bytes accessed | tf_op | source)
XLA Modules:
  0.0 162.2 jit_solution(12415592687924011148)
XLA Ops:
  0.6 12.4 %collective-permute-start = (bf16[5120,512]{1,0:T(8,128)(2,1)}, bf16[5120,512]{1,0:T(8,128)(2,1)}, u32[]{:S(2)}, u32[]{:S(2)}) collective-permute-start(bf16[5120,512]{1,0:T(8,128)(2,1)} %param.10), channel_id=1, source_target_pairs={{0,1},{1,0},{2,3},{3,2},{4,5},{5,4},{6,7},{7,6},{8,9},{9,8},{10,11... | collective-permute-start | bytes 15728648 | tf_op jit(solution)/shard_map/weights/ppermute | solution.py:41
  13.1 1.7 %copy.18 = bf16[2,16,8,512]{3,2,0,1:T(8,128)(2,1)} copy(bf16[2,16,8,512]{3,2,1,0:T(8,128)(2,1)} %bitcast.26) | data formatting | bytes 524288 | tf_op jit(solution)/shard_map/tokens/reshape | solution.py:314
  14.8 8.1 %all-to-all-start = ((bf16[16,16,512]{2,1,0:T(8,128)(2,1)}), bf16[16,16,512]{2,1,0:T(8,128)(2,1)S(1)}, u32[]{:S(2)}, u32[]{:S(2)}) async-start(bf16[16,16,512]{2,1,0:T(8,128)(2,1)} %bitcast.19), calls=%async_computation | async-start | bytes 524288 | tf_op jit(solution)/shard_map/tokens/all_to_all | solution.py:315
  22.8 2.0 %collective-permute-start.1 = (bf16[16,5120]{1,0:T(8,128)(2,1)}, bf16[16,5120]{1,0:T(8,128)(2,1)S(1)}, u32[]{:S(2)}, u32[]{:S(2)}) collective-permute-start(bf16[16,5120]{1,0:T(8,128)(2,1)} %patch_ref.1), channel_id=1, source_target_pairs={{0,1},{1,0},{2,3},{3,2},{4,5},{5,4},{6,7},{7,6},{8,9},{9,8},{10,11... | collective-permute-start | bytes 491528 | tf_op jit(solution)/shard_map/tokens/ppermute | solution.py:41
  24.9 1.5 collective-permute-done.1.got_ref
  26.3 10.2 %all-to-all-done = bf16[16,16,512]{2,1,0:T(8,128)(2,1)S(1)} async-done(((bf16[16,16,512]{2,1,0:T(8,128)(2,1)}), bf16[16,16,512]{2,1,0:T(8,128)(2,1)S(1)}, u32[]{:S(2)}, u32[]{:S(2)}) %all-to-all-start) | async-done | bytes 262176 | tf_op jit(solution)/shard_map/tokens/all_to_all | solution.py:315
  36.6 2.9 %collective-permute-start.2 = (bf16[256,512]{1,0:T(8,128)(2,1)S(1)}, bf16[256,512]{1,0:T(8,128)(2,1)S(1)}, u32[]{:S(2)}, u32[]{:S(2)}) collective-permute-start(bf16[256,512]{1,0:T(8,128)(2,1)S(1)} %bitcast.24), channel_id=1, source_target_pairs={{0,1},{1,0},{2,3},{3,2},{4,5},{5,4},{6,7},{7,6},{8,9},{9,8},{10,11... | collective-permute-start | bytes 786440 | tf_op jit(solution)/shard_map/tokens/ppermute | solution.py:41
  39.5 0.0 copy-start
  39.5 0.9 copy-done
  40.5 0.2 collective-permute-done.2.got_t
  40.7 0.0 collective-permute-done
  40.7 0.7 copy-done.4
  41.4 5.4 %hidden_part.1 = bf16[4,2,320,256]{3,2,1,0:T(8,128)(2,1)} custom-call(s32[1]{0:T(128)} %bitcast.1.core.place, bf16[4,2,2,320,512]{4,3,2,1,0:T(8,128)(2,1)} %bitcast.23, bf16[4,2,2,320,512]{4,3,2,1,0:T(8,128)(2,1)} %bitcast.3.got_w, bf16[256,512]{1,0:T(8,128)(2,1)} %bitcast.25, bf16[256,512]{1,0:T(8,128)(2,1)} %copy-done.4), custom_call_target="tpu_custom_call" | custom-call | flops 1 | bytes 1 | tf_op jit(solution)/shard_map/hidden/hidden_part/pallas_call | solution.py:65
  46.7 2.3 %collective-permute-start.5 = (bf16[320,5120]{1,0:T(8,128)(2,1)}, bf16[320,5120]{1,0:T(8,128)(2,1)}, u32[]{:S(2)}, u32[]{:S(2)}) collective-permute-start(bf16[320,5120]{1,0:T(8,128)(2,1)} %bitcast.8.own_w), channel_id=1, source_target_pairs={{0,1},{1,0},{2,3},{3,2},{4,5},{5,4},{6,7},{7,6},{8,9},{9,8},{10,11... | collective-permute-start | bytes 9830408 | tf_op jit(solution)/shard_map/hidden/ppermute | solution.py:41
  49.0 3.6 %all-to-all-start.1 = ((bf16[4,2,320,256]{3,2,1,0:T(8,128)(2,1)}), bf16[4,2,320,256]{3,2,1,0:T(8,128)(2,1)S(1)}, u32[]{:S(2)}, u32[]{:S(2)}) async-start(bf16[4,2,320,256]{3,2,1,0:T(8,128)(2,1)} %hidden_part.1), calls=%async_computation.1 | async-start | bytes 2621440 | tf_op jit(solution)/shard_map/hidden/all_to_all | solution.py:331
  52.6 0.0 copy-start.5
  52.6 2.1 %collective-permute-start.6 = (bf16[2,16,2560]{2,1,0:T(8,128)(2,1)S(1)}, bf16[2,16,2560]{2,1,0:T(8,128)(2,1)S(1)}, u32[]{:S(2)}, u32[]{:S(2)}) collective-permute-start(bf16[2,16,2560]{2,1,0:T(8,128)(2,1)S(1)} %pack_patches.1.own_ref), channel_id=1, source_target_pairs={{0,2},{2,0},{1,3},{3,1},{4,6},{6,4},{5,7},{7,5},{8,10},{10,8},{9,1... | collective-permute-start | bytes 491528 | tf_op jit(solution)/shard_map/hidden/ppermute | solution.py:41
  54.6 15.8 %all-to-all-done.1.v_ref = bf16[4,2,320,256]{3,2,1,0:T(8,128)(2,1)S(1)} async-done(((bf16[4,2,320,256]{3,2,1,0:T(8,128)(2,1)}), bf16[4,2,320,256]{3,2,1,0:T(8,128)(2,1)S(1)}, u32[]{:S(2)}, u32[]{:S(2)}) %all-to-all-start.1) | async-done | bytes 1310752 | tf_op jit(solution)/shard_map/hidden/all_to_all | solution.py:331
  70.4 0.1 sum_parts.1
  70.5 1.9 %collective-permute-start.3 = (bf16[320,256]{1,0:T(8,128)(2,1)S(1)}, bf16[320,256]{1,0:T(8,128)(2,1)S(1)}, u32[]{:S(2)}, u32[]{:S(2)}) collective-permute-start(bf16[320,256]{1,0:T(8,128)(2,1)S(1)} %sum_parts.1), channel_id=1, source_target_pairs={{0,2},{2,0},{1,3},{3,1},{4,6},{6,4},{5,7},{7,5},{8,10},{10,8},{9,1... | collective-permute-start | bytes 491528 | tf_op jit(solution)/shard_map/hidden/ppermute | solution.py:41
  72.5 0.1 fusion.3.slope_ref
  72.6 0.0 collective-permute-done.6.beyond_ref
  72.6 1.2 spread_patches.1
  73.8 3.5 %all-to-all-start.3 = ((bf16[4,2,2,16,2560]{4,3,2,1,0:T(8,128)(2,1)}), bf16[4,2,2,16,2560]{4,3,2,1,0:T(8,128)(2,1)S(1)}, u32[]{:S(2)}, u32[]{:S(2)}) async-start(bf16[4,2,2,16,2560]{4,3,2,1,0:T(8,128)(2,1)} %spread_patches.1), calls=%async_computation.3 | async-start | bytes 2621440 | tf_op jit(solution)/shard_map/hidden/all_to_all | solution.py:338
  77.3 0.0 copy-start.2
  77.4 6.1 %collective-permute-done.3.v_ref = bf16[320,256]{1,0:T(8,128)(2,1)S(1)} collective-permute-done((bf16[320,256]{1,0:T(8,128)(2,1)S(1)}, bf16[320,256]{1,0:T(8,128)(2,1)S(1)}, u32[]{:S(2)}, u32[]{:S(2)}) %collective-permute-start.3) | collective-permute-done | bytes 163872 | tf_op jit(solution)/shard_map/hidden/ppermute | solution.py:41
  83.5 0.3 act_rows.1.own_a
  83.9 10.8 %collective-permute-start.4 = (bf16[4,2,2,16,320]{4,3,2,1,0:T(8,128)(2,1)S(1)}, bf16[4,2,2,16,320]{4,3,2,1,0:T(8,128)(2,1)S(1)}, u32[]{:S(2)}, u32[]{:S(2)}) collective-permute-start(bf16[4,2,2,16,320]{4,3,2,1,0:T(8,128)(2,1)S(1)} %act_rows.1.own_a), channel_id=1, source_target_pairs={{0,1},{1,0},{2,3},{3,2},{4,5},{5,4},{6,7},{7,6},{8,9},{9,8},{10,11... | collective-permute-start | bytes 491528 | tf_op jit(solution)/shard_map/merged/ppermute | solution.py:41
  94.7 1.0 collective-permute-done.4.got_a
  95.7 0.0 collective-permute-done.5.got_w
  95.7 4.0 %merged_part.1.grad_ref = bf16[4,2,2,16,2560]{4,3,2,1,0:T(8,128)(2,1)} custom-call(s32[1]{0:T(128)} %bitcast.1.core.place, bf16[4,2,2,16,320]{4,3,2,1,0:T(8,128)(2,1)S(1)} %act_rows.1.own_a, bf16[4,2,2,16,320]{4,3,2,1,0:T(8,128)(2,1)S(1)} %collective-permute-done.4.got_a, bf16[320,5120]{1,0:T(8,128)(2,1)} %bitcast.8.own_w, ...), custom_call_target="tpu_custom_call" | custom-call | flops 1 | bytes 1 | tf_op jit(solution)/shard_map/merged/merged_part/pallas_call | solution.py:166
  99.7 0.0 all-to-all-done.3.patch_ref
  99.7 3.8 %all-to-all-start.2 = ((bf16[8,32,2560]{2,1,0:T(8,128)(2,1)}), bf16[8,32,2560]{2,1,0:T(8,128)(2,1)S(1)}, u32[]{:S(2)}, u32[]{:S(2)}) async-start(bf16[8,32,2560]{2,1,0:T(8,128)(2,1)} %bitcast.9), calls=%async_computation.2 | async-start | bytes 2621440 | tf_op jit(solution)/shard_map/merged/all_to_all | solution.py:342
  103.6 2.2 %gain_terms.1 = f32[1,1280]{1,0:T(1,128)S(1)} custom-call(s32[1]{0:T(128)} %bitcast.place, bf16[4,2,2,16,2560]{4,3,2,1,0:T(8,128)(2,1)} %merged_part.1.grad_ref, bf16[4,2,2,16,2560]{4,3,2,1,0:T(8,128)(2,1)S(1)} %all-to-all-done.3.patch_ref), custom_call_target="tpu_custom_call" | custom-call | flops 20000000000 | bytes 1 | tf_op jit(solution)/shard_map/merged/gain_terms/pallas_call | solution.py:259
  105.8 0.0 copy-start.6
  105.8 0.0 copy-start.1
  105.8 15.2 %psum.7 = f32[10,128]{1,0:T(8,128)S(1)} all-reduce(f32[10,128]{1,0:T(8,128)S(1)} %bitcast.27), channel_id=1, replica_groups=mesh['y'=8,'zl'=6,'x'=4,'zh'=2,'co'=2] {'y'}, use_global_device_ids=true, to_apply=%region_0.0 | all-reduce | flops 1280 | bytes 10240 | tf_op jit(solution)/shard_map/merged/psum | solution.py:346
  121.0 0.5 all-to-all-done.2
  121.5 0.1 sum_halves.1
  121.6 5.8 %collective-permute-start.7 = (bf16[2,16,2560]{2,1,0:T(8,128)(2,1)S(1)}, bf16[2,16,2560]{2,1,0:T(8,128)(2,1)S(1)}, u32[]{:S(2)}, u32[]{:S(2)}) collective-permute-start(bf16[2,16,2560]{2,1,0:T(8,128)(2,1)S(1)} %sum_halves.1), channel_id=1, source_target_pairs={{0,2},{2,0},{1,3},{3,1},{4,6},{6,4},{5,7},{7,5},{8,10},{10,8},{9,1... | collective-permute-start | bytes 491528 | tf_op jit(solution)/shard_map/merged/ppermute | solution.py:41
  127.3 0.6 broadcast_in_dim.4
  128.0 7.5 %all-to-all-start.4 = ((f32[8,10,128]{2,1,0:T(8,128)}), f32[8,10,128]{2,1,0:T(8,128)S(1)}, u32[]{:S(2)}, u32[]{:S(2)}) async-start(f32[8,10,128]{2,1,0:T(8,128)} %broadcast_in_dim.4), calls=%async_computation.4 | async-start | bytes 131072 | tf_op jit(solution)/shard_map/gain/all_to_all | solution.py:301
  135.5 4.8 %all-to-all-done.4 = f32[8,10,128]{2,1,0:T(8,128)S(1)} async-done(((f32[8,10,128]{2,1,0:T(8,128)}), f32[8,10,128]{2,1,0:T(8,128)S(1)}, u32[]{:S(2)}, u32[]{:S(2)}) %all-to-all-start.4) | async-done | bytes 40992 | tf_op jit(solution)/shard_map/gain/all_to_all | solution.py:301
  140.3 0.7 broadcast_in_dim.5
  141.0 11.1 %all-to-all-start.5 = ((f32[12,10,128]{2,1,0:T(8,128)}), f32[12,10,128]{2,1,0:T(8,128)S(1)}, u32[]{:S(2)}, u32[]{:S(2)}) async-start(f32[12,10,128]{2,1,0:T(8,128)} %broadcast_in_dim.5), calls=%async_computation.5 | async-start | bytes 196608 | tf_op jit(solution)/shard_map/gain/all_to_all | solution.py:301
  152.1 0.9 norm_part.1
  153.1 8.5 %all-to-all-done.5 = f32[12,10,128]{2,1,0:T(8,128)S(1)} async-done(((f32[12,10,128]{2,1,0:T(8,128)}), f32[12,10,128]{2,1,0:T(8,128)S(1)}, u32[]{:S(2)}, u32[]{:S(2)}) %all-to-all-start.5) | async-done | bytes 61472 | tf_op jit(solution)/shard_map/gain/all_to_all | solution.py:301
  161.6 0.6 multiply_bitcast_fusion
  (14 shorter events, 0.1 us)
Async XLA Ops:
  0.6 40.0 %collective-permute-start = (bf16[5120,512]{1,0:T(8,128)(2,1)}, bf16[5120,512]{1,0:T(8,128)(2,1)}, u32[]{:S(2)}, u32[]{:S(2)}) collective-permute-start(bf16[5120,512]{1,0:T(8,128)(2,1)} %param.10), channel_id=1, source_target_pairs={{0,1},{1,0},{2,3},{3,2},{4,5},{5,4},{6,7},{7,6},{8,9},{9,8},{10,11... | collective-permute-start | bytes 15728648 | tf_op jit(solution)/shard_map/weights/ppermute | solution.py:41
  14.8 21.8 %all-to-all-start = ((bf16[16,16,512]{2,1,0:T(8,128)(2,1)}), bf16[16,16,512]{2,1,0:T(8,128)(2,1)S(1)}, u32[]{:S(2)}, u32[]{:S(2)}) async-start(bf16[16,16,512]{2,1,0:T(8,128)(2,1)} %bitcast.19), calls=%async_computation | async-start | bytes 524288 | tf_op jit(solution)/shard_map/tokens/all_to_all | solution.py:315
  22.8 3.5 %collective-permute-start.1 = (bf16[16,5120]{1,0:T(8,128)(2,1)}, bf16[16,5120]{1,0:T(8,128)(2,1)S(1)}, u32[]{:S(2)}, u32[]{:S(2)}) collective-permute-start(bf16[16,5120]{1,0:T(8,128)(2,1)} %patch_ref.1), channel_id=1, source_target_pairs={{0,1},{1,0},{2,3},{3,2},{4,5},{5,4},{6,7},{7,6},{8,9},{9,8},{10,11... | collective-permute-start | bytes 491528 | tf_op jit(solution)/shard_map/tokens/ppermute | solution.py:41
  36.6 4.1 %copy-start.3 = (bf16[16,16,512]{2,1,0:T(8,128)(2,1)}, bf16[16,16,512]{2,1,0:T(8,128)(2,1)S(1)}, u32[]{:S(2)}) copy-start(bf16[16,16,512]{2,1,0:T(8,128)(2,1)S(1)} %all-to-all-done) | copy-start | bytes 786436
  36.6 4.1 %collective-permute-start.2 = (bf16[256,512]{1,0:T(8,128)(2,1)S(1)}, bf16[256,512]{1,0:T(8,128)(2,1)S(1)}, u32[]{:S(2)}, u32[]{:S(2)}) collective-permute-start(bf16[256,512]{1,0:T(8,128)(2,1)S(1)} %bitcast.24), channel_id=1, source_target_pairs={{0,1},{1,0},{2,3},{3,2},{4,5},{5,4},{6,7},{7,6},{8,9},{9,8},{10,11... | collective-permute-start | bytes 786440 | tf_op jit(solution)/shard_map/tokens/ppermute | solution.py:41
  39.5 0.9 copy-start
  40.7 0.7 copy-start.4
  46.7 49.0 %collective-permute-start.5 = (bf16[320,5120]{1,0:T(8,128)(2,1)}, bf16[320,5120]{1,0:T(8,128)(2,1)}, u32[]{:S(2)}, u32[]{:S(2)}) collective-permute-start(bf16[320,5120]{1,0:T(8,128)(2,1)} %bitcast.8.own_w), channel_id=1, source_target_pairs={{0,1},{1,0},{2,3},{3,2},{4,5},{5,4},{6,7},{7,6},{8,9},{9,8},{10,11... | collective-permute-start | bytes 9830408 | tf_op jit(solution)/shard_map/hidden/ppermute | solution.py:41
  49.0 21.4 %all-to-all-start.1 = ((bf16[4,2,320,256]{3,2,1,0:T(8,128)(2,1)}), bf16[4,2,320,256]{3,2,1,0:T(8,128)(2,1)S(1)}, u32[]{:S(2)}, u32[]{:S(2)}) async-start(bf16[4,2,320,256]{3,2,1,0:T(8,128)(2,1)} %hidden_part.1), calls=%async_computation.1 | async-start | bytes 2621440 | tf_op jit(solution)/shard_map/hidden/all_to_all | solution.py:331
  52.6 19.9 %copy-start.5 = (bf16[320,256]{1,0:T(8,128)(2,1)S(1)}, bf16[320,256]{1,0:T(8,128)(2,1)}, u32[]{:S(2)}) copy-start(bf16[320,256]{1,0:T(8,128)(2,1)} %param.8) | copy-start | bytes 491524
  52.6 20.0 %collective-permute-start.6 = (bf16[2,16,2560]{2,1,0:T(8,128)(2,1)S(1)}, bf16[2,16,2560]{2,1,0:T(8,128)(2,1)S(1)}, u32[]{:S(2)}, u32[]{:S(2)}) collective-permute-start(bf16[2,16,2560]{2,1,0:T(8,128)(2,1)S(1)} %pack_patches.1.own_ref), channel_id=1, source_target_pairs={{0,2},{2,0},{1,3},{3,1},{4,6},{6,4},{5,7},{7,5},{8,10},{10,8},{9,1... | collective-permute-start | bytes 491528 | tf_op jit(solution)/shard_map/hidden/ppermute | solution.py:41
  70.5 13.0 %collective-permute-start.3 = (bf16[320,256]{1,0:T(8,128)(2,1)S(1)}, bf16[320,256]{1,0:T(8,128)(2,1)S(1)}, u32[]{:S(2)}, u32[]{:S(2)}) collective-permute-start(bf16[320,256]{1,0:T(8,128)(2,1)S(1)} %sum_parts.1), channel_id=1, source_target_pairs={{0,2},{2,0},{1,3},{3,1},{4,6},{6,4},{5,7},{7,5},{8,10},{10,8},{9,1... | collective-permute-start | bytes 491528 | tf_op jit(solution)/shard_map/hidden/ppermute | solution.py:41
  73.8 25.9 %all-to-all-start.3 = ((bf16[4,2,2,16,2560]{4,3,2,1,0:T(8,128)(2,1)}), bf16[4,2,2,16,2560]{4,3,2,1,0:T(8,128)(2,1)S(1)}, u32[]{:S(2)}, u32[]{:S(2)}) async-start(bf16[4,2,2,16,2560]{4,3,2,1,0:T(8,128)(2,1)} %spread_patches.1), calls=%async_computation.3 | async-start | bytes 2621440 | tf_op jit(solution)/shard_map/hidden/all_to_all | solution.py:338
  77.3 6.2 %copy-start.2 = (s32[256]{0:T(256)S(1)}, s32[256]{0:T(256)}, u32[]{:S(2)}) copy-start(s32[256]{0:T(256)} %param.13) | copy-start | bytes 3076
  83.9 11.9 %collective-permute-start.4 = (bf16[4,2,2,16,320]{4,3,2,1,0:T(8,128)(2,1)S(1)}, bf16[4,2,2,16,320]{4,3,2,1,0:T(8,128)(2,1)S(1)}, u32[]{:S(2)}, u32[]{:S(2)}) collective-permute-start(bf16[4,2,2,16,320]{4,3,2,1,0:T(8,128)(2,1)S(1)} %act_rows.1.own_a), channel_id=1, source_target_pairs={{0,1},{1,0},{2,3},{3,2},{4,5},{5,4},{6,7},{7,6},{8,9},{9,8},{10,11... | collective-permute-start | bytes 491528 | tf_op jit(solution)/shard_map/merged/ppermute | solution.py:41
  99.7 21.8 %all-to-all-start.2 = ((bf16[8,32,2560]{2,1,0:T(8,128)(2,1)}), bf16[8,32,2560]{2,1,0:T(8,128)(2,1)S(1)}, u32[]{:S(2)}, u32[]{:S(2)}) async-start(bf16[8,32,2560]{2,1,0:T(8,128)(2,1)} %bitcast.9), calls=%async_computation.2 | async-start | bytes 2621440 | tf_op jit(solution)/shard_map/merged/all_to_all | solution.py:342
  105.8 29.7 %copy-start.6 = (f32[1280]{0:T(1024)S(1)}, f32[1280]{0:T(1024)}, u32[]{:S(2)}) copy-start(f32[1280]{0:T(1024)} %param.12) | copy-start | bytes 15364
  105.8 46.3 %copy-start.1 = (bf16[16,5120]{1,0:T(8,128)(2,1)S(1)}, bf16[16,5120]{1,0:T(8,128)(2,1)}, u32[]{:S(2)}) copy-start(bf16[16,5120]{1,0:T(8,128)(2,1)} %patch_ref.1) | copy-start | bytes 491524
  121.6 30.6 %collective-permute-start.7 = (bf16[2,16,2560]{2,1,0:T(8,128)(2,1)S(1)}, bf16[2,16,2560]{2,1,0:T(8,128)(2,1)S(1)}, u32[]{:S(2)}, u32[]{:S(2)}) collective-permute-start(bf16[2,16,2560]{2,1,0:T(8,128)(2,1)S(1)} %sum_halves.1), channel_id=1, source_target_pairs={{0,2},{2,0},{1,3},{3,1},{4,6},{6,4},{5,7},{7,5},{8,10},{10,8},{9,1... | collective-permute-start | bytes 491528 | tf_op jit(solution)/shard_map/merged/ppermute | solution.py:41
  128.0 12.3 %all-to-all-start.4 = ((f32[8,10,128]{2,1,0:T(8,128)}), f32[8,10,128]{2,1,0:T(8,128)S(1)}, u32[]{:S(2)}, u32[]{:S(2)}) async-start(f32[8,10,128]{2,1,0:T(8,128)} %broadcast_in_dim.4), calls=%async_computation.4 | async-start | bytes 131072 | tf_op jit(solution)/shard_map/gain/all_to_all | solution.py:301
  141.0 20.6 %all-to-all-start.5 = ((f32[12,10,128]{2,1,0:T(8,128)}), f32[12,10,128]{2,1,0:T(8,128)S(1)}, u32[]{:S(2)}, u32[]{:S(2)}) async-start(f32[12,10,128]{2,1,0:T(8,128)} %broadcast_in_dim.5), calls=%async_computation.5 | async-start | bytes 196608 | tf_op jit(solution)/shard_map/gain/all_to_all | solution.py:301

commit v8 on v7

--- a/solution.py
+++ b/solution.py
@@ -71,7 +71,7 @@
             out_specs=pl.BlockSpec((1, NZH, units, count), lambda i, s: (i, 0, 0, 0)),
         ),
         out_shape=jax.ShapeDtypeStruct((NX, NZH, units, count), BF16),
-        compiler_params=params(60),
+        compiler_params=params(52),
         cost_estimate=cost(),
         name="hidden_part",
     )(core, *weights, *tokens)
@@ -330,7 +330,7 @@
         sums = hidden_part(weights_2, tokens, core)
         parts = lax.all_to_all(sums, "x", 0, 0, tiled=True)
         ready = tie(patches, sums)
-        weights_1 = (w_fc1_t, swap(tie(w_fc1_t, ready), "co"))
+        weights_1 = (w_fc1_t, swap(w_fc1_t, "co"))
         beyond = swap(ready, "zh")
         far = sum_parts(parts, far_z)
         got = widen(swap(far, "zh"))
@@ -348,11 +348,11 @@
         far = sum_halves(parts, far_z)
         got = swap(far, "zh")
     with jax.named_scope("gain"):
-        terms = sum_over(tie(terms, far), ("x", "co"), NX * NCO)
+        terms = sum_over(tie(terms, far), ("zl", "zh"), NZL * NZH)
     with jax.named_scope("norm"):
         patch_grad = norm_part(parts, got, patch_in, norm_gain, near_z)
     with jax.named_scope("gain"):
-        terms = sum_over(terms, ("zl", "zh"), NZL * NZH)
+        terms = sum_over(terms, ("x", "co"), NX * NCO)
         gain_grad = terms.reshape(-1) / (NY * NZL * ctx)
     return (patch_grad, gain_grad)
 

time: 163 us -> 159 us (0.975)
  waiting for transfers between devices: 48.7 us -> 37.8 us
  starting transfers between devices: 77.8 us -> 86.4 us
  local copies, waits for them, and re-layouts: 4.64 us -> 3 us
    all_to_all x2, waiting for transfers between devices: 13.3 us -> 3.91 us  [sum_over(): return jnp.sum(lax.all_to_all(rows, axes, 0, 0, tiled=True), axis=0)]
    all_to_all x2, starting transfers between devices: 18.6 us -> 26.1 us  [sum_over(): return jnp.sum(lax.all_to_all(rows, axes, 0, 0, tiled=True), axis=0)]
    all_to_all x1, starting transfers between devices: 3.84 us -> 7.15 us  [local(): lax.all_to_all(sums.reshape(NX * NCO, NZH * own, half), ('x', 'co'), 0, 0...]
    ppermute x8, starting transfers between devices: 40.2 us -> 37.9 us  [swap(): return lax.ppermute(value, axis, [(0, 1), (1, 0)])]
  transfers between devices with their start and end apart: 14 -> 14, of which waited for: 9 -> 7; matrix products, arithmetic and copies ran while one was open for 2% -> 2% of each run, Pallas kernels for 5% -> 9%
where the time goes in v8:
time: 159 us; the launch traced here: 158 us
  starting transfers between devices  86.4 us (54%)
  waiting for transfers between devices  37.8 us (24%)
  blocking collectives  15.1 us (9%)
  Pallas kernels  13.9 us (9%)
  local copies, waits for them, and re-layouts  3 us (2%)
    ppermute x8, starting transfers between devices, swap(): return lax.ppermute(value, axis, [(0, 1), (1, 0)])  37.9 us
    all_to_all x2, starting transfers between devices, sum_over(): return jnp.sum(lax.all_to_all(rows, axes, 0, 0, tiled=True), axis=0)  26.1 us
    all_to_all x1, waiting for transfers between devices, local(): parts = lax.all_to_all(sums, 'x', 0, 0, tiled=True)  15.3 us
    psum x1, blocking collectives, local(): terms = lax.psum(terms, 'y')  15.1 us
    all_to_all x1, waiting for transfers between devices, local(): lax.all_to_all(outgoing, CTX, 0, 0, tiled=True).reshape(group, depth // ctx)  10.2 us
    all_to_all x1, starting transfers between devices, local(): lax.all_to_all(outgoing, CTX, 0, 0, tiled=True).reshape(group, depth // ctx)  8.08 us
    ppermute x8, waiting for transfers between devices, swap(): return lax.ppermute(value, axis, [(0, 1), (1, 0)])  7.8 us
    all_to_all x1, starting transfers between devices, local(): lax.all_to_all(sums.reshape(NX * NCO, NZH * own, half), ('x', 'co'), 0, 0...  7.15 us
  transfers between devices with their start and end apart: 14, of which 7 were waited for; matrix products, arithmetic and copies ran while one was open for 2% of the time, Pallas kernels for 9%

profile of v8, /device:TPU:1, one launch (start us, length us, event | category | flops | bytes accessed | tf_op | source)
XLA Modules:
  0.0 157.9 jit_solution(10534862399896740744)
XLA Ops:
  0.6 12.4 %collective-permute-start = (bf16[5120,512]{1,0:T(8,128)(2,1)}, bf16[5120,512]{1,0:T(8,128)(2,1)}, u32[]{:S(2)}, u32[]{:S(2)}) collective-permute-start(bf16[5120,512]{1,0:T(8,128)(2,1)} %param.10), channel_id=1, source_target_pairs={{0,1},{1,0},{2,3},{3,2},{4,5},{5,4},{6,7},{7,6},{8,9},{9,8},{10,11... | collective-permute-start | bytes 15728648 | tf_op jit(solution)/shard_map/weights/ppermute | solution.py:41
  13.1 1.7 %copy.18 = bf16[2,16,8,512]{3,2,0,1:T(8,128)(2,1)} copy(bf16[2,16,8,512]{3,2,1,0:T(8,128)(2,1)} %bitcast.28) | data formatting | bytes 524288 | tf_op jit(solution)/shard_map/tokens/reshape | solution.py:314
  14.8 8.1 %all-to-all-start = ((bf16[16,16,512]{2,1,0:T(8,128)(2,1)}), bf16[16,16,512]{2,1,0:T(8,128)(2,1)S(1)}, u32[]{:S(2)}, u32[]{:S(2)}) async-start(bf16[16,16,512]{2,1,0:T(8,128)(2,1)} %bitcast.19), calls=%async_computation | async-start | bytes 524288 | tf_op jit(solution)/shard_map/tokens/all_to_all | solution.py:315
  22.8 2.0 %collective-permute-start.1 = (bf16[16,5120]{1,0:T(8,128)(2,1)}, bf16[16,5120]{1,0:T(8,128)(2,1)S(1)}, u32[]{:S(2)}, u32[]{:S(2)}) collective-permute-start(bf16[16,5120]{1,0:T(8,128)(2,1)} %patch_ref.1), channel_id=1, source_target_pairs={{0,1},{1,0},{2,3},{3,2},{4,5},{5,4},{6,7},{7,6},{8,9},{9,8},{10,11... | collective-permute-start | bytes 491528 | tf_op jit(solution)/shard_map/tokens/ppermute | solution.py:41
  24.9 1.5 collective-permute-done.1.got_ref
  26.3 10.2 %all-to-all-done = bf16[16,16,512]{2,1,0:T(8,128)(2,1)S(1)} async-done(((bf16[16,16,512]{2,1,0:T(8,128)(2,1)}), bf16[16,16,512]{2,1,0:T(8,128)(2,1)S(1)}, u32[]{:S(2)}, u32[]{:S(2)}) %all-to-all-start) | async-done | bytes 262176 | tf_op jit(solution)/shard_map/tokens/all_to_all | solution.py:315
  36.6 2.9 %collective-permute-start.2 = (bf16[256,512]{1,0:T(8,128)(2,1)S(1)}, bf16[256,512]{1,0:T(8,128)(2,1)S(1)}, u32[]{:S(2)}, u32[]{:S(2)}) collective-permute-start(bf16[256,512]{1,0:T(8,128)(2,1)S(1)} %bitcast.24), channel_id=1, source_target_pairs={{0,1},{1,0},{2,3},{3,2},{4,5},{5,4},{6,7},{7,6},{8,9},{9,8},{10,11... | collective-permute-start | bytes 786440 | tf_op jit(solution)/shard_map/tokens/ppermute | solution.py:41
  39.5 1.9 %collective-permute-start.5 = (bf16[320,5120]{1,0:T(8,128)(2,1)}, bf16[320,5120]{1,0:T(8,128)(2,1)}, u32[]{:S(2)}, u32[]{:S(2)}) collective-permute-start(bf16[320,5120]{1,0:T(8,128)(2,1)} %bitcast.22), channel_id=1, source_target_pairs={{0,1},{1,0},{2,3},{3,2},{4,5},{5,4},{6,7},{7,6},{8,9},{9,8},{10,11... | collective-permute-start | bytes 9830408 | tf_op jit(solution)/shard_map/hidden/ppermute | solution.py:41
  41.4 0.0 collective-permute-done.2.got_t
  41.5 0.0 collective-permute-done
  41.5 5.2 %hidden_part.1 = bf16[4,2,320,256]{3,2,1,0:T(8,128)(2,1)} custom-call(s32[1]{0:T(128)} %bitcast.1.core.place, bf16[4,2,2,320,512]{4,3,2,1,0:T(8,128)(2,1)} %bitcast.27, bf16[4,2,2,320,512]{4,3,2,1,0:T(8,128)(2,1)} %bitcast.3.got_w, bf16[256,512]{1,0:T(8,128)(2,1)S(1)} %bitcast.25, bf16[256,512]{1,0:T(8,128)(2,1)S(1)} %collective-permute-done.2.got_t), custom_call_target="tpu_custom_call" | custom-call | flops 1 | bytes 1 | tf_op jit(solution)/shard_map/hidden/hidden_part/pallas_call | solution.py:65
  46.7 3.7 %all-to-all-start.1 = ((bf16[4,2,320,256]{3,2,1,0:T(8,128)(2,1)}), bf16[4,2,320,256]{3,2,1,0:T(8,128)(2,1)S(1)}, u32[]{:S(2)}, u32[]{:S(2)}) async-start(bf16[4,2,320,256]{3,2,1,0:T(8,128)(2,1)} %hidden_part.1), calls=%async_computation.1 | async-start | bytes 2621440 | tf_op jit(solution)/shard_map/hidden/all_to_all | solution.py:331
  50.4 0.0 copy-start.3
  50.4 0.0 copy-done.1
  50.4 2.1 %collective-permute-start.6 = (bf16[2,16,2560]{2,1,0:T(8,128)(2,1)S(1)}, bf16[2,16,2560]{2,1,0:T(8,128)(2,1)S(1)}, u32[]{:S(2)}, u32[]{:S(2)}) collective-permute-start(bf16[2,16,2560]{2,1,0:T(8,128)(2,1)S(1)} %pack_patches.1.own_ref), channel_id=1, source_target_pairs={{0,2},{2,0},{1,3},{3,1},{4,6},{6,4},{5,7},{7,5},{8,10},{10,8},{9,1... | collective-permute-start | bytes 491528 | tf_op jit(solution)/shard_map/hidden/ppermute | solution.py:41
  52.6 15.3 %all-to-all-done.1.v_ref = bf16[4,2,320,256]{3,2,1,0:T(8,128)(2,1)S(1)} async-done(((bf16[4,2,320,256]{3,2,1,0:T(8,128)(2,1)}), bf16[4,2,320,256]{3,2,1,0:T(8,128)(2,1)S(1)}, u32[]{:S(2)}, u32[]{:S(2)}) %all-to-all-start.1) | async-done | bytes 1310752 | tf_op jit(solution)/shard_map/hidden/all_to_all | solution.py:331
  67.9 0.1 sum_parts.1
  67.9 2.2 %collective-permute-start.3 = (bf16[320,256]{1,0:T(8,128)(2,1)S(1)}, bf16[320,256]{1,0:T(8,128)(2,1)S(1)}, u32[]{:S(2)}, u32[]{:S(2)}) collective-permute-start(bf16[320,256]{1,0:T(8,128)(2,1)S(1)} %sum_parts.1), channel_id=1, source_target_pairs={{0,2},{2,0},{1,3},{3,1},{4,6},{6,4},{5,7},{7,5},{8,10},{10,8},{9,1... | collective-permute-start | bytes 491528 | tf_op jit(solution)/shard_map/hidden/ppermute | solution.py:41
  70.2 0.0 copy-done.3
  70.2 0.1 fusion.3.slope_ref
  70.3 0.0 collective-permute-done.6.beyond_ref
  70.3 1.1 spread_patches.1
  71.5 3.5 %all-to-all-start.3 = ((bf16[4,2,2,16,2560]{4,3,2,1,0:T(8,128)(2,1)}), bf16[4,2,2,16,2560]{4,3,2,1,0:T(8,128)(2,1)S(1)}, u32[]{:S(2)}, u32[]{:S(2)}) async-start(bf16[4,2,2,16,2560]{4,3,2,1,0:T(8,128)(2,1)} %spread_patches.1), calls=%async_computation.3 | async-start | bytes 2621440 | tf_op jit(solution)/shard_map/hidden/all_to_all | solution.py:338
  75.0 0.0 copy-start.2
  75.0 5.3 %collective-permute-done.3.v_ref = bf16[320,256]{1,0:T(8,128)(2,1)S(1)} collective-permute-done((bf16[320,256]{1,0:T(8,128)(2,1)S(1)}, bf16[320,256]{1,0:T(8,128)(2,1)S(1)}, u32[]{:S(2)}, u32[]{:S(2)}) %collective-permute-start.3) | collective-permute-done | bytes 163872 | tf_op jit(solution)/shard_map/hidden/ppermute | solution.py:41
  80.4 0.3 act_rows.1.own_a
  80.7 4.6 %collective-permute-start.4 = (bf16[4,2,2,16,320]{4,3,2,1,0:T(8,128)(2,1)S(1)}, bf16[4,2,2,16,320]{4,3,2,1,0:T(8,128)(2,1)S(1)}, u32[]{:S(2)}, u32[]{:S(2)}) collective-permute-start(bf16[4,2,2,16,320]{4,3,2,1,0:T(8,128)(2,1)S(1)} %act_rows.1.own_a), channel_id=1, source_target_pairs={{0,1},{1,0},{2,3},{3,2},{4,5},{5,4},{6,7},{7,6},{8,9},{9,8},{10,11... | collective-permute-start | bytes 491528 | tf_op jit(solution)/shard_map/merged/ppermute | solution.py:41
  85.3 0.0 collective-permute-done.5.got_w
  85.3 1.0 collective-permute-done.4.got_a
  86.4 3.8 %merged_part.1.grad_ref = bf16[4,2,2,16,2560]{4,3,2,1,0:T(8,128)(2,1)} custom-call(s32[1]{0:T(128)} %bitcast.1.core.place, bf16[4,2,2,16,320]{4,3,2,1,0:T(8,128)(2,1)S(1)} %act_rows.1.own_a, bf16[4,2,2,16,320]{4,3,2,1,0:T(8,128)(2,1)S(1)} %collective-permute-done.4.got_a, bf16[320,5120]{1,0:T(8,128)(2,1)S(1)} %bitcast.23, ...), custom_call_target="tpu_custom_call" | custom-call | flops 1 | bytes 1 | tf_op jit(solution)/shard_map/merged/merged_part/pallas_call | solution.py:166
  90.2 0.0 all-to-all-done.3.patch_ref
  90.2 7.2 %all-to-all-start.2 = ((bf16[8,32,2560]{2,1,0:T(8,128)(2,1)}), bf16[8,32,2560]{2,1,0:T(8,128)(2,1)S(1)}, u32[]{:S(2)}, u32[]{:S(2)}) async-start(bf16[8,32,2560]{2,1,0:T(8,128)(2,1)} %bitcast.9), calls=%async_computation.2 | async-start | bytes 2621440 | tf_op jit(solution)/shard_map/merged/all_to_all | solution.py:342
  97.3 2.2 %gain_terms.1 = f32[1,1280]{1,0:T(1,128)S(1)} custom-call(s32[1]{0:T(128)} %bitcast.place, bf16[4,2,2,16,2560]{4,3,2,1,0:T(8,128)(2,1)} %merged_part.1.grad_ref, bf16[4,2,2,16,2560]{4,3,2,1,0:T(8,128)(2,1)S(1)} %all-to-all-done.3.patch_ref), custom_call_target="tpu_custom_call" | custom-call | flops 20000000000 | bytes 1 | tf_op jit(solution)/shard_map/merged/gain_terms/pallas_call | solution.py:259
  99.5 0.0 copy-start.4
  99.6 15.1 %psum.7 = f32[10,128]{1,0:T(8,128)S(1)} all-reduce(f32[10,128]{1,0:T(8,128)S(1)} %bitcast.29), channel_id=1, replica_groups=mesh['y'=8,'zl'=6,'x'=4,'zh'=2,'co'=2] {'y'}, use_global_device_ids=true, to_apply=%region_0.0 | all-reduce | flops 1280 | bytes 10240 | tf_op jit(solution)/shard_map/merged/psum | solution.py:346
  114.7 0.6 all-to-all-done.2
  115.2 0.1 sum_halves.1
  115.3 0.6 broadcast_in_dim.4
  116.0 14.7 %all-to-all-start.4 = ((f32[12,10,128]{2,1,0:T(8,128)}), f32[12,10,128]{2,1,0:T(8,128)S(1)}, u32[]{:S(2)}, u32[]{:S(2)}) async-start(f32[12,10,128]{2,1,0:T(8,128)} %broadcast_in_dim.4), calls=%async_computation.4 | async-start | bytes 196608 | tf_op jit(solution)/shard_map/gain/all_to_all | solution.py:301
  130.7 9.6 %collective-permute-start.7 = (bf16[2,16,2560]{2,1,0:T(8,128)(2,1)S(1)}, bf16[2,16,2560]{2,1,0:T(8,128)(2,1)S(1)}, u32[]{:S(2)}, u32[]{:S(2)}) collective-permute-start(bf16[2,16,2560]{2,1,0:T(8,128)(2,1)S(1)} %sum_halves.1), channel_id=1, source_target_pairs={{0,2},{2,0},{1,3},{3,1},{4,6},{6,4},{5,7},{7,5},{8,10},{10,8},{9,1... | collective-permute-start | bytes 491528 | tf_op jit(solution)/shard_map/merged/ppermute | solution.py:41
  140.3 0.0 copy-done.4
  140.4 0.0 all-to-all-done.4
  140.4 0.6 broadcast_in_dim.5
  141.0 11.4 %all-to-all-start.5 = ((f32[8,10,128]{2,1,0:T(8,128)}), f32[8,10,128]{2,1,0:T(8,128)S(1)}, u32[]{:S(2)}, u32[]{:S(2)}) async-start(f32[8,10,128]{2,1,0:T(8,128)} %broadcast_in_dim.5), calls=%async_computation.5 | async-start | bytes 131072 | tf_op jit(solution)/shard_map/gain/all_to_all | solution.py:301
  152.4 0.0 collective-permute-done.7.got_ref
  152.4 0.9 norm_part.1
  153.3 3.9 %all-to-all-done.5 = f32[8,10,128]{2,1,0:T(8,128)S(1)} async-done(((f32[8,10,128]{2,1,0:T(8,128)}), f32[8,10,128]{2,1,0:T(8,128)S(1)}, u32[]{:S(2)}, u32[]{:S(2)}) %all-to-all-start.5) | async-done | bytes 40992 | tf_op jit(solution)/shard_map/gain/all_to_all | solution.py:301
  157.3 0.6 multiply_bitcast_fusion
  (10 shorter events, 0.1 us)
Async XLA Ops:
  0.6 40.8 %collective-permute-start = (bf16[5120,512]{1,0:T(8,128)(2,1)}, bf16[5120,512]{1,0:T(8,128)(2,1)}, u32[]{:S(2)}, u32[]{:S(2)}) collective-permute-start(bf16[5120,512]{1,0:T(8,128)(2,1)} %param.10), channel_id=1, source_target_pairs={{0,1},{1,0},{2,3},{3,2},{4,5},{5,4},{6,7},{7,6},{8,9},{9,8},{10,11... | collective-permute-start | bytes 15728648 | tf_op jit(solution)/shard_map/weights/ppermute | solution.py:41
  14.8 21.8 %all-to-all-start = ((bf16[16,16,512]{2,1,0:T(8,128)(2,1)}), bf16[16,16,512]{2,1,0:T(8,128)(2,1)S(1)}, u32[]{:S(2)}, u32[]{:S(2)}) async-start(bf16[16,16,512]{2,1,0:T(8,128)(2,1)} %bitcast.19), calls=%async_computation | async-start | bytes 524288 | tf_op jit(solution)/shard_map/tokens/all_to_all | solution.py:315
  22.8 3.5 %collective-permute-start.1 = (bf16[16,5120]{1,0:T(8,128)(2,1)}, bf16[16,5120]{1,0:T(8,128)(2,1)S(1)}, u32[]{:S(2)}, u32[]{:S(2)}) collective-permute-start(bf16[16,5120]{1,0:T(8,128)(2,1)} %patch_ref.1), channel_id=1, source_target_pairs={{0,1},{1,0},{2,3},{3,2},{4,5},{5,4},{6,7},{7,6},{8,9},{9,8},{10,11... | collective-permute-start | bytes 491528 | tf_op jit(solution)/shard_map/tokens/ppermute | solution.py:41
  36.6 4.9 %collective-permute-start.2 = (bf16[256,512]{1,0:T(8,128)(2,1)S(1)}, bf16[256,512]{1,0:T(8,128)(2,1)S(1)}, u32[]{:S(2)}, u32[]{:S(2)}) collective-permute-start(bf16[256,512]{1,0:T(8,128)(2,1)S(1)} %bitcast.24), channel_id=1, source_target_pairs={{0,1},{1,0},{2,3},{3,2},{4,5},{5,4},{6,7},{7,6},{8,9},{9,8},{10,11... | collective-permute-start | bytes 786440 | tf_op jit(solution)/shard_map/tokens/ppermute | solution.py:41
  39.5 45.8 %collective-permute-start.5 = (bf16[320,5120]{1,0:T(8,128)(2,1)}, bf16[320,5120]{1,0:T(8,128)(2,1)}, u32[]{:S(2)}, u32[]{:S(2)}) collective-permute-start(bf16[320,5120]{1,0:T(8,128)(2,1)} %bitcast.22), channel_id=1, source_target_pairs={{0,1},{1,0},{2,3},{3,2},{4,5},{5,4},{6,7},{7,6},{8,9},{9,8},{10,11... | collective-permute-start | bytes 9830408 | tf_op jit(solution)/shard_map/hidden/ppermute | solution.py:41
  46.7 3.7 %copy-start.1 = (bf16[16,5120]{1,0:T(8,128)(2,1)S(1)}, bf16[16,5120]{1,0:T(8,128)(2,1)}, u32[]{:S(2)}) copy-start(bf16[16,5120]{1,0:T(8,128)(2,1)} %patch_ref.1) | copy-start | bytes 491524
  46.7 21.2 %all-to-all-start.1 = ((bf16[4,2,320,256]{3,2,1,0:T(8,128)(2,1)}), bf16[4,2,320,256]{3,2,1,0:T(8,128)(2,1)S(1)}, u32[]{:S(2)}, u32[]{:S(2)}) async-start(bf16[4,2,320,256]{3,2,1,0:T(8,128)(2,1)} %hidden_part.1), calls=%async_computation.1 | async-start | bytes 2621440 | tf_op jit(solution)/shard_map/hidden/all_to_all | solution.py:331
  50.4 19.8 %copy-start.3 = (bf16[320,256]{1,0:T(8,128)(2,1)S(1)}, bf16[320,256]{1,0:T(8,128)(2,1)}, u32[]{:S(2)}) copy-start(bf16[320,256]{1,0:T(8,128)(2,1)} %param.8) | copy-start | bytes 491524
  50.4 19.9 %collective-permute-start.6 = (bf16[2,16,2560]{2,1,0:T(8,128)(2,1)S(1)}, bf16[2,16,2560]{2,1,0:T(8,128)(2,1)S(1)}, u32[]{:S(2)}, u32[]{:S(2)}) collective-permute-start(bf16[2,16,2560]{2,1,0:T(8,128)(2,1)S(1)} %pack_patches.1.own_ref), channel_id=1, source_target_pairs={{0,2},{2,0},{1,3},{3,1},{4,6},{6,4},{5,7},{7,5},{8,10},{10,8},{9,1... | collective-permute-start | bytes 491528 | tf_op jit(solution)/shard_map/hidden/ppermute | solution.py:41
  67.9 12.4 %collective-permute-start.3 = (bf16[320,256]{1,0:T(8,128)(2,1)S(1)}, bf16[320,256]{1,0:T(8,128)(2,1)S(1)}, u32[]{:S(2)}, u32[]{:S(2)}) collective-permute-start(bf16[320,256]{1,0:T(8,128)(2,1)S(1)} %sum_parts.1), channel_id=1, source_target_pairs={{0,2},{2,0},{1,3},{3,1},{4,6},{6,4},{5,7},{7,5},{8,10},{10,8},{9,1... | collective-permute-start | bytes 491528 | tf_op jit(solution)/shard_map/hidden/ppermute | solution.py:41
  71.5 18.7 %all-to-all-start.3 = ((bf16[4,2,2,16,2560]{4,3,2,1,0:T(8,128)(2,1)}), bf16[4,2,2,16,2560]{4,3,2,1,0:T(8,128)(2,1)S(1)}, u32[]{:S(2)}, u32[]{:S(2)}) async-start(bf16[4,2,2,16,2560]{4,3,2,1,0:T(8,128)(2,1)} %spread_patches.1), calls=%async_computation.3 | async-start | bytes 2621440 | tf_op jit(solution)/shard_map/hidden/all_to_all | solution.py:338
  75.0 5.3 %copy-start.2 = (s32[256]{0:T(256)S(1)}, s32[256]{0:T(256)}, u32[]{:S(2)}) copy-start(s32[256]{0:T(256)} %param.13) | copy-start | bytes 3076
  80.3 6.1 %copy-start = (bf16[5120,320]{0,1:T(8,128)(2,1)S(1)}, bf16[5120,320]{0,1:T(8,128)(2,1)}, u32[]{:S(2)}) copy-start(bf16[5120,320]{0,1:T(8,128)(2,1)} %param.9) | copy-start | bytes 9830404
  80.7 5.7 %collective-permute-start.4 = (bf16[4,2,2,16,320]{4,3,2,1,0:T(8,128)(2,1)S(1)}, bf16[4,2,2,16,320]{4,3,2,1,0:T(8,128)(2,1)S(1)}, u32[]{:S(2)}, u32[]{:S(2)}) collective-permute-start(bf16[4,2,2,16,320]{4,3,2,1,0:T(8,128)(2,1)S(1)} %act_rows.1.own_a), channel_id=1, source_target_pairs={{0,1},{1,0},{2,3},{3,2},{4,5},{5,4},{6,7},{7,6},{8,9},{9,8},{10,11... | collective-permute-start | bytes 491528 | tf_op jit(solution)/shard_map/merged/ppermute | solution.py:41
  90.2 25.1 %all-to-all-start.2 = ((bf16[8,32,2560]{2,1,0:T(8,128)(2,1)}), bf16[8,32,2560]{2,1,0:T(8,128)(2,1)S(1)}, u32[]{:S(2)}, u32[]{:S(2)}) async-start(bf16[8,32,2560]{2,1,0:T(8,128)(2,1)} %bitcast.9), calls=%async_computation.2 | async-start | bytes 2621440 | tf_op jit(solution)/shard_map/merged/all_to_all | solution.py:342
  99.5 40.8 %copy-start.4 = (f32[1280]{0:T(1024)S(1)}, f32[1280]{0:T(1024)}, u32[]{:S(2)}) copy-start(f32[1280]{0:T(1024)} %param.12) | copy-start | bytes 15364
  116.0 24.4 %all-to-all-start.4 = ((f32[12,10,128]{2,1,0:T(8,128)}), f32[12,10,128]{2,1,0:T(8,128)S(1)}, u32[]{:S(2)}, u32[]{:S(2)}) async-start(f32[12,10,128]{2,1,0:T(8,128)} %broadcast_in_dim.4), calls=%async_computation.4 | async-start | bytes 196608 | tf_op jit(solution)/shard_map/gain/all_to_all | solution.py:301
  130.7 21.7 %collective-permute-start.7 = (bf16[2,16,2560]{2,1,0:T(8,128)(2,1)S(1)}, bf16[2,16,2560]{2,1,0:T(8,128)(2,1)S(1)}, u32[]{:S(2)}, u32[]{:S(2)}) collective-permute-start(bf16[2,16,2560]{2,1,0:T(8,128)(2,1)S(1)} %sum_halves.1), channel_id=1, source_target_pairs={{0,2},{2,0},{1,3},{3,1},{4,6},{6,4},{5,7},{7,5},{8,10},{10,8},{9,1... | collective-permute-start | bytes 491528 | tf_op jit(solution)/shard_map/merged/ppermute | solution.py:41
  141.0 16.2 %all-to-all-start.5 = ((f32[8,10,128]{2,1,0:T(8,128)}), f32[8,10,128]{2,1,0:T(8,128)S(1)}, u32[]{:S(2)}, u32[]{:S(2)}) async-start(f32[8,10,128]{2,1,0:T(8,128)} %broadcast_in_dim.5), calls=%async_computation.5 | async-start | bytes 131072 | tf_op jit(solution)/shard_map/gain/all_to_all | solution.py:301

commit v9 on v8

--- a/solution.py
+++ b/solution.py
@@ -219,20 +219,19 @@
     )(core, own, got)
 
 
-def spread_kernel(own_ref, beyond_ref, out_ref):
+def spread_kernel(own_ref, out_ref):
     for x in range(NX):
-        out_ref[x, 0] = own_ref[...]
-        out_ref[x, 1] = beyond_ref[...]
-
-
-def spread_patches(own, beyond):
+        out_ref[x] = own_ref[...]
+
+
+def spread_patches(own):
     return pl.pallas_call(
         spread_kernel,
-        out_shape=jax.ShapeDtypeStruct((NX, NZH) + own.shape, BF16),
+        out_shape=jax.ShapeDtypeStruct((NX,) + own.shape, BF16),
         compiler_params=params(),
         cost_estimate=cost(),
         name="spread_patches",
-    )(own, beyond)
+    )(own)
 
 
 def norm_of(patch):
@@ -240,31 +239,33 @@
     return patch * inv_rms, inv_rms
 
 
-def gain_kernel(place, grad_ref, patch_ref, out_ref):
+def gain_kernel(place, grad_ref, beyond_ref, *refs):
+    out_ref = refs[-1]
     width = out_ref.shape[1]
     terms = jnp.zeros((1, width), F32)
-    for x in range(NX):
-        for k in range(NZH):
-            z = place[0] if k == 0 else 1 - place[0]
+    for k in range(NX):
+        here = (lax.rem(place[1] + k, NX), place[0], refs[k])
+        there = (k, 1 - place[0], beyond_ref.at[k])
+        for x, z, patch_ref in (here, there):
             for c in range(NCO):
                 for p in range(grad_ref.shape[4] // width):
                     cols = pl.ds(p * width, width)
-                    normed, _ = norm_of(patch_ref[x, k, c, :, cols].astype(F32))
+                    normed, _ = norm_of(patch_ref[c, :, cols].astype(F32))
                     grad = grad_ref[x, c, z, :, cols].astype(F32)
                     terms += jnp.sum(grad * normed, axis=0, keepdims=True)
     out_ref[...] = terms
 
 
-def gain_terms(grads, patches, place, width):
+def gain_terms(grads, beyond, around, place, width):
     return pl.pallas_call(
         gain_kernel,
-        in_specs=[IN_SMEM] + [IN_VMEM] * 2,
+        in_specs=[IN_SMEM] + [IN_VMEM] * (2 + NX),
         out_specs=IN_VMEM,
         out_shape=jax.ShapeDtypeStruct((1, width), F32),
         compiler_params=params(),
         cost_estimate=cost(LONG),
         name="gain_terms",
-    )(place, grads, patches)
+    )(place, grads, beyond, *around)
 
 
 def norm_kernel(place, v_ref, got_ref, patch_ref, gain_ref, out_ref):
@@ -314,14 +315,15 @@
         outgoing = grad_tokens.reshape(own, ctx, depth // ctx).transpose(1, 0, 2)
         tokens = lax.all_to_all(outgoing, CTX, 0, 0, tiled=True).reshape(group, depth // ctx)
         beside = swap(patch_in, "co")
-        tokens, beside = lax.optimization_barrier((tokens, beside))
+        patches = pack_patches(patch_in, beside, core)
+        around = [
+            lax.ppermute(patches, "x", [(i, (i - d) % NX) for i in range(NX)]) for d in (1, 2, 3)
+        ]
+        tokens, around = lax.optimization_barrier((tokens, around))
         tokens = (tokens, swap(tokens, "co"))
     with jax.named_scope("weights"):
         weights_2 = (w_fc2, swap(w_fc2, "co"))
         w_fc1_t = w_fc1.T
-
-    with jax.named_scope("patches"):
-        patches = pack_patches(patch_in, beside, core)
 
     def tie(value, first):
         return lax.optimization_barrier((value, first))[0]
@@ -334,15 +336,16 @@
         beyond = swap(ready, "zh")
         far = sum_parts(parts, far_z)
         got = widen(swap(far, "zh"))
-        around = spread_patches(tie(patches, far), beyond)
-        around = lax.all_to_all(around, "x", 0, 0, tiled=True)
+        beyond = spread_patches(tie(beyond, far))
+        beyond = lax.all_to_all(beyond, "x", 0, 0, tiled=True)
     with jax.named_scope("merged"):
         act = act_rows(parts, got, slope, owner_pos, near_z)
         sums = merged_part((act, swap(act, "co")), weights_1, core)
         parts = lax.all_to_all(
             sums.reshape(NX * NCO, NZH * own, half), ("x", "co"), 0, 0, tiled=True
         ).reshape(NX * NCO, NZH, own, half)
-        terms = gain_terms(sums, around, near_z, norm_gain.shape[0]).reshape(-1, 128)
+        here = jnp.stack([zh, lax.axis_index("x").astype(jnp.int32)])
+        terms = gain_terms(sums, beyond, [patches] + around, here, norm_gain.shape[0]).reshape(-1, 128)
         terms = lax.psum(terms, "y")
         parts, terms = lax.optimization_barrier((parts, terms))
         far = sum_halves(parts, far_z)

time: 159 us -> 166 us (1.044)
  starting transfers between devices: 86.4 us -> 105 us
  waiting for transfers between devices: 37.8 us -> 22.5 us
  local copies, waits for them, and re-layouts: 3 us -> 6.47 us
    ppermute x8, starting transfers between devices: 37.9 us -> 51.3 us  [swap(): return lax.ppermute(value, axis, [(0, 1), (1, 0)])]
    all_to_all x1, waiting for transfers between devices: 10.2 us -> 0.01 us  [local(): lax.all_to_all(outgoing, CTX, 0, 0, tiled=True).reshape(group, depth // ctx)]
    ppermute x0 -> x3, starting transfers between devices: none -> 9.48 us  [local(): lax.ppermute(patches, 'x', [(i, (i - d) % NX) for i in range(NX)])]
    ppermute x0 -> x3, waiting for transfers between devices: none -> 7.51 us  [local(): lax.ppermute(patches, 'x', [(i, (i - d) % NX) for i in range(NX)])]
    all_to_all x1, waiting for transfers between devices: 15.3 us -> 8.05 us  [local(): parts = lax.all_to_all(sums, 'x', 0, 0, tiled=True)]
    ppermute x8, waiting for transfers between devices: 7.8 us -> 2.45 us  [swap(): return lax.ppermute(value, axis, [(0, 1), (1, 0)])]
    unnamed x10 -> x12, local copies, waits for them, and re-layouts: 0.03 us -> 3.48 us
    all_to_all x2, starting transfers between devices: 26.1 us -> 24 us  [sum_over(): return jnp.sum(lax.all_to_all(rows, axes, 0, 0, tiled=True), axis=0)]
  transfers between devices with their start and end apart: 14 -> 17, of which waited for: 7 -> 8; matrix products, arithmetic and copies ran while one was open for 2% -> 2% of each run, Pallas kernels for 9% -> 8%
where the time goes in v9:
time: 166 us; the launch traced here: 165 us
  starting transfers between devices  105 us (63%)
  waiting for transfers between devices  22.5 us (14%)
  blocking collectives  15 us (9%)
  Pallas kernels  13.7 us (8%)
  local copies, waits for them, and re-layouts  6.47 us (4%)
    ppermute x8, starting transfers between devices, swap(): return lax.ppermute(value, axis, [(0, 1), (1, 0)])  51.3 us
    all_to_all x2, starting transfers between devices, sum_over(): return jnp.sum(lax.all_to_all(rows, axes, 0, 0, tiled=True), axis=0)  24 us
    psum x1, blocking collectives, local(): terms = lax.psum(terms, 'y')  15 us
    ppermute x3, starting transfers between devices, local(): lax.ppermute(patches, 'x', [(i, (i - d) % NX) for i in range(NX)])  9.48 us
    all_to_all x1, starting transfers between devices, local(): lax.all_to_all(outgoing, CTX, 0, 0, tiled=True).reshape(group, depth // ctx)  8.08 us
    all_to_all x1, waiting for transfers between devices, local(): parts = lax.all_to_all(sums, 'x', 0, 0, tiled=True)  8.05 us
    ppermute x3, waiting for transfers between devices, local(): lax.ppermute(patches, 'x', [(i, (i - d) % NX) for i in range(NX)])  7.51 us
    pallas_call x1, Pallas kernels, hidden_part(): pl.pallas_call(hidden_kernel, grid_spec=pltpu.PrefetchScalarGridSpec(num_...  5.25 us
  transfers between devices with their start and end apart: 17, of which 8 were waited for; matrix products, arithmetic and copies ran while one was open for 2% of the time, Pallas kernels for 8%

profile of v9, /device:TPU:1, one launch (start us, length us, event | category | flops | bytes accessed | tf_op | source)
XLA Modules:
  0.0 164.5 jit_solution(2464403726013317298)
XLA Ops:
  0.6 12.4 %collective-permute-start = (bf16[5120,512]{1,0:T(8,128)(2,1)}, bf16[5120,512]{1,0:T(8,128)(2,1)}, u32[]{:S(2)}, u32[]{:S(2)}) collective-permute-start(bf16[5120,512]{1,0:T(8,128)(2,1)} %param.10), channel_id=1, source_target_pairs={{0,1},{1,0},{2,3},{3,2},{4,5},{5,4},{6,7},{7,6},{8,9},{9,8},{10,11... | collective-permute-start | bytes 15728648 | tf_op jit(solution)/shard_map/weights/ppermute | solution.py:41
  13.1 1.7 %copy.18 = bf16[2,16,8,512]{3,2,0,1:T(8,128)(2,1)} copy(bf16[2,16,8,512]{3,2,1,0:T(8,128)(2,1)} %bitcast.29) | data formatting | bytes 524288 | tf_op jit(solution)/shard_map/tokens/reshape | solution.py:315
  14.8 8.1 %all-to-all-start = ((bf16[16,16,512]{2,1,0:T(8,128)(2,1)}), bf16[16,16,512]{2,1,0:T(8,128)(2,1)S(1)}, u32[]{:S(2)}, u32[]{:S(2)}) async-start(bf16[16,16,512]{2,1,0:T(8,128)(2,1)} %bitcast.20), calls=%async_computation | async-start | bytes 524288 | tf_op jit(solution)/shard_map/tokens/all_to_all | solution.py:316
  22.8 2.0 %collective-permute-start.1 = (bf16[16,5120]{1,0:T(8,128)(2,1)}, bf16[16,5120]{1,0:T(8,128)(2,1)S(1)}, u32[]{:S(2)}, u32[]{:S(2)}) collective-permute-start(bf16[16,5120]{1,0:T(8,128)(2,1)} %patch_ref.1), channel_id=1, source_target_pairs={{0,1},{1,0},{2,3},{3,2},{4,5},{5,4},{6,7},{7,6},{8,9},{9,8},{10,11... | collective-permute-start | bytes 491528 | tf_op jit(solution)/shard_map/tokens/ppermute | solution.py:41
  24.9 1.5 collective-permute-done.1.got_ref
  26.3 0.9 copy-done.1
  27.3 4.5 %collective-permute-start.2 = (bf16[2,16,2560]{2,1,0:T(8,128)(2,1)S(1)}, bf16[2,16,2560]{2,1,0:T(8,128)(2,1)S(1)}, u32[]{:S(2)}, u32[]{:S(2)}) collective-permute-start(bf16[2,16,2560]{2,1,0:T(8,128)(2,1)S(1)} %pack_patches.1.refs_0_), channel_id=1, source_target_pairs={{0,12},{4,0},{8,4},{12,8},{1,13},{5,1},{9,5},{13,9},{2,14},{6,2},{... | collective-permute-start | bytes 491528 | tf_op jit(solution)/shard_map/tokens/ppermute | solution.py:320
  31.8 2.5 %collective-permute-start.3 = (bf16[2,16,2560]{2,1,0:T(8,128)(2,1)S(1)}, bf16[2,16,2560]{2,1,0:T(8,128)(2,1)S(1)}, u32[]{:S(2)}, u32[]{:S(2)}) collective-permute-start(bf16[2,16,2560]{2,1,0:T(8,128)(2,1)S(1)} %pack_patches.1.refs_0_), channel_id=1, source_target_pairs={{0,8},{4,12},{8,0},{12,4},{1,9},{5,13},{9,1},{13,5},{2,10},{6,14},... | collective-permute-start | bytes 491528 | tf_op jit(solution)/shard_map/tokens/ppermute | solution.py:320
  34.3 2.5 %collective-permute-start.4 = (bf16[2,16,2560]{2,1,0:T(8,128)(2,1)S(1)}, bf16[2,16,2560]{2,1,0:T(8,128)(2,1)S(1)}, u32[]{:S(2)}, u32[]{:S(2)}) collective-permute-start(bf16[2,16,2560]{2,1,0:T(8,128)(2,1)S(1)} %pack_patches.1.refs_0_), channel_id=1, source_target_pairs={{0,4},{4,8},{8,12},{12,0},{1,5},{5,9},{9,13},{13,1},{2,6},{6,10},{... | collective-permute-start | bytes 491528 | tf_op jit(solution)/shard_map/tokens/ppermute | solution.py:320
  36.8 3.0 %collective-permute-done.2.refs_1_ = bf16[2,16,2560]{2,1,0:T(8,128)(2,1)S(1)} collective-permute-done((bf16[2,16,2560]{2,1,0:T(8,128)(2,1)S(1)}, bf16[2,16,2560]{2,1,0:T(8,128)(2,1)S(1)}, u32[]{:S(2)}, u32[]{:S(2)}) %collective-permute-start.2) | collective-permute-done | bytes 163872 | tf_op jit(solution)/shard_map/tokens/ppermute | solution.py:320
  39.8 0.5 collective-permute-done.3.refs_2_
  40.3 4.0 %collective-permute-done.4.refs_3_ = bf16[2,16,2560]{2,1,0:T(8,128)(2,1)S(1)} collective-permute-done((bf16[2,16,2560]{2,1,0:T(8,128)(2,1)S(1)}, bf16[2,16,2560]{2,1,0:T(8,128)(2,1)S(1)}, u32[]{:S(2)}, u32[]{:S(2)}) %collective-permute-start.4) | collective-permute-done | bytes 163872 | tf_op jit(solution)/shard_map/tokens/ppermute | solution.py:320
  44.3 2.9 %collective-permute-start.5 = (bf16[256,512]{1,0:T(8,128)(2,1)S(1)}, bf16[256,512]{1,0:T(8,128)(2,1)S(1)}, u32[]{:S(2)}, u32[]{:S(2)}) collective-permute-start(bf16[256,512]{1,0:T(8,128)(2,1)S(1)} %bitcast.25), channel_id=1, source_target_pairs={{0,1},{1,0},{2,3},{3,2},{4,5},{5,4},{6,7},{7,6},{8,9},{9,8},{10,11... | collective-permute-start | bytes 786440 | tf_op jit(solution)/shard_map/tokens/ppermute | solution.py:41
  47.2 1.9 %collective-permute-start.8 = (bf16[320,5120]{1,0:T(8,128)(2,1)}, bf16[320,5120]{1,0:T(8,128)(2,1)}, u32[]{:S(2)}, u32[]{:S(2)}) collective-permute-start(bf16[320,5120]{1,0:T(8,128)(2,1)} %bitcast.23), channel_id=1, source_target_pairs={{0,1},{1,0},{2,3},{3,2},{4,5},{5,4},{6,7},{7,6},{8,9},{9,8},{10,11... | collective-permute-start | bytes 9830408 | tf_op jit(solution)/shard_map/hidden/ppermute | solution.py:41
  49.2 0.0 collective-permute-done.5.got_t
  49.2 0.0 collective-permute-done
  49.2 5.3 %hidden_part.1 = bf16[4,2,320,256]{3,2,1,0:T(8,128)(2,1)} custom-call(s32[1]{0:T(128)} %bitcast.1.core.place, bf16[4,2,2,320,512]{4,3,2,1,0:T(8,128)(2,1)} %bitcast.28, bf16[4,2,2,320,512]{4,3,2,1,0:T(8,128)(2,1)} %bitcast.3.got_w, bf16[256,512]{1,0:T(8,128)(2,1)S(1)} %bitcast.26, bf16[256,512]{1,0:T(8,128)(2,1)S(1)} %collective-permute-done.5.got_t), custom_call_target="tpu_custom_call" | custom-call | flops 1 | bytes 1 | tf_op jit(solution)/shard_map/hidden/hidden_part/pallas_call | solution.py:65
  54.4 3.7 %all-to-all-start.1 = ((bf16[4,2,320,256]{3,2,1,0:T(8,128)(2,1)}), bf16[4,2,320,256]{3,2,1,0:T(8,128)(2,1)S(1)}, u32[]{:S(2)}, u32[]{:S(2)}) async-start(bf16[4,2,320,256]{3,2,1,0:T(8,128)(2,1)} %hidden_part.1), calls=%async_computation.1 | async-start | bytes 2621440 | tf_op jit(solution)/shard_map/hidden/all_to_all | solution.py:333
  58.1 9.4 %collective-permute-start.9 = (bf16[2,16,2560]{2,1,0:T(8,128)(2,1)S(1)}, bf16[2,16,2560]{2,1,0:T(8,128)(2,1)S(1)}, u32[]{:S(2)}, u32[]{:S(2)}) collective-permute-start(bf16[2,16,2560]{2,1,0:T(8,128)(2,1)S(1)} %pack_patches.1.refs_0_), channel_id=1, source_target_pairs={{0,2},{2,0},{1,3},{3,1},{4,6},{6,4},{5,7},{7,5},{8,10},{10,8},{9,1... | collective-permute-start | bytes 491528 | tf_op jit(solution)/shard_map/hidden/ppermute | solution.py:41
  67.5 8.0 %all-to-all-done.1.v_ref = bf16[4,2,320,256]{3,2,1,0:T(8,128)(2,1)S(1)} async-done(((bf16[4,2,320,256]{3,2,1,0:T(8,128)(2,1)}), bf16[4,2,320,256]{3,2,1,0:T(8,128)(2,1)S(1)}, u32[]{:S(2)}, u32[]{:S(2)}) %all-to-all-start.1) | async-done | bytes 1310752 | tf_op jit(solution)/shard_map/hidden/all_to_all | solution.py:333
  75.6 0.1 sum_parts.1
  75.7 9.4 %collective-permute-start.6 = (bf16[320,256]{1,0:T(8,128)(2,1)S(1)}, bf16[320,256]{1,0:T(8,128)(2,1)S(1)}, u32[]{:S(2)}, u32[]{:S(2)}) collective-permute-start(bf16[320,256]{1,0:T(8,128)(2,1)S(1)} %sum_parts.1), channel_id=1, source_target_pairs={{0,2},{2,0},{1,3},{3,1},{4,6},{6,4},{5,7},{7,5},{8,10},{10,8},{9,1... | collective-permute-start | bytes 491528 | tf_op jit(solution)/shard_map/hidden/ppermute | solution.py:41
  85.1 0.1 fusion.3.slope_ref
  85.2 0.0 collective-permute-done.9.own_ref
  85.3 0.9 spread_patches.1
  86.1 3.5 %all-to-all-start.3 = ((bf16[4,2,16,2560]{3,2,1,0:T(8,128)(2,1)}), bf16[4,2,16,2560]{3,2,1,0:T(8,128)(2,1)S(1)}, u32[]{:S(2)}, u32[]{:S(2)}) async-start(bf16[4,2,16,2560]{3,2,1,0:T(8,128)(2,1)} %spread_patches.1), calls=%async_computation.3 | async-start | bytes 1310720 | tf_op jit(solution)/shard_map/hidden/all_to_all | solution.py:340
  89.6 0.0 copy-start.3
  89.7 0.6 copy-done.3
  90.3 0.3 act_rows.1.own_a
  90.7 3.5 %collective-permute-start.7 = (bf16[4,2,2,16,320]{4,3,2,1,0:T(8,128)(2,1)S(1)}, bf16[4,2,2,16,320]{4,3,2,1,0:T(8,128)(2,1)S(1)}, u32[]{:S(2)}, u32[]{:S(2)}) collective-permute-start(bf16[4,2,2,16,320]{4,3,2,1,0:T(8,128)(2,1)S(1)} %act_rows.1.own_a), channel_id=1, source_target_pairs={{0,1},{1,0},{2,3},{3,2},{4,5},{5,4},{6,7},{7,6},{8,9},{9,8},{10,11... | collective-permute-start | bytes 491528 | tf_op jit(solution)/shard_map/merged/ppermute | solution.py:41
  94.2 0.1 pad_add_fusion.place
  94.3 0.0 collective-permute-done.8.got_w
  94.3 1.0 collective-permute-done.7.got_a
  95.2 1.9 %copy-done = bf16[5120,320]{0,1:T(8,128)(2,1)S(1)} copy-done((bf16[5120,320]{0,1:T(8,128)(2,1)S(1)}, bf16[5120,320]{0,1:T(8,128)(2,1)}, u32[]{:S(2)}) %copy-start) | copy-done | bytes 3276824
  97.2 3.8 %merged_part.1.grad_ref = bf16[4,2,2,16,2560]{4,3,2,1,0:T(8,128)(2,1)} custom-call(s32[1]{0:T(128)} %bitcast.1.core.place, bf16[4,2,2,16,320]{4,3,2,1,0:T(8,128)(2,1)S(1)} %act_rows.1.own_a, bf16[4,2,2,16,320]{4,3,2,1,0:T(8,128)(2,1)S(1)} %collective-permute-done.7.got_a, bf16[320,5120]{1,0:T(8,128)(2,1)S(1)} %bitcast.24, ...), custom_call_target="tpu_custom_call" | custom-call | flops 1 | bytes 1 | tf_op jit(solution)/shard_map/merged/merged_part/pallas_call | solution.py:166
  101.0 5.1 %all-to-all-start.2 = ((bf16[8,32,2560]{2,1,0:T(8,128)(2,1)}), bf16[8,32,2560]{2,1,0:T(8,128)(2,1)S(1)}, u32[]{:S(2)}, u32[]{:S(2)}) async-start(bf16[8,32,2560]{2,1,0:T(8,128)(2,1)} %bitcast.9), calls=%async_computation.2 | async-start | bytes 2621440 | tf_op jit(solution)/shard_map/merged/all_to_all | solution.py:344
  106.1 2.3 %gain_terms.1 = f32[1,1280]{1,0:T(1,128)S(1)} custom-call(s32[2]{0:T(128)S(1)} %pad_add_fusion.place, bf16[4,2,2,16,2560]{4,3,2,1,0:T(8,128)(2,1)} %merged_part.1.grad_ref, bf16[4,2,16,2560]{3,2,1,0:T(8,128)(2,1)S(1)} %all-to-all-done.3.beyond_ref, bf16[2,16,2560]{2,1,0:T(8,128)(2,1)S(1)} %pack_patches.1.refs_0_, ...), custom_call_target="tpu_custom_call" | custom-call | flops 20000000000 | bytes 1 | tf_op jit(solution)/shard_map/merged/gain_terms/pallas_call | solution.py:260
  108.4 15.0 %psum.7 = f32[10,128]{1,0:T(8,128)S(1)} all-reduce(f32[10,128]{1,0:T(8,128)S(1)} %bitcast.30), channel_id=1, replica_groups=mesh['y'=8,'zl'=6,'x'=4,'zh'=2,'co'=2] {'y'}, use_global_device_ids=true, to_apply=%region_0.0 | all-reduce | flops 1280 | bytes 10240 | tf_op jit(solution)/shard_map/merged/psum | solution.py:349
  123.4 0.6 all-to-all-done.2
  124.0 0.1 sum_halves.1
  124.1 0.6 broadcast_in_dim.4
  124.7 12.6 %all-to-all-start.4 = ((f32[12,10,128]{2,1,0:T(8,128)}), f32[12,10,128]{2,1,0:T(8,128)S(1)}, u32[]{:S(2)}, u32[]{:S(2)}) async-start(f32[12,10,128]{2,1,0:T(8,128)} %broadcast_in_dim.4), calls=%async_computation.4 | async-start | bytes 196608 | tf_op jit(solution)/shard_map/gain/all_to_all | solution.py:302
  137.3 9.6 %collective-permute-start.10 = (bf16[2,16,2560]{2,1,0:T(8,128)(2,1)S(1)}, bf16[2,16,2560]{2,1,0:T(8,128)(2,1)S(1)}, u32[]{:S(2)}, u32[]{:S(2)}) collective-permute-start(bf16[2,16,2560]{2,1,0:T(8,128)(2,1)S(1)} %sum_halves.1), channel_id=1, source_target_pairs={{0,2},{2,0},{1,3},{3,1},{4,6},{6,4},{5,7},{7,5},{8,10},{10,8},{9,1... | collective-permute-start | bytes 491528 | tf_op jit(solution)/shard_map/merged/ppermute | solution.py:41
  147.0 0.6 broadcast_in_dim.5
  147.7 11.4 %all-to-all-start.5 = ((f32[8,10,128]{2,1,0:T(8,128)}), f32[8,10,128]{2,1,0:T(8,128)S(1)}, u32[]{:S(2)}, u32[]{:S(2)}) async-start(f32[8,10,128]{2,1,0:T(8,128)} %broadcast_in_dim.5), calls=%async_computation.5 | async-start | bytes 131072 | tf_op jit(solution)/shard_map/gain/all_to_all | solution.py:302
  159.1 0.9 norm_part.1
  160.0 3.9 %all-to-all-done.5 = f32[8,10,128]{2,1,0:T(8,128)S(1)} async-done(((f32[8,10,128]{2,1,0:T(8,128)}), f32[8,10,128]{2,1,0:T(8,128)S(1)}, u32[]{:S(2)}, u32[]{:S(2)}) %all-to-all-start.5) | async-done | bytes 40992 | tf_op jit(solution)/shard_map/gain/all_to_all | solution.py:302
  163.9 0.6 multiply_bitcast_fusion
  (19 shorter events, 0.1 us)
Async XLA Ops:
  0.6 48.5 %collective-permute-start = (bf16[5120,512]{1,0:T(8,128)(2,1)}, bf16[5120,512]{1,0:T(8,128)(2,1)}, u32[]{:S(2)}, u32[]{:S(2)}) collective-permute-start(bf16[5120,512]{1,0:T(8,128)(2,1)} %param.10), channel_id=1, source_target_pairs={{0,1},{1,0},{2,3},{3,2},{4,5},{5,4},{6,7},{7,6},{8,9},{9,8},{10,11... | collective-permute-start | bytes 15728648 | tf_op jit(solution)/shard_map/weights/ppermute | solution.py:41
  14.8 29.5 %all-to-all-start = ((bf16[16,16,512]{2,1,0:T(8,128)(2,1)}), bf16[16,16,512]{2,1,0:T(8,128)(2,1)S(1)}, u32[]{:S(2)}, u32[]{:S(2)}) async-start(bf16[16,16,512]{2,1,0:T(8,128)(2,1)} %bitcast.20), calls=%async_computation | async-start | bytes 524288 | tf_op jit(solution)/shard_map/tokens/all_to_all | solution.py:316
  22.8 3.5 %collective-permute-start.1 = (bf16[16,5120]{1,0:T(8,128)(2,1)}, bf16[16,5120]{1,0:T(8,128)(2,1)S(1)}, u32[]{:S(2)}, u32[]{:S(2)}) collective-permute-start(bf16[16,5120]{1,0:T(8,128)(2,1)} %patch_ref.1), channel_id=1, source_target_pairs={{0,1},{1,0},{2,3},{3,2},{4,5},{5,4},{6,7},{7,6},{8,9},{9,8},{10,11... | collective-permute-start | bytes 491528 | tf_op jit(solution)/shard_map/tokens/ppermute | solution.py:41
  26.3 0.9 copy-start.1
  27.3 12.5 %collective-permute-start.2 = (bf16[2,16,2560]{2,1,0:T(8,128)(2,1)S(1)}, bf16[2,16,2560]{2,1,0:T(8,128)(2,1)S(1)}, u32[]{:S(2)}, u32[]{:S(2)}) collective-permute-start(bf16[2,16,2560]{2,1,0:T(8,128)(2,1)S(1)} %pack_patches.1.refs_0_), channel_id=1, source_target_pairs={{0,12},{4,0},{8,4},{12,8},{1,13},{5,1},{9,5},{13,9},{2,14},{6,2},{... | collective-permute-start | bytes 491528 | tf_op jit(solution)/shard_map/tokens/ppermute | solution.py:320
  31.8 8.5 %collective-permute-start.3 = (bf16[2,16,2560]{2,1,0:T(8,128)(2,1)S(1)}, bf16[2,16,2560]{2,1,0:T(8,128)(2,1)S(1)}, u32[]{:S(2)}, u32[]{:S(2)}) collective-permute-start(bf16[2,16,2560]{2,1,0:T(8,128)(2,1)S(1)} %pack_patches.1.refs_0_), channel_id=1, source_target_pairs={{0,8},{4,12},{8,0},{12,4},{1,9},{5,13},{9,1},{13,5},{2,10},{6,14},... | collective-permute-start | bytes 491528 | tf_op jit(solution)/shard_map/tokens/ppermute | solution.py:320
  34.3 10.0 %collective-permute-start.4 = (bf16[2,16,2560]{2,1,0:T(8,128)(2,1)S(1)}, bf16[2,16,2560]{2,1,0:T(8,128)(2,1)S(1)}, u32[]{:S(2)}, u32[]{:S(2)}) collective-permute-start(bf16[2,16,2560]{2,1,0:T(8,128)(2,1)S(1)} %pack_patches.1.refs_0_), channel_id=1, source_target_pairs={{0,4},{4,8},{8,12},{12,0},{1,5},{5,9},{9,13},{13,1},{2,6},{6,10},{... | collective-permute-start | bytes 491528 | tf_op jit(solution)/shard_map/tokens/ppermute | solution.py:320
  44.3 4.9 %collective-permute-start.5 = (bf16[256,512]{1,0:T(8,128)(2,1)S(1)}, bf16[256,512]{1,0:T(8,128)(2,1)S(1)}, u32[]{:S(2)}, u32[]{:S(2)}) collective-permute-start(bf16[256,512]{1,0:T(8,128)(2,1)S(1)} %bitcast.25), channel_id=1, source_target_pairs={{0,1},{1,0},{2,3},{3,2},{4,5},{5,4},{6,7},{7,6},{8,9},{9,8},{10,11... | collective-permute-start | bytes 786440 | tf_op jit(solution)/shard_map/tokens/ppermute | solution.py:41
  47.2 47.1 %collective-permute-start.8 = (bf16[320,5120]{1,0:T(8,128)(2,1)}, bf16[320,5120]{1,0:T(8,128)(2,1)}, u32[]{:S(2)}, u32[]{:S(2)}) collective-permute-start(bf16[320,5120]{1,0:T(8,128)(2,1)} %bitcast.23), channel_id=1, source_target_pairs={{0,1},{1,0},{2,3},{3,2},{4,5},{5,4},{6,7},{7,6},{8,9},{9,8},{10,11... | collective-permute-start | bytes 9830408 | tf_op jit(solution)/shard_map/hidden/ppermute | solution.py:41
  54.4 30.7 %copy-start.4 = (bf16[320,256]{1,0:T(8,128)(2,1)S(1)}, bf16[320,256]{1,0:T(8,128)(2,1)}, u32[]{:S(2)}) copy-start(bf16[320,256]{1,0:T(8,128)(2,1)} %param.8) | copy-start | bytes 491524
  54.4 21.1 %all-to-all-start.1 = ((bf16[4,2,320,256]{3,2,1,0:T(8,128)(2,1)}), bf16[4,2,320,256]{3,2,1,0:T(8,128)(2,1)S(1)}, u32[]{:S(2)}, u32[]{:S(2)}) async-start(bf16[4,2,320,256]{3,2,1,0:T(8,128)(2,1)} %hidden_part.1), calls=%async_computation.1 | async-start | bytes 2621440 | tf_op jit(solution)/shard_map/hidden/all_to_all | solution.py:333
  58.1 27.1 %collective-permute-start.9 = (bf16[2,16,2560]{2,1,0:T(8,128)(2,1)S(1)}, bf16[2,16,2560]{2,1,0:T(8,128)(2,1)S(1)}, u32[]{:S(2)}, u32[]{:S(2)}) collective-permute-start(bf16[2,16,2560]{2,1,0:T(8,128)(2,1)S(1)} %pack_patches.1.refs_0_), channel_id=1, source_target_pairs={{0,2},{2,0},{1,3},{3,1},{4,6},{6,4},{5,7},{7,5},{8,10},{10,8},{9,1... | collective-permute-start | bytes 491528 | tf_op jit(solution)/shard_map/hidden/ppermute | solution.py:41
  75.7 14.0 %collective-permute-start.6 = (bf16[320,256]{1,0:T(8,128)(2,1)S(1)}, bf16[320,256]{1,0:T(8,128)(2,1)S(1)}, u32[]{:S(2)}, u32[]{:S(2)}) collective-permute-start(bf16[320,256]{1,0:T(8,128)(2,1)S(1)} %sum_parts.1), channel_id=1, source_target_pairs={{0,2},{2,0},{1,3},{3,1},{4,6},{6,4},{5,7},{7,5},{8,10},{10,8},{9,1... | collective-permute-start | bytes 491528 | tf_op jit(solution)/shard_map/hidden/ppermute | solution.py:41
  86.1 14.8 %all-to-all-start.3 = ((bf16[4,2,16,2560]{3,2,1,0:T(8,128)(2,1)}), bf16[4,2,16,2560]{3,2,1,0:T(8,128)(2,1)S(1)}, u32[]{:S(2)}, u32[]{:S(2)}) async-start(bf16[4,2,16,2560]{3,2,1,0:T(8,128)(2,1)} %spread_patches.1), calls=%async_computation.3 | async-start | bytes 1310720 | tf_op jit(solution)/shard_map/hidden/all_to_all | solution.py:340
  89.6 0.7 copy-start.3
  90.7 4.6 %collective-permute-start.7 = (bf16[4,2,2,16,320]{4,3,2,1,0:T(8,128)(2,1)S(1)}, bf16[4,2,2,16,320]{4,3,2,1,0:T(8,128)(2,1)S(1)}, u32[]{:S(2)}, u32[]{:S(2)}) collective-permute-start(bf16[4,2,2,16,320]{4,3,2,1,0:T(8,128)(2,1)S(1)} %act_rows.1.own_a), channel_id=1, source_target_pairs={{0,1},{1,0},{2,3},{3,2},{4,5},{5,4},{6,7},{7,6},{8,9},{9,8},{10,11... | collective-permute-start | bytes 491528 | tf_op jit(solution)/shard_map/merged/ppermute | solution.py:41
  95.2 1.9 %copy-start = (bf16[5120,320]{0,1:T(8,128)(2,1)S(1)}, bf16[5120,320]{0,1:T(8,128)(2,1)}, u32[]{:S(2)}) copy-start(bf16[5120,320]{0,1:T(8,128)(2,1)} %param.9) | copy-start | bytes 9830404
  101.0 23.0 %all-to-all-start.2 = ((bf16[8,32,2560]{2,1,0:T(8,128)(2,1)}), bf16[8,32,2560]{2,1,0:T(8,128)(2,1)S(1)}, u32[]{:S(2)}, u32[]{:S(2)}) async-start(bf16[8,32,2560]{2,1,0:T(8,128)(2,1)} %bitcast.9), calls=%async_computation.2 | async-start | bytes 2621440 | tf_op jit(solution)/shard_map/merged/all_to_all | solution.py:344
  106.1 40.9 %copy-start.5 = (f32[1280]{0:T(1024)S(1)}, f32[1280]{0:T(1024)}, u32[]{:S(2)}) copy-start(f32[1280]{0:T(1024)} %param.12) | copy-start | bytes 15364
  106.1 53.0 %copy-start.2 = (bf16[16,5120]{1,0:T(8,128)(2,1)S(1)}, bf16[16,5120]{1,0:T(8,128)(2,1)}, u32[]{:S(2)}) copy-start(bf16[16,5120]{1,0:T(8,128)(2,1)} %patch_ref.1) | copy-start | bytes 491524
  124.7 22.3 %all-to-all-start.4 = ((f32[12,10,128]{2,1,0:T(8,128)}), f32[12,10,128]{2,1,0:T(8,128)S(1)}, u32[]{:S(2)}, u32[]{:S(2)}) async-start(f32[12,10,128]{2,1,0:T(8,128)} %broadcast_in_dim.4), calls=%async_computation.4 | async-start | bytes 196608 | tf_op jit(solution)/shard_map/gain/all_to_all | solution.py:302
  137.3 21.7 %collective-permute-start.10 = (bf16[2,16,2560]{2,1,0:T(8,128)(2,1)S(1)}, bf16[2,16,2560]{2,1,0:T(8,128)(2,1)S(1)}, u32[]{:S(2)}, u32[]{:S(2)}) collective-permute-start(bf16[2,16,2560]{2,1,0:T(8,128)(2,1)S(1)} %sum_halves.1), channel_id=1, source_target_pairs={{0,2},{2,0},{1,3},{3,1},{4,6},{6,4},{5,7},{7,5},{8,10},{10,8},{9,1... | collective-permute-start | bytes 491528 | tf_op jit(solution)/shard_map/merged/ppermute | solution.py:41
  147.7 16.3 %all-to-all-start.5 = ((f32[8,10,128]{2,1,0:T(8,128)}), f32[8,10,128]{2,1,0:T(8,128)S(1)}, u32[]{:S(2)}, u32[]{:S(2)}) async-start(f32[8,10,128]{2,1,0:T(8,128)} %broadcast_in_dim.5), calls=%async_computation.5 | async-start | bytes 131072 | tf_op jit(solution)/shard_map/gain/all_to_all | solution.py:302

commit v10 on v6

--- a/solution.py
+++ b/solution.py
@@ -71,7 +71,7 @@
             out_specs=pl.BlockSpec((1, NZH, units, count), lambda i, s: (i, 0, 0, 0)),
         ),
         out_shape=jax.ShapeDtypeStruct((NX, NZH, units, count), BF16),
-        compiler_params=params(60),
+        compiler_params=params(52),
         cost_estimate=cost(),
         name="hidden_part",
     )(core, *weights, *tokens)
@@ -100,8 +100,22 @@
     )(place, parts)
 
 
+def wide_kernel(v_ref, out_ref):
+    out_ref[...] = v_ref[...].astype(F32)
+
+
+def widen(value):
+    return pl.pallas_call(
+        wide_kernel,
+        out_shape=jax.ShapeDtypeStruct(value.shape, F32),
+        compiler_params=params(),
+        cost_estimate=cost(LONG),
+        name="widen",
+    )(value)
+
+
 def act_kernel(place, v_ref, got_ref, slope_ref, pos_ref, out_ref):
-    act = ((total_of(v_ref, place[0]) + got_ref[...].astype(F32)) * slope_ref[...]).astype(BF16)
+    act = ((total_of(v_ref, place[0]) + got_ref[...]) * slope_ref[...]).astype(BF16)
     count = act.shape[1]
     pick = (lax.broadcasted_iota(jnp.int32, (count, count), 0) == pos_ref[...]).astype(F32)
     pick = pick.T.astype(BF16)
@@ -302,10 +316,10 @@
         sums = hidden_part(weights_2, tokens, core)
         parts = lax.all_to_all(sums, "x", 0, 0, tiled=True)
         ready = tie(patches, sums)
-        weights_1 = (w_fc1_t, swap(tie(w_fc1_t, ready), "co"))
+        weights_1 = (w_fc1_t, swap(w_fc1_t, "co"))
         beyond = swap(ready, "zh")
         far = sum_parts(parts, far_z)
-        got = swap(far, "zh")
+        got = widen(swap(far, "zh"))
         patches = jnp.stack([tie(patches, far), beyond])
         around = [patches] + [
             lax.ppermute(patches, "x", [(i, (i - d) % NX) for i in range(NX)]) for d in (1, 2, 3)
@@ -318,16 +332,16 @@
         ).reshape(NX * NCO, NZH, own, half)
         here = jnp.stack([lax.axis_index("x").astype(jnp.int32), zh])
         terms = gain_terms(sums, around, here, norm_gain.shape[0]).reshape(-1, 128)
-        terms = lax.psum(terms, "co")
+        terms = lax.psum(terms, "y")
         parts, terms = lax.optimization_barrier((parts, terms))
         far = sum_halves(parts, far_z)
         got = swap(far, "zh")
     with jax.named_scope("gain"):
-        terms = sum_over(tie(terms, far), ("x", "y"), NX * NY)
+        terms = sum_over(tie(terms, far), ("zl", "zh"), NZL * NZH)
     with jax.named_scope("norm"):
         patch_grad = norm_part(parts, got, patch_in, norm_gain, near_z)
     with jax.named_scope("gain"):
-        terms = sum_over(terms, ("zl", "zh"), NZL * NZH)
+        terms = sum_over(terms, ("x", "co"), NX * NCO)
         gain_grad = terms.reshape(-1) / (NY * NZL * ctx)
     return (patch_grad, gain_grad)
 

time: 162 us -> 156 us (0.963)
  the two profiles are of different devices: /device:TPU:8 before, /device:TPU:1 now
where the time goes in v10:
time: 156 us; the launch traced here: 155 us
  starting transfers between devices  86.1 us (55%)
  waiting for transfers between devices  34.3 us (22%)
  blocking collectives  15 us (10%)
  Pallas kernels  12.8 us (8%)
  local copies, waits for them, and re-layouts  4.92 us (3%)
    ppermute x8, starting transfers between devices, swap(): return lax.ppermute(value, axis, [(0, 1), (1, 0)])  39.6 us
    all_to_all x2, starting transfers between devices, sum_over(): return jnp.sum(lax.all_to_all(rows, axes, 0, 0, tiled=True), axis=0)  23 us
    psum x1, blocking collectives, local(): terms = lax.psum(terms, 'y')  15 us
    all_to_all x1, waiting for transfers between devices, local(): parts = lax.all_to_all(sums, 'x', 0, 0, tiled=True)  13.2 us
    all_to_all x1, waiting for transfers between devices, local(): lax.all_to_all(outgoing, CTX, 0, 0, tiled=True).reshape(group, depth // ctx)  10.2 us
    all_to_all x1, starting transfers between devices, local(): lax.all_to_all(outgoing, CTX, 0, 0, tiled=True).reshape(group, depth // ctx)  8.08 us
    ppermute x3, starting transfers between devices, local(): lax.ppermute(patches, 'x', [(i, (i - d) % NX) for i in range(NX)])  7.81 us
    ppermute x8, waiting for transfers between devices, swap(): return lax.ppermute(value, axis, [(0, 1), (1, 0)])  6.41 us
  transfers between devices with their start and end apart: 16, of which 8 were waited for; matrix products, arithmetic and copies ran while one was open for 2% of the time, Pallas kernels for 5%

profile of v10, /device:TPU:1, one launch (start us, length us, event | category | flops | bytes accessed | tf_op | source)
XLA Modules:
  0.0 155.0 jit_solution(16521331785094229306)
XLA Ops:
  0.6 12.4 %collective-permute-start = (bf16[5120,512]{1,0:T(8,128)(2,1)}, bf16[5120,512]{1,0:T(8,128)(2,1)}, u32[]{:S(2)}, u32[]{:S(2)}) collective-permute-start(bf16[5120,512]{1,0:T(8,128)(2,1)} %param.10), channel_id=1, source_target_pairs={{0,1},{1,0},{2,3},{3,2},{4,5},{5,4},{6,7},{7,6},{8,9},{9,8},{10,11... | collective-permute-start | bytes 15728648 | tf_op jit(solution)/shard_map/weights/ppermute | solution.py:41
  13.1 1.7 %copy.18 = bf16[2,16,8,512]{3,2,0,1:T(8,128)(2,1)} copy(bf16[2,16,8,512]{3,2,1,0:T(8,128)(2,1)} %bitcast.32) | data formatting | bytes 524288 | tf_op jit(solution)/shard_map/tokens/reshape | solution.py:300
  14.8 8.1 %all-to-all-start = ((bf16[16,16,512]{2,1,0:T(8,128)(2,1)}), bf16[16,16,512]{2,1,0:T(8,128)(2,1)S(1)}, u32[]{:S(2)}, u32[]{:S(2)}) async-start(bf16[16,16,512]{2,1,0:T(8,128)(2,1)} %bitcast.22), calls=%async_computation | async-start | bytes 524288 | tf_op jit(solution)/shard_map/tokens/all_to_all | solution.py:301
  22.8 2.0 %collective-permute-start.1 = (bf16[16,5120]{1,0:T(8,128)(2,1)}, bf16[16,5120]{1,0:T(8,128)(2,1)S(1)}, u32[]{:S(2)}, u32[]{:S(2)}) collective-permute-start(bf16[16,5120]{1,0:T(8,128)(2,1)} %patch_ref.1), channel_id=1, source_target_pairs={{0,1},{1,0},{2,3},{3,2},{4,5},{5,4},{6,7},{7,6},{8,9},{9,8},{10,11... | collective-permute-start | bytes 491528 | tf_op jit(solution)/shard_map/tokens/ppermute | solution.py:41
  24.9 1.5 collective-permute-done.1.got_ref
  26.3 10.2 %all-to-all-done = bf16[16,16,512]{2,1,0:T(8,128)(2,1)S(1)} async-done(((bf16[16,16,512]{2,1,0:T(8,128)(2,1)}), bf16[16,16,512]{2,1,0:T(8,128)(2,1)S(1)}, u32[]{:S(2)}, u32[]{:S(2)}) %all-to-all-start) | async-done | bytes 262176 | tf_op jit(solution)/shard_map/tokens/all_to_all | solution.py:301
  36.6 2.9 %collective-permute-start.2 = (bf16[256,512]{1,0:T(8,128)(2,1)S(1)}, bf16[256,512]{1,0:T(8,128)(2,1)S(1)}, u32[]{:S(2)}, u32[]{:S(2)}) collective-permute-start(bf16[256,512]{1,0:T(8,128)(2,1)S(1)} %bitcast.27), channel_id=1, source_target_pairs={{0,1},{1,0},{2,3},{3,2},{4,5},{5,4},{6,7},{7,6},{8,9},{9,8},{10,11... | collective-permute-start | bytes 786440 | tf_op jit(solution)/shard_map/tokens/ppermute | solution.py:41
  39.5 1.1 collective-permute-done.2.got_t
  40.7 0.0 collective-permute-done
  40.7 5.3 %hidden_part.1 = bf16[4,2,320,256]{3,2,1,0:T(8,128)(2,1)} custom-call(s32[1]{0:T(128)} %bitcast.1.core.place, bf16[4,2,2,320,512]{4,3,2,1,0:T(8,128)(2,1)} %bitcast.31, bf16[4,2,2,320,512]{4,3,2,1,0:T(8,128)(2,1)} %bitcast.3.got_w, bf16[256,512]{1,0:T(8,128)(2,1)S(1)} %bitcast.28, bf16[256,512]{1,0:T(8,128)(2,1)S(1)} %collective-permute-done.2.got_t), custom_call_target="tpu_custom_call" | custom-call | flops 1 | bytes 1 | tf_op jit(solution)/shard_map/hidden/hidden_part/pallas_call | solution.py:65
  46.0 3.5 %all-to-all-start.1 = ((bf16[4,2,320,256]{3,2,1,0:T(8,128)(2,1)}), bf16[4,2,320,256]{3,2,1,0:T(8,128)(2,1)S(1)}, u32[]{:S(2)}, u32[]{:S(2)}) async-start(bf16[4,2,320,256]{3,2,1,0:T(8,128)(2,1)} %hidden_part.1), calls=%async_computation.1 | async-start | bytes 2621440 | tf_op jit(solution)/shard_map/hidden/all_to_all | solution.py:317
  49.5 2.3 %collective-permute-start.5 = (bf16[320,5120]{1,0:T(8,128)(2,1)}, bf16[320,5120]{1,0:T(8,128)(2,1)}, u32[]{:S(2)}, u32[]{:S(2)}) collective-permute-start(bf16[320,5120]{1,0:T(8,128)(2,1)} %bitcast.25), channel_id=1, source_target_pairs={{0,1},{1,0},{2,3},{3,2},{4,5},{5,4},{6,7},{7,6},{8,9},{9,8},{10,11... | collective-permute-start | bytes 9830408 | tf_op jit(solution)/shard_map/hidden/ppermute | solution.py:41
  51.8 1.9 %collective-permute-start.6 = (bf16[2,16,2560]{2,1,0:T(8,128)(2,1)S(1)}, bf16[2,16,2560]{2,1,0:T(8,128)(2,1)S(1)}, u32[]{:S(2)}, u32[]{:S(2)}) collective-permute-start(bf16[2,16,2560]{2,1,0:T(8,128)(2,1)S(1)} %pack_patches.1), channel_id=1, source_target_pairs={{0,2},{2,0},{1,3},{3,1},{4,6},{6,4},{5,7},{7,5},{8,10},{10,8},{9,1... | collective-permute-start | bytes 491528 | tf_op jit(solution)/shard_map/hidden/ppermute | solution.py:41
  53.8 0.1 fusion.3.slope_ref
  53.9 13.2 %all-to-all-done.1.v_ref = bf16[4,2,320,256]{3,2,1,0:T(8,128)(2,1)S(1)} async-done(((bf16[4,2,320,256]{3,2,1,0:T(8,128)(2,1)}), bf16[4,2,320,256]{3,2,1,0:T(8,128)(2,1)S(1)}, u32[]{:S(2)}, u32[]{:S(2)}) %all-to-all-start.1) | async-done | bytes 1310752 | tf_op jit(solution)/shard_map/hidden/all_to_all | solution.py:317
  67.1 0.1 sum_parts.1
  67.2 1.9 %collective-permute-start.3 = (bf16[320,256]{1,0:T(8,128)(2,1)S(1)}, bf16[320,256]{1,0:T(8,128)(2,1)S(1)}, u32[]{:S(2)}, u32[]{:S(2)}) collective-permute-start(bf16[320,256]{1,0:T(8,128)(2,1)S(1)} %sum_parts.1), channel_id=1, source_target_pairs={{0,2},{2,0},{1,3},{3,1},{4,6},{6,4},{5,7},{7,5},{8,10},{10,8},{9,1... | collective-permute-start | bytes 491528 | tf_op jit(solution)/shard_map/hidden/ppermute | solution.py:41
  69.2 0.0 collective-permute-done.6
  69.2 0.0 copy-start.2
  69.2 2.8 %collective-permute-start.7 = (bf16[2,2,16,2560]{3,2,1,0:T(8,128)(2,1)S(1)}, bf16[2,2,16,2560]{3,2,1,0:T(8,128)(2,1)S(1)}, u32[]{:S(2)}, u32[]{:S(2)}) collective-permute-start(bf16[2,2,16,2560]{3,2,1,0:T(8,128)(2,1)S(1)} %pad_maximum_fusion.refs_0_), channel_id=1, source_target_pairs={{0,12},{4,0},{8,4},{12,8},{1,13},{5,1},{9,5},{13,9},{2,14},{6,2},{... | collective-permute-start | bytes 983048 | tf_op jit(solution)/shard_map/hidden/ppermute | solution.py:325
  72.0 3.1 %collective-permute-start.8 = (bf16[2,2,16,2560]{3,2,1,0:T(8,128)(2,1)S(1)}, bf16[2,2,16,2560]{3,2,1,0:T(8,128)(2,1)S(1)}, u32[]{:S(2)}, u32[]{:S(2)}) collective-permute-start(bf16[2,2,16,2560]{3,2,1,0:T(8,128)(2,1)S(1)} %pad_maximum_fusion.refs_0_), channel_id=1, source_target_pairs={{0,8},{4,12},{8,0},{12,4},{1,9},{5,13},{9,1},{13,5},{2,10},{6,14},... | collective-permute-start | bytes 983048 | tf_op jit(solution)/shard_map/hidden/ppermute | solution.py:325
  75.1 1.9 %collective-permute-start.9 = (bf16[2,2,16,2560]{3,2,1,0:T(8,128)(2,1)S(1)}, bf16[2,2,16,2560]{3,2,1,0:T(8,128)(2,1)S(1)}, u32[]{:S(2)}, u32[]{:S(2)}) collective-permute-start(bf16[2,2,16,2560]{3,2,1,0:T(8,128)(2,1)S(1)} %pad_maximum_fusion.refs_0_), channel_id=1, source_target_pairs={{0,4},{4,8},{8,12},{12,0},{1,5},{5,9},{9,13},{13,1},{2,6},{6,10},{... | collective-permute-start | bytes 983048 | tf_op jit(solution)/shard_map/hidden/ppermute | solution.py:325
  77.1 2.8 %collective-permute-done.3.v_ref = bf16[320,256]{1,0:T(8,128)(2,1)S(1)} collective-permute-done((bf16[320,256]{1,0:T(8,128)(2,1)S(1)}, bf16[320,256]{1,0:T(8,128)(2,1)S(1)}, u32[]{:S(2)}, u32[]{:S(2)}) %collective-permute-start.3) | collective-permute-done | bytes 163872 | tf_op jit(solution)/shard_map/hidden/ppermute | solution.py:41
  79.9 0.3 act_rows.1.own_a
  80.3 6.5 %collective-permute-start.4 = (bf16[4,2,2,16,320]{4,3,2,1,0:T(8,128)(2,1)S(1)}, bf16[4,2,2,16,320]{4,3,2,1,0:T(8,128)(2,1)S(1)}, u32[]{:S(2)}, u32[]{:S(2)}) collective-permute-start(bf16[4,2,2,16,320]{4,3,2,1,0:T(8,128)(2,1)S(1)} %act_rows.1.own_a), channel_id=1, source_target_pairs={{0,1},{1,0},{2,3},{3,2},{4,5},{5,4},{6,7},{7,6},{8,9},{9,8},{10,11... | collective-permute-start | bytes 491528 | tf_op jit(solution)/shard_map/merged/ppermute | solution.py:41
  86.8 0.1 pad_add_fusion.place
  86.8 0.0 collective-permute-done.5.got_w
  86.8 1.0 collective-permute-done.4.got_a
  87.8 1.9 %copy-done = bf16[5120,320]{0,1:T(8,128)(2,1)S(1)} copy-done((bf16[5120,320]{0,1:T(8,128)(2,1)S(1)}, bf16[5120,320]{0,1:T(8,128)(2,1)}, u32[]{:S(2)}) %copy-start) | copy-done | bytes 3276824
  89.7 3.8 %merged_part.1.grad_ref = bf16[4,2,2,16,2560]{4,3,2,1,0:T(8,128)(2,1)} custom-call(s32[1]{0:T(128)} %bitcast.1.core.place, bf16[4,2,2,16,320]{4,3,2,1,0:T(8,128)(2,1)S(1)} %act_rows.1.own_a, bf16[4,2,2,16,320]{4,3,2,1,0:T(8,128)(2,1)S(1)} %collective-permute-done.4.got_a, bf16[320,5120]{1,0:T(8,128)(2,1)S(1)} %bitcast.26, ...), custom_call_target="tpu_custom_call" | custom-call | flops 1 | bytes 1 | tf_op jit(solution)/shard_map/merged/merged_part/pallas_call | solution.py:166
  93.5 4.0 %all-to-all-start.2 = ((bf16[8,32,2560]{2,1,0:T(8,128)(2,1)}), bf16[8,32,2560]{2,1,0:T(8,128)(2,1)S(1)}, u32[]{:S(2)}, u32[]{:S(2)}) async-start(bf16[8,32,2560]{2,1,0:T(8,128)(2,1)} %bitcast.9), calls=%async_computation.2 | async-start | bytes 2621440 | tf_op jit(solution)/shard_map/merged/all_to_all | solution.py:330
  97.5 0.0 collective-permute-done.7.refs_1_
  97.5 0.0 collective-permute-done.8.refs_2_
  97.5 0.0 collective-permute-done.9.refs_3_
  97.5 2.2 %gain_terms.1 = f32[1,1280]{1,0:T(1,128)S(1)} custom-call(s32[2]{0:T(128)S(1)} %pad_add_fusion.place, bf16[4,2,2,16,2560]{4,3,2,1,0:T(8,128)(2,1)} %merged_part.1.grad_ref, bf16[2,2,16,2560]{3,2,1,0:T(8,128)(2,1)S(1)} %pad_maximum_fusion.refs_0_, bf16[2,2,16,2560]{3,2,1,0:T(8,128)(2,1)S(1)} %collective-permute-done.7.refs_1_, ...), custom_call_target="tpu_custom_call" | custom-call | flops 20000000000 | bytes 1 | tf_op jit(solution)/shard_map/merged/gain_terms/pallas_call | solution.py:245
  99.8 15.0 %psum.7 = f32[10,128]{1,0:T(8,128)S(1)} all-reduce(f32[10,128]{1,0:T(8,128)S(1)} %bitcast.34), channel_id=1, replica_groups=mesh['y'=8,'zl'=6,'x'=4,'zh'=2,'co'=2] {'y'}, use_global_device_ids=true, to_apply=%region_0.0 | all-reduce | flops 1280 | bytes 10240 | tf_op jit(solution)/shard_map/merged/psum | solution.py:335
  114.9 0.6 all-to-all-done.2
  115.4 0.1 sum_halves.1
  115.5 0.6 broadcast_in_dim.4
  116.2 11.6 %all-to-all-start.3 = ((f32[12,10,128]{2,1,0:T(8,128)}), f32[12,10,128]{2,1,0:T(8,128)S(1)}, u32[]{:S(2)}, u32[]{:S(2)}) async-start(f32[12,10,128]{2,1,0:T(8,128)} %broadcast_in_dim.4), calls=%async_computation.3 | async-start | bytes 196608 | tf_op jit(solution)/shard_map/gain/all_to_all | solution.py:287
  127.8 9.6 %collective-permute-start.10 = (bf16[2,16,2560]{2,1,0:T(8,128)(2,1)S(1)}, bf16[2,16,2560]{2,1,0:T(8,128)(2,1)S(1)}, u32[]{:S(2)}, u32[]{:S(2)}) collective-permute-start(bf16[2,16,2560]{2,1,0:T(8,128)(2,1)S(1)} %sum_halves.1), channel_id=1, source_target_pairs={{0,2},{2,0},{1,3},{3,1},{4,6},{6,4},{5,7},{7,5},{8,10},{10,8},{9,1... | collective-permute-start | bytes 491528 | tf_op jit(solution)/shard_map/merged/ppermute | solution.py:41
  137.5 0.0 all-to-all-done.3
  137.5 0.6 broadcast_in_dim.5
  138.1 11.4 %all-to-all-start.4 = ((f32[8,10,128]{2,1,0:T(8,128)}), f32[8,10,128]{2,1,0:T(8,128)S(1)}, u32[]{:S(2)}, u32[]{:S(2)}) async-start(f32[8,10,128]{2,1,0:T(8,128)} %broadcast_in_dim.5), calls=%async_computation.4 | async-start | bytes 131072 | tf_op jit(solution)/shard_map/gain/all_to_all | solution.py:287
  149.5 0.0 collective-permute-done.10.got_ref
  149.5 0.9 norm_part.1
  150.5 3.9 %all-to-all-done.4 = f32[8,10,128]{2,1,0:T(8,128)S(1)} async-done(((f32[8,10,128]{2,1,0:T(8,128)}), f32[8,10,128]{2,1,0:T(8,128)S(1)}, u32[]{:S(2)}, u32[]{:S(2)}) %all-to-all-start.4) | async-done | bytes 40992 | tf_op jit(solution)/shard_map/gain/all_to_all | solution.py:287
  154.4 0.6 multiply_bitcast_fusion
  (15 shorter events, 0.1 us)
Async XLA Ops:
  0.6 40.0 %collective-permute-start = (bf16[5120,512]{1,0:T(8,128)(2,1)}, bf16[5120,512]{1,0:T(8,128)(2,1)}, u32[]{:S(2)}, u32[]{:S(2)}) collective-permute-start(bf16[5120,512]{1,0:T(8,128)(2,1)} %param.10), channel_id=1, source_target_pairs={{0,1},{1,0},{2,3},{3,2},{4,5},{5,4},{6,7},{7,6},{8,9},{9,8},{10,11... | collective-permute-start | bytes 15728648 | tf_op jit(solution)/shard_map/weights/ppermute | solution.py:41
  14.8 21.8 %all-to-all-start = ((bf16[16,16,512]{2,1,0:T(8,128)(2,1)}), bf16[16,16,512]{2,1,0:T(8,128)(2,1)S(1)}, u32[]{:S(2)}, u32[]{:S(2)}) async-start(bf16[16,16,512]{2,1,0:T(8,128)(2,1)} %bitcast.22), calls=%async_computation | async-start | bytes 524288 | tf_op jit(solution)/shard_map/tokens/all_to_all | solution.py:301
  22.8 3.5 %collective-permute-start.1 = (bf16[16,5120]{1,0:T(8,128)(2,1)}, bf16[16,5120]{1,0:T(8,128)(2,1)S(1)}, u32[]{:S(2)}, u32[]{:S(2)}) collective-permute-start(bf16[16,5120]{1,0:T(8,128)(2,1)} %patch_ref.1), channel_id=1, source_target_pairs={{0,1},{1,0},{2,3},{3,2},{4,5},{5,4},{6,7},{7,6},{8,9},{9,8},{10,11... | collective-permute-start | bytes 491528 | tf_op jit(solution)/shard_map/tokens/ppermute | solution.py:41
  36.6 4.1 %collective-permute-start.2 = (bf16[256,512]{1,0:T(8,128)(2,1)S(1)}, bf16[256,512]{1,0:T(8,128)(2,1)S(1)}, u32[]{:S(2)}, u32[]{:S(2)}) collective-permute-start(bf16[256,512]{1,0:T(8,128)(2,1)S(1)} %bitcast.27), channel_id=1, source_target_pairs={{0,1},{1,0},{2,3},{3,2},{4,5},{5,4},{6,7},{7,6},{8,9},{9,8},{10,11... | collective-permute-start | bytes 786440 | tf_op jit(solution)/shard_map/tokens/ppermute | solution.py:41
  40.7 11.1 %copy-start.1 = (bf16[16,5120]{1,0:T(8,128)(2,1)S(1)}, bf16[16,5120]{1,0:T(8,128)(2,1)}, u32[]{:S(2)}) copy-start(bf16[16,5120]{1,0:T(8,128)(2,1)} %patch_ref.1) | copy-start | bytes 491524
  40.7 13.1 %copy-start.3 = (bf16[320,256]{1,0:T(8,128)(2,1)S(1)}, bf16[320,256]{1,0:T(8,128)(2,1)}, u32[]{:S(2)}) copy-start(bf16[320,256]{1,0:T(8,128)(2,1)} %param.8) | copy-start | bytes 491524
  46.0 21.2 %all-to-all-start.1 = ((bf16[4,2,320,256]{3,2,1,0:T(8,128)(2,1)}), bf16[4,2,320,256]{3,2,1,0:T(8,128)(2,1)S(1)}, u32[]{:S(2)}, u32[]{:S(2)}) async-start(bf16[4,2,320,256]{3,2,1,0:T(8,128)(2,1)} %hidden_part.1), calls=%async_computation.1 | async-start | bytes 2621440 | tf_op jit(solution)/shard_map/hidden/all_to_all | solution.py:317
  49.5 37.3 %collective-permute-start.5 = (bf16[320,5120]{1,0:T(8,128)(2,1)}, bf16[320,5120]{1,0:T(8,128)(2,1)}, u32[]{:S(2)}, u32[]{:S(2)}) collective-permute-start(bf16[320,5120]{1,0:T(8,128)(2,1)} %bitcast.25), channel_id=1, source_target_pairs={{0,1},{1,0},{2,3},{3,2},{4,5},{5,4},{6,7},{7,6},{8,9},{9,8},{10,11... | collective-permute-start | bytes 9830408 | tf_op jit(solution)/shard_map/hidden/ppermute | solution.py:41
  51.8 17.3 %collective-permute-start.6 = (bf16[2,16,2560]{2,1,0:T(8,128)(2,1)S(1)}, bf16[2,16,2560]{2,1,0:T(8,128)(2,1)S(1)}, u32[]{:S(2)}, u32[]{:S(2)}) collective-permute-start(bf16[2,16,2560]{2,1,0:T(8,128)(2,1)S(1)} %pack_patches.1), channel_id=1, source_target_pairs={{0,2},{2,0},{1,3},{3,1},{4,6},{6,4},{5,7},{7,5},{8,10},{10,8},{9,1... | collective-permute-start | bytes 491528 | tf_op jit(solution)/shard_map/hidden/ppermute | solution.py:41
  67.2 12.7 %collective-permute-start.3 = (bf16[320,256]{1,0:T(8,128)(2,1)S(1)}, bf16[320,256]{1,0:T(8,128)(2,1)S(1)}, u32[]{:S(2)}, u32[]{:S(2)}) collective-permute-start(bf16[320,256]{1,0:T(8,128)(2,1)S(1)} %sum_parts.1), channel_id=1, source_target_pairs={{0,2},{2,0},{1,3},{3,1},{4,6},{6,4},{5,7},{7,5},{8,10},{10,8},{9,1... | collective-permute-start | bytes 491528 | tf_op jit(solution)/shard_map/hidden/ppermute | solution.py:41
  69.2 10.7 %copy-start.2 = (s32[256]{0:T(256)S(1)}, s32[256]{0:T(256)}, u32[]{:S(2)}) copy-start(s32[256]{0:T(256)} %param.13) | copy-start | bytes 3076
  69.2 28.3 %collective-permute-start.7 = (bf16[2,2,16,2560]{3,2,1,0:T(8,128)(2,1)S(1)}, bf16[2,2,16,2560]{3,2,1,0:T(8,128)(2,1)S(1)}, u32[]{:S(2)}, u32[]{:S(2)}) collective-permute-start(bf16[2,2,16,2560]{3,2,1,0:T(8,128)(2,1)S(1)} %pad_maximum_fusion.refs_0_), channel_id=1, source_target_pairs={{0,12},{4,0},{8,4},{12,8},{1,13},{5,1},{9,5},{13,9},{2,14},{6,2},{... | collective-permute-start | bytes 983048 | tf_op jit(solution)/shard_map/hidden/ppermute | solution.py:325
  72.0 25.5 %collective-permute-start.8 = (bf16[2,2,16,2560]{3,2,1,0:T(8,128)(2,1)S(1)}, bf16[2,2,16,2560]{3,2,1,0:T(8,128)(2,1)S(1)}, u32[]{:S(2)}, u32[]{:S(2)}) collective-permute-start(bf16[2,2,16,2560]{3,2,1,0:T(8,128)(2,1)S(1)} %pad_maximum_fusion.refs_0_), channel_id=1, source_target_pairs={{0,8},{4,12},{8,0},{12,4},{1,9},{5,13},{9,1},{13,5},{2,10},{6,14},... | collective-permute-start | bytes 983048 | tf_op jit(solution)/shard_map/hidden/ppermute | solution.py:325
  75.1 22.4 %collective-permute-start.9 = (bf16[2,2,16,2560]{3,2,1,0:T(8,128)(2,1)S(1)}, bf16[2,2,16,2560]{3,2,1,0:T(8,128)(2,1)S(1)}, u32[]{:S(2)}, u32[]{:S(2)}) collective-permute-start(bf16[2,2,16,2560]{3,2,1,0:T(8,128)(2,1)S(1)} %pad_maximum_fusion.refs_0_), channel_id=1, source_target_pairs={{0,4},{4,8},{8,12},{12,0},{1,5},{5,9},{9,13},{13,1},{2,6},{6,10},{... | collective-permute-start | bytes 983048 | tf_op jit(solution)/shard_map/hidden/ppermute | solution.py:325
  80.3 7.5 %collective-permute-start.4 = (bf16[4,2,2,16,320]{4,3,2,1,0:T(8,128)(2,1)S(1)}, bf16[4,2,2,16,320]{4,3,2,1,0:T(8,128)(2,1)S(1)}, u32[]{:S(2)}, u32[]{:S(2)}) collective-permute-start(bf16[4,2,2,16,320]{4,3,2,1,0:T(8,128)(2,1)S(1)} %act_rows.1.own_a), channel_id=1, source_target_pairs={{0,1},{1,0},{2,3},{3,2},{4,5},{5,4},{6,7},{7,6},{8,9},{9,8},{10,11... | collective-permute-start | bytes 491528 | tf_op jit(solution)/shard_map/merged/ppermute | solution.py:41
  87.8 1.9 %copy-start = (bf16[5120,320]{0,1:T(8,128)(2,1)S(1)}, bf16[5120,320]{0,1:T(8,128)(2,1)}, u32[]{:S(2)}) copy-start(bf16[5120,320]{0,1:T(8,128)(2,1)} %param.9) | copy-start | bytes 9830404
  93.5 21.9 %all-to-all-start.2 = ((bf16[8,32,2560]{2,1,0:T(8,128)(2,1)}), bf16[8,32,2560]{2,1,0:T(8,128)(2,1)S(1)}, u32[]{:S(2)}, u32[]{:S(2)}) async-start(bf16[8,32,2560]{2,1,0:T(8,128)(2,1)} %bitcast.9), calls=%async_computation.2 | async-start | bytes 2621440 | tf_op jit(solution)/shard_map/merged/all_to_all | solution.py:330
  97.5 39.9 %copy-start.4 = (f32[1280]{0:T(1024)S(1)}, f32[1280]{0:T(1024)}, u32[]{:S(2)}) copy-start(f32[1280]{0:T(1024)} %param.12) | copy-start | bytes 15364
  116.2 21.3 %all-to-all-start.3 = ((f32[12,10,128]{2,1,0:T(8,128)}), f32[12,10,128]{2,1,0:T(8,128)S(1)}, u32[]{:S(2)}, u32[]{:S(2)}) async-start(f32[12,10,128]{2,1,0:T(8,128)} %broadcast_in_dim.4), calls=%async_computation.3 | async-start | bytes 196608 | tf_op jit(solution)/shard_map/gain/all_to_all | solution.py:287
  127.8 21.7 %collective-permute-start.10 = (bf16[2,16,2560]{2,1,0:T(8,128)(2,1)S(1)}, bf16[2,16,2560]{2,1,0:T(8,128)(2,1)S(1)}, u32[]{:S(2)}, u32[]{:S(2)}) collective-permute-start(bf16[2,16,2560]{2,1,0:T(8,128)(2,1)S(1)} %sum_halves.1), channel_id=1, source_target_pairs={{0,2},{2,0},{1,3},{3,1},{4,6},{6,4},{5,7},{7,5},{8,10},{10,8},{9,1... | collective-permute-start | bytes 491528 | tf_op jit(solution)/shard_map/merged/ppermute | solution.py:41
  138.1 16.2 %all-to-all-start.4 = ((f32[8,10,128]{2,1,0:T(8,128)}), f32[8,10,128]{2,1,0:T(8,128)S(1)}, u32[]{:S(2)}, u32[]{:S(2)}) async-start(f32[8,10,128]{2,1,0:T(8,128)} %broadcast_in_dim.5), calls=%async_computation.4 | async-start | bytes 131072 | tf_op jit(solution)/shard_map/gain/all_to_all | solution.py:287

commit v11 on v10

--- a/solution.py
+++ b/solution.py
@@ -172,7 +172,7 @@
             out_specs=pl.BlockSpec(shape + (cols // steps,), lambda i, s: (0, 0, 0, 0, i)),
         ),
         out_shape=jax.ShapeDtypeStruct(shape + (cols,), BF16),
-        compiler_params=params(),
+        compiler_params=params(52),
         cost_estimate=cost(),
         name="merged_part",
     )(core, *acts, *weights)

time: 156 us -> 154 us (0.987)
  local copies, waits for them, and re-layouts: 4.92 us -> 2.99 us
    unnamed x10 -> x8, local copies, waits for them, and re-layouts: 1.94 us -> 0.02 us
where the time goes in v11:
time: 154 us; the launch traced here: 153 us
  starting transfers between devices  86.1 us (56%)
  waiting for transfers between devices  34.3 us (22%)
  blocking collectives  15 us (10%)
  Pallas kernels  13 us (8%)
  local copies, waits for them, and re-layouts  2.99 us (2%)
    ppermute x8, starting transfers between devices, swap(): return lax.ppermute(value, axis, [(0, 1), (1, 0)])  39.6 us
    all_to_all x2, starting transfers between devices, sum_over(): return jnp.sum(lax.all_to_all(rows, axes, 0, 0, tiled=True), axis=0)  23 us
    psum x1, blocking collectives, local(): terms = lax.psum(terms, 'y')  15 us
    all_to_all x1, waiting for transfers between devices, local(): parts = lax.all_to_all(sums, 'x', 0, 0, tiled=True)  13.2 us
    all_to_all x1, waiting for transfers between devices, local(): lax.all_to_all(outgoing, CTX, 0, 0, tiled=True).reshape(group, depth // ctx)  10.2 us
    all_to_all x1, starting transfers between devices, local(): lax.all_to_all(outgoing, CTX, 0, 0, tiled=True).reshape(group, depth // ctx)  8.08 us
    ppermute x3, starting transfers between devices, local(): lax.ppermute(patches, 'x', [(i, (i - d) % NX) for i in range(NX)])  7.81 us
    ppermute x8, waiting for transfers between devices, swap(): return lax.ppermute(value, axis, [(0, 1), (1, 0)])  6.41 us
  transfers between devices with their start and end apart: 16, of which 8 were waited for; matrix products, arithmetic and copies ran while one was open for 2% of the time, Pallas kernels for 5%

profile of v11, /device:TPU:1, one launch (start us, length us, event | category | flops | bytes accessed | tf_op | source)
XLA Modules:
  0.0 153.3 jit_solution(6651485444066445991)
XLA Ops:
  0.6 12.4 %collective-permute-start = (bf16[5120,512]{1,0:T(8,128)(2,1)}, bf16[5120,512]{1,0:T(8,128)(2,1)}, u32[]{:S(2)}, u32[]{:S(2)}) collective-permute-start(bf16[5120,512]{1,0:T(8,128)(2,1)} %param.10), channel_id=1, source_target_pairs={{0,1},{1,0},{2,3},{3,2},{4,5},{5,4},{6,7},{7,6},{8,9},{9,8},{10,11... | collective-permute-start | bytes 15728648 | tf_op jit(solution)/shard_map/weights/ppermute | solution.py:41
  13.1 1.7 %copy.18 = bf16[2,16,8,512]{3,2,0,1:T(8,128)(2,1)} copy(bf16[2,16,8,512]{3,2,1,0:T(8,128)(2,1)} %bitcast.32) | data formatting | bytes 524288 | tf_op jit(solution)/shard_map/tokens/reshape | solution.py:300
  14.8 8.1 %all-to-all-start = ((bf16[16,16,512]{2,1,0:T(8,128)(2,1)}), bf16[16,16,512]{2,1,0:T(8,128)(2,1)S(1)}, u32[]{:S(2)}, u32[]{:S(2)}) async-start(bf16[16,16,512]{2,1,0:T(8,128)(2,1)} %bitcast.22), calls=%async_computation | async-start | bytes 524288 | tf_op jit(solution)/shard_map/tokens/all_to_all | solution.py:301
  22.8 2.0 %collective-permute-start.1 = (bf16[16,5120]{1,0:T(8,128)(2,1)}, bf16[16,5120]{1,0:T(8,128)(2,1)S(1)}, u32[]{:S(2)}, u32[]{:S(2)}) collective-permute-start(bf16[16,5120]{1,0:T(8,128)(2,1)} %patch_ref.1), channel_id=1, source_target_pairs={{0,1},{1,0},{2,3},{3,2},{4,5},{5,4},{6,7},{7,6},{8,9},{9,8},{10,11... | collective-permute-start | bytes 491528 | tf_op jit(solution)/shard_map/tokens/ppermute | solution.py:41
  24.9 1.5 collective-permute-done.1.got_ref
  26.3 10.2 %all-to-all-done = bf16[16,16,512]{2,1,0:T(8,128)(2,1)S(1)} async-done(((bf16[16,16,512]{2,1,0:T(8,128)(2,1)}), bf16[16,16,512]{2,1,0:T(8,128)(2,1)S(1)}, u32[]{:S(2)}, u32[]{:S(2)}) %all-to-all-start) | async-done | bytes 262176 | tf_op jit(solution)/shard_map/tokens/all_to_all | solution.py:301
  36.6 2.9 %collective-permute-start.2 = (bf16[256,512]{1,0:T(8,128)(2,1)S(1)}, bf16[256,512]{1,0:T(8,128)(2,1)S(1)}, u32[]{:S(2)}, u32[]{:S(2)}) collective-permute-start(bf16[256,512]{1,0:T(8,128)(2,1)S(1)} %bitcast.25), channel_id=1, source_target_pairs={{0,1},{1,0},{2,3},{3,2},{4,5},{5,4},{6,7},{7,6},{8,9},{9,8},{10,11... | collective-permute-start | bytes 786440 | tf_op jit(solution)/shard_map/tokens/ppermute | solution.py:41
  39.5 1.1 collective-permute-done.2.got_t
  40.6 0.0 collective-permute-done
  40.7 5.3 %hidden_part.1 = bf16[4,2,320,256]{3,2,1,0:T(8,128)(2,1)} custom-call(s32[1]{0:T(128)} %bitcast.1.core.place, bf16[4,2,2,320,512]{4,3,2,1,0:T(8,128)(2,1)} %bitcast.29, bf16[4,2,2,320,512]{4,3,2,1,0:T(8,128)(2,1)} %bitcast.3.got_w, bf16[256,512]{1,0:T(8,128)(2,1)S(1)} %bitcast.26, bf16[256,512]{1,0:T(8,128)(2,1)S(1)} %collective-permute-done.2.got_t), custom_call_target="tpu_custom_call" | custom-call | flops 1 | bytes 1 | tf_op jit(solution)/shard_map/hidden/hidden_part/pallas_call | solution.py:65
  45.9 3.5 %all-to-all-start.1 = ((bf16[4,2,320,256]{3,2,1,0:T(8,128)(2,1)}), bf16[4,2,320,256]{3,2,1,0:T(8,128)(2,1)S(1)}, u32[]{:S(2)}, u32[]{:S(2)}) async-start(bf16[4,2,320,256]{3,2,1,0:T(8,128)(2,1)} %hidden_part.1), calls=%async_computation.1 | async-start | bytes 2621440 | tf_op jit(solution)/shard_map/hidden/all_to_all | solution.py:317
  49.5 2.3 %collective-permute-start.5 = (bf16[320,5120]{1,0:T(8,128)(2,1)}, bf16[320,5120]{1,0:T(8,128)(2,1)}, u32[]{:S(2)}, u32[]{:S(2)}) collective-permute-start(bf16[320,5120]{1,0:T(8,128)(2,1)} %bitcast.30), channel_id=1, source_target_pairs={{0,1},{1,0},{2,3},{3,2},{4,5},{5,4},{6,7},{7,6},{8,9},{9,8},{10,11... | collective-permute-start | bytes 9830408 | tf_op jit(solution)/shard_map/hidden/ppermute | solution.py:41
  51.8 1.9 %collective-permute-start.6 = (bf16[2,16,2560]{2,1,0:T(8,128)(2,1)S(1)}, bf16[2,16,2560]{2,1,0:T(8,128)(2,1)S(1)}, u32[]{:S(2)}, u32[]{:S(2)}) collective-permute-start(bf16[2,16,2560]{2,1,0:T(8,128)(2,1)S(1)} %pack_patches.1), channel_id=1, source_target_pairs={{0,2},{2,0},{1,3},{3,1},{4,6},{6,4},{5,7},{7,5},{8,10},{10,8},{9,1... | collective-permute-start | bytes 491528 | tf_op jit(solution)/shard_map/hidden/ppermute | solution.py:41
  53.7 0.0 copy-done.2
  53.7 0.1 fusion.3.slope_ref
  53.9 13.2 %all-to-all-done.1.v_ref = bf16[4,2,320,256]{3,2,1,0:T(8,128)(2,1)S(1)} async-done(((bf16[4,2,320,256]{3,2,1,0:T(8,128)(2,1)}), bf16[4,2,320,256]{3,2,1,0:T(8,128)(2,1)S(1)}, u32[]{:S(2)}, u32[]{:S(2)}) %all-to-all-start.1) | async-done | bytes 1310752 | tf_op jit(solution)/shard_map/hidden/all_to_all | solution.py:317
  67.1 0.1 sum_parts.1
  67.2 1.9 %collective-permute-start.3 = (bf16[320,256]{1,0:T(8,128)(2,1)S(1)}, bf16[320,256]{1,0:T(8,128)(2,1)S(1)}, u32[]{:S(2)}, u32[]{:S(2)}) collective-permute-start(bf16[320,256]{1,0:T(8,128)(2,1)S(1)} %sum_parts.1), channel_id=1, source_target_pairs={{0,2},{2,0},{1,3},{3,1},{4,6},{6,4},{5,7},{7,5},{8,10},{10,8},{9,1... | collective-permute-start | bytes 491528 | tf_op jit(solution)/shard_map/hidden/ppermute | solution.py:41
  69.1 0.0 collective-permute-done.6
  69.2 0.0 copy-start.1
  69.2 2.8 %collective-permute-start.7 = (bf16[2,2,16,2560]{3,2,1,0:T(8,128)(2,1)S(1)}, bf16[2,2,16,2560]{3,2,1,0:T(8,128)(2,1)S(1)}, u32[]{:S(2)}, u32[]{:S(2)}) collective-permute-start(bf16[2,2,16,2560]{3,2,1,0:T(8,128)(2,1)S(1)} %pad_maximum_fusion.refs_0_), channel_id=1, source_target_pairs={{0,12},{4,0},{8,4},{12,8},{1,13},{5,1},{9,5},{13,9},{2,14},{6,2},{... | collective-permute-start | bytes 983048 | tf_op jit(solution)/shard_map/hidden/ppermute | solution.py:325
  72.0 3.1 %collective-permute-start.8 = (bf16[2,2,16,2560]{3,2,1,0:T(8,128)(2,1)S(1)}, bf16[2,2,16,2560]{3,2,1,0:T(8,128)(2,1)S(1)}, u32[]{:S(2)}, u32[]{:S(2)}) collective-permute-start(bf16[2,2,16,2560]{3,2,1,0:T(8,128)(2,1)S(1)} %pad_maximum_fusion.refs_0_), channel_id=1, source_target_pairs={{0,8},{4,12},{8,0},{12,4},{1,9},{5,13},{9,1},{13,5},{2,10},{6,14},... | collective-permute-start | bytes 983048 | tf_op jit(solution)/shard_map/hidden/ppermute | solution.py:325
  75.1 1.9 %collective-permute-start.9 = (bf16[2,2,16,2560]{3,2,1,0:T(8,128)(2,1)S(1)}, bf16[2,2,16,2560]{3,2,1,0:T(8,128)(2,1)S(1)}, u32[]{:S(2)}, u32[]{:S(2)}) collective-permute-start(bf16[2,2,16,2560]{3,2,1,0:T(8,128)(2,1)S(1)} %pad_maximum_fusion.refs_0_), channel_id=1, source_target_pairs={{0,4},{4,8},{8,12},{12,0},{1,5},{5,9},{9,13},{13,1},{2,6},{6,10},{... | collective-permute-start | bytes 983048 | tf_op jit(solution)/shard_map/hidden/ppermute | solution.py:325
  77.0 2.8 %collective-permute-done.3.v_ref = bf16[320,256]{1,0:T(8,128)(2,1)S(1)} collective-permute-done((bf16[320,256]{1,0:T(8,128)(2,1)S(1)}, bf16[320,256]{1,0:T(8,128)(2,1)S(1)}, u32[]{:S(2)}, u32[]{:S(2)}) %collective-permute-start.3) | collective-permute-done | bytes 163872 | tf_op jit(solution)/shard_map/hidden/ppermute | solution.py:41
  79.9 0.3 act_rows.1.own_a
  80.3 6.5 %collective-permute-start.4 = (bf16[4,2,2,16,320]{4,3,2,1,0:T(8,128)(2,1)S(1)}, bf16[4,2,2,16,320]{4,3,2,1,0:T(8,128)(2,1)S(1)}, u32[]{:S(2)}, u32[]{:S(2)}) collective-permute-start(bf16[4,2,2,16,320]{4,3,2,1,0:T(8,128)(2,1)S(1)} %act_rows.1.own_a), channel_id=1, source_target_pairs={{0,1},{1,0},{2,3},{3,2},{4,5},{5,4},{6,7},{7,6},{8,9},{9,8},{10,11... | collective-permute-start | bytes 491528 | tf_op jit(solution)/shard_map/merged/ppermute | solution.py:41
  86.7 0.1 pad_add_fusion.place
  86.8 0.0 collective-permute-done.5.got_w
  86.8 1.0 collective-permute-done.4.got_a
  87.8 4.0 %merged_part.1.grad_ref = bf16[4,2,2,16,2560]{4,3,2,1,0:T(8,128)(2,1)} custom-call(s32[1]{0:T(128)} %bitcast.1.core.place, bf16[4,2,2,16,320]{4,3,2,1,0:T(8,128)(2,1)S(1)} %act_rows.1.own_a, bf16[4,2,2,16,320]{4,3,2,1,0:T(8,128)(2,1)S(1)} %collective-permute-done.4.got_a, bf16[320,5120]{1,0:T(8,128)(2,1)} %bitcast.31, ...), custom_call_target="tpu_custom_call" | custom-call | flops 1 | bytes 1 | tf_op jit(solution)/shard_map/merged/merged_part/pallas_call | solution.py:166
  91.8 4.0 %all-to-all-start.2 = ((bf16[8,32,2560]{2,1,0:T(8,128)(2,1)}), bf16[8,32,2560]{2,1,0:T(8,128)(2,1)S(1)}, u32[]{:S(2)}, u32[]{:S(2)}) async-start(bf16[8,32,2560]{2,1,0:T(8,128)(2,1)} %bitcast.9), calls=%async_computation.2 | async-start | bytes 2621440 | tf_op jit(solution)/shard_map/merged/all_to_all | solution.py:330
  95.8 0.0 collective-permute-done.7.refs_1_
  95.8 0.0 collective-permute-done.8.refs_2_
  95.8 0.0 collective-permute-done.9.refs_3_
  95.8 2.2 %gain_terms.1 = f32[1,1280]{1,0:T(1,128)S(1)} custom-call(s32[2]{0:T(128)S(1)} %pad_add_fusion.place, bf16[4,2,2,16,2560]{4,3,2,1,0:T(8,128)(2,1)} %merged_part.1.grad_ref, bf16[2,2,16,2560]{3,2,1,0:T(8,128)(2,1)S(1)} %pad_maximum_fusion.refs_0_, bf16[2,2,16,2560]{3,2,1,0:T(8,128)(2,1)S(1)} %collective-permute-done.7.refs_1_, ...), custom_call_target="tpu_custom_call" | custom-call | flops 20000000000 | bytes 1 | tf_op jit(solution)/shard_map/merged/gain_terms/pallas_call | solution.py:245
  98.1 15.0 %psum.7 = f32[10,128]{1,0:T(8,128)S(1)} all-reduce(f32[10,128]{1,0:T(8,128)S(1)} %bitcast.34), channel_id=1, replica_groups=mesh['y'=8,'zl'=6,'x'=4,'zh'=2,'co'=2] {'y'}, use_global_device_ids=true, to_apply=%region_0.0 | all-reduce | flops 1280 | bytes 10240 | tf_op jit(solution)/shard_map/merged/psum | solution.py:335
  113.2 0.6 all-to-all-done.2
  113.7 0.1 sum_halves.1
  113.8 0.6 broadcast_in_dim.4
  114.4 11.6 %all-to-all-start.3 = ((f32[12,10,128]{2,1,0:T(8,128)}), f32[12,10,128]{2,1,0:T(8,128)S(1)}, u32[]{:S(2)}, u32[]{:S(2)}) async-start(f32[12,10,128]{2,1,0:T(8,128)} %broadcast_in_dim.4), calls=%async_computation.3 | async-start | bytes 196608 | tf_op jit(solution)/shard_map/gain/all_to_all | solution.py:287
  126.1 9.6 %collective-permute-start.10 = (bf16[2,16,2560]{2,1,0:T(8,128)(2,1)S(1)}, bf16[2,16,2560]{2,1,0:T(8,128)(2,1)S(1)}, u32[]{:S(2)}, u32[]{:S(2)}) collective-permute-start(bf16[2,16,2560]{2,1,0:T(8,128)(2,1)S(1)} %sum_halves.1), channel_id=1, source_target_pairs={{0,2},{2,0},{1,3},{3,1},{4,6},{6,4},{5,7},{7,5},{8,10},{10,8},{9,1... | collective-permute-start | bytes 491528 | tf_op jit(solution)/shard_map/merged/ppermute | solution.py:41
  135.8 0.0 all-to-all-done.3
  135.8 0.6 broadcast_in_dim.5
  136.4 11.4 %all-to-all-start.4 = ((f32[8,10,128]{2,1,0:T(8,128)}), f32[8,10,128]{2,1,0:T(8,128)S(1)}, u32[]{:S(2)}, u32[]{:S(2)}) async-start(f32[8,10,128]{2,1,0:T(8,128)} %broadcast_in_dim.5), calls=%async_computation.4 | async-start | bytes 131072 | tf_op jit(solution)/shard_map/gain/all_to_all | solution.py:287
  147.8 0.0 collective-permute-done.10.got_ref
  147.8 0.9 norm_part.1
  148.8 3.9 %all-to-all-done.4 = f32[8,10,128]{2,1,0:T(8,128)S(1)} async-done(((f32[8,10,128]{2,1,0:T(8,128)}), f32[8,10,128]{2,1,0:T(8,128)S(1)}, u32[]{:S(2)}, u32[]{:S(2)}) %all-to-all-start.4) | async-done | bytes 40992 | tf_op jit(solution)/shard_map/gain/all_to_all | solution.py:287
  152.7 0.6 multiply_bitcast_fusion
  (13 shorter events, 0.1 us)
Async XLA Ops:
  0.6 40.0 %collective-permute-start = (bf16[5120,512]{1,0:T(8,128)(2,1)}, bf16[5120,512]{1,0:T(8,128)(2,1)}, u32[]{:S(2)}, u32[]{:S(2)}) collective-permute-start(bf16[5120,512]{1,0:T(8,128)(2,1)} %param.10), channel_id=1, source_target_pairs={{0,1},{1,0},{2,3},{3,2},{4,5},{5,4},{6,7},{7,6},{8,9},{9,8},{10,11... | collective-permute-start | bytes 15728648 | tf_op jit(solution)/shard_map/weights/ppermute | solution.py:41
  14.8 21.8 %all-to-all-start = ((bf16[16,16,512]{2,1,0:T(8,128)(2,1)}), bf16[16,16,512]{2,1,0:T(8,128)(2,1)S(1)}, u32[]{:S(2)}, u32[]{:S(2)}) async-start(bf16[16,16,512]{2,1,0:T(8,128)(2,1)} %bitcast.22), calls=%async_computation | async-start | bytes 524288 | tf_op jit(solution)/shard_map/tokens/all_to_all | solution.py:301
  22.8 3.5 %collective-permute-start.1 = (bf16[16,5120]{1,0:T(8,128)(2,1)}, bf16[16,5120]{1,0:T(8,128)(2,1)S(1)}, u32[]{:S(2)}, u32[]{:S(2)}) collective-permute-start(bf16[16,5120]{1,0:T(8,128)(2,1)} %patch_ref.1), channel_id=1, source_target_pairs={{0,1},{1,0},{2,3},{3,2},{4,5},{5,4},{6,7},{7,6},{8,9},{9,8},{10,11... | collective-permute-start | bytes 491528 | tf_op jit(solution)/shard_map/tokens/ppermute | solution.py:41
  36.6 4.1 %collective-permute-start.2 = (bf16[256,512]{1,0:T(8,128)(2,1)S(1)}, bf16[256,512]{1,0:T(8,128)(2,1)S(1)}, u32[]{:S(2)}, u32[]{:S(2)}) collective-permute-start(bf16[256,512]{1,0:T(8,128)(2,1)S(1)} %bitcast.25), channel_id=1, source_target_pairs={{0,1},{1,0},{2,3},{3,2},{4,5},{5,4},{6,7},{7,6},{8,9},{9,8},{10,11... | collective-permute-start | bytes 786440 | tf_op jit(solution)/shard_map/tokens/ppermute | solution.py:41
  40.6 11.1 %copy-start = (bf16[16,5120]{1,0:T(8,128)(2,1)S(1)}, bf16[16,5120]{1,0:T(8,128)(2,1)}, u32[]{:S(2)}) copy-start(bf16[16,5120]{1,0:T(8,128)(2,1)} %patch_ref.1) | copy-start | bytes 491524
  40.6 13.1 %copy-start.2 = (bf16[320,256]{1,0:T(8,128)(2,1)S(1)}, bf16[320,256]{1,0:T(8,128)(2,1)}, u32[]{:S(2)}) copy-start(bf16[320,256]{1,0:T(8,128)(2,1)} %param.8) | copy-start | bytes 491524
  45.9 21.2 %all-to-all-start.1 = ((bf16[4,2,320,256]{3,2,1,0:T(8,128)(2,1)}), bf16[4,2,320,256]{3,2,1,0:T(8,128)(2,1)S(1)}, u32[]{:S(2)}, u32[]{:S(2)}) async-start(bf16[4,2,320,256]{3,2,1,0:T(8,128)(2,1)} %hidden_part.1), calls=%async_computation.1 | async-start | bytes 2621440 | tf_op jit(solution)/shard_map/hidden/all_to_all | solution.py:317
  49.5 37.4 %collective-permute-start.5 = (bf16[320,5120]{1,0:T(8,128)(2,1)}, bf16[320,5120]{1,0:T(8,128)(2,1)}, u32[]{:S(2)}, u32[]{:S(2)}) collective-permute-start(bf16[320,5120]{1,0:T(8,128)(2,1)} %bitcast.30), channel_id=1, source_target_pairs={{0,1},{1,0},{2,3},{3,2},{4,5},{5,4},{6,7},{7,6},{8,9},{9,8},{10,11... | collective-permute-start | bytes 9830408 | tf_op jit(solution)/shard_map/hidden/ppermute | solution.py:41
  51.8 17.3 %collective-permute-start.6 = (bf16[2,16,2560]{2,1,0:T(8,128)(2,1)S(1)}, bf16[2,16,2560]{2,1,0:T(8,128)(2,1)S(1)}, u32[]{:S(2)}, u32[]{:S(2)}) collective-permute-start(bf16[2,16,2560]{2,1,0:T(8,128)(2,1)S(1)} %pack_patches.1), channel_id=1, source_target_pairs={{0,2},{2,0},{1,3},{3,1},{4,6},{6,4},{5,7},{7,5},{8,10},{10,8},{9,1... | collective-permute-start | bytes 491528 | tf_op jit(solution)/shard_map/hidden/ppermute | solution.py:41
  67.2 12.7 %collective-permute-start.3 = (bf16[320,256]{1,0:T(8,128)(2,1)S(1)}, bf16[320,256]{1,0:T(8,128)(2,1)S(1)}, u32[]{:S(2)}, u32[]{:S(2)}) collective-permute-start(bf16[320,256]{1,0:T(8,128)(2,1)S(1)} %sum_parts.1), channel_id=1, source_target_pairs={{0,2},{2,0},{1,3},{3,1},{4,6},{6,4},{5,7},{7,5},{8,10},{10,8},{9,1... | collective-permute-start | bytes 491528 | tf_op jit(solution)/shard_map/hidden/ppermute | solution.py:41
  69.2 10.7 %copy-start.1 = (s32[256]{0:T(256)S(1)}, s32[256]{0:T(256)}, u32[]{:S(2)}) copy-start(s32[256]{0:T(256)} %param.13) | copy-start | bytes 3076
  69.2 26.6 %collective-permute-start.7 = (bf16[2,2,16,2560]{3,2,1,0:T(8,128)(2,1)S(1)}, bf16[2,2,16,2560]{3,2,1,0:T(8,128)(2,1)S(1)}, u32[]{:S(2)}, u32[]{:S(2)}) collective-permute-start(bf16[2,2,16,2560]{3,2,1,0:T(8,128)(2,1)S(1)} %pad_maximum_fusion.refs_0_), channel_id=1, source_target_pairs={{0,12},{4,0},{8,4},{12,8},{1,13},{5,1},{9,5},{13,9},{2,14},{6,2},{... | collective-permute-start | bytes 983048 | tf_op jit(solution)/shard_map/hidden/ppermute | solution.py:325
  72.0 23.8 %collective-permute-start.8 = (bf16[2,2,16,2560]{3,2,1,0:T(8,128)(2,1)S(1)}, bf16[2,2,16,2560]{3,2,1,0:T(8,128)(2,1)S(1)}, u32[]{:S(2)}, u32[]{:S(2)}) collective-permute-start(bf16[2,2,16,2560]{3,2,1,0:T(8,128)(2,1)S(1)} %pad_maximum_fusion.refs_0_), channel_id=1, source_target_pairs={{0,8},{4,12},{8,0},{12,4},{1,9},{5,13},{9,1},{13,5},{2,10},{6,14},... | collective-permute-start | bytes 983048 | tf_op jit(solution)/shard_map/hidden/ppermute | solution.py:325
  75.1 20.7 %collective-permute-start.9 = (bf16[2,2,16,2560]{3,2,1,0:T(8,128)(2,1)S(1)}, bf16[2,2,16,2560]{3,2,1,0:T(8,128)(2,1)S(1)}, u32[]{:S(2)}, u32[]{:S(2)}) collective-permute-start(bf16[2,2,16,2560]{3,2,1,0:T(8,128)(2,1)S(1)} %pad_maximum_fusion.refs_0_), channel_id=1, source_target_pairs={{0,4},{4,8},{8,12},{12,0},{1,5},{5,9},{9,13},{13,1},{2,6},{6,10},{... | collective-permute-start | bytes 983048 | tf_op jit(solution)/shard_map/hidden/ppermute | solution.py:325
  80.3 7.5 %collective-permute-start.4 = (bf16[4,2,2,16,320]{4,3,2,1,0:T(8,128)(2,1)S(1)}, bf16[4,2,2,16,320]{4,3,2,1,0:T(8,128)(2,1)S(1)}, u32[]{:S(2)}, u32[]{:S(2)}) collective-permute-start(bf16[4,2,2,16,320]{4,3,2,1,0:T(8,128)(2,1)S(1)} %act_rows.1.own_a), channel_id=1, source_target_pairs={{0,1},{1,0},{2,3},{3,2},{4,5},{5,4},{6,7},{7,6},{8,9},{9,8},{10,11... | collective-permute-start | bytes 491528 | tf_op jit(solution)/shard_map/merged/ppermute | solution.py:41
  91.8 21.9 %all-to-all-start.2 = ((bf16[8,32,2560]{2,1,0:T(8,128)(2,1)}), bf16[8,32,2560]{2,1,0:T(8,128)(2,1)S(1)}, u32[]{:S(2)}, u32[]{:S(2)}) async-start(bf16[8,32,2560]{2,1,0:T(8,128)(2,1)} %bitcast.9), calls=%async_computation.2 | async-start | bytes 2621440 | tf_op jit(solution)/shard_map/merged/all_to_all | solution.py:330
  95.8 39.9 %copy-start.3 = (f32[1280]{0:T(1024)S(1)}, f32[1280]{0:T(1024)}, u32[]{:S(2)}) copy-start(f32[1280]{0:T(1024)} %param.12) | copy-start | bytes 15364
  114.4 21.3 %all-to-all-start.3 = ((f32[12,10,128]{2,1,0:T(8,128)}), f32[12,10,128]{2,1,0:T(8,128)S(1)}, u32[]{:S(2)}, u32[]{:S(2)}) async-start(f32[12,10,128]{2,1,0:T(8,128)} %broadcast_in_dim.4), calls=%async_computation.3 | async-start | bytes 196608 | tf_op jit(solution)/shard_map/gain/all_to_all | solution.py:287
  126.1 21.7 %collective-permute-start.10 = (bf16[2,16,2560]{2,1,0:T(8,128)(2,1)S(1)}, bf16[2,16,2560]{2,1,0:T(8,128)(2,1)S(1)}, u32[]{:S(2)}, u32[]{:S(2)}) collective-permute-start(bf16[2,16,2560]{2,1,0:T(8,128)(2,1)S(1)} %sum_halves.1), channel_id=1, source_target_pairs={{0,2},{2,0},{1,3},{3,1},{4,6},{6,4},{5,7},{7,5},{8,10},{10,8},{9,1... | collective-permute-start | bytes 491528 | tf_op jit(solution)/shard_map/merged/ppermute | solution.py:41
  136.4 16.2 %all-to-all-start.4 = ((f32[8,10,128]{2,1,0:T(8,128)}), f32[8,10,128]{2,1,0:T(8,128)S(1)}, u32[]{:S(2)}, u32[]{:S(2)}) async-start(f32[8,10,128]{2,1,0:T(8,128)} %broadcast_in_dim.5), calls=%async_computation.4 | async-start | bytes 131072 | tf_op jit(solution)/shard_map/gain/all_to_all | solution.py:287

commit v12 on v11

--- a/solution.py
+++ b/solution.py
@@ -199,17 +199,19 @@
     )(place, parts)
 
 
-def pack_kernel(core, own_ref, got_ref, out_ref):
+def pack_kernel(width, core, own_ref, got_ref, out_ref):
     half = out_ref.shape[2]
-    cols = pl.ds(pl.multiple_of(core[0] * half, 128), half)
-    out_ref[core[0]] = own_ref[:, cols]
-    out_ref[1 - core[0]] = got_ref[:, cols]
-
-
-def pack_patches(own, got, core):
+    for c, ref in ((core[0], own_ref), (1 - core[0], got_ref)):
+        for p in range(half // width):
+            cols = pl.ds(pl.multiple_of(core[0] * half + p * width, 128), width)
+            normed, _ = norm_of(ref[:, cols].astype(F32))
+            out_ref[c, :, p * width : (p + 1) * width] = normed.astype(BF16)
+
+
+def pack_patches(own, got, core, width):
     rows, cols = own.shape
     return pl.pallas_call(
-        pack_kernel,
+        functools.partial(pack_kernel, width),
         in_specs=[IN_SMEM, IN_VMEM, IN_VMEM],
         out_specs=IN_VMEM,
         out_shape=jax.ShapeDtypeStruct((NCO, rows, cols // NCO), BF16),
@@ -235,7 +237,7 @@
             for c in range(NCO):
                 for p in range(grad_ref.shape[4] // width):
                     cols = pl.ds(p * width, width)
-                    normed, _ = norm_of(patch_ref[k, c, :, cols].astype(F32))
+                    normed = patch_ref[k, c, :, cols].astype(F32)
                     grad = grad_ref[x, c, z, :, cols].astype(F32)
                     terms += jnp.sum(grad * normed, axis=0, keepdims=True)
     out_ref[...] = terms
@@ -307,7 +309,7 @@
         w_fc1_t = w_fc1.T
 
     with jax.named_scope("patches"):
-        patches = pack_patches(patch_in, beside, core)
+        patches = pack_patches(patch_in, beside, core, norm_gain.shape[0])
 
     def tie(value, first):
         return lax.optimization_barrier((value, first))[0]

time: 154 us -> 154 us (level)
  no operation moved by 1% of the time
where the time goes in v12:
time: 154 us; the launch traced here: 153 us
  starting transfers between devices  85.9 us (56%)
  waiting for transfers between devices  34.2 us (22%)
  blocking collectives  15.3 us (10%)
  Pallas kernels  12.8 us (8%)
  local copies, waits for them, and re-layouts  2.99 us (2%)
    ppermute x8, starting transfers between devices, swap(): return lax.ppermute(value, axis, [(0, 1), (1, 0)])  39.8 us
    all_to_all x2, starting transfers between devices, sum_over(): return jnp.sum(lax.all_to_all(rows, axes, 0, 0, tiled=True), axis=0)  22.7 us
    psum x1, blocking collectives, local(): terms = lax.psum(terms, 'y')  15.3 us
    all_to_all x1, waiting for transfers between devices, local(): parts = lax.all_to_all(sums, 'x', 0, 0, tiled=True)  13.1 us
    all_to_all x1, waiting for transfers between devices, local(): lax.all_to_all(outgoing, CTX, 0, 0, tiled=True).reshape(group, depth // ctx)  10.2 us
    all_to_all x1, starting transfers between devices, local(): lax.all_to_all(outgoing, CTX, 0, 0, tiled=True).reshape(group, depth // ctx)  8.08 us
    ppermute x3, starting transfers between devices, local(): lax.ppermute(patches, 'x', [(i, (i - d) % NX) for i in range(NX)])  7.81 us
    ppermute x8, waiting for transfers between devices, swap(): return lax.ppermute(value, axis, [(0, 1), (1, 0)])  6.41 us
  transfers between devices with their start and end apart: 16, of which 8 were waited for; matrix products, arithmetic and copies ran while one was open for 2% of the time, Pallas kernels for 5%

profile of v12, /device:TPU:1, one launch (start us, length us, event | category | flops | bytes accessed | tf_op | source)
XLA Modules:
  0.0 153.0 jit_solution(1507167436607987418)
XLA Ops:
  0.6 12.4 %collective-permute-start = (bf16[5120,512]{1,0:T(8,128)(2,1)}, bf16[5120,512]{1,0:T(8,128)(2,1)}, u32[]{:S(2)}, u32[]{:S(2)}) collective-permute-start(bf16[5120,512]{1,0:T(8,128)(2,1)} %param.10), channel_id=1, source_target_pairs={{0,1},{1,0},{2,3},{3,2},{4,5},{5,4},{6,7},{7,6},{8,9},{9,8},{10,11... | collective-permute-start | bytes 15728648 | tf_op jit(solution)/shard_map/weights/ppermute | solution.py:41
  13.1 1.7 %copy.18 = bf16[2,16,8,512]{3,2,0,1:T(8,128)(2,1)} copy(bf16[2,16,8,512]{3,2,1,0:T(8,128)(2,1)} %bitcast.32) | data formatting | bytes 524288 | tf_op jit(solution)/shard_map/tokens/reshape | solution.py:302
  14.8 8.1 %all-to-all-start = ((bf16[16,16,512]{2,1,0:T(8,128)(2,1)}), bf16[16,16,512]{2,1,0:T(8,128)(2,1)S(1)}, u32[]{:S(2)}, u32[]{:S(2)}) async-start(bf16[16,16,512]{2,1,0:T(8,128)(2,1)} %bitcast.22), calls=%async_computation | async-start | bytes 524288 | tf_op jit(solution)/shard_map/tokens/all_to_all | solution.py:303
  22.8 2.0 %collective-permute-start.1 = (bf16[16,5120]{1,0:T(8,128)(2,1)}, bf16[16,5120]{1,0:T(8,128)(2,1)S(1)}, u32[]{:S(2)}, u32[]{:S(2)}) collective-permute-start(bf16[16,5120]{1,0:T(8,128)(2,1)} %patch_ref.1), channel_id=1, source_target_pairs={{0,1},{1,0},{2,3},{3,2},{4,5},{5,4},{6,7},{7,6},{8,9},{9,8},{10,11... | collective-permute-start | bytes 491528 | tf_op jit(solution)/shard_map/tokens/ppermute | solution.py:41
  24.9 1.5 collective-permute-done.1.got_ref
  26.3 10.2 %all-to-all-done = bf16[16,16,512]{2,1,0:T(8,128)(2,1)S(1)} async-done(((bf16[16,16,512]{2,1,0:T(8,128)(2,1)}), bf16[16,16,512]{2,1,0:T(8,128)(2,1)S(1)}, u32[]{:S(2)}, u32[]{:S(2)}) %all-to-all-start) | async-done | bytes 262176 | tf_op jit(solution)/shard_map/tokens/all_to_all | solution.py:303
  36.6 2.9 %collective-permute-start.2 = (bf16[256,512]{1,0:T(8,128)(2,1)S(1)}, bf16[256,512]{1,0:T(8,128)(2,1)S(1)}, u32[]{:S(2)}, u32[]{:S(2)}) collective-permute-start(bf16[256,512]{1,0:T(8,128)(2,1)S(1)} %bitcast.25), channel_id=1, source_target_pairs={{0,1},{1,0},{2,3},{3,2},{4,5},{5,4},{6,7},{7,6},{8,9},{9,8},{10,11... | collective-permute-start | bytes 786440 | tf_op jit(solution)/shard_map/tokens/ppermute | solution.py:41
  39.5 1.1 collective-permute-done.2.got_t
  40.6 0.0 collective-permute-done
  40.7 5.3 %hidden_part.1 = bf16[4,2,320,256]{3,2,1,0:T(8,128)(2,1)} custom-call(s32[1]{0:T(128)} %bitcast.1.core.place, bf16[4,2,2,320,512]{4,3,2,1,0:T(8,128)(2,1)} %bitcast.29, bf16[4,2,2,320,512]{4,3,2,1,0:T(8,128)(2,1)} %bitcast.3.got_w, bf16[256,512]{1,0:T(8,128)(2,1)S(1)} %bitcast.26, bf16[256,512]{1,0:T(8,128)(2,1)S(1)} %collective-permute-done.2.got_t), custom_call_target="tpu_custom_call" | custom-call | flops 1 | bytes 1 | tf_op jit(solution)/shard_map/hidden/hidden_part/pallas_call | solution.py:65
  45.9 3.5 %all-to-all-start.1 = ((bf16[4,2,320,256]{3,2,1,0:T(8,128)(2,1)}), bf16[4,2,320,256]{3,2,1,0:T(8,128)(2,1)S(1)}, u32[]{:S(2)}, u32[]{:S(2)}) async-start(bf16[4,2,320,256]{3,2,1,0:T(8,128)(2,1)} %hidden_part.1), calls=%async_computation.1 | async-start | bytes 2621440 | tf_op jit(solution)/shard_map/hidden/all_to_all | solution.py:319
  49.5 2.3 %collective-permute-start.5 = (bf16[320,5120]{1,0:T(8,128)(2,1)}, bf16[320,5120]{1,0:T(8,128)(2,1)}, u32[]{:S(2)}, u32[]{:S(2)}) collective-permute-start(bf16[320,5120]{1,0:T(8,128)(2,1)} %bitcast.30), channel_id=1, source_target_pairs={{0,1},{1,0},{2,3},{3,2},{4,5},{5,4},{6,7},{7,6},{8,9},{9,8},{10,11... | collective-permute-start | bytes 9830408 | tf_op jit(solution)/shard_map/hidden/ppermute | solution.py:41
  51.8 0.1 pack_patches.1
  51.9 1.9 %collective-permute-start.6 = (bf16[2,16,2560]{2,1,0:T(8,128)(2,1)S(1)}, bf16[2,16,2560]{2,1,0:T(8,128)(2,1)S(1)}, u32[]{:S(2)}, u32[]{:S(2)}) collective-permute-start(bf16[2,16,2560]{2,1,0:T(8,128)(2,1)S(1)} %pack_patches.1), channel_id=1, source_target_pairs={{0,2},{2,0},{1,3},{3,1},{4,6},{6,4},{5,7},{7,5},{8,10},{10,8},{9,1... | collective-permute-start | bytes 491528 | tf_op jit(solution)/shard_map/hidden/ppermute | solution.py:41
  53.9 0.1 fusion.3.slope_ref
  54.0 13.1 %all-to-all-done.1.v_ref = bf16[4,2,320,256]{3,2,1,0:T(8,128)(2,1)S(1)} async-done(((bf16[4,2,320,256]{3,2,1,0:T(8,128)(2,1)}), bf16[4,2,320,256]{3,2,1,0:T(8,128)(2,1)S(1)}, u32[]{:S(2)}, u32[]{:S(2)}) %all-to-all-start.1) | async-done | bytes 1310752 | tf_op jit(solution)/shard_map/hidden/all_to_all | solution.py:319
  67.1 0.1 sum_parts.1
  67.2 1.9 %collective-permute-start.3 = (bf16[320,256]{1,0:T(8,128)(2,1)S(1)}, bf16[320,256]{1,0:T(8,128)(2,1)S(1)}, u32[]{:S(2)}, u32[]{:S(2)}) collective-permute-start(bf16[320,256]{1,0:T(8,128)(2,1)S(1)} %sum_parts.1), channel_id=1, source_target_pairs={{0,2},{2,0},{1,3},{3,1},{4,6},{6,4},{5,7},{7,5},{8,10},{10,8},{9,1... | collective-permute-start | bytes 491528 | tf_op jit(solution)/shard_map/hidden/ppermute | solution.py:41
  69.1 0.0 collective-permute-done.6
  69.2 0.0 copy-start.1
  69.2 2.8 %collective-permute-start.7 = (bf16[2,2,16,2560]{3,2,1,0:T(8,128)(2,1)S(1)}, bf16[2,2,16,2560]{3,2,1,0:T(8,128)(2,1)S(1)}, u32[]{:S(2)}, u32[]{:S(2)}) collective-permute-start(bf16[2,2,16,2560]{3,2,1,0:T(8,128)(2,1)S(1)} %pad_maximum_fusion.refs_0_), channel_id=1, source_target_pairs={{0,12},{4,0},{8,4},{12,8},{1,13},{5,1},{9,5},{13,9},{2,14},{6,2},{... | collective-permute-start | bytes 983048 | tf_op jit(solution)/shard_map/hidden/ppermute | solution.py:327
  72.0 3.1 %collective-permute-start.8 = (bf16[2,2,16,2560]{3,2,1,0:T(8,128)(2,1)S(1)}, bf16[2,2,16,2560]{3,2,1,0:T(8,128)(2,1)S(1)}, u32[]{:S(2)}, u32[]{:S(2)}) collective-permute-start(bf16[2,2,16,2560]{3,2,1,0:T(8,128)(2,1)S(1)} %pad_maximum_fusion.refs_0_), channel_id=1, source_target_pairs={{0,8},{4,12},{8,0},{12,4},{1,9},{5,13},{9,1},{13,5},{2,10},{6,14},... | collective-permute-start | bytes 983048 | tf_op jit(solution)/shard_map/hidden/ppermute | solution.py:327
  75.1 1.9 %collective-permute-start.9 = (bf16[2,2,16,2560]{3,2,1,0:T(8,128)(2,1)S(1)}, bf16[2,2,16,2560]{3,2,1,0:T(8,128)(2,1)S(1)}, u32[]{:S(2)}, u32[]{:S(2)}) collective-permute-start(bf16[2,2,16,2560]{3,2,1,0:T(8,128)(2,1)S(1)} %pad_maximum_fusion.refs_0_), channel_id=1, source_target_pairs={{0,4},{4,8},{8,12},{12,0},{1,5},{5,9},{9,13},{13,1},{2,6},{6,10},{... | collective-permute-start | bytes 983048 | tf_op jit(solution)/shard_map/hidden/ppermute | solution.py:327
  77.0 2.8 %collective-permute-done.3.v_ref = bf16[320,256]{1,0:T(8,128)(2,1)S(1)} collective-permute-done((bf16[320,256]{1,0:T(8,128)(2,1)S(1)}, bf16[320,256]{1,0:T(8,128)(2,1)S(1)}, u32[]{:S(2)}, u32[]{:S(2)}) %collective-permute-start.3) | collective-permute-done | bytes 163872 | tf_op jit(solution)/shard_map/hidden/ppermute | solution.py:41
  79.9 0.3 act_rows.1.own_a
  80.3 6.6 %collective-permute-start.4 = (bf16[4,2,2,16,320]{4,3,2,1,0:T(8,128)(2,1)S(1)}, bf16[4,2,2,16,320]{4,3,2,1,0:T(8,128)(2,1)S(1)}, u32[]{:S(2)}, u32[]{:S(2)}) collective-permute-start(bf16[4,2,2,16,320]{4,3,2,1,0:T(8,128)(2,1)S(1)} %act_rows.1.own_a), channel_id=1, source_target_pairs={{0,1},{1,0},{2,3},{3,2},{4,5},{5,4},{6,7},{7,6},{8,9},{9,8},{10,11... | collective-permute-start | bytes 491528 | tf_op jit(solution)/shard_map/merged/ppermute | solution.py:41
  86.9 0.1 pad_add_fusion.place
  86.9 0.0 collective-permute-done.5.got_w
  86.9 1.0 collective-permute-done.4.got_a
  87.9 4.0 %merged_part.1.grad_ref = bf16[4,2,2,16,2560]{4,3,2,1,0:T(8,128)(2,1)} custom-call(s32[1]{0:T(128)} %bitcast.1.core.place, bf16[4,2,2,16,320]{4,3,2,1,0:T(8,128)(2,1)S(1)} %act_rows.1.own_a, bf16[4,2,2,16,320]{4,3,2,1,0:T(8,128)(2,1)S(1)} %collective-permute-done.4.got_a, bf16[320,5120]{1,0:T(8,128)(2,1)} %bitcast.31, ...), custom_call_target="tpu_custom_call" | custom-call | flops 1 | bytes 1 | tf_op jit(solution)/shard_map/merged/merged_part/pallas_call | solution.py:166
  91.9 4.0 %all-to-all-start.2 = ((bf16[8,32,2560]{2,1,0:T(8,128)(2,1)}), bf16[8,32,2560]{2,1,0:T(8,128)(2,1)S(1)}, u32[]{:S(2)}, u32[]{:S(2)}) async-start(bf16[8,32,2560]{2,1,0:T(8,128)(2,1)} %bitcast.9), calls=%async_computation.2 | async-start | bytes 2621440 | tf_op jit(solution)/shard_map/merged/all_to_all | solution.py:332
  95.9 0.0 collective-permute-done.7.refs_1_
  95.9 0.0 collective-permute-done.8.refs_2_
  95.9 0.0 collective-permute-done.9.refs_3_
  95.9 2.0 %gain_terms.1 = f32[1,1280]{1,0:T(1,128)S(1)} custom-call(s32[2]{0:T(128)S(1)} %pad_add_fusion.place, bf16[4,2,2,16,2560]{4,3,2,1,0:T(8,128)(2,1)} %merged_part.1.grad_ref, bf16[2,2,16,2560]{3,2,1,0:T(8,128)(2,1)S(1)} %pad_maximum_fusion.refs_0_, bf16[2,2,16,2560]{3,2,1,0:T(8,128)(2,1)S(1)} %collective-permute-done.7.refs_1_, ...), custom_call_target="tpu_custom_call" | custom-call | flops 20000000000 | bytes 1 | tf_op jit(solution)/shard_map/merged/gain_terms/pallas_call | solution.py:247
  97.9 15.3 %psum.7 = f32[10,128]{1,0:T(8,128)S(1)} all-reduce(f32[10,128]{1,0:T(8,128)S(1)} %bitcast.34), channel_id=1, replica_groups=mesh['y'=8,'zl'=6,'x'=4,'zh'=2,'co'=2] {'y'}, use_global_device_ids=true, to_apply=%region_0.0 | all-reduce | flops 1280 | bytes 10240 | tf_op jit(solution)/shard_map/merged/psum | solution.py:337
  113.3 0.6 all-to-all-done.2
  113.8 0.1 sum_halves.1
  113.9 0.6 broadcast_in_dim.4
  114.6 11.5 %all-to-all-start.3 = ((f32[12,10,128]{2,1,0:T(8,128)}), f32[12,10,128]{2,1,0:T(8,128)S(1)}, u32[]{:S(2)}, u32[]{:S(2)}) async-start(f32[12,10,128]{2,1,0:T(8,128)} %broadcast_in_dim.4), calls=%async_computation.3 | async-start | bytes 196608 | tf_op jit(solution)/shard_map/gain/all_to_all | solution.py:289
  126.1 9.6 %collective-permute-start.10 = (bf16[2,16,2560]{2,1,0:T(8,128)(2,1)S(1)}, bf16[2,16,2560]{2,1,0:T(8,128)(2,1)S(1)}, u32[]{:S(2)}, u32[]{:S(2)}) collective-permute-start(bf16[2,16,2560]{2,1,0:T(8,128)(2,1)S(1)} %sum_halves.1), channel_id=1, source_target_pairs={{0,2},{2,0},{1,3},{3,1},{4,6},{6,4},{5,7},{7,5},{8,10},{10,8},{9,1... | collective-permute-start | bytes 491528 | tf_op jit(solution)/shard_map/merged/ppermute | solution.py:41
  135.8 0.0 all-to-all-done.3
  135.8 0.6 broadcast_in_dim.5
  136.4 11.1 %all-to-all-start.4 = ((f32[8,10,128]{2,1,0:T(8,128)}), f32[8,10,128]{2,1,0:T(8,128)S(1)}, u32[]{:S(2)}, u32[]{:S(2)}) async-start(f32[8,10,128]{2,1,0:T(8,128)} %broadcast_in_dim.5), calls=%async_computation.4 | async-start | bytes 131072 | tf_op jit(solution)/shard_map/gain/all_to_all | solution.py:289
  147.6 0.0 collective-permute-done.10.got_ref
  147.6 0.9 norm_part.1
  148.5 3.9 %all-to-all-done.4 = f32[8,10,128]{2,1,0:T(8,128)S(1)} async-done(((f32[8,10,128]{2,1,0:T(8,128)}), f32[8,10,128]{2,1,0:T(8,128)S(1)}, u32[]{:S(2)}, u32[]{:S(2)}) %all-to-all-start.4) | async-done | bytes 40992 | tf_op jit(solution)/shard_map/gain/all_to_all | solution.py:289
  152.4 0.6 multiply_bitcast_fusion
  (13 shorter events, 0.1 us)
Async XLA Ops:
  0.6 40.0 %collective-permute-start = (bf16[5120,512]{1,0:T(8,128)(2,1)}, bf16[5120,512]{1,0:T(8,128)(2,1)}, u32[]{:S(2)}, u32[]{:S(2)}) collective-permute-start(bf16[5120,512]{1,0:T(8,128)(2,1)} %param.10), channel_id=1, source_target_pairs={{0,1},{1,0},{2,3},{3,2},{4,5},{5,4},{6,7},{7,6},{8,9},{9,8},{10,11... | collective-permute-start | bytes 15728648 | tf_op jit(solution)/shard_map/weights/ppermute | solution.py:41
  14.8 21.8 %all-to-all-start = ((bf16[16,16,512]{2,1,0:T(8,128)(2,1)}), bf16[16,16,512]{2,1,0:T(8,128)(2,1)S(1)}, u32[]{:S(2)}, u32[]{:S(2)}) async-start(bf16[16,16,512]{2,1,0:T(8,128)(2,1)} %bitcast.22), calls=%async_computation | async-start | bytes 524288 | tf_op jit(solution)/shard_map/tokens/all_to_all | solution.py:303
  22.8 3.5 %collective-permute-start.1 = (bf16[16,5120]{1,0:T(8,128)(2,1)}, bf16[16,5120]{1,0:T(8,128)(2,1)S(1)}, u32[]{:S(2)}, u32[]{:S(2)}) collective-permute-start(bf16[16,5120]{1,0:T(8,128)(2,1)} %patch_ref.1), channel_id=1, source_target_pairs={{0,1},{1,0},{2,3},{3,2},{4,5},{5,4},{6,7},{7,6},{8,9},{9,8},{10,11... | collective-permute-start | bytes 491528 | tf_op jit(solution)/shard_map/tokens/ppermute | solution.py:41
  36.6 4.1 %collective-permute-start.2 = (bf16[256,512]{1,0:T(8,128)(2,1)S(1)}, bf16[256,512]{1,0:T(8,128)(2,1)S(1)}, u32[]{:S(2)}, u32[]{:S(2)}) collective-permute-start(bf16[256,512]{1,0:T(8,128)(2,1)S(1)} %bitcast.25), channel_id=1, source_target_pairs={{0,1},{1,0},{2,3},{3,2},{4,5},{5,4},{6,7},{7,6},{8,9},{9,8},{10,11... | collective-permute-start | bytes 786440 | tf_op jit(solution)/shard_map/tokens/ppermute | solution.py:41
  40.6 11.1 %copy-start = (bf16[16,5120]{1,0:T(8,128)(2,1)S(1)}, bf16[16,5120]{1,0:T(8,128)(2,1)}, u32[]{:S(2)}) copy-start(bf16[16,5120]{1,0:T(8,128)(2,1)} %patch_ref.1) | copy-start | bytes 491524
  40.6 13.2 %copy-start.2 = (bf16[320,256]{1,0:T(8,128)(2,1)S(1)}, bf16[320,256]{1,0:T(8,128)(2,1)}, u32[]{:S(2)}) copy-start(bf16[320,256]{1,0:T(8,128)(2,1)} %param.8) | copy-start | bytes 491524
  45.9 21.2 %all-to-all-start.1 = ((bf16[4,2,320,256]{3,2,1,0:T(8,128)(2,1)}), bf16[4,2,320,256]{3,2,1,0:T(8,128)(2,1)S(1)}, u32[]{:S(2)}, u32[]{:S(2)}) async-start(bf16[4,2,320,256]{3,2,1,0:T(8,128)(2,1)} %hidden_part.1), calls=%async_computation.1 | async-start | bytes 2621440 | tf_op jit(solution)/shard_map/hidden/all_to_all | solution.py:319
  49.5 37.5 %collective-permute-start.5 = (bf16[320,5120]{1,0:T(8,128)(2,1)}, bf16[320,5120]{1,0:T(8,128)(2,1)}, u32[]{:S(2)}, u32[]{:S(2)}) collective-permute-start(bf16[320,5120]{1,0:T(8,128)(2,1)} %bitcast.30), channel_id=1, source_target_pairs={{0,1},{1,0},{2,3},{3,2},{4,5},{5,4},{6,7},{7,6},{8,9},{9,8},{10,11... | collective-permute-start | bytes 9830408 | tf_op jit(solution)/shard_map/hidden/ppermute | solution.py:41
  51.9 17.2 %collective-permute-start.6 = (bf16[2,16,2560]{2,1,0:T(8,128)(2,1)S(1)}, bf16[2,16,2560]{2,1,0:T(8,128)(2,1)S(1)}, u32[]{:S(2)}, u32[]{:S(2)}) collective-permute-start(bf16[2,16,2560]{2,1,0:T(8,128)(2,1)S(1)} %pack_patches.1), channel_id=1, source_target_pairs={{0,2},{2,0},{1,3},{3,1},{4,6},{6,4},{5,7},{7,5},{8,10},{10,8},{9,1... | collective-permute-start | bytes 491528 | tf_op jit(solution)/shard_map/hidden/ppermute | solution.py:41
  67.2 12.7 %collective-permute-start.3 = (bf16[320,256]{1,0:T(8,128)(2,1)S(1)}, bf16[320,256]{1,0:T(8,128)(2,1)S(1)}, u32[]{:S(2)}, u32[]{:S(2)}) collective-permute-start(bf16[320,256]{1,0:T(8,128)(2,1)S(1)} %sum_parts.1), channel_id=1, source_target_pairs={{0,2},{2,0},{1,3},{3,1},{4,6},{6,4},{5,7},{7,5},{8,10},{10,8},{9,1... | collective-permute-start | bytes 491528 | tf_op jit(solution)/shard_map/hidden/ppermute | solution.py:41
  69.2 10.7 %copy-start.1 = (s32[256]{0:T(256)S(1)}, s32[256]{0:T(256)}, u32[]{:S(2)}) copy-start(s32[256]{0:T(256)} %param.13) | copy-start | bytes 3076
  69.2 26.7 %collective-permute-start.7 = (bf16[2,2,16,2560]{3,2,1,0:T(8,128)(2,1)S(1)}, bf16[2,2,16,2560]{3,2,1,0:T(8,128)(2,1)S(1)}, u32[]{:S(2)}, u32[]{:S(2)}) collective-permute-start(bf16[2,2,16,2560]{3,2,1,0:T(8,128)(2,1)S(1)} %pad_maximum_fusion.refs_0_), channel_id=1, source_target_pairs={{0,12},{4,0},{8,4},{12,8},{1,13},{5,1},{9,5},{13,9},{2,14},{6,2},{... | collective-permute-start | bytes 983048 | tf_op jit(solution)/shard_map/hidden/ppermute | solution.py:327
  72.0 23.9 %collective-permute-start.8 = (bf16[2,2,16,2560]{3,2,1,0:T(8,128)(2,1)S(1)}, bf16[2,2,16,2560]{3,2,1,0:T(8,128)(2,1)S(1)}, u32[]{:S(2)}, u32[]{:S(2)}) collective-permute-start(bf16[2,2,16,2560]{3,2,1,0:T(8,128)(2,1)S(1)} %pad_maximum_fusion.refs_0_), channel_id=1, source_target_pairs={{0,8},{4,12},{8,0},{12,4},{1,9},{5,13},{9,1},{13,5},{2,10},{6,14},... | collective-permute-start | bytes 983048 | tf_op jit(solution)/shard_map/hidden/ppermute | solution.py:327
  75.1 20.8 %collective-permute-start.9 = (bf16[2,2,16,2560]{3,2,1,0:T(8,128)(2,1)S(1)}, bf16[2,2,16,2560]{3,2,1,0:T(8,128)(2,1)S(1)}, u32[]{:S(2)}, u32[]{:S(2)}) collective-permute-start(bf16[2,2,16,2560]{3,2,1,0:T(8,128)(2,1)S(1)} %pad_maximum_fusion.refs_0_), channel_id=1, source_target_pairs={{0,4},{4,8},{8,12},{12,0},{1,5},{5,9},{9,13},{13,1},{2,6},{6,10},{... | collective-permute-start | bytes 983048 | tf_op jit(solution)/shard_map/hidden/ppermute | solution.py:327
  80.3 7.6 %collective-permute-start.4 = (bf16[4,2,2,16,320]{4,3,2,1,0:T(8,128)(2,1)S(1)}, bf16[4,2,2,16,320]{4,3,2,1,0:T(8,128)(2,1)S(1)}, u32[]{:S(2)}, u32[]{:S(2)}) collective-permute-start(bf16[4,2,2,16,320]{4,3,2,1,0:T(8,128)(2,1)S(1)} %act_rows.1.own_a), channel_id=1, source_target_pairs={{0,1},{1,0},{2,3},{3,2},{4,5},{5,4},{6,7},{7,6},{8,9},{9,8},{10,11... | collective-permute-start | bytes 491528 | tf_op jit(solution)/shard_map/merged/ppermute | solution.py:41
  91.9 21.9 %all-to-all-start.2 = ((bf16[8,32,2560]{2,1,0:T(8,128)(2,1)}), bf16[8,32,2560]{2,1,0:T(8,128)(2,1)S(1)}, u32[]{:S(2)}, u32[]{:S(2)}) async-start(bf16[8,32,2560]{2,1,0:T(8,128)(2,1)} %bitcast.9), calls=%async_computation.2 | async-start | bytes 2621440 | tf_op jit(solution)/shard_map/merged/all_to_all | solution.py:332
  95.9 39.8 %copy-start.3 = (f32[1280]{0:T(1024)S(1)}, f32[1280]{0:T(1024)}, u32[]{:S(2)}) copy-start(f32[1280]{0:T(1024)} %param.12) | copy-start | bytes 15364
  114.6 21.2 %all-to-all-start.3 = ((f32[12,10,128]{2,1,0:T(8,128)}), f32[12,10,128]{2,1,0:T(8,128)S(1)}, u32[]{:S(2)}, u32[]{:S(2)}) async-start(f32[12,10,128]{2,1,0:T(8,128)} %broadcast_in_dim.4), calls=%async_computation.3 | async-start | bytes 196608 | tf_op jit(solution)/shard_map/gain/all_to_all | solution.py:289
  126.1 21.5 %collective-permute-start.10 = (bf16[2,16,2560]{2,1,0:T(8,128)(2,1)S(1)}, bf16[2,16,2560]{2,1,0:T(8,128)(2,1)S(1)}, u32[]{:S(2)}, u32[]{:S(2)}) collective-permute-start(bf16[2,16,2560]{2,1,0:T(8,128)(2,1)S(1)} %sum_halves.1), channel_id=1, source_target_pairs={{0,2},{2,0},{1,3},{3,1},{4,6},{6,4},{5,7},{7,5},{8,10},{10,8},{9,1... | collective-permute-start | bytes 491528 | tf_op jit(solution)/shard_map/merged/ppermute | solution.py:41
  136.4 16.0 %all-to-all-start.4 = ((f32[8,10,128]{2,1,0:T(8,128)}), f32[8,10,128]{2,1,0:T(8,128)S(1)}, u32[]{:S(2)}, u32[]{:S(2)}) async-start(f32[8,10,128]{2,1,0:T(8,128)} %broadcast_in_dim.5), calls=%async_computation.4 | async-start | bytes 131072 | tf_op jit(solution)/shard_map/gain/all_to_all | solution.py:289
